TPU v7x, 512 devices: a whole 4x8x8 slice. The times are simulated.
512 devices in a mesh: section: 16 (over z, core), dp: 4 (over x), tp: 8 (over y).
Axes of the slice: x: 4, y: 8, z: 8, core: 2. Of those that a mesh axis runs over, the one named last changes fastest.
Arguments:
- hidden_in: bfloat16 [4, 128, 4096], P(None, 'dp', 'tp'), may hold values from -6 to 6
- rotation: bfloat16 [4096, 4096], P(('section', 'dp'), 'tp'), may hold values from -0.09375 to 0.09375
- proj: bfloat16 [16, 4096, 4096], P('section', None, 'tp'), may hold values from -0.09375 to 0.09375
- norm_gain: float32 [16, 4096], P('section'), may hold values from 0.5 to 8
- quant_exp: int32 [16, 32], P('section', 'tp'), may hold values from 0 to 7
Outputs:
- rotation_grad: float32 [4096, 4096], P(('section', 'dp'), 'tp')
- loss: float32 [], replicated
All inputs are finite; a program needn't handle non-finite values.
Results may differ from a plain program's by a relative error of at most 0.04.
Values may be sent and summed in bfloat16 or wider, within the bound.
No kernel may reach another device: no remote copies, remote signals or barrier semaphores. Data moves between devices by JAX's collectives and lax.ppermute only.
A program may use at most 64 MiB of HBM per device.

v0:
```python
import math

import jax
import jax.numpy as jnp
from jax import lax
from jax.sharding import PartitionSpec as P

D = 4096
GROUP = 128


norm_eps = 1e-05
full_turn = 2.0 * math.pi


def from_behind(value, axis, steps):
    count = lax.axis_size(axis)
    leading, last = (max(0, -steps), min(count, count - steps))
    return lax.ppermute(value, axis, [(source, source + steps) for source in range(leading, last)])


def quantize(values, scale):
    ratio = values / scale
    stair = ratio - jnp.sin(full_turn * ratio) / full_turn
    return scale * jnp.clip(stair, -8.0, 7.0)


def staircase_slope(values, scale):
    ratio = values / scale
    stair = ratio - jnp.sin(full_turn * ratio) / full_turn
    inside = (stair > -8.0) & (stair < 7.0)
    return jnp.where(inside, 1.0 - jnp.cos(full_turn * ratio), 0.0)


def local(hidden_in, rotation, proj, norm_gain, quant_exp):
    section_count = lax.axis_size("section")
    replicas = lax.axis_size("dp")
    section_pos = lax.axis_index("section")
    micro_count, tok_rows, part_cols = hidden_in.shape
    rot_cols = lax.all_gather(rotation, ("section", "dp"), axis=0, tiled=True)
    weight_cols = proj[0]
    gain_row = norm_gain[0]
    scale_cols = jnp.repeat(jnp.exp2(quant_exp[0].astype(jnp.float32) * 0.25) * 0.125, GROUP)

    def advance(step_num, carry):
        inbox, kept_normed, kept_rotated = carry
        mb_index = step_num - section_pos
        is_valid = (mb_index >= 0) & (mb_index < micro_count)
        slot_index = jnp.clip(mb_index, 0, micro_count - 1)
        first_rows = lax.dynamic_index_in_dim(
            hidden_in, jnp.clip(step_num, 0, micro_count - 1), 0, keepdims=False
        )
        slice_in = jnp.where(section_pos == 0, first_rows, inbox)
        full_rows = lax.all_gather(slice_in, "tp", axis=1, tiled=True)
        wide_rows = full_rows.astype(jnp.float32)
        mean_square = jnp.mean(wide_rows * wide_rows, axis=-1, keepdims=True)
        normed = (wide_rows * lax.rsqrt(mean_square + norm_eps) * gain_row).astype(jnp.bfloat16)
        rotated = lax.cond(
            is_valid,
            lambda: jnp.dot(normed, rot_cols, preferred_element_type=jnp.float32),
            lambda: jnp.zeros((tok_rows, part_cols), jnp.float32),
        )
        quantized = quantize(rotated, scale_cols).astype(jnp.bfloat16)
        quant_full = lax.all_gather(quantized, "tp", axis=1, tiled=True)
        update = lax.cond(
            is_valid,
            lambda: jnp.dot(quant_full, weight_cols, preferred_element_type=jnp.float32),
            lambda: jnp.zeros((tok_rows, part_cols), jnp.float32),
        )
        outgoing = (slice_in.astype(jnp.float32) + update).astype(jnp.bfloat16)
        old_normed = lax.dynamic_index_in_dim(kept_normed, slot_index, 0, keepdims=False)
        kept_normed = lax.dynamic_update_index_in_dim(
            kept_normed, jnp.where(is_valid, normed, old_normed), slot_index, 0
        )
        old_rotated = lax.dynamic_index_in_dim(kept_rotated, slot_index, 0, keepdims=False)
        kept_rotated = lax.dynamic_update_index_in_dim(
            kept_rotated, jnp.where(is_valid, rotated, old_rotated), slot_index, 0
        )
        inbox = from_behind(outgoing, "section", 1)
        return (inbox, kept_normed, kept_rotated)

    start_carry = (
        jnp.zeros((tok_rows, part_cols), jnp.bfloat16),
        jnp.zeros((micro_count, tok_rows, D), jnp.bfloat16),
        jnp.zeros((micro_count, tok_rows, part_cols), jnp.float32),
    )
    inbox, kept_normed, kept_rotated = lax.fori_loop(
        0, section_count + micro_count - 1, advance, start_carry
    )
    rotated_all = kept_rotated.reshape(micro_count * tok_rows, part_cols)
    level = quantize(rotated_all, scale_cols)
    error_part = level - rotated_all
    grad_rot = (error_part * (staircase_slope(rotated_all, scale_cols) - 1.0)).astype(jnp.bfloat16)
    own_loss = jnp.sum(error_part * error_part)
    grad_all = lax.all_gather(grad_rot, "dp", axis=0, tiled=True)
    row_block = D // (section_count * replicas)
    blocks = kept_normed.reshape(micro_count * tok_rows, section_count, replicas, row_block)
    terms = jnp.einsum(
        "nkr,nc->krc",
        lax.all_to_all(blocks, "dp", split_axis=2, concat_axis=0, tiled=True)[:, :, 0, :],
        grad_all,
        preferred_element_type=jnp.float32,
    )
    terms = terms.reshape(section_count * row_block, part_cols)
    factor = 1.0 / math.sqrt(section_count * micro_count * tok_rows * replicas)
    norm_count = micro_count * tok_rows * replicas * D
    grad_share = lax.psum_scatter(
        terms.astype(jnp.bfloat16), "section", scatter_dimension=0, tiled=True
    ).astype(jnp.float32)
    loss_total = lax.psum(own_loss, ("section", "dp", "tp"))
    return (grad_share * factor, loss_total / norm_count)


def solution(mesh):
    placed = (
        P(None, "dp", "tp"),
        P(("section", "dp"), "tp"),
        P("section", None, "tp"),
        P("section", None),
        P("section", "tp"),
    )
    return jax.shard_map(
        local,
        mesh=mesh,
        in_specs=placed,
        out_specs=(P(("section", "dp"), "tp"), P()),
        check_vma=False,
    )
```

profile of v0, /device:TPU:1, one launch (start us, length us, event | category | flops | bytes accessed | tf_op | source)
XLA Modules:
  0.0 1371.9 jit_solution(11617710329207932234)
XLA Ops:
  8.6 93.8 %all-gather.2.cloned.1.call-done = bf16[4096,512]{1,0:T(8,128)(2,1)} async-done(((bf16[64,512]{1,0:T(8,128)(2,1)}), bf16[4096,512]{1,0:T(8,128)(2,1)}) %all-gather.2.cloned.1.call-update) | async-done | bytes 4194320 | tf_op jit(solution)/shard_map/all_gather | solution.py:40
  102.5 1109.0 %while.19 = (s32[]{:T(128)}, bf16[32,512]{1,0:T(8,128)(2,1)S(1)}, bf16[4,32,4096]{2,1,0:T(8,128)(2,1)S(1)}, f32[4,32,512]{2,1,0:T(8,128)S(1)}, pred[]{:T(512)}, ...) while((s32[]{:T(128)}, bf16[32,512]{1,0:T(8,128)(2,1)S(1)}, ...), condition=%wide.region_6.7_spmd.clone, body=%wide.region_0.6_spmd.clone.sunk | while | flops 269680704 | bytes 12276962 | solution.py:87
  103.3 19.5 %all_gather.28 = bf16[32,4096]{1,0:T(8,128)(2,1)S(1)} all-gather(bf16[32,512]{1,0:T(8,128)(2,1)S(1)} %bitcast_select_fusion.4), channel_id=1, replica_groups=mesh['section'=16,'dp'=4,'tp'=8] {'tp'}, dimensions={1}, use_global_device_ids=true | all-gather | bytes 294912 | tf_op jit(solution)/shard_map/while/body/eval_jaxpr/all_gather | solution.py:54
  124.3 18.8 %all_gather.29 = bf16[32,4096]{1,0:T(8,128)(2,1)S(1)} all-gather(bf16[32,512]{1,0:T(8,128)(2,1)S(1)} %multiply_convert_fusion.2), channel_id=1, replica_groups=mesh['section'=16,'dp'=4,'tp'=8] {'tp'}, dimensions={1}, use_global_device_ids=true | all-gather | bytes 294912 | tf_op jit(solution)/shard_map/while/body/eval_jaxpr/all_gather | solution.py:64
  143.1 14.8 %collective-permute-start = (bf16[32,512]{1,0:T(8,128)(2,1)S(1)}, bf16[32,512]{1,0:T(8,128)(2,1)S(1)}, u32[]{:S(2)}, u32[]{:S(2)}) collective-permute-start(bf16[32,512]{1,0:T(8,128)(2,1)S(1)} %add_convert_fusion.2), channel_id=1, source_target_pairs={{0,32},{32,64},{64,96},{96,128},{128,160},{160,192},{192,224},{224... | collective-permute-start | bytes 98312 | tf_op jit(solution)/shard_map/while/body/eval_jaxpr/ppermute | solution.py:19
  157.9 5.8 collective-permute-done
  164.5 18.8 %all_gather.28 = bf16[32,4096]{1,0:T(8,128)(2,1)S(1)} all-gather(bf16[32,512]{1,0:T(8,128)(2,1)S(1)} %bitcast_select_fusion.4), channel_id=1, replica_groups=mesh['section'=16,'dp'=4,'tp'=8] {'tp'}, dimensions={1}, use_global_device_ids=true | all-gather | bytes 294912 | tf_op jit(solution)/shard_map/while/body/eval_jaxpr/all_gather | solution.py:54
  187.8 18.6 %all_gather.29 = bf16[32,4096]{1,0:T(8,128)(2,1)S(1)} all-gather(bf16[32,512]{1,0:T(8,128)(2,1)S(1)} %multiply_convert_fusion.2), channel_id=1, replica_groups=mesh['section'=16,'dp'=4,'tp'=8] {'tp'}, dimensions={1}, use_global_device_ids=true | all-gather | bytes 294912 | tf_op jit(solution)/shard_map/while/body/eval_jaxpr/all_gather | solution.py:64
  209.4 5.6 collective-permute-start
  215.1 8.8 collective-permute-done
  224.6 18.9 %all_gather.28 = bf16[32,4096]{1,0:T(8,128)(2,1)S(1)} all-gather(bf16[32,512]{1,0:T(8,128)(2,1)S(1)} %bitcast_select_fusion.4), channel_id=1, replica_groups=mesh['section'=16,'dp'=4,'tp'=8] {'tp'}, dimensions={1}, use_global_device_ids=true | all-gather | bytes 294912 | tf_op jit(solution)/shard_map/while/body/eval_jaxpr/all_gather | solution.py:54
  248.0 18.5 %all_gather.29 = bf16[32,4096]{1,0:T(8,128)(2,1)S(1)} all-gather(bf16[32,512]{1,0:T(8,128)(2,1)S(1)} %multiply_convert_fusion.2), channel_id=1, replica_groups=mesh['section'=16,'dp'=4,'tp'=8] {'tp'}, dimensions={1}, use_global_device_ids=true | all-gather | bytes 294912 | tf_op jit(solution)/shard_map/while/body/eval_jaxpr/all_gather | solution.py:64
  269.5 8.6 collective-permute-start
  278.2 5.8 collective-permute-done
  284.7 18.8 %all_gather.28 = bf16[32,4096]{1,0:T(8,128)(2,1)S(1)} all-gather(bf16[32,512]{1,0:T(8,128)(2,1)S(1)} %bitcast_select_fusion.4), channel_id=1, replica_groups=mesh['section'=16,'dp'=4,'tp'=8] {'tp'}, dimensions={1}, use_global_device_ids=true | all-gather | bytes 294912 | tf_op jit(solution)/shard_map/while/body/eval_jaxpr/all_gather | solution.py:54
  308.0 18.6 %all_gather.29 = bf16[32,4096]{1,0:T(8,128)(2,1)S(1)} all-gather(bf16[32,512]{1,0:T(8,128)(2,1)S(1)} %multiply_convert_fusion.2), channel_id=1, replica_groups=mesh['section'=16,'dp'=4,'tp'=8] {'tp'}, dimensions={1}, use_global_device_ids=true | all-gather | bytes 294912 | tf_op jit(solution)/shard_map/while/body/eval_jaxpr/all_gather | solution.py:64
  329.6 11.6 collective-permute-start
  344.9 18.9 %all_gather.28 = bf16[32,4096]{1,0:T(8,128)(2,1)S(1)} all-gather(bf16[32,512]{1,0:T(8,128)(2,1)S(1)} %bitcast_select_fusion.4), channel_id=1, replica_groups=mesh['section'=16,'dp'=4,'tp'=8] {'tp'}, dimensions={1}, use_global_device_ids=true | all-gather | bytes 294912 | tf_op jit(solution)/shard_map/while/body/eval_jaxpr/all_gather | solution.py:54
  368.2 18.7 %all_gather.29 = bf16[32,4096]{1,0:T(8,128)(2,1)S(1)} all-gather(bf16[32,512]{1,0:T(8,128)(2,1)S(1)} %multiply_convert_fusion.2), channel_id=1, replica_groups=mesh['section'=16,'dp'=4,'tp'=8] {'tp'}, dimensions={1}, use_global_device_ids=true | all-gather | bytes 294912 | tf_op jit(solution)/shard_map/while/body/eval_jaxpr/all_gather | solution.py:64
  390.0 14.5 %collective-permute-start = (bf16[32,512]{1,0:T(8,128)(2,1)S(1)}, bf16[32,512]{1,0:T(8,128)(2,1)S(1)}, u32[]{:S(2)}, u32[]{:S(2)}) collective-permute-start(bf16[32,512]{1,0:T(8,128)(2,1)S(1)} %add_convert_fusion.2), channel_id=1, source_target_pairs={{0,32},{32,64},{64,96},{96,128},{128,160},{160,192},{192,224},{224... | collective-permute-start | bytes 98312 | tf_op jit(solution)/shard_map/while/body/eval_jaxpr/ppermute | solution.py:19
  406.2 19.1 %all_gather.28 = bf16[32,4096]{1,0:T(8,128)(2,1)S(1)} all-gather(bf16[32,512]{1,0:T(8,128)(2,1)S(1)} %bitcast_select_fusion.4), channel_id=1, replica_groups=mesh['section'=16,'dp'=4,'tp'=8] {'tp'}, dimensions={1}, use_global_device_ids=true | all-gather | bytes 294912 | tf_op jit(solution)/shard_map/while/body/eval_jaxpr/all_gather | solution.py:54
  426.7 19.2 %all_gather.29 = bf16[32,4096]{1,0:T(8,128)(2,1)S(1)} all-gather(bf16[32,512]{1,0:T(8,128)(2,1)S(1)} %multiply_convert_fusion.2), channel_id=1, replica_groups=mesh['section'=16,'dp'=4,'tp'=8] {'tp'}, dimensions={1}, use_global_device_ids=true | all-gather | bytes 294912 | tf_op jit(solution)/shard_map/while/body/eval_jaxpr/all_gather | solution.py:64
  446.0 21.6 %collective-permute-start = (bf16[32,512]{1,0:T(8,128)(2,1)S(1)}, bf16[32,512]{1,0:T(8,128)(2,1)S(1)}, u32[]{:S(2)}, u32[]{:S(2)}) collective-permute-start(bf16[32,512]{1,0:T(8,128)(2,1)S(1)} %add_convert_fusion.2), channel_id=1, source_target_pairs={{0,32},{32,64},{64,96},{96,128},{128,160},{160,192},{192,224},{224... | collective-permute-start | bytes 98312 | tf_op jit(solution)/shard_map/while/body/eval_jaxpr/ppermute | solution.py:19
  469.3 18.9 %all_gather.28 = bf16[32,4096]{1,0:T(8,128)(2,1)S(1)} all-gather(bf16[32,512]{1,0:T(8,128)(2,1)S(1)} %bitcast_select_fusion.4), channel_id=1, replica_groups=mesh['section'=16,'dp'=4,'tp'=8] {'tp'}, dimensions={1}, use_global_device_ids=true | all-gather | bytes 294912 | tf_op jit(solution)/shard_map/while/body/eval_jaxpr/all_gather | solution.py:54
  489.7 19.0 %all_gather.29 = bf16[32,4096]{1,0:T(8,128)(2,1)S(1)} all-gather(bf16[32,512]{1,0:T(8,128)(2,1)S(1)} %multiply_convert_fusion.2), channel_id=1, replica_groups=mesh['section'=16,'dp'=4,'tp'=8] {'tp'}, dimensions={1}, use_global_device_ids=true | all-gather | bytes 294912 | tf_op jit(solution)/shard_map/while/body/eval_jaxpr/all_gather | solution.py:64
  508.7 16.1 %collective-permute-start = (bf16[32,512]{1,0:T(8,128)(2,1)S(1)}, bf16[32,512]{1,0:T(8,128)(2,1)S(1)}, u32[]{:S(2)}, u32[]{:S(2)}) collective-permute-start(bf16[32,512]{1,0:T(8,128)(2,1)S(1)} %add_convert_fusion.2), channel_id=1, source_target_pairs={{0,32},{32,64},{64,96},{96,128},{128,160},{160,192},{192,224},{224... | collective-permute-start | bytes 98312 | tf_op jit(solution)/shard_map/while/body/eval_jaxpr/ppermute | solution.py:19
  526.6 19.3 %all_gather.28 = bf16[32,4096]{1,0:T(8,128)(2,1)S(1)} all-gather(bf16[32,512]{1,0:T(8,128)(2,1)S(1)} %bitcast_select_fusion.4), channel_id=1, replica_groups=mesh['section'=16,'dp'=4,'tp'=8] {'tp'}, dimensions={1}, use_global_device_ids=true | all-gather | bytes 294912 | tf_op jit(solution)/shard_map/while/body/eval_jaxpr/all_gather | solution.py:54
  547.4 18.7 %all_gather.29 = bf16[32,4096]{1,0:T(8,128)(2,1)S(1)} all-gather(bf16[32,512]{1,0:T(8,128)(2,1)S(1)} %multiply_convert_fusion.2), channel_id=1, replica_groups=mesh['section'=16,'dp'=4,'tp'=8] {'tp'}, dimensions={1}, use_global_device_ids=true | all-gather | bytes 294912 | tf_op jit(solution)/shard_map/while/body/eval_jaxpr/all_gather | solution.py:64
  566.2 15.7 %collective-permute-start = (bf16[32,512]{1,0:T(8,128)(2,1)S(1)}, bf16[32,512]{1,0:T(8,128)(2,1)S(1)}, u32[]{:S(2)}, u32[]{:S(2)}) collective-permute-start(bf16[32,512]{1,0:T(8,128)(2,1)S(1)} %add_convert_fusion.2), channel_id=1, source_target_pairs={{0,32},{32,64},{64,96},{96,128},{128,160},{160,192},{192,224},{224... | collective-permute-start | bytes 98312 | tf_op jit(solution)/shard_map/while/body/eval_jaxpr/ppermute | solution.py:19
  583.7 18.8 %all_gather.28 = bf16[32,4096]{1,0:T(8,128)(2,1)S(1)} all-gather(bf16[32,512]{1,0:T(8,128)(2,1)S(1)} %bitcast_select_fusion.4), channel_id=1, replica_groups=mesh['section'=16,'dp'=4,'tp'=8] {'tp'}, dimensions={1}, use_global_device_ids=true | all-gather | bytes 294912 | tf_op jit(solution)/shard_map/while/body/eval_jaxpr/all_gather | solution.py:54
  604.0 19.0 %all_gather.29 = bf16[32,4096]{1,0:T(8,128)(2,1)S(1)} all-gather(bf16[32,512]{1,0:T(8,128)(2,1)S(1)} %multiply_convert_fusion.2), channel_id=1, replica_groups=mesh['section'=16,'dp'=4,'tp'=8] {'tp'}, dimensions={1}, use_global_device_ids=true | all-gather | bytes 294912 | tf_op jit(solution)/shard_map/while/body/eval_jaxpr/all_gather | solution.py:64
  623.0 16.1 %collective-permute-start = (bf16[32,512]{1,0:T(8,128)(2,1)S(1)}, bf16[32,512]{1,0:T(8,128)(2,1)S(1)}, u32[]{:S(2)}, u32[]{:S(2)}) collective-permute-start(bf16[32,512]{1,0:T(8,128)(2,1)S(1)} %add_convert_fusion.2), channel_id=1, source_target_pairs={{0,32},{32,64},{64,96},{96,128},{128,160},{160,192},{192,224},{224... | collective-permute-start | bytes 98312 | tf_op jit(solution)/shard_map/while/body/eval_jaxpr/ppermute | solution.py:19
  640.9 18.6 %all_gather.28 = bf16[32,4096]{1,0:T(8,128)(2,1)S(1)} all-gather(bf16[32,512]{1,0:T(8,128)(2,1)S(1)} %bitcast_select_fusion.4), channel_id=1, replica_groups=mesh['section'=16,'dp'=4,'tp'=8] {'tp'}, dimensions={1}, use_global_device_ids=true | all-gather | bytes 294912 | tf_op jit(solution)/shard_map/while/body/eval_jaxpr/all_gather | solution.py:54
  661.0 19.0 %all_gather.29 = bf16[32,4096]{1,0:T(8,128)(2,1)S(1)} all-gather(bf16[32,512]{1,0:T(8,128)(2,1)S(1)} %multiply_convert_fusion.2), channel_id=1, replica_groups=mesh['section'=16,'dp'=4,'tp'=8] {'tp'}, dimensions={1}, use_global_device_ids=true | all-gather | bytes 294912 | tf_op jit(solution)/shard_map/while/body/eval_jaxpr/all_gather | solution.py:64
  680.1 16.2 %collective-permute-start = (bf16[32,512]{1,0:T(8,128)(2,1)S(1)}, bf16[32,512]{1,0:T(8,128)(2,1)S(1)}, u32[]{:S(2)}, u32[]{:S(2)}) collective-permute-start(bf16[32,512]{1,0:T(8,128)(2,1)S(1)} %add_convert_fusion.2), channel_id=1, source_target_pairs={{0,32},{32,64},{64,96},{96,128},{128,160},{160,192},{192,224},{224... | collective-permute-start | bytes 98312 | tf_op jit(solution)/shard_map/while/body/eval_jaxpr/ppermute | solution.py:19
  698.0 18.4 %all_gather.28 = bf16[32,4096]{1,0:T(8,128)(2,1)S(1)} all-gather(bf16[32,512]{1,0:T(8,128)(2,1)S(1)} %bitcast_select_fusion.4), channel_id=1, replica_groups=mesh['section'=16,'dp'=4,'tp'=8] {'tp'}, dimensions={1}, use_global_device_ids=true | all-gather | bytes 294912 | tf_op jit(solution)/shard_map/while/body/eval_jaxpr/all_gather | solution.py:54
  717.9 18.7 %all_gather.29 = bf16[32,4096]{1,0:T(8,128)(2,1)S(1)} all-gather(bf16[32,512]{1,0:T(8,128)(2,1)S(1)} %multiply_convert_fusion.2), channel_id=1, replica_groups=mesh['section'=16,'dp'=4,'tp'=8] {'tp'}, dimensions={1}, use_global_device_ids=true | all-gather | bytes 294912 | tf_op jit(solution)/shard_map/while/body/eval_jaxpr/all_gather | solution.py:64
  736.7 16.7 %collective-permute-start = (bf16[32,512]{1,0:T(8,128)(2,1)S(1)}, bf16[32,512]{1,0:T(8,128)(2,1)S(1)}, u32[]{:S(2)}, u32[]{:S(2)}) collective-permute-start(bf16[32,512]{1,0:T(8,128)(2,1)S(1)} %add_convert_fusion.2), channel_id=1, source_target_pairs={{0,32},{32,64},{64,96},{96,128},{128,160},{160,192},{192,224},{224... | collective-permute-start | bytes 98312 | tf_op jit(solution)/shard_map/while/body/eval_jaxpr/ppermute | solution.py:19
  755.1 18.5 %all_gather.28 = bf16[32,4096]{1,0:T(8,128)(2,1)S(1)} all-gather(bf16[32,512]{1,0:T(8,128)(2,1)S(1)} %bitcast_select_fusion.4), channel_id=1, replica_groups=mesh['section'=16,'dp'=4,'tp'=8] {'tp'}, dimensions={1}, use_global_device_ids=true | all-gather | bytes 294912 | tf_op jit(solution)/shard_map/while/body/eval_jaxpr/all_gather | solution.py:54
  775.1 18.5 %all_gather.29 = bf16[32,4096]{1,0:T(8,128)(2,1)S(1)} all-gather(bf16[32,512]{1,0:T(8,128)(2,1)S(1)} %multiply_convert_fusion.2), channel_id=1, replica_groups=mesh['section'=16,'dp'=4,'tp'=8] {'tp'}, dimensions={1}, use_global_device_ids=true | all-gather | bytes 294912 | tf_op jit(solution)/shard_map/while/body/eval_jaxpr/all_gather | solution.py:64
  793.7 16.8 %collective-permute-start = (bf16[32,512]{1,0:T(8,128)(2,1)S(1)}, bf16[32,512]{1,0:T(8,128)(2,1)S(1)}, u32[]{:S(2)}, u32[]{:S(2)}) collective-permute-start(bf16[32,512]{1,0:T(8,128)(2,1)S(1)} %add_convert_fusion.2), channel_id=1, source_target_pairs={{0,32},{32,64},{64,96},{96,128},{128,160},{160,192},{192,224},{224... | collective-permute-start | bytes 98312 | tf_op jit(solution)/shard_map/while/body/eval_jaxpr/ppermute | solution.py:19
  812.3 18.5 %all_gather.28 = bf16[32,4096]{1,0:T(8,128)(2,1)S(1)} all-gather(bf16[32,512]{1,0:T(8,128)(2,1)S(1)} %bitcast_select_fusion.4), channel_id=1, replica_groups=mesh['section'=16,'dp'=4,'tp'=8] {'tp'}, dimensions={1}, use_global_device_ids=true | all-gather | bytes 294912 | tf_op jit(solution)/shard_map/while/body/eval_jaxpr/all_gather | solution.py:54
  832.2 18.7 %all_gather.29 = bf16[32,4096]{1,0:T(8,128)(2,1)S(1)} all-gather(bf16[32,512]{1,0:T(8,128)(2,1)S(1)} %multiply_convert_fusion.2), channel_id=1, replica_groups=mesh['section'=16,'dp'=4,'tp'=8] {'tp'}, dimensions={1}, use_global_device_ids=true | all-gather | bytes 294912 | tf_op jit(solution)/shard_map/while/body/eval_jaxpr/all_gather | solution.py:64
  850.9 16.8 %collective-permute-start = (bf16[32,512]{1,0:T(8,128)(2,1)S(1)}, bf16[32,512]{1,0:T(8,128)(2,1)S(1)}, u32[]{:S(2)}, u32[]{:S(2)}) collective-permute-start(bf16[32,512]{1,0:T(8,128)(2,1)S(1)} %add_convert_fusion.2), channel_id=1, source_target_pairs={{0,32},{32,64},{64,96},{96,128},{128,160},{160,192},{192,224},{224... | collective-permute-start | bytes 98312 | tf_op jit(solution)/shard_map/while/body/eval_jaxpr/ppermute | solution.py:19
  869.5 18.5 %all_gather.28 = bf16[32,4096]{1,0:T(8,128)(2,1)S(1)} all-gather(bf16[32,512]{1,0:T(8,128)(2,1)S(1)} %bitcast_select_fusion.4), channel_id=1, replica_groups=mesh['section'=16,'dp'=4,'tp'=8] {'tp'}, dimensions={1}, use_global_device_ids=true | all-gather | bytes 294912 | tf_op jit(solution)/shard_map/while/body/eval_jaxpr/all_gather | solution.py:54
  889.4 18.6 %all_gather.29 = bf16[32,4096]{1,0:T(8,128)(2,1)S(1)} all-gather(bf16[32,512]{1,0:T(8,128)(2,1)S(1)} %multiply_convert_fusion.2), channel_id=1, replica_groups=mesh['section'=16,'dp'=4,'tp'=8] {'tp'}, dimensions={1}, use_global_device_ids=true | all-gather | bytes 294912 | tf_op jit(solution)/shard_map/while/body/eval_jaxpr/all_gather | solution.py:64
  908.1 16.7 %collective-permute-start = (bf16[32,512]{1,0:T(8,128)(2,1)S(1)}, bf16[32,512]{1,0:T(8,128)(2,1)S(1)}, u32[]{:S(2)}, u32[]{:S(2)}) collective-permute-start(bf16[32,512]{1,0:T(8,128)(2,1)S(1)} %add_convert_fusion.2), channel_id=1, source_target_pairs={{0,32},{32,64},{64,96},{96,128},{128,160},{160,192},{192,224},{224... | collective-permute-start | bytes 98312 | tf_op jit(solution)/shard_map/while/body/eval_jaxpr/ppermute | solution.py:19
  926.5 18.6 %all_gather.28 = bf16[32,4096]{1,0:T(8,128)(2,1)S(1)} all-gather(bf16[32,512]{1,0:T(8,128)(2,1)S(1)} %bitcast_select_fusion.4), channel_id=1, replica_groups=mesh['section'=16,'dp'=4,'tp'=8] {'tp'}, dimensions={1}, use_global_device_ids=true | all-gather | bytes 294912 | tf_op jit(solution)/shard_map/while/body/eval_jaxpr/all_gather | solution.py:54
  946.6 19.5 %all_gather.29 = bf16[32,4096]{1,0:T(8,128)(2,1)S(1)} all-gather(bf16[32,512]{1,0:T(8,128)(2,1)S(1)} %multiply_convert_fusion.2), channel_id=1, replica_groups=mesh['section'=16,'dp'=4,'tp'=8] {'tp'}, dimensions={1}, use_global_device_ids=true | all-gather | bytes 294912 | tf_op jit(solution)/shard_map/while/body/eval_jaxpr/all_gather | solution.py:64
  966.1 15.8 %collective-permute-start = (bf16[32,512]{1,0:T(8,128)(2,1)S(1)}, bf16[32,512]{1,0:T(8,128)(2,1)S(1)}, u32[]{:S(2)}, u32[]{:S(2)}) collective-permute-start(bf16[32,512]{1,0:T(8,128)(2,1)S(1)} %add_convert_fusion.2), channel_id=1, source_target_pairs={{0,32},{32,64},{64,96},{96,128},{128,160},{160,192},{192,224},{224... | collective-permute-start | bytes 98312 | tf_op jit(solution)/shard_map/while/body/eval_jaxpr/ppermute | solution.py:19
  983.6 19.0 %all_gather.28 = bf16[32,4096]{1,0:T(8,128)(2,1)S(1)} all-gather(bf16[32,512]{1,0:T(8,128)(2,1)S(1)} %bitcast_select_fusion.4), channel_id=1, replica_groups=mesh['section'=16,'dp'=4,'tp'=8] {'tp'}, dimensions={1}, use_global_device_ids=true | all-gather | bytes 294912 | tf_op jit(solution)/shard_map/while/body/eval_jaxpr/all_gather | solution.py:54
  1004.1 19.1 %all_gather.29 = bf16[32,4096]{1,0:T(8,128)(2,1)S(1)} all-gather(bf16[32,512]{1,0:T(8,128)(2,1)S(1)} %multiply_convert_fusion.2), channel_id=1, replica_groups=mesh['section'=16,'dp'=4,'tp'=8] {'tp'}, dimensions={1}, use_global_device_ids=true | all-gather | bytes 294912 | tf_op jit(solution)/shard_map/while/body/eval_jaxpr/all_gather | solution.py:64
  1023.2 15.8 %collective-permute-start = (bf16[32,512]{1,0:T(8,128)(2,1)S(1)}, bf16[32,512]{1,0:T(8,128)(2,1)S(1)}, u32[]{:S(2)}, u32[]{:S(2)}) collective-permute-start(bf16[32,512]{1,0:T(8,128)(2,1)S(1)} %add_convert_fusion.2), channel_id=1, source_target_pairs={{0,32},{32,64},{64,96},{96,128},{128,160},{160,192},{192,224},{224... | collective-permute-start | bytes 98312 | tf_op jit(solution)/shard_map/while/body/eval_jaxpr/ppermute | solution.py:19
  1040.8 19.3 %all_gather.28 = bf16[32,4096]{1,0:T(8,128)(2,1)S(1)} all-gather(bf16[32,512]{1,0:T(8,128)(2,1)S(1)} %bitcast_select_fusion.4), channel_id=1, replica_groups=mesh['section'=16,'dp'=4,'tp'=8] {'tp'}, dimensions={1}, use_global_device_ids=true | all-gather | bytes 294912 | tf_op jit(solution)/shard_map/while/body/eval_jaxpr/all_gather | solution.py:54
  1061.6 18.5 %all_gather.29 = bf16[32,4096]{1,0:T(8,128)(2,1)S(1)} all-gather(bf16[32,512]{1,0:T(8,128)(2,1)S(1)} %multiply_convert_fusion.2), channel_id=1, replica_groups=mesh['section'=16,'dp'=4,'tp'=8] {'tp'}, dimensions={1}, use_global_device_ids=true | all-gather | bytes 294912 | tf_op jit(solution)/shard_map/while/body/eval_jaxpr/all_gather | solution.py:64
  1080.2 16.1 %collective-permute-start = (bf16[32,512]{1,0:T(8,128)(2,1)S(1)}, bf16[32,512]{1,0:T(8,128)(2,1)S(1)}, u32[]{:S(2)}, u32[]{:S(2)}) collective-permute-start(bf16[32,512]{1,0:T(8,128)(2,1)S(1)} %add_convert_fusion.2), channel_id=1, source_target_pairs={{0,32},{32,64},{64,96},{96,128},{128,160},{160,192},{192,224},{224... | collective-permute-start | bytes 98312 | tf_op jit(solution)/shard_map/while/body/eval_jaxpr/ppermute | solution.py:19
  1098.0 19.1 %all_gather.28 = bf16[32,4096]{1,0:T(8,128)(2,1)S(1)} all-gather(bf16[32,512]{1,0:T(8,128)(2,1)S(1)} %bitcast_select_fusion.4), channel_id=1, replica_groups=mesh['section'=16,'dp'=4,'tp'=8] {'tp'}, dimensions={1}, use_global_device_ids=true | all-gather | bytes 294912 | tf_op jit(solution)/shard_map/while/body/eval_jaxpr/all_gather | solution.py:54
  1118.6 19.2 %all_gather.29 = bf16[32,4096]{1,0:T(8,128)(2,1)S(1)} all-gather(bf16[32,512]{1,0:T(8,128)(2,1)S(1)} %multiply_convert_fusion.2), channel_id=1, replica_groups=mesh['section'=16,'dp'=4,'tp'=8] {'tp'}, dimensions={1}, use_global_device_ids=true | all-gather | bytes 294912 | tf_op jit(solution)/shard_map/while/body/eval_jaxpr/all_gather | solution.py:64
  1137.8 15.5 %collective-permute-start = (bf16[32,512]{1,0:T(8,128)(2,1)S(1)}, bf16[32,512]{1,0:T(8,128)(2,1)S(1)}, u32[]{:S(2)}, u32[]{:S(2)}) collective-permute-start(bf16[32,512]{1,0:T(8,128)(2,1)S(1)} %add_convert_fusion.2), channel_id=1, source_target_pairs={{0,32},{32,64},{64,96},{96,128},{128,160},{160,192},{192,224},{224... | collective-permute-start | bytes 98312 | tf_op jit(solution)/shard_map/while/body/eval_jaxpr/ppermute | solution.py:19
  1155.1 19.0 %all_gather.28 = bf16[32,4096]{1,0:T(8,128)(2,1)S(1)} all-gather(bf16[32,512]{1,0:T(8,128)(2,1)S(1)} %bitcast_select_fusion.4), channel_id=1, replica_groups=mesh['section'=16,'dp'=4,'tp'=8] {'tp'}, dimensions={1}, use_global_device_ids=true | all-gather | bytes 294912 | tf_op jit(solution)/shard_map/while/body/eval_jaxpr/all_gather | solution.py:54
  1175.6 19.0 %all_gather.29 = bf16[32,4096]{1,0:T(8,128)(2,1)S(1)} all-gather(bf16[32,512]{1,0:T(8,128)(2,1)S(1)} %multiply_convert_fusion.2), channel_id=1, replica_groups=mesh['section'=16,'dp'=4,'tp'=8] {'tp'}, dimensions={1}, use_global_device_ids=true | all-gather | bytes 294912 | tf_op jit(solution)/shard_map/while/body/eval_jaxpr/all_gather | solution.py:64
  1194.6 15.9 %collective-permute-start = (bf16[32,512]{1,0:T(8,128)(2,1)S(1)}, bf16[32,512]{1,0:T(8,128)(2,1)S(1)}, u32[]{:S(2)}, u32[]{:S(2)}) collective-permute-start(bf16[32,512]{1,0:T(8,128)(2,1)S(1)} %add_convert_fusion.2), channel_id=1, source_target_pairs={{0,32},{32,64},{64,96},{96,128},{128,160},{160,192},{192,224},{224... | collective-permute-start | bytes 98312 | tf_op jit(solution)/shard_map/while/body/eval_jaxpr/ppermute | solution.py:19
  1221.5 13.8 %all_gather.23 = bf16[512,512]{1,0:T(8,128)(2,1)S(1)} all-gather(bf16[128,512]{1,0:T(8,128)(2,1)S(1)} %fusion.6), channel_id=1, replica_groups=mesh['section'=16,'dp'=4,'tp'=8] {'dp'}, dimensions={0}, use_global_device_ids=true | all-gather | bytes 655360 | tf_op jit(solution)/shard_map/all_gather | solution.py:95
  1239.8 121.9 %psum.7 = f32[]{:T(128)} all-reduce(f32[]{:T(128)} %multiply_reduce_fusion), channel_id=1, replica_groups=mesh['section'=16,'dp'=4,'tp'=8] {'section','dp','tp'}, use_global_device_ids=true, to_apply=%region_9.10 | all-reduce | flops 1 | bytes 8 | tf_op jit(solution)/shard_map/psum | solution.py:110
  (302 shorter events, 125.3 us)
Async XLA Ops:
  7.2 95.2 %all-gather.2.cloned.1.call-start = ((), (), s32[]{:S(2)}) async-start(), calls=%async_computation.2 | async-start | bytes 4259840 | tf_op jit(solution)/shard_map/all_gather | solution.py:40
  143.1 20.6 %collective-permute-start = (bf16[32,512]{1,0:T(8,128)(2,1)S(1)}, bf16[32,512]{1,0:T(8,128)(2,1)S(1)}, u32[]{:S(2)}, u32[]{:S(2)}) collective-permute-start(bf16[32,512]{1,0:T(8,128)(2,1)S(1)} %add_convert_fusion.2), channel_id=1, source_target_pairs={{0,32},{32,64},{64,96},{96,128},{128,160},{160,192},{192,224},{224... | collective-permute-start | bytes 98312 | tf_op jit(solution)/shard_map/while/body/eval_jaxpr/ppermute | solution.py:19
  209.4 14.5 %collective-permute-start = (bf16[32,512]{1,0:T(8,128)(2,1)S(1)}, bf16[32,512]{1,0:T(8,128)(2,1)S(1)}, u32[]{:S(2)}, u32[]{:S(2)}) collective-permute-start(bf16[32,512]{1,0:T(8,128)(2,1)S(1)} %add_convert_fusion.2), channel_id=1, source_target_pairs={{0,32},{32,64},{64,96},{96,128},{128,160},{160,192},{192,224},{224... | collective-permute-start | bytes 98312 | tf_op jit(solution)/shard_map/while/body/eval_jaxpr/ppermute | solution.py:19
  269.5 14.4 %collective-permute-start = (bf16[32,512]{1,0:T(8,128)(2,1)S(1)}, bf16[32,512]{1,0:T(8,128)(2,1)S(1)}, u32[]{:S(2)}, u32[]{:S(2)}) collective-permute-start(bf16[32,512]{1,0:T(8,128)(2,1)S(1)} %add_convert_fusion.2), channel_id=1, source_target_pairs={{0,32},{32,64},{64,96},{96,128},{128,160},{160,192},{192,224},{224... | collective-permute-start | bytes 98312 | tf_op jit(solution)/shard_map/while/body/eval_jaxpr/ppermute | solution.py:19
  329.6 14.5 %collective-permute-start = (bf16[32,512]{1,0:T(8,128)(2,1)S(1)}, bf16[32,512]{1,0:T(8,128)(2,1)S(1)}, u32[]{:S(2)}, u32[]{:S(2)}) collective-permute-start(bf16[32,512]{1,0:T(8,128)(2,1)S(1)} %add_convert_fusion.2), channel_id=1, source_target_pairs={{0,32},{32,64},{64,96},{96,128},{128,160},{160,192},{192,224},{224... | collective-permute-start | bytes 98312 | tf_op jit(solution)/shard_map/while/body/eval_jaxpr/ppermute | solution.py:19
  390.0 15.5 %collective-permute-start = (bf16[32,512]{1,0:T(8,128)(2,1)S(1)}, bf16[32,512]{1,0:T(8,128)(2,1)S(1)}, u32[]{:S(2)}, u32[]{:S(2)}) collective-permute-start(bf16[32,512]{1,0:T(8,128)(2,1)S(1)} %add_convert_fusion.2), channel_id=1, source_target_pairs={{0,32},{32,64},{64,96},{96,128},{128,160},{160,192},{192,224},{224... | collective-permute-start | bytes 98312 | tf_op jit(solution)/shard_map/while/body/eval_jaxpr/ppermute | solution.py:19
  446.0 22.6 %collective-permute-start = (bf16[32,512]{1,0:T(8,128)(2,1)S(1)}, bf16[32,512]{1,0:T(8,128)(2,1)S(1)}, u32[]{:S(2)}, u32[]{:S(2)}) collective-permute-start(bf16[32,512]{1,0:T(8,128)(2,1)S(1)} %add_convert_fusion.2), channel_id=1, source_target_pairs={{0,32},{32,64},{64,96},{96,128},{128,160},{160,192},{192,224},{224... | collective-permute-start | bytes 98312 | tf_op jit(solution)/shard_map/while/body/eval_jaxpr/ppermute | solution.py:19
  508.7 17.1 %collective-permute-start = (bf16[32,512]{1,0:T(8,128)(2,1)S(1)}, bf16[32,512]{1,0:T(8,128)(2,1)S(1)}, u32[]{:S(2)}, u32[]{:S(2)}) collective-permute-start(bf16[32,512]{1,0:T(8,128)(2,1)S(1)} %add_convert_fusion.2), channel_id=1, source_target_pairs={{0,32},{32,64},{64,96},{96,128},{128,160},{160,192},{192,224},{224... | collective-permute-start | bytes 98312 | tf_op jit(solution)/shard_map/while/body/eval_jaxpr/ppermute | solution.py:19
  566.2 16.8 %collective-permute-start = (bf16[32,512]{1,0:T(8,128)(2,1)S(1)}, bf16[32,512]{1,0:T(8,128)(2,1)S(1)}, u32[]{:S(2)}, u32[]{:S(2)}) collective-permute-start(bf16[32,512]{1,0:T(8,128)(2,1)S(1)} %add_convert_fusion.2), channel_id=1, source_target_pairs={{0,32},{32,64},{64,96},{96,128},{128,160},{160,192},{192,224},{224... | collective-permute-start | bytes 98312 | tf_op jit(solution)/shard_map/while/body/eval_jaxpr/ppermute | solution.py:19
  623.0 17.1 %collective-permute-start = (bf16[32,512]{1,0:T(8,128)(2,1)S(1)}, bf16[32,512]{1,0:T(8,128)(2,1)S(1)}, u32[]{:S(2)}, u32[]{:S(2)}) collective-permute-start(bf16[32,512]{1,0:T(8,128)(2,1)S(1)} %add_convert_fusion.2), channel_id=1, source_target_pairs={{0,32},{32,64},{64,96},{96,128},{128,160},{160,192},{192,224},{224... | collective-permute-start | bytes 98312 | tf_op jit(solution)/shard_map/while/body/eval_jaxpr/ppermute | solution.py:19
  680.1 17.2 %collective-permute-start = (bf16[32,512]{1,0:T(8,128)(2,1)S(1)}, bf16[32,512]{1,0:T(8,128)(2,1)S(1)}, u32[]{:S(2)}, u32[]{:S(2)}) collective-permute-start(bf16[32,512]{1,0:T(8,128)(2,1)S(1)} %add_convert_fusion.2), channel_id=1, source_target_pairs={{0,32},{32,64},{64,96},{96,128},{128,160},{160,192},{192,224},{224... | collective-permute-start | bytes 98312 | tf_op jit(solution)/shard_map/while/body/eval_jaxpr/ppermute | solution.py:19
  736.7 17.7 %collective-permute-start = (bf16[32,512]{1,0:T(8,128)(2,1)S(1)}, bf16[32,512]{1,0:T(8,128)(2,1)S(1)}, u32[]{:S(2)}, u32[]{:S(2)}) collective-permute-start(bf16[32,512]{1,0:T(8,128)(2,1)S(1)} %add_convert_fusion.2), channel_id=1, source_target_pairs={{0,32},{32,64},{64,96},{96,128},{128,160},{160,192},{192,224},{224... | collective-permute-start | bytes 98312 | tf_op jit(solution)/shard_map/while/body/eval_jaxpr/ppermute | solution.py:19
  793.7 17.8 %collective-permute-start = (bf16[32,512]{1,0:T(8,128)(2,1)S(1)}, bf16[32,512]{1,0:T(8,128)(2,1)S(1)}, u32[]{:S(2)}, u32[]{:S(2)}) collective-permute-start(bf16[32,512]{1,0:T(8,128)(2,1)S(1)} %add_convert_fusion.2), channel_id=1, source_target_pairs={{0,32},{32,64},{64,96},{96,128},{128,160},{160,192},{192,224},{224... | collective-permute-start | bytes 98312 | tf_op jit(solution)/shard_map/while/body/eval_jaxpr/ppermute | solution.py:19
  850.9 17.8 %collective-permute-start = (bf16[32,512]{1,0:T(8,128)(2,1)S(1)}, bf16[32,512]{1,0:T(8,128)(2,1)S(1)}, u32[]{:S(2)}, u32[]{:S(2)}) collective-permute-start(bf16[32,512]{1,0:T(8,128)(2,1)S(1)} %add_convert_fusion.2), channel_id=1, source_target_pairs={{0,32},{32,64},{64,96},{96,128},{128,160},{160,192},{192,224},{224... | collective-permute-start | bytes 98312 | tf_op jit(solution)/shard_map/while/body/eval_jaxpr/ppermute | solution.py:19
  908.1 17.7 %collective-permute-start = (bf16[32,512]{1,0:T(8,128)(2,1)S(1)}, bf16[32,512]{1,0:T(8,128)(2,1)S(1)}, u32[]{:S(2)}, u32[]{:S(2)}) collective-permute-start(bf16[32,512]{1,0:T(8,128)(2,1)S(1)} %add_convert_fusion.2), channel_id=1, source_target_pairs={{0,32},{32,64},{64,96},{96,128},{128,160},{160,192},{192,224},{224... | collective-permute-start | bytes 98312 | tf_op jit(solution)/shard_map/while/body/eval_jaxpr/ppermute | solution.py:19
  966.1 16.8 %collective-permute-start = (bf16[32,512]{1,0:T(8,128)(2,1)S(1)}, bf16[32,512]{1,0:T(8,128)(2,1)S(1)}, u32[]{:S(2)}, u32[]{:S(2)}) collective-permute-start(bf16[32,512]{1,0:T(8,128)(2,1)S(1)} %add_convert_fusion.2), channel_id=1, source_target_pairs={{0,32},{32,64},{64,96},{96,128},{128,160},{160,192},{192,224},{224... | collective-permute-start | bytes 98312 | tf_op jit(solution)/shard_map/while/body/eval_jaxpr/ppermute | solution.py:19
  1023.2 16.8 %collective-permute-start = (bf16[32,512]{1,0:T(8,128)(2,1)S(1)}, bf16[32,512]{1,0:T(8,128)(2,1)S(1)}, u32[]{:S(2)}, u32[]{:S(2)}) collective-permute-start(bf16[32,512]{1,0:T(8,128)(2,1)S(1)} %add_convert_fusion.2), channel_id=1, source_target_pairs={{0,32},{32,64},{64,96},{96,128},{128,160},{160,192},{192,224},{224... | collective-permute-start | bytes 98312 | tf_op jit(solution)/shard_map/while/body/eval_jaxpr/ppermute | solution.py:19
  1080.2 17.1 %collective-permute-start = (bf16[32,512]{1,0:T(8,128)(2,1)S(1)}, bf16[32,512]{1,0:T(8,128)(2,1)S(1)}, u32[]{:S(2)}, u32[]{:S(2)}) collective-permute-start(bf16[32,512]{1,0:T(8,128)(2,1)S(1)} %add_convert_fusion.2), channel_id=1, source_target_pairs={{0,32},{32,64},{64,96},{96,128},{128,160},{160,192},{192,224},{224... | collective-permute-start | bytes 98312 | tf_op jit(solution)/shard_map/while/body/eval_jaxpr/ppermute | solution.py:19
  1137.8 16.6 %collective-permute-start = (bf16[32,512]{1,0:T(8,128)(2,1)S(1)}, bf16[32,512]{1,0:T(8,128)(2,1)S(1)}, u32[]{:S(2)}, u32[]{:S(2)}) collective-permute-start(bf16[32,512]{1,0:T(8,128)(2,1)S(1)} %add_convert_fusion.2), channel_id=1, source_target_pairs={{0,32},{32,64},{64,96},{96,128},{128,160},{160,192},{192,224},{224... | collective-permute-start | bytes 98312 | tf_op jit(solution)/shard_map/while/body/eval_jaxpr/ppermute | solution.py:19
  1194.6 16.9 %collective-permute-start = (bf16[32,512]{1,0:T(8,128)(2,1)S(1)}, bf16[32,512]{1,0:T(8,128)(2,1)S(1)}, u32[]{:S(2)}, u32[]{:S(2)}) collective-permute-start(bf16[32,512]{1,0:T(8,128)(2,1)S(1)} %add_convert_fusion.2), channel_id=1, source_target_pairs={{0,32},{32,64},{64,96},{96,128},{128,160},{160,192},{192,224},{224... | collective-permute-start | bytes 98312 | tf_op jit(solution)/shard_map/while/body/eval_jaxpr/ppermute | solution.py:19
  1216.7 18.6 %all-to-all-start = ((bf16[128,16,4,64]{0,3,1,2:T(8,128)(2,1)}), bf16[128,16,4,64]{0,3,1,2:T(8,128)(2,1)S(1)}, u32[]{:S(2)}, u32[]{:S(2)}) async-start(bf16[128,16,4,64]{0,3,1,2:T(8,128)(2,1)} %copy.8), calls=%async_computation | async-start | bytes 2097152 | tf_op jit(solution)/shard_map/all_to_all | solution.py:100
  1220.2 142.2 %reduce-scatter.2.cloned.1.call-start = ((), (), s32[]{:S(2)}) async-start(), calls=%async_computation.3 | async-start | bytes 1114112 | tf_op jit(solution)/shard_map/reduce_scatter | solution.py:107
Sparse Core Ops, SparseCore 0:
  11.3 90.9 all-gather.1
  1238.4 83.6 reduce-scatter.1
where the time goes:
time: 1380 us; the launch traced here: 1370 us
  blocking collectives  853 us (62%)
  starting transfers between devices  290 us (21%)
  waiting for transfers between devices  132 us (10%)
  other arithmetic  44.9 us (3%)
  matrix products  25.6 us (2%)
  between operations  15.9 us (1%)
    all_gather x19, blocking collectives, advance(): full_rows = lax.all_gather(slice_in, 'tp', axis=1, tiled=True)  359 us
    all_gather x19, blocking collectives, advance(): quant_full = lax.all_gather(quantized, 'tp', axis=1, tiled=True)  358 us
    ppermute x19, starting transfers between devices, from_behind(): lax.ppermute(value, axis, [(source, source + steps) for source in range(l...  287 us
    psum x1, blocking collectives, local(): loss_total = lax.psum(own_loss, ('section', 'dp', 'tp'))  122 us
    all_gather x1, waiting for transfers between devices, local(): rot_cols = lax.all_gather(rotation, ('section', 'dp'), axis=0, tiled=True)  93.8 us
    ppermute x19, waiting for transfers between devices, from_behind(): lax.ppermute(value, axis, [(source, source + steps) for source in range(l...  37.6 us
  transfers between devices with their start and end apart: 22, of which 20 were waited for; matrix products, arithmetic and copies ran while one was open for 0% of the time, Pallas kernels for 0%

commit v1 on v0

v1 whole, which is shorter than its diff:
```python
import math

import jax
import jax.numpy as jnp
from jax import lax
from jax.experimental import pallas as pl
from jax.experimental.pallas import tpu as pltpu
from jax.sharding import PartitionSpec as P

D = 4096
GROUP = 128
STAGE = 4

norm_eps = 1e-05
full_turn = 2.0 * math.pi


def quantize(values, scale):
    ratio = values / scale
    stair = ratio - jnp.sin(full_turn * ratio) / full_turn
    return scale * jnp.clip(stair, -8.0, 7.0)


def staircase_slope(values, scale):
    ratio = values / scale
    stair = ratio - jnp.sin(full_turn * ratio) / full_turn
    inside = (stair > -8.0) & (stair < 7.0)
    return jnp.where(inside, 1.0 - jnp.cos(full_turn * ratio), 0.0)


def gather(value, axis):
    copies = jnp.broadcast_to(value[None], (lax.axis_size(axis),) + value.shape)
    return lax.all_to_all(copies, axis, 0, 0, tiled=True)


def total_of(value, axis):
    return jnp.sum(gather(value, axis), axis=0)


def crossed(value, mask):
    return lax.ppermute(value, "section", [(i, i ^ mask) for i in range(lax.axis_size("section"))])


def order_kernel(place_ref, own, by1, by2, by3, out, sems):
    sources = (own, by1, by2, by3)
    place = place_ref[0]
    for layer in range(STAGE):
        for mask in range(STAGE):
            @pl.when((place ^ layer) == mask)
            def _():
                pltpu.make_async_copy(sources[mask], out.at[layer], sems.at[layer]).start()
    for layer in range(STAGE):
        pltpu.make_async_copy(own, out.at[layer], sems.at[layer]).wait()


def in_order(place, own, by1, by2, by3):
    anywhere = pl.BlockSpec(memory_space=pl.ANY)
    return pl.pallas_call(
        order_kernel,
        out_shape=jax.ShapeDtypeStruct((STAGE,) + own.shape, own.dtype),
        in_specs=[pl.BlockSpec(memory_space=pltpu.SMEM)] + [anywhere] * 4,
        out_specs=anywhere,
        scratch_shapes=[pltpu.SemaphoreType.DMA((STAGE,))],
        name="in_order",
    )(place, own, by1, by2, by3)


def local(hidden_in, rotation, proj, norm_gain, quant_exp):
    sections = lax.axis_size("section")
    replicas = lax.axis_size("dp")
    section_pos = lax.axis_index("section")
    micro_count, tok_rows, part_cols = hidden_in.shape
    stages = sections // STAGE
    stage_pos = section_pos // STAGE
    place = section_pos % STAGE

    own = proj[0]
    by1 = crossed(own, 1)
    by2 = crossed(own, 2)
    by3 = crossed(by2, 1)
    rot_cols = lax.all_gather(rotation, ("section", "dp"), axis=0, tiled=True)
    scale_row = jnp.repeat(jnp.exp2(quant_exp.astype(jnp.float32) * 0.25) * 0.125, GROUP, axis=1)
    params = jnp.concatenate([norm_gain, scale_row], axis=1)
    groups = [[STAGE * g + i for i in range(STAGE)] for g in range(stages)]
    params = lax.all_gather(params, "section", axis=0, tiled=True, axis_index_groups=groups)
    gains, scales = params[:, :D], params[:, D:]
    weights = in_order(place[None].astype(jnp.int32), own, by1, by2, by3)

    stream = lax.dynamic_index_in_dim(hidden_in, place, 0, keepdims=False)
    kept_normed = None
    kept_rotated = None
    for stage in range(stages):
        normed_list, rotated_list = [], []
        for layer in range(STAGE):
            rows = gather(stream, "tp").transpose(1, 0, 2).reshape(tok_rows, D).astype(jnp.float32)
            mean_square = jnp.mean(rows * rows, axis=-1, keepdims=True)
            normed = (rows * lax.rsqrt(mean_square + norm_eps) * gains[layer]).astype(jnp.bfloat16)
            rotated = jnp.dot(normed, rot_cols, preferred_element_type=jnp.float32)
            normed_list.append(normed)
            rotated_list.append(rotated)
            if stage == stages - 1 and layer == STAGE - 1:
                break
            quantized = quantize(rotated, scales[layer]).astype(jnp.bfloat16)
            quant_full = gather(quantized, "tp").transpose(1, 0, 2).reshape(tok_rows, D)
            update = jnp.dot(quant_full, weights[layer], preferred_element_type=jnp.float32)
            stream = (stream.astype(jnp.float32) + update).astype(jnp.bfloat16)
        normed_now = jnp.concatenate(normed_list, axis=0)
        rotated_now = jnp.concatenate(rotated_list, axis=0)
        if stage == 0:
            kept_normed, kept_rotated = normed_now, rotated_now
        else:
            valid = stage_pos == stage
            kept_normed = jnp.where(valid, normed_now, kept_normed)
            kept_rotated = jnp.where(valid, rotated_now, kept_rotated)
        if stage < stages - 1:
            stream = lax.ppermute(
                stream, "section", [(i, i + STAGE) for i in range(sections - STAGE)]
            )

    all_rows = STAGE * tok_rows
    row_scales = jnp.repeat(scales, tok_rows, axis=0)
    level = quantize(kept_rotated, row_scales)
    error_part = level - kept_rotated
    grad_rot = (error_part * (staircase_slope(kept_rotated, row_scales) - 1.0)).astype(jnp.bfloat16)
    loss = jnp.full((8, 128), jnp.sum(error_part * error_part), jnp.float32)
    for axis in ("tp", "dp", "section"):
        loss = total_of(loss, axis)

    grad_all = gather(grad_rot, "dp").reshape(replicas * all_rows, part_cols)
    row_block = D // (sections * replicas)
    blocks = kept_normed.reshape(all_rows, sections, replicas, row_block)
    blocks = blocks.transpose(2, 0, 1, 3).reshape(replicas, all_rows, sections * row_block)
    normed_all = lax.all_to_all(blocks, "dp", 0, 0, tiled=True).reshape(replicas * all_rows, sections * row_block)
    terms = lax.dot_general(
        normed_all, grad_all, (((0,), (0,)), ((), ())), preferred_element_type=jnp.float32
    )
    halves = terms.reshape(sections // 2, 2, row_block, part_cols)
    core = section_pos % 2
    mine = lax.dynamic_index_in_dim(halves, core, 1, keepdims=False)
    other = lax.dynamic_index_in_dim(halves, 1 - core, 1, keepdims=False).astype(jnp.bfloat16)
    pair_sum = (mine + crossed(other, 1).astype(jnp.float32)).astype(jnp.bfloat16)
    same_core = [[2 * z + c for z in range(sections // 2)] for c in range(2)]
    parts = lax.all_to_all(pair_sum, "section", 0, 0, axis_index_groups=same_core, tiled=True)
    grad_share = jnp.sum(parts.astype(jnp.float32), axis=0)
    factor = 1.0 / math.sqrt(sections * all_rows * replicas)
    norm_count = all_rows * replicas * D
    return (grad_share * factor, loss[0, 0] / norm_count)


def solution(mesh):
    placed = (
        P(None, "dp", "tp"),
        P(("section", "dp"), "tp"),
        P("section", None, "tp"),
        P("section", None),
        P("section", "tp"),
    )
    return jax.shard_map(
        local,
        mesh=mesh,
        in_specs=placed,
        out_specs=(P(("section", "dp"), "tp"), P()),
        check_vma=False,
    )
```

time: 1380 us -> 1310 us (0.949)
  Pallas kernels: 0 us -> 509 us
  blocking collectives: 853 us -> 350 us
  starting transfers between devices: 290 us -> 125 us
  local copies, waits for them, and re-layouts: 8.79 us -> 71.7 us
  matrix products: 25.6 us -> 50.3 us
    all_gather x39 -> x1, blocking collectives: 731 us -> 5.39 us  [local(): lax.all_gather(params, 'section', axis=0, tiled=True, axis_index_groups=g...]
    pallas_call x0 -> x1, Pallas kernels: none -> 509 us  [in_order(): pl.pallas_call(order_kernel, out_shape=jax.ShapeDtypeStruct((STAGE,) + ow...]
    all_to_all x0 -> x28, blocking collectives: none -> 344 us  [gather(): return lax.all_to_all(copies, axis, 0, 0, tiled=True)]
    ppermute x19 -> x7, starting transfers between devices: 287 us -> 77.5 us  [the longest x4 58.6 us: crossed(): lax.ppermute(value, 'section', [(i, i ^ mask) for i in range(lax.axis_siz...]
    psum x1 -> x0, blocking collectives: 122 us -> none  [local(): loss_total = lax.psum(own_loss, ('section', 'dp', 'tp'))]
    all_gather x1, waiting for transfers between devices: 93.8 us -> 0.02 us  [local(): rot_cols = lax.all_gather(rotation, ('section', 'dp'), axis=0, tiled=True)]
    ppermute x19 -> x7, waiting for transfers between devices: 37.6 us -> 95.9 us  [the longest x4 92.9 us: crossed(): lax.ppermute(value, 'section', [(i, i ^ mask) for i in range(lax.axis_siz...]
    convert_element_type x0 -> x49, local copies, waits for them, and re-layouts: none -> 56 us  [the longest x48 55.9 us: local(): gather(stream, 'tp').transpose(1, 0, 2).reshape(tok_rows, D)]
  transfers between devices with their start and end apart: 22 -> 17, of which waited for: 20 -> 10; matrix products, arithmetic and copies ran while one was open for 0% -> 6% of each run, Pallas kernels for 0% -> 39%
where the time goes in v1:
time: 1310 us; the launch traced here: 1300 us
  Pallas kernels  509 us (39%)
  blocking collectives  350 us (27%)
  waiting for transfers between devices  138 us (11%)
  starting transfers between devices  125 us (10%)
  local copies, waits for them, and re-layouts  71.7 us (5%)
  matrix products  50.3 us (4%)
  other arithmetic  36.4 us (3%)
  between operations  17.7 us (1%)
    pallas_call x1, Pallas kernels, in_order(): pl.pallas_call(order_kernel, out_shape=jax.ShapeDtypeStruct((STAGE,) + ow...  509 us
    all_to_all x28, blocking collectives, gather(): return lax.all_to_all(copies, axis, 0, 0, tiled=True)  344 us
    ppermute x4, waiting for transfers between devices, crossed(): lax.ppermute(value, 'section', [(i, i ^ mask) for i in range(lax.axis_siz...  92.9 us
    ppermute x4, starting transfers between devices, crossed(): lax.ppermute(value, 'section', [(i, i ^ mask) for i in range(lax.axis_siz...  58.6 us
    convert_element_type x48, local copies, waits for them, and re-layouts, local(): gather(stream, 'tp').transpose(1, 0, 2).reshape(tok_rows, D)  55.9 us
    all_to_all x7, starting transfers between devices, gather(): return lax.all_to_all(copies, axis, 0, 0, tiled=True)  40.2 us
    dot_general x16, matrix products, local(): rotated = jnp.dot(normed, rot_cols, preferred_element_type=jnp.float32)  29.7 us
  transfers between devices with their start and end apart: 17, of which 10 were waited for; matrix products, arithmetic and copies ran while one was open for 6% of the time, Pallas kernels for 39%

profile of v1, /device:TPU:1, one launch (start us, length us, event | category | flops | bytes accessed | tf_op | source)
XLA Modules:
  0.0 1298.5 jit_solution(17652226775975274375)
XLA Ops:
  7.9 4.8 collective-permute-start.1
  12.8 5.9 collective-permute-start
  18.6 92.9 %collective-permute-done.1.by2 = bf16[4096,512]{1,0:T(8,128)(2,1)} collective-permute-done((bf16[4096,512]{1,0:T(8,128)(2,1)}, bf16[4096,512]{1,0:T(8,128)(2,1)}, u32[]{:S(2)}, u32[]{:S(2)}) %collective-permute-start.1) | collective-permute-done | bytes 4194336 | tf_op jit(solution)/shard_map/ppermute | solution.py:41
  111.5 7.3 collective-permute-start.2
  119.5 6.8 all-to-all-start
  127.8 5.4 all-gather
  134.7 4.1 all-to-all-done
  139.1 3.3 multiply_convert_fusion.63
  143.1 3.4 all-to-all-start.1
  146.5 509.4 %in_order.1 = bf16[4,4096,512]{2,1,0:T(8,128)(2,1)} custom-call(s32[1]{0:T(128)} %bitcast.8.place_ref, bf16[4096,512]{1,0:T(8,128)(2,1)} %bitcast.279, bf16[4096,512]{1,0:T(8,128)(2,1)} %collective-permute-done.by1, bf16[4096,512]{1,0:T(8,128)(2,1)} %collective-permute-done.1.by2, bf16[4096,512]{1,0:T(8,128)(2,1)} %collective-permute-done.2.by3), custom_call_target="tpu_custom_call" | custom-call | tf_op jit(solution)/shard_map/in_order/pallas_call | solution.py:58
  656.0 3.1 fusion.26
  659.2 16.5 %all_to_all.185 = bf16[8,32,512]{2,1,0:T(8,128)(2,1)S(1)} all-to-all(bf16[8,32,512]{2,1,0:T(8,128)(2,1)S(1)} %broadcast_in_dim.84), channel_id=1, replica_groups=mesh['section'=16,'dp'=4,'tp'=8] {'tp'}, dimensions={0} | all-to-all | bytes 524288 | tf_op jit(solution)/shard_map/all_to_all | solution.py:33
  677.8 12.3 all_to_all.186
  690.1 3.0 add_convert_fusion.7
  693.2 11.9 all_to_all.187
  707.1 11.8 all_to_all.188
  719.8 11.7 all_to_all.189
  733.6 11.7 all_to_all.190
  746.2 5.8 collective-permute-start.3
  753.0 11.7 all_to_all.191
  767.6 11.7 all_to_all.192
  780.2 12.5 all_to_all.193
  795.5 11.7 all_to_all.194
  808.2 15.0 %all_to_all.195 = bf16[8,32,512]{2,1,0:T(8,128)(2,1)S(1)} all-to-all(bf16[8,32,512]{2,1,0:T(8,128)(2,1)S(1)} %broadcast_in_dim.94), channel_id=1, replica_groups=mesh['section'=16,'dp'=4,'tp'=8] {'tp'}, dimensions={0} | all-to-all | bytes 524288 | tf_op jit(solution)/shard_map/all_to_all | solution.py:33
  826.0 13.6 %all_to_all.196 = bf16[8,32,512]{2,1,0:T(8,128)(2,1)S(1)} all-to-all(bf16[8,32,512]{2,1,0:T(8,128)(2,1)S(1)} %broadcast_in_dim.95), channel_id=1, replica_groups=mesh['section'=16,'dp'=4,'tp'=8] {'tp'}, dimensions={0} | all-to-all | bytes 524288 | tf_op jit(solution)/shard_map/all_to_all | solution.py:33
  840.5 11.9 all_to_all.197
  855.3 13.6 %all_to_all.198 = bf16[8,32,512]{2,1,0:T(8,128)(2,1)S(1)} all-to-all(bf16[8,32,512]{2,1,0:T(8,128)(2,1)S(1)} %broadcast_in_dim.97), channel_id=1, replica_groups=mesh['section'=16,'dp'=4,'tp'=8] {'tp'}, dimensions={0} | all-to-all | bytes 524288 | tf_op jit(solution)/shard_map/all_to_all | solution.py:33
  869.7 6.4 collective-permute-start.4
  877.1 11.8 all_to_all.199
  891.8 11.7 all_to_all.200
  904.4 11.7 all_to_all.201
  919.0 11.7 all_to_all.202
  931.6 11.7 all_to_all.203
  946.2 11.7 all_to_all.204
  958.8 11.7 all_to_all.205
  973.4 12.6 all_to_all.206
  986.8 6.8 collective-permute-start.5
  994.6 11.7 all_to_all.207
  1009.2 11.7 all_to_all.208
  1021.8 11.8 all_to_all.209
  1036.5 11.8 all_to_all.210
  1049.2 11.8 all_to_all.211
  1064.7 3.8 all-to-all-start.29
  1092.5 2.6 reshape.677
  1118.9 3.0 add_convert_fusion
  1122.6 6.5 all-to-all-start.30
  1129.3 5.9 multiply_convert_fusion.2
  1141.1 2.6 reshape.676
  1143.9 4.3 multiply_convert_fusion
  1148.2 6.1 fusion.15
  1154.4 2.9 copy.111
  1157.4 4.2 all-to-all-start.31
  1162.3 3.1 fusion.64
  1168.1 3.3 all-to-all-done.31
  1172.3 4.1 all-to-all-start.32
  1177.6 5.9 all-to-all-done.32
  1185.3 40.6 %collective-permute-start.6 = (bf16[8,64,512]{2,1,0:T(8,128)(2,1)S(1)}, bf16[8,64,512]{2,1,0:T(8,128)(2,1)S(1)}, u32[]{:S(2)}, u32[]{:S(2)}) collective-permute-start(bf16[8,64,512]{2,1,0:T(8,128)(2,1)S(1)} %fusion.47), channel_id=1, source_target_pairs={{0,32},{32,0},{64,96},{96,64},{128,160},{160,128},{192,224},{224,1... | collective-permute-start | bytes 1572872 | tf_op jit(solution)/shard_map/ppermute | solution.py:41
  1226.6 12.9 all_to_all.212
  1240.1 3.3 all-to-all-start.35
  1243.3 4.2 all-to-all-done.35
  1248.2 12.2 all-to-all-start.36
  1261.3 6.8 all-to-all-done.36
  1268.2 3.5 all-to-all-start.33
  1272.8 16.8 %all-to-all-done.33 = bf16[8,64,512]{2,1,0:T(8,128)(2,1)S(1)} async-done(((bf16[8,64,512]{2,1,0:T(8,128)(2,1)}), bf16[8,64,512]{2,1,0:T(8,128)(2,1)S(1)}, u32[]{:S(2)}, u32[]{:S(2)}) %all-to-all-start.33) | async-done | bytes 524320 | tf_op jit(solution)/shard_map/all_to_all | solution.py:143
  (333 shorter events, 122.3 us)
Async XLA Ops:
  7.2 111.6 %copy-start = (bf16[4,32,512]{2,1,0:T(8,128)(2,1)S(1)}, bf16[4,32,512]{2,1,0:T(8,128)(2,1)}, u32[]{:S(2)}) copy-start(bf16[4,32,512]{2,1,0:T(8,128)(2,1)} %param.5) | copy-start | bytes 393220
  7.2 131.9 %all-gather.3.cloned.1.call-start = ((), (), s32[]{:S(2)}) async-start(), calls=%async_computation.37 | async-start | bytes 4259840 | tf_op jit(solution)/shard_map/all_gather | solution.py:81
  7.9 103.6 %collective-permute-start.1 = (bf16[4096,512]{1,0:T(8,128)(2,1)}, bf16[4096,512]{1,0:T(8,128)(2,1)}, u32[]{:S(2)}, u32[]{:S(2)}) collective-permute-start(bf16[4096,512]{1,0:T(8,128)(2,1)} %bitcast.277), channel_id=1, source_target_pairs={{0,64},{32,96},{64,0},{96,32},{128,192},{160,224},{192,128},{224,1... | collective-permute-start | bytes 12582920 | tf_op jit(solution)/shard_map/ppermute | solution.py:41
  12.8 133.8 %collective-permute-start = (bf16[4096,512]{1,0:T(8,128)(2,1)}, bf16[4096,512]{1,0:T(8,128)(2,1)}, u32[]{:S(2)}, u32[]{:S(2)}) collective-permute-start(bf16[4096,512]{1,0:T(8,128)(2,1)} %bitcast.278), channel_id=1, source_target_pairs={{0,32},{32,0},{64,96},{96,64},{128,160},{160,128},{192,224},{224,1... | collective-permute-start | bytes 12582920 | tf_op jit(solution)/shard_map/ppermute | solution.py:41
  111.5 35.0 %collective-permute-start.2 = (bf16[4096,512]{1,0:T(8,128)(2,1)}, bf16[4096,512]{1,0:T(8,128)(2,1)}, u32[]{:S(2)}, u32[]{:S(2)}) collective-permute-start(bf16[4096,512]{1,0:T(8,128)(2,1)} %collective-permute-done.1.by2), channel_id=1, source_target_pairs={{0,32},{32,0},{64,96},{96,64},{128,160},{160,128},{192,224},{224,1... | collective-permute-start | bytes 12582920 | tf_op jit(solution)/shard_map/ppermute | solution.py:41
  119.5 19.2 %all-to-all-start = ((bf16[8,32,512]{2,1,0:T(8,128)(2,1)}), bf16[8,32,512]{2,1,0:T(8,128)(2,1)S(1)}, u32[]{:S(2)}, u32[]{:S(2)}) async-start(bf16[8,32,512]{2,1,0:T(8,128)(2,1)} %broadcast_in_dim.81), calls=%async_computation | async-start | bytes 524288 | tf_op jit(solution)/shard_map/all_to_all | solution.py:33
  139.0 516.9 %copy-start.33 = (f32[32]{0:T(128)}, f32[32]{0:T(128)S(1)}, u32[]{:S(2)}) copy-start(f32[32]{0:T(128)S(1)} %add_rsqrt_fusion.15) | copy-start | bytes 388
  143.1 512.8 %all-to-all-start.1 = ((bf16[8,32,512]{2,1,0:T(8,128)(2,1)}), bf16[8,32,512]{2,1,0:T(8,128)(2,1)S(1)}, u32[]{:S(2)}, u32[]{:S(2)}) async-start(bf16[8,32,512]{2,1,0:T(8,128)(2,1)} %broadcast_in_dim.82), calls=%async_computation.1 | async-start | bytes 524288 | tf_op jit(solution)/shard_map/all_to_all | solution.py:33
  656.0 20.1 %copy-start.2 = (bf16[4096,512]{1,0:T(8,128)(2,1)S(1)}, bf16[4096,512]{1,0:T(8,128)(2,1)}, u32[]{:S(2)}) copy-start(bf16[4096,512]{1,0:T(8,128)(2,1)} %all-gather.3.cloned.1.call-done) | copy-start | bytes 12582916
  676.0 14.1 %copy-start.37 = (f32[32]{0:T(128)}, f32[32]{0:T(128)S(1)}, u32[]{:S(2)}) copy-start(f32[32]{0:T(128)S(1)} %add_rsqrt_fusion.14) | copy-start | bytes 388
  676.1 42.9 %copy-start.3 = (bf16[4,4096,512]{2,1,0:T(8,128)(2,1)S(1)}, bf16[4,4096,512]{2,1,0:T(8,128)(2,1)}, u32[]{:S(2)}) copy-start(bf16[4,4096,512]{2,1,0:T(8,128)(2,1)} %in_order.1) | copy-start | bytes 50331652
  705.4 13.6 %copy-start.35 = (f32[32]{0:T(128)}, f32[32]{0:T(128)S(1)}, u32[]{:S(2)}) copy-start(f32[32]{0:T(128)S(1)} %add_rsqrt_fusion.13) | copy-start | bytes 388
  731.9 14.3 %copy-start.39 = (f32[32]{0:T(128)}, f32[32]{0:T(128)S(1)}, u32[]{:S(2)}) copy-start(f32[32]{0:T(128)S(1)} %add_rsqrt_fusion.12) | copy-start | bytes 388
  746.2 6.8 collective-permute-start.3
  765.9 13.5 %copy-start.41 = (f32[32]{0:T(128)}, f32[32]{0:T(128)S(1)}, u32[]{:S(2)}) copy-start(f32[32]{0:T(128)S(1)} %add_rsqrt_fusion.11) | copy-start | bytes 388
  793.8 13.5 %copy-start.45 = (f32[32]{0:T(128)}, f32[32]{0:T(128)S(1)}, u32[]{:S(2)}) copy-start(f32[32]{0:T(128)S(1)} %add_rsqrt_fusion.10) | copy-start | bytes 388
  824.3 15.3 %copy-start.43 = (f32[32]{0:T(128)}, f32[32]{0:T(128)S(1)}, u32[]{:S(2)}) copy-start(f32[32]{0:T(128)S(1)} %add_rsqrt_fusion.9) | copy-start | bytes 388
  853.6 15.3 %copy-start.47 = (f32[32]{0:T(128)}, f32[32]{0:T(128)S(1)}, u32[]{:S(2)}) copy-start(f32[32]{0:T(128)S(1)} %add_rsqrt_fusion.8) | copy-start | bytes 388
  869.7 7.4 collective-permute-start.4
  890.1 13.5 %copy-start.49 = (f32[32]{0:T(128)}, f32[32]{0:T(128)S(1)}, u32[]{:S(2)}) copy-start(f32[32]{0:T(128)S(1)} %add_rsqrt_fusion.7) | copy-start | bytes 388
  917.3 14.3 %copy-start.53 = (f32[32]{0:T(128)}, f32[32]{0:T(128)S(1)}, u32[]{:S(2)}) copy-start(f32[32]{0:T(128)S(1)} %add_rsqrt_fusion.6) | copy-start | bytes 388
  944.5 13.5 %copy-start.51 = (f32[32]{0:T(128)}, f32[32]{0:T(128)S(1)}, u32[]{:S(2)}) copy-start(f32[32]{0:T(128)S(1)} %add_rsqrt_fusion.5) | copy-start | bytes 388
  971.7 15.2 %copy-start.55 = (f32[32]{0:T(128)}, f32[32]{0:T(128)S(1)}, u32[]{:S(2)}) copy-start(f32[32]{0:T(128)S(1)} %add_rsqrt_fusion.4) | copy-start | bytes 388
  986.8 7.8 collective-permute-start.5
  1007.5 13.5 %copy-start.57 = (f32[32]{0:T(128)}, f32[32]{0:T(128)S(1)}, u32[]{:S(2)}) copy-start(f32[32]{0:T(128)S(1)} %add_rsqrt_fusion.3) | copy-start | bytes 388
  1034.8 13.6 %copy-start.61 = (f32[32]{0:T(128)}, f32[32]{0:T(128)S(1)}, u32[]{:S(2)}) copy-start(f32[32]{0:T(128)S(1)} %add_rsqrt_fusion.2) | copy-start | bytes 388
  1049.2 13.1 %copy-start.32 = (bf16[32,512]{1,0:T(8,128)(2,1)}, bf16[32,512]{1,0:T(8,128)(2,1)S(1)}, u32[]{:S(2)}) copy-start(bf16[32,512]{1,0:T(8,128)(2,1)S(1)} %fusion.27) | copy-start | bytes 98308
  1061.1 8.1 copy-start.30
  1061.1 8.8 copy-start.29
  1062.2 10.3 copy-start.59
  1064.7 54.2 %all-to-all-start.29 = ((bf16[8,32,512]{2,1,0:T(8,128)(2,1)}), bf16[8,32,512]{2,1,0:T(8,128)(2,1)S(1)}, u32[]{:S(2)}, u32[]{:S(2)}) async-start(bf16[8,32,512]{2,1,0:T(8,128)(2,1)} %broadcast_in_dim.111), calls=%async_computation.29 | async-start | bytes 524288 | tf_op jit(solution)/shard_map/all_to_all | solution.py:33
  1113.9 15.3 %copy-start.34 = (f32[32]{0:T(128)S(1)}, f32[32]{0:T(128)}, u32[]{:S(2)}) copy-start(f32[32]{0:T(128)} %copy-done.33) | copy-start | bytes 388
  1113.9 15.3 %copy-start.38 = (f32[32]{0:T(128)S(1)}, f32[32]{0:T(128)}, u32[]{:S(2)}) copy-start(f32[32]{0:T(128)} %copy-done.37) | copy-start | bytes 388
  1113.9 15.3 %copy-start.42 = (f32[32]{0:T(128)S(1)}, f32[32]{0:T(128)}, u32[]{:S(2)}) copy-start(f32[32]{0:T(128)} %copy-done.41) | copy-start | bytes 388
  1113.9 15.3 %copy-start.46 = (f32[32]{0:T(128)S(1)}, f32[32]{0:T(128)}, u32[]{:S(2)}) copy-start(f32[32]{0:T(128)} %copy-done.45) | copy-start | bytes 388
  1113.9 15.3 %copy-start.50 = (f32[32]{0:T(128)S(1)}, f32[32]{0:T(128)}, u32[]{:S(2)}) copy-start(f32[32]{0:T(128)} %copy-done.49) | copy-start | bytes 388
  1114.1 15.1 %copy-start.54 = (f32[32]{0:T(128)S(1)}, f32[32]{0:T(128)}, u32[]{:S(2)}) copy-start(f32[32]{0:T(128)} %copy-done.53) | copy-start | bytes 388
  1114.1 15.1 %copy-start.58 = (f32[32]{0:T(128)S(1)}, f32[32]{0:T(128)}, u32[]{:S(2)}) copy-start(f32[32]{0:T(128)} %copy-done.57) | copy-start | bytes 388
  1114.1 15.1 %copy-start.62 = (f32[32]{0:T(128)S(1)}, f32[32]{0:T(128)}, u32[]{:S(2)}) copy-start(f32[32]{0:T(128)} %copy-done.61) | copy-start | bytes 388
  1122.6 16.3 %all-to-all-start.30 = ((bf16[8,32,512]{2,1,0:T(8,128)(2,1)}), bf16[8,32,512]{2,1,0:T(8,128)(2,1)S(1)}, u32[]{:S(2)}, u32[]{:S(2)}) async-start(bf16[8,32,512]{2,1,0:T(8,128)(2,1)} %broadcast_in_dim.112), calls=%async_computation.30 | async-start | bytes 524288 | tf_op jit(solution)/shard_map/all_to_all | solution.py:33
  1135.1 8.6 copy-start.36
  1135.1 8.6 copy-start.40
  1135.2 8.6 copy-start.44
  1135.2 8.6 copy-start.48
  1135.2 8.6 copy-start.52
  1135.2 8.6 copy-start.56
  1135.2 8.6 copy-start.60
  1157.3 8.1 copy-start.19
  1157.3 8.1 copy-start.20
  1157.3 8.1 copy-start.21
  1157.3 8.1 copy-start.22
  1157.3 8.1 copy-start.23
  1157.3 8.1 copy-start.24
  1157.3 8.1 copy-start.25
  1157.4 8.1 copy-start.26
  1157.4 8.1 copy-start.27
  1157.4 8.1 copy-start.28
  1157.4 14.1 %all-to-all-start.31 = ((bf16[4,128,1024]{1,2,0:T(8,128)(2,1)}), bf16[4,128,1024]{1,2,0:T(8,128)(2,1)S(1)}, u32[]{:S(2)}, u32[]{:S(2)}) async-start(bf16[4,128,1024]{1,2,0:T(8,128)(2,1)} %bitcast.50), calls=%async_computation.31 | async-start | bytes 2097152 | tf_op jit(solution)/shard_map/all_to_all | solution.py:133
  1172.3 11.1 all-to-all-start.32
  1183.5 106.9 %copy-start.1 = (bf16[4,32,512]{2,1,0:T(8,128)(2,1)S(1)}, bf16[4,32,512]{2,1,0:T(8,128)(2,1)}, u32[]{:S(2)}) copy-start(bf16[4,32,512]{2,1,0:T(8,128)(2,1)} %param.5) | copy-start | bytes 393220
  1185.3 75.0 %collective-permute-start.6 = (bf16[8,64,512]{2,1,0:T(8,128)(2,1)S(1)}, bf16[8,64,512]{2,1,0:T(8,128)(2,1)S(1)}, u32[]{:S(2)}, u32[]{:S(2)}) collective-permute-start(bf16[8,64,512]{2,1,0:T(8,128)(2,1)S(1)} %fusion.47), channel_id=1, source_target_pairs={{0,32},{32,0},{64,96},{96,64},{128,160},{160,128},{192,224},{224,1... | collective-permute-start | bytes 1572872 | tf_op jit(solution)/shard_map/ppermute | solution.py:41
  1240.1 7.4 all-to-all-start.35
  1248.2 20.0 %all-to-all-start.36 = ((f32[16,8,128]{2,1,0:T(8,128)}), f32[16,8,128]{2,1,0:T(8,128)S(1)}, u32[]{:S(2)}, u32[]{:S(2)}) async-start(f32[16,8,128]{2,1,0:T(8,128)} %broadcast_in_dim.117), calls=%async_computation.36 | async-start | bytes 131072 | tf_op jit(solution)/shard_map/all_to_all | solution.py:33
  1268.2 21.5 %all-to-all-start.33 = ((bf16[8,64,512]{2,1,0:T(8,128)(2,1)}), bf16[8,64,512]{2,1,0:T(8,128)(2,1)S(1)}, u32[]{:S(2)}, u32[]{:S(2)}) async-start(bf16[8,64,512]{2,1,0:T(8,128)(2,1)} %fusion.30), calls=%async_computation.33 | async-start | bytes 1048576 | tf_op jit(solution)/shard_map/all_to_all | solution.py:143
  (16 other events, 89.3 us)
Sparse Core Ops, SparseCore 0:
  11.4 91.9 all-gather.2

commit v2 on v1

v2 whole, which is shorter than its diff:
```python
import math

import jax
import jax.numpy as jnp
from jax import lax
from jax.sharding import PartitionSpec as P

D = 4096
GROUP = 128
STAGE = 4

norm_eps = 1e-05
full_turn = 2.0 * math.pi

SIN_TERMS = (3.141592653536291, -5.167712764624543, 2.5501633189471025,
             -0.5992521978250058, 0.08205040181365181, -0.007028386419353805)
COS_TERMS = (0.9999999997799043, -4.934802137078827, 4.058709159556301,
             -1.3352120030506605, 0.23493731381815505, -0.024396324355626643)


def horner(terms, square):
    total = jnp.full_like(square, terms[-1])
    for term in terms[-2::-1]:
        total = total * square + term
    return total


def half_turn(ratio):
    part = ratio - jnp.round(ratio)
    square = part * part
    return part * horner(SIN_TERMS, square), horner(COS_TERMS, square)


def quantize(values, scale):
    ratio = values / scale
    sine, cosine = half_turn(ratio)
    return scale * jnp.clip(ratio - sine * cosine / math.pi, -8.0, 7.0)


def level_and_slope(values, scale):
    ratio = values / scale
    sine, cosine = half_turn(ratio)
    stair = ratio - sine * cosine / math.pi
    inside = (stair > -8.0) & (stair < 7.0)
    level = scale * jnp.clip(stair, -8.0, 7.0)
    return level, jnp.where(inside, 2.0 * sine * sine, 0.0)


def copies_of(value, count):
    return jnp.broadcast_to(value[None], (count,) + value.shape)


def gather(value, axis):
    return lax.all_to_all(copies_of(value, lax.axis_size(axis)), axis, 0, 0, tiled=True)


def crossed(value, mask):
    return lax.ppermute(value, "section", [(i, i ^ mask) for i in range(lax.axis_size("section"))])


def local(hidden_in, rotation, proj, norm_gain, quant_exp):
    sections = lax.axis_size("section")
    replicas = lax.axis_size("dp")
    section_pos = lax.axis_index("section")
    micro_count, tok_rows, part_cols = hidden_in.shape
    stages = sections // STAGE
    planes = sections // 2
    stage_pos = section_pos // STAGE
    place = section_pos % STAGE
    core = section_pos % 2
    lower = place < 2
    same_core = [[2 * z + c for z in range(planes)] for c in range(2)]
    row_block = rotation.shape[0]

    own = proj[0]
    by1 = crossed(own, 1)
    along_z = lax.all_to_all(
        copies_of(rotation, planes), "section", 0, 0, axis_index_groups=same_core, tiled=True
    )
    along_z, own_later = lax.optimization_barrier((along_z, own))
    by2 = crossed(own_later, 2)
    along_x = gather(along_z, "dp")
    other_rows = crossed(along_x, 1)
    even_rows = jnp.where(core == 0, along_x, other_rows)
    odd_rows = jnp.where(core == 0, other_rows, along_x)
    rot_cols = jnp.stack([even_rows, odd_rows]).transpose(2, 0, 1, 3, 4).reshape(D, part_cols)

    scale_row = jnp.repeat(jnp.exp2(quant_exp.astype(jnp.float32) * 0.25) * 0.125, GROUP, axis=1)
    params = jnp.concatenate([norm_gain, scale_row], axis=1)
    groups = [[STAGE * g + i for i in range(STAGE)] for g in range(stages)]
    params = lax.all_gather(params, "section", axis=0, tiled=True, axis_index_groups=groups)
    gains, scales = params[:, :D], params[:, D:]

    weights = jnp.zeros((STAGE,) + own.shape, own.dtype)
    weights = lax.dynamic_update_index_in_dim(weights, own, place, 0)
    weights = lax.dynamic_update_index_in_dim(weights, by1, place ^ 1, 0)

    def rotate(stream, layer):
        rows = gather(stream, "tp").transpose(1, 0, 2).reshape(stream.shape[0], D).astype(jnp.float32)
        mean_square = jnp.mean(rows * rows, axis=-1, keepdims=True)
        normed = (rows * lax.rsqrt(mean_square + norm_eps) * gains[layer]).astype(jnp.bfloat16)
        return normed, jnp.dot(normed, rot_cols, preferred_element_type=jnp.float32)

    def project(stream, rotated, layer):
        quantized = quantize(rotated, scales[layer]).astype(jnp.bfloat16)
        quant_full = gather(quantized, "tp").transpose(1, 0, 2).reshape(stream.shape[0], D)
        update = jnp.dot(quant_full, weights[layer], preferred_element_type=jnp.float32)
        return (stream.astype(jnp.float32) + update).astype(jnp.bfloat16)

    stream = jnp.concatenate(
        [lax.dynamic_index_in_dim(hidden_in, core + k, 0, keepdims=False) for k in (0, 2)], axis=0
    )
    early = []
    for layer in (0, 1):
        normed, rotated = rotate(stream, layer)
        early.append((normed, rotated))
        stream = project(stream, rotated, layer)
    first, second = stream[:tok_rows], stream[tok_rows:]
    stream = jnp.where(lower, first, crossed(second, 2))
    stream, by2 = lax.optimization_barrier((stream, by2))
    by3 = crossed(by2, 1)
    weights = lax.dynamic_update_index_in_dim(weights, by2, place ^ 2, 0)
    weights = lax.dynamic_update_index_in_dim(weights, by3, place ^ 3, 0)
    early_normed = jnp.concatenate([n for n, _ in early], axis=0).reshape(2, 2, tok_rows, D)
    early_rotated = jnp.concatenate([r for _, r in early], axis=0).reshape(2, 2, tok_rows, part_cols)
    moved_normed = crossed(early_normed[:, 1], 2)
    moved_rotated = crossed(early_rotated[:, 1], 2)
    early_normed = jnp.where(lower, early_normed[:, 0], moved_normed)
    early_rotated = jnp.where(lower, early_rotated[:, 0], moved_rotated)
    kept_normed = kept_rotated = None

    for stage in range(stages):
        normed_list, rotated_list = [], []
        for layer in range(STAGE):
            if stage == 0 and layer < 2:
                normed_list.append(early_normed[layer])
                rotated_list.append(early_rotated[layer])
                continue
            normed, rotated = rotate(stream, layer)
            normed_list.append(normed)
            rotated_list.append(rotated)
            if stage < stages - 1 or layer < STAGE - 1:
                stream = project(stream, rotated, layer)
        normed_now = jnp.concatenate(normed_list, axis=0)
        rotated_now = jnp.concatenate(rotated_list, axis=0)
        if stage == 0:
            kept_normed, kept_rotated = normed_now, rotated_now
        else:
            valid = stage_pos == stage
            kept_normed = jnp.where(valid, normed_now, kept_normed)
            kept_rotated = jnp.where(valid, rotated_now, kept_rotated)
        if stage < stages - 1:
            stream = lax.ppermute(
                stream, "section", [(i, i + STAGE) for i in range(sections - STAGE)]
            )

    all_rows = STAGE * tok_rows
    turned = lax.optimization_barrier(kept_normed.T)
    turned = turned.reshape(sections, replicas, row_block, all_rows).transpose(1, 0, 2, 3)
    turned = lax.all_to_all(turned, "dp", 0, 0, tiled=True)
    turned = turned.transpose(1, 2, 0, 3).reshape(sections * row_block, replicas * all_rows)
    row_scales = jnp.repeat(scales, tok_rows, axis=0)
    level, slope = level_and_slope(kept_rotated, row_scales)
    error_part = level - kept_rotated
    grad_rot = (error_part * (slope - 1.0)).astype(jnp.bfloat16)
    grad_all = gather(grad_rot, "dp").reshape(replicas * all_rows, part_cols)
    terms = jnp.dot(turned, grad_all, preferred_element_type=jnp.float32)

    loss = jnp.full((8, 128), jnp.sum(error_part * error_part), jnp.float32)
    loss = jnp.sum(gather(loss, "tp"), axis=0)
    loss = loss + crossed(loss, 1)
    loss = jnp.sum(gather(loss, "dp"), axis=0)
    high = lax.reduce_precision(loss[0, 0], 8, 7)
    middle = lax.reduce_precision(loss[0, 0] - high, 8, 7)
    low = loss[0, 0] - high - middle
    lane = lax.broadcasted_iota(jnp.int32, (16, part_cols), 1)
    tail_rows = jnp.where(lane == 0, high, jnp.where(lane == 1, middle, jnp.where(lane == 2, low, 0.0)))
    tail_rows = tail_rows.astype(jnp.bfloat16)

    halves = terms.reshape(planes, 2, row_block, part_cols)
    mine = lax.dynamic_index_in_dim(halves, core, 1, keepdims=False)
    other = lax.dynamic_index_in_dim(halves, 1 - core, 1, keepdims=False).astype(jnp.bfloat16)
    pair_sum = (mine + crossed(other, 1).astype(jnp.float32)).astype(jnp.bfloat16)
    sent = jnp.concatenate([pair_sum, copies_of(tail_rows, planes)], axis=1)
    parts = lax.all_to_all(sent, "section", 0, 0, axis_index_groups=same_core, tiled=True)
    sums = jnp.sum(parts.astype(jnp.float32), axis=0)
    factor = 1.0 / math.sqrt(sections * all_rows * replicas)
    norm_count = all_rows * replicas * D
    return (sums[:row_block] * factor, jnp.sum(sums[row_block, :3]) / norm_count)


def solution(mesh):
    placed = (
        P(None, "dp", "tp"),
        P(("section", "dp"), "tp"),
        P("section", None, "tp"),
        P("section", None),
        P("section", "tp"),
    )
    return jax.shard_map(
        local,
        mesh=mesh,
        in_specs=placed,
        out_specs=(P(("section", "dp"), "tp"), P()),
        check_vma=False,
    )
```

time: 1310 us -> 789 us (0.60)
  Pallas kernels: 509 us -> 0 us
  blocking collectives: 350 us -> 225 us
  waiting for transfers between devices: 138 us -> 205 us
  matrix products: 50.3 us -> 90.7 us
  starting transfers between devices: 125 us -> 162 us
    pallas_call x1 -> x0, Pallas kernels: 509 us -> none  [in_order(): pl.pallas_call(order_kernel, out_shape=jax.ShapeDtypeStruct((STAGE,) + ow...]
    all_to_all x9 -> x23, waiting for transfers between devices: 41.1 us -> 196 us  [the longest x22 190 us: gather(): lax.all_to_all(copies_of(value, lax.axis_size(axis)), axis, 0, 0, tiled=T...]
    all_to_all x28 -> x15, blocking collectives: 344 us -> 220 us  [the longest x13 164 us: gather(): lax.all_to_all(copies_of(value, lax.axis_size(axis)), axis, 0, 0, tiled=T...]
    ppermute x4 -> x9, waiting for transfers between devices: 92.9 us -> 6.64 us  [crossed(): lax.ppermute(value, 'section', [(i, i ^ mask) for i in range(lax.axis_siz...]
    convert_element_type x48 -> x32, local copies, waits for them, and re-layouts: 55.9 us -> 10.5 us  [the longest x16 10.1 us: rotate(): gather(stream, 'tp').transpose(1, 0, 2).reshape(stream.shape[0], D)]
    all_to_all x9 -> x23, starting transfers between devices: 47.8 us -> 90.1 us  [the longest x22 86.4 us: gather(): lax.all_to_all(copies_of(value, lax.axis_size(axis)), axis, 0, 0, tiled=T...]
    dot_general x32, matrix products: 50.3 us -> 90.7 us  [the longest x15 45 us: project(): jnp.dot(quant_full, weights[layer], preferred_element_type=jnp.float32)]
    broadcast_in_dim x34 -> x37, local copies, waits for them, and re-layouts: 5.69 us -> 25.1 us  [the longest x36 18.4 us: copies_of(): return jnp.broadcast_to(value[None], (count,) + value.shape)]
  transfers between devices with their start and end apart: 17 -> 35, of which waited for: 10 -> 27; matrix products, arithmetic and copies ran while one was open for 6% -> 12% of each run, Pallas kernels for 39% -> 0%
where the time goes in v2:
time: 789 us; the launch traced here: 784 us
  blocking collectives  225 us (29%)
  waiting for transfers between devices  205 us (26%)
  starting transfers between devices  162 us (21%)
  matrix products  90.7 us (11%)
  local copies, waits for them, and re-layouts  69.5 us (9%)
  other arithmetic  23.6 us (3%)
  between operations  8.02 us (1%)
    all_to_all x22, waiting for transfers between devices, gather(): lax.all_to_all(copies_of(value, lax.axis_size(axis)), axis, 0, 0, tiled=T...  190 us
    all_to_all x13, blocking collectives, gather(): lax.all_to_all(copies_of(value, lax.axis_size(axis)), axis, 0, 0, tiled=T...  164 us
    all_to_all x22, starting transfers between devices, gather(): lax.all_to_all(copies_of(value, lax.axis_size(axis)), axis, 0, 0, tiled=T...  86.4 us
    ppermute x9, starting transfers between devices, crossed(): lax.ppermute(value, 'section', [(i, i ^ mask) for i in range(lax.axis_siz...  61 us
    dot_general x15, matrix products, project(): jnp.dot(quant_full, weights[layer], preferred_element_type=jnp.float32)  45 us
    dot_general x16, matrix products, rotate(): jnp.dot(normed, rot_cols, preferred_element_type=jnp.float32)  44 us
    all_to_all x1, blocking collectives, local(): lax.all_to_all(sent, 'section', 0, 0, axis_index_groups=same_core, tiled=...  29.1 us
    all_to_all x1, blocking collectives, local(): lax.all_to_all(copies_of(rotation, planes), 'section', 0, 0, axis_index_g...  26.7 us
  transfers between devices with their start and end apart: 35, of which 27 were waited for; matrix products, arithmetic and copies ran while one was open for 12% of the time, Pallas kernels for 0%

profile of v2, /device:TPU:1, one launch (start us, length us, event | category | flops | bytes accessed | tf_op | source)
XLA Modules:
  0.0 783.8 jit_solution(16929005521681610087)
XLA Ops:
  1.6 26.7 %all_to_all.190 = bf16[8,64,512]{2,1,0:T(8,128)(2,1)S(1)} all-to-all(bf16[8,64,512]{2,1,0:T(8,128)(2,1)S(1)} %broadcast_in_dim.113), channel_id=1, replica_groups={{0,64,128,192,256,320,384,448},{32,96,160,224,288,352,416,480},{1,65,12..., dimensions={0} | all-to-all | bytes 1048576 | tf_op jit(solution)/shard_map/all_to_all | solution.py:77
  29.8 4.1 all-to-all-start.2
  33.9 4.6 collective-permute-start.1
  38.7 18.9 %all-to-all-done.2 = bf16[4,8,64,512]{3,2,1,0:T(8,128)(2,1)S(1)} async-done(((bf16[4,8,64,512]{3,2,1,0:T(8,128)(2,1)}), bf16[4,8,64,512]{3,2,1,0:T(8,128)(2,1)S(1)}, u32[]{:S(2)}, u32[]{:S(2)}) %all-to-all-start.2) | async-done | bytes 2097184 | tf_op jit(solution)/shard_map/all_to_all | solution.py:54
  58.4 6.8 all-to-all-start
  66.7 5.8 collective-permute-start
  72.6 5.1 all-gather
  78.5 6.7 broadcast_in_dim.116
  96.1 6.9 all-to-all-start.3
  103.0 4.5 bitcast_dynamic-update-slice_fusion.2
  107.5 13.5 %all-to-all-done.3 = bf16[8,64,512]{2,1,0:T(8,128)(2,1)S(1)} async-done(((bf16[8,64,512]{2,1,0:T(8,128)(2,1)}), bf16[8,64,512]{2,1,0:T(8,128)(2,1)S(1)}, u32[]{:S(2)}, u32[]{:S(2)}) %all-to-all-start.3) | async-done | bytes 524320 | tf_op jit(solution)/shard_map/all_to_all | solution.py:54
  124.9 3.5 all-to-all-start.4
  128.5 17.9 %all-to-all-done.4 = bf16[8,64,512]{2,1,0:T(8,128)(2,1)S(1)} async-done(((bf16[8,64,512]{2,1,0:T(8,128)(2,1)}), bf16[8,64,512]{2,1,0:T(8,128)(2,1)S(1)}, u32[]{:S(2)}, u32[]{:S(2)}) %all-to-all-start.4) | async-done | bytes 524320 | tf_op jit(solution)/shard_map/all_to_all | solution.py:54
  146.8 3.7 multiply_convert_fusion.16
  150.5 20.2 %all_to_all.191 = bf16[8,64,512]{2,1,0:T(8,128)(2,1)S(1)} all-to-all(bf16[8,64,512]{2,1,0:T(8,128)(2,1)S(1)} %broadcast_in_dim.119), channel_id=1, replica_groups=mesh['section'=16,'dp'=4,'tp'=8] {'tp'}, dimensions={0} | all-to-all | bytes 1048576 | tf_op jit(solution)/shard_map/all_to_all | solution.py:54
  177.1 5.8 collective-permute-done.2
  186.4 6.9 all-to-all-start.6
  193.4 12.3 %all-to-all-done.6 = bf16[8,32,512]{2,1,0:T(8,128)(2,1)S(1)} async-done(((bf16[8,32,512]{2,1,0:T(8,128)(2,1)}), bf16[8,32,512]{2,1,0:T(8,128)(2,1)S(1)}, u32[]{:S(2)}, u32[]{:S(2)}) %all-to-all-start.6) | async-done | bytes 262176 | tf_op jit(solution)/shard_map/all_to_all | solution.py:54
  206.0 3.6 multiply_convert_fusion.30
  213.8 4.4 bitcast_dynamic-update-slice_fusion.1
  218.2 7.7 all-to-all-done.7
  226.0 4.6 bitcast_dynamic-update-slice_fusion
  237.8 12.2 %all-to-all-done.8 = bf16[8,32,512]{2,1,0:T(8,128)(2,1)S(1)} async-done(((bf16[8,32,512]{2,1,0:T(8,128)(2,1)}), bf16[8,32,512]{2,1,0:T(8,128)(2,1)S(1)}, u32[]{:S(2)}, u32[]{:S(2)}) %all-to-all-start.8) | async-done | bytes 262176 | tf_op jit(solution)/shard_map/all_to_all | solution.py:54
  250.3 3.6 multiply_convert_fusion.29
  254.0 14.5 %all_to_all.192 = bf16[8,32,512]{2,1,0:T(8,128)(2,1)S(1)} all-to-all(bf16[8,32,512]{2,1,0:T(8,128)(2,1)S(1)} %broadcast_in_dim.125), channel_id=1, replica_groups=mesh['section'=16,'dp'=4,'tp'=8] {'tp'}, dimensions={0} | all-to-all | bytes 524288 | tf_op jit(solution)/shard_map/all_to_all | solution.py:54
  274.1 11.7 %all_to_all.193 = bf16[8,32,512]{2,1,0:T(8,128)(2,1)S(1)} all-to-all(bf16[8,32,512]{2,1,0:T(8,128)(2,1)S(1)} %broadcast_in_dim.126), channel_id=1, replica_groups=mesh['section'=16,'dp'=4,'tp'=8] {'tp'}, dimensions={0} | all-to-all | bytes 524288 | tf_op jit(solution)/shard_map/all_to_all | solution.py:54
  288.0 12.5 %all_to_all.194 = bf16[8,32,512]{2,1,0:T(8,128)(2,1)S(1)} all-to-all(bf16[8,32,512]{2,1,0:T(8,128)(2,1)S(1)} %broadcast_in_dim.127), channel_id=1, replica_groups=mesh['section'=16,'dp'=4,'tp'=8] {'tp'}, dimensions={0} | all-to-all | bytes 524288 | tf_op jit(solution)/shard_map/all_to_all | solution.py:54
  303.6 12.0 %all_to_all.195 = bf16[8,32,512]{2,1,0:T(8,128)(2,1)S(1)} all-to-all(bf16[8,32,512]{2,1,0:T(8,128)(2,1)S(1)} %broadcast_in_dim.128), channel_id=1, replica_groups=mesh['section'=16,'dp'=4,'tp'=8] {'tp'}, dimensions={0} | all-to-all | bytes 524288 | tf_op jit(solution)/shard_map/all_to_all | solution.py:54
  317.3 11.7 %all_to_all.196 = bf16[8,32,512]{2,1,0:T(8,128)(2,1)S(1)} all-to-all(bf16[8,32,512]{2,1,0:T(8,128)(2,1)S(1)} %broadcast_in_dim.129), channel_id=1, replica_groups=mesh['section'=16,'dp'=4,'tp'=8] {'tp'}, dimensions={0} | all-to-all | bytes 524288 | tf_op jit(solution)/shard_map/all_to_all | solution.py:54
  332.1 11.7 %all_to_all.197 = bf16[8,32,512]{2,1,0:T(8,128)(2,1)S(1)} all-to-all(bf16[8,32,512]{2,1,0:T(8,128)(2,1)S(1)} %broadcast_in_dim.130), channel_id=1, replica_groups=mesh['section'=16,'dp'=4,'tp'=8] {'tp'}, dimensions={0} | all-to-all | bytes 524288 | tf_op jit(solution)/shard_map/all_to_all | solution.py:54
  346.1 11.7 %all_to_all.198 = bf16[8,32,512]{2,1,0:T(8,128)(2,1)S(1)} all-to-all(bf16[8,32,512]{2,1,0:T(8,128)(2,1)S(1)} %broadcast_in_dim.131), channel_id=1, replica_groups=mesh['section'=16,'dp'=4,'tp'=8] {'tp'}, dimensions={0} | all-to-all | bytes 524288 | tf_op jit(solution)/shard_map/all_to_all | solution.py:54
  360.9 11.7 %all_to_all.199 = bf16[8,32,512]{2,1,0:T(8,128)(2,1)S(1)} all-to-all(bf16[8,32,512]{2,1,0:T(8,128)(2,1)S(1)} %broadcast_in_dim.132), channel_id=1, replica_groups=mesh['section'=16,'dp'=4,'tp'=8] {'tp'}, dimensions={0} | all-to-all | bytes 524288 | tf_op jit(solution)/shard_map/all_to_all | solution.py:54
  374.8 11.6 %all_to_all.200 = bf16[8,32,512]{2,1,0:T(8,128)(2,1)S(1)} all-to-all(bf16[8,32,512]{2,1,0:T(8,128)(2,1)S(1)} %broadcast_in_dim.133), channel_id=1, replica_groups=mesh['section'=16,'dp'=4,'tp'=8] {'tp'}, dimensions={0} | all-to-all | bytes 524288 | tf_op jit(solution)/shard_map/all_to_all | solution.py:54
  389.5 4.2 collective-permute-start.6
  394.7 11.7 %all_to_all.201 = bf16[8,32,512]{2,1,0:T(8,128)(2,1)S(1)} all-to-all(bf16[8,32,512]{2,1,0:T(8,128)(2,1)S(1)} %broadcast_in_dim.134), channel_id=1, replica_groups=mesh['section'=16,'dp'=4,'tp'=8] {'tp'}, dimensions={0} | all-to-all | bytes 524288 | tf_op jit(solution)/shard_map/all_to_all | solution.py:54
  408.2 13.7 %all_to_all.202 = bf16[8,32,512]{2,1,0:T(8,128)(2,1)S(1)} all-to-all(bf16[8,32,512]{2,1,0:T(8,128)(2,1)S(1)} %broadcast_in_dim.135), channel_id=1, replica_groups=mesh['section'=16,'dp'=4,'tp'=8] {'tp'}, dimensions={0} | all-to-all | bytes 524288 | tf_op jit(solution)/shard_map/all_to_all | solution.py:54
  430.9 7.6 all-to-all-done.20
  439.0 3.7 multiply_convert_fusion.23
  451.3 5.1 all-to-all-done.21
  466.3 9.2 %all-to-all-done.22 = bf16[8,32,512]{2,1,0:T(8,128)(2,1)S(1)} async-done(((bf16[8,32,512]{2,1,0:T(8,128)(2,1)}), bf16[8,32,512]{2,1,0:T(8,128)(2,1)S(1)}, u32[]{:S(2)}, u32[]{:S(2)}) %all-to-all-start.22) | async-done | bytes 262176 | tf_op jit(solution)/shard_map/all_to_all | solution.py:54
  476.2 3.6 multiply_convert_fusion.22
  486.1 9.8 %all-to-all-done.23 = bf16[8,32,512]{2,1,0:T(8,128)(2,1)S(1)} async-done(((bf16[8,32,512]{2,1,0:T(8,128)(2,1)}), bf16[8,32,512]{2,1,0:T(8,128)(2,1)S(1)}, u32[]{:S(2)}, u32[]{:S(2)}) %all-to-all-start.23) | async-done | bytes 262176 | tf_op jit(solution)/shard_map/all_to_all | solution.py:54
  508.3 4.4 all-to-all-done.24
  513.6 3.6 multiply_convert_fusion.21
  522.5 8.6 %all-to-all-done.25 = bf16[8,32,512]{2,1,0:T(8,128)(2,1)S(1)} async-done(((bf16[8,32,512]{2,1,0:T(8,128)(2,1)}), bf16[8,32,512]{2,1,0:T(8,128)(2,1)S(1)}, u32[]{:S(2)}, u32[]{:S(2)}) %all-to-all-start.25) | async-done | bytes 262176 | tf_op jit(solution)/shard_map/all_to_all | solution.py:54
  534.1 5.1 collective-permute-start.7
  546.2 9.1 %all-to-all-done.26 = bf16[8,32,512]{2,1,0:T(8,128)(2,1)S(1)} async-done(((bf16[8,32,512]{2,1,0:T(8,128)(2,1)}), bf16[8,32,512]{2,1,0:T(8,128)(2,1)S(1)}, u32[]{:S(2)}, u32[]{:S(2)}) %all-to-all-start.26) | async-done | bytes 262176 | tf_op jit(solution)/shard_map/all_to_all | solution.py:54
  555.7 3.6 multiply_convert_fusion.20
  560.0 3.6 all-to-all-start.27
  564.7 8.3 %all-to-all-done.27 = bf16[8,32,512]{2,1,0:T(8,128)(2,1)S(1)} async-done(((bf16[8,32,512]{2,1,0:T(8,128)(2,1)}), bf16[8,32,512]{2,1,0:T(8,128)(2,1)S(1)}, u32[]{:S(2)}, u32[]{:S(2)}) %all-to-all-start.27) | async-done | bytes 262176 | tf_op jit(solution)/shard_map/all_to_all | solution.py:54
  582.1 7.4 all-to-all-done.28
  589.9 3.6 multiply_convert_fusion.19
  597.9 9.0 %all-to-all-done.29 = bf16[8,32,512]{2,1,0:T(8,128)(2,1)S(1)} async-done(((bf16[8,32,512]{2,1,0:T(8,128)(2,1)}), bf16[8,32,512]{2,1,0:T(8,128)(2,1)S(1)}, u32[]{:S(2)}, u32[]{:S(2)}) %all-to-all-start.29) | async-done | bytes 262176 | tf_op jit(solution)/shard_map/all_to_all | solution.py:54
  616.0 7.4 all-to-all-done.30
  623.8 3.6 multiply_convert_fusion.18
  632.6 8.2 %all-to-all-done.31 = bf16[8,32,512]{2,1,0:T(8,128)(2,1)S(1)} async-done(((bf16[8,32,512]{2,1,0:T(8,128)(2,1)}), bf16[8,32,512]{2,1,0:T(8,128)(2,1)S(1)}, u32[]{:S(2)}, u32[]{:S(2)}) %all-to-all-start.31) | async-done | bytes 262176 | tf_op jit(solution)/shard_map/all_to_all | solution.py:54
  651.3 5.9 all-to-all-done.32
  662.4 3.7 all-to-all-start.33
  669.8 6.0 all-to-all-done.33
  683.5 3.6 all-to-all-done.34
  689.7 33.5 %collective-permute-start.10 = (bf16[8,64,512]{2,1,0:T(8,128)(2,1)S(1)}, bf16[8,64,512]{2,1,0:T(8,128)(2,1)S(1)}, u32[]{:S(2)}, u32[]{:S(2)}) collective-permute-start(bf16[8,64,512]{2,1,0:T(8,128)(2,1)S(1)} %fusion.67), channel_id=1, source_target_pairs={{0,32},{32,0},{64,96},{96,64},{128,160},{160,128},{192,224},{224,1... | collective-permute-start | bytes 1572872 | tf_op jit(solution)/shard_map/ppermute | solution.py:58
  724.7 9.2 %all_to_all.203 = f32[8,8,128]{2,1,0:T(8,128)S(1)} all-to-all(f32[8,8,128]{2,1,0:T(8,128)S(1)} %broadcast_in_dim_broadcast_in_dim_broadcast_in_dim.3), channel_id=1, replica_groups=mesh['section'=16,'dp'=4,'tp'=8] {'tp'}, dimensions={0} | all-to-all | bytes 65536 | tf_op jit(solution)/shard_map/all_to_all | solution.py:54
  741.7 4.2 all-to-all-done.36
  751.6 29.1 %all_to_all.204 = bf16[8,80,512]{2,1,0:T(8,128)(2,1)S(1)} all-to-all(bf16[8,80,512]{2,1,0:T(8,128)(2,1)S(1)} %pad_maximum_fusion.2), channel_id=1, replica_groups={{0,64,128,192,256,320,384,448},{32,96,160,224,288,352,416,480},{1,65,12..., dimensions={0} | all-to-all | bytes 1310720 | tf_op jit(solution)/shard_map/all_to_all | solution.py:185
  (396 shorter events, 207.0 us)
Async XLA Ops:
  0.6 38.0 %copy-start.52 = (bf16[4,32,512]{2,1,0:T(8,128)(2,1)S(1)}, bf16[4,32,512]{2,1,0:T(8,128)(2,1)}, u32[]{:S(2)}) copy-start(bf16[4,32,512]{2,1,0:T(8,128)(2,1)} %param.5) | copy-start | bytes 393220
  1.6 37.1 %copy-start.69 = (s32[1,4]{1,0:T(1,128)S(1)}, s32[1,4]{1,0:T(1,128)}, u32[]{:S(2)}) copy-start(s32[1,4]{1,0:T(1,128)} %param.9) | copy-start | bytes 52
  29.8 42.8 %copy-start.53 = (f32[1,4096]{1,0:T(1,128)S(1)}, f32[1,4096]{1,0:T(1,128)}, u32[]{:S(2)}) copy-start(f32[1,4096]{1,0:T(1,128)} %param.8) | copy-start | bytes 49156
  29.8 27.8 %all-to-all-start.2 = ((bf16[4,8,64,512]{3,2,1,0:T(8,128)(2,1)}), bf16[4,8,64,512]{3,2,1,0:T(8,128)(2,1)S(1)}, u32[]{:S(2)}, u32[]{:S(2)}) async-start(bf16[4,8,64,512]{3,2,1,0:T(8,128)(2,1)} %broadcast_in_dim.114), calls=%async_computation.2 | async-start | bytes 4194304 | tf_op jit(solution)/shard_map/all_to_all | solution.py:54
  33.9 69.1 %collective-permute-start.1 = (bf16[4096,512]{1,0:T(8,128)(2,1)}, bf16[4096,512]{1,0:T(8,128)(2,1)}, u32[]{:S(2)}, u32[]{:S(2)}) collective-permute-start(bf16[4096,512]{1,0:T(8,128)(2,1)} %bitcast.400), channel_id=1, source_target_pairs={{0,32},{32,0},{64,96},{96,64},{128,160},{160,128},{192,224},{224,1... | collective-permute-start | bytes 12582920 | tf_op jit(solution)/shard_map/ppermute | solution.py:58
  58.4 29.1 %all-to-all-start = ((bf16[8,64,512]{2,1,0:T(8,128)(2,1)}), bf16[8,64,512]{2,1,0:T(8,128)(2,1)S(1)}, u32[]{:S(2)}, u32[]{:S(2)}) async-start(bf16[8,64,512]{2,1,0:T(8,128)(2,1)} %broadcast_in_dim.112), calls=%async_computation | async-start | bytes 1048576 | tf_op jit(solution)/shard_map/all_to_all | solution.py:54
  66.7 23.3 %collective-permute-start = (bf16[4,8,64,512]{3,2,0,1:T(8,128)(2,1)}, bf16[4,8,64,512]{3,2,0,1:T(8,128)(2,1)}, u32[]{:S(2)}, u32[]{:S(2)}) collective-permute-start(bf16[4,8,64,512]{3,2,0,1:T(8,128)(2,1)} %copy.117), channel_id=1, source_target_pairs={{0,32},{32,0},{64,96},{96,64},{128,160},{160,128},{192,224},{224,1... | collective-permute-start | bytes 6291464 | tf_op jit(solution)/shard_map/ppermute | solution.py:58
  78.5 266.1 %copy-start.40 = (f32[1,512]{1,0:T(1,128)}, f32[1,512]{1,0:T(1,128)S(1)}, u32[]{:S(2)}) copy-start(f32[1,512]{1,0:T(1,128)S(1)} %get-tuple-element.29) | copy-start | bytes 6148
  78.5 294.9 %copy-start.47 = (f32[1,512]{1,0:T(1,128)}, f32[1,512]{1,0:T(1,128)S(1)}, u32[]{:S(2)}) copy-start(f32[1,512]{1,0:T(1,128)S(1)} %get-tuple-element.28) | copy-start | bytes 6148
  78.5 328.3 %copy-start.45 = (f32[1,512]{1,0:T(1,128)}, f32[1,512]{1,0:T(1,128)S(1)}, u32[]{:S(2)}) copy-start(f32[1,512]{1,0:T(1,128)S(1)} %get-tuple-element.31) | copy-start | bytes 6148
  78.5 360.4 %copy-start.43 = (f32[1,512]{1,0:T(1,128)}, f32[1,512]{1,0:T(1,128)S(1)}, u32[]{:S(2)}) copy-start(f32[1,512]{1,0:T(1,128)S(1)} %get-tuple-element.30) | copy-start | bytes 6148
  88.0 95.0 %collective-permute-start.3 = (bf16[4096,512]{1,0:T(8,128)(2,1)}, bf16[4096,512]{1,0:T(8,128)(2,1)}, u32[]{:S(2)}, u32[]{:S(2)}) collective-permute-start(bf16[4096,512]{1,0:T(8,128)(2,1)} %bitcast.401), channel_id=1, source_target_pairs={{0,64},{32,96},{64,0},{96,32},{128,192},{160,224},{192,128},{224,1... | collective-permute-start | bytes 12582920 | tf_op jit(solution)/shard_map/ppermute | solution.py:58
  96.1 24.9 %all-to-all-start.3 = ((bf16[8,64,512]{2,1,0:T(8,128)(2,1)}), bf16[8,64,512]{2,1,0:T(8,128)(2,1)S(1)}, u32[]{:S(2)}, u32[]{:S(2)}) async-start(bf16[8,64,512]{2,1,0:T(8,128)(2,1)} %broadcast_in_dim.115), calls=%async_computation.3 | async-start | bytes 1048576 | tf_op jit(solution)/shard_map/all_to_all | solution.py:54
  124.9 21.4 %all-to-all-start.4 = ((bf16[8,64,512]{2,1,0:T(8,128)(2,1)}), bf16[8,64,512]{2,1,0:T(8,128)(2,1)S(1)}, u32[]{:S(2)}, u32[]{:S(2)}) async-start(bf16[8,64,512]{2,1,0:T(8,128)(2,1)} %broadcast_in_dim.118), calls=%async_computation.4 | async-start | bytes 1048576 | tf_op jit(solution)/shard_map/all_to_all | solution.py:54
  128.4 310.3 %copy-start.17 = (f32[8,512]{1,0:T(8,128)}, f32[8,512]{1,0:T(8,128)S(1)}, u32[]{:S(2)}) copy-start(f32[8,512]{1,0:T(8,128)S(1)} %mul.1344) | copy-start | bytes 49156
  146.5 24.2 %copy-start.58 = (f32[64]{0:T(128)}, f32[64]{0:T(128)S(1)}, u32[]{:S(2)}) copy-start(f32[64]{0:T(128)S(1)} %add_rsqrt_fusion.14) | copy-start | bytes 772
  173.8 9.1 %collective-permute-start.2 = (bf16[32,512]{1,0:T(8,128)(2,1)S(1)}, bf16[32,512]{1,0:T(8,128)(2,1)S(1)}, u32[]{:S(2)}, u32[]{:S(2)}) collective-permute-start(bf16[32,512]{1,0:T(8,128)(2,1)S(1)} %slice.162), channel_id=1, source_target_pairs={{0,64},{32,96},{64,0},{96,32},{128,192},{160,224},{192,128},{224,1... | collective-permute-start | bytes 98312 | tf_op jit(solution)/shard_map/ppermute | solution.py:58
  182.9 43.1 %collective-permute-start.4 = (bf16[4096,512]{1,0:T(8,128)(2,1)}, bf16[4096,512]{1,0:T(8,128)(2,1)}, u32[]{:S(2)}, u32[]{:S(2)}) collective-permute-start(bf16[4096,512]{1,0:T(8,128)(2,1)} %collective-permute-done.3), channel_id=1, source_target_pairs={{0,32},{32,0},{64,96},{96,64},{128,160},{160,128},{192,224},{224,1... | collective-permute-start | bytes 12582920 | tf_op jit(solution)/shard_map/ppermute | solution.py:58
  186.4 19.3 %all-to-all-start.6 = ((bf16[8,32,512]{2,1,0:T(8,128)(2,1)}), bf16[8,32,512]{2,1,0:T(8,128)(2,1)S(1)}, u32[]{:S(2)}, u32[]{:S(2)}) async-start(bf16[8,32,512]{2,1,0:T(8,128)(2,1)} %broadcast_in_dim.120), calls=%async_computation.6 | async-start | bytes 524288 | tf_op jit(solution)/shard_map/all_to_all | solution.py:54
  193.3 150.7 %copy-start.22 = (f32[8,512]{1,0:T(8,128)}, f32[8,512]{1,0:T(8,128)S(1)}, u32[]{:S(2)}) copy-start(f32[8,512]{1,0:T(8,128)S(1)} %mul.1365) | copy-start | bytes 49156
  205.9 12.3 %copy-start.62 = (f32[32]{0:T(128)}, f32[32]{0:T(128)S(1)}, u32[]{:S(2)}) copy-start(f32[32]{0:T(128)S(1)} %add_rsqrt_fusion.13) | copy-start | bytes 388
  210.4 15.6 %all-to-all-start.7 = ((bf16[8,32,512]{2,1,0:T(8,128)(2,1)}), bf16[8,32,512]{2,1,0:T(8,128)(2,1)S(1)}, u32[]{:S(2)}, u32[]{:S(2)}) async-start(bf16[8,32,512]{2,1,0:T(8,128)(2,1)} %broadcast_in_dim.121), calls=%async_computation.7 | async-start | bytes 524288 | tf_op jit(solution)/shard_map/all_to_all | solution.py:54
  234.3 15.6 %all-to-all-start.8 = ((bf16[8,32,512]{2,1,0:T(8,128)(2,1)}), bf16[8,32,512]{2,1,0:T(8,128)(2,1)S(1)}, u32[]{:S(2)}, u32[]{:S(2)}) async-start(bf16[8,32,512]{2,1,0:T(8,128)(2,1)} %broadcast_in_dim.124), calls=%async_computation.8 | async-start | bytes 524288 | tf_op jit(solution)/shard_map/all_to_all | solution.py:54
  237.8 135.0 %copy-start.19 = (f32[8,512]{1,0:T(8,128)}, f32[8,512]{1,0:T(8,128)S(1)}, u32[]{:S(2)}) copy-start(f32[8,512]{1,0:T(8,128)S(1)} %mul.1386) | copy-start | bytes 49156
  250.1 21.3 %copy-start.63 = (f32[32]{0:T(128)}, f32[32]{0:T(128)S(1)}, u32[]{:S(2)}) copy-start(f32[32]{0:T(128)S(1)} %add_rsqrt_fusion.12) | copy-start | bytes 388
  253.9 32.6 %copy-start.1 = (bf16[2,4,8,64,512]{4,3,1,0,2:T(8,128)(2,1)S(1)}, bf16[2,4,8,64,512]{4,3,1,0,2:T(8,128)(2,1)}, u32[]{:S(2)}) copy-start(bf16[2,4,8,64,512]{4,3,1,0,2:T(8,128)(2,1)} %copy-done) | copy-start | bytes 12582916
  271.5 2.6 collective-permute-start.5
  315.7 16.4 %copy-start.55 = (f32[32]{0:T(128)}, f32[32]{0:T(128)S(1)}, u32[]{:S(2)}) copy-start(f32[32]{0:T(128)S(1)} %add_rsqrt_fusion.10) | copy-start | bytes 388
  389.5 5.2 collective-permute-start.6
  406.6 15.3 %copy-start.57 = (f32[32]{0:T(128)}, f32[32]{0:T(128)S(1)}, u32[]{:S(2)}) copy-start(f32[32]{0:T(128)S(1)} %add_rsqrt_fusion.7) | copy-start | bytes 388
  424.9 17.7 %copy-start.48 = (bf16[32,512]{1,0:T(8,128)(2,1)}, bf16[32,512]{1,0:T(8,128)(2,1)S(1)}, u32[]{:S(2)}) copy-start(bf16[32,512]{1,0:T(8,128)(2,1)S(1)} %add_convert_fusion.7) | copy-start | bytes 98308
  425.7 12.9 %all-to-all-start.20 = ((bf16[8,32,512]{2,1,0:T(8,128)(2,1)}), bf16[8,32,512]{2,1,0:T(8,128)(2,1)S(1)}, u32[]{:S(2)}, u32[]{:S(2)}) async-start(bf16[8,32,512]{2,1,0:T(8,128)(2,1)} %broadcast_in_dim.136), calls=%async_computation.20 | async-start | bytes 524288 | tf_op jit(solution)/shard_map/all_to_all | solution.py:54
  443.3 13.1 %all-to-all-start.21 = ((bf16[8,32,512]{2,1,0:T(8,128)(2,1)}), bf16[8,32,512]{2,1,0:T(8,128)(2,1)S(1)}, u32[]{:S(2)}, u32[]{:S(2)}) async-start(bf16[8,32,512]{2,1,0:T(8,128)(2,1)} %broadcast_in_dim.137), calls=%async_computation.21 | async-start | bytes 524288 | tf_op jit(solution)/shard_map/all_to_all | solution.py:54
  448.7 59.6 %collective-permute-start.9 = (f32[2,32,512]{2,1,0:T(8,128)}, f32[2,32,512]{2,1,0:T(8,128)}, u32[]{:S(2)}, u32[]{:S(2)}) collective-permute-start(f32[2,32,512]{2,1,0:T(8,128)} %slice_bitcast_fusion.29), channel_id=1, source_target_pairs={{0,64},{32,96},{64,0},{96,32},{128,192},{160,224},{192,128},{224,1... | collective-permute-start | bytes 393224 | tf_op jit(solution)/shard_map/ppermute | solution.py:58
  456.5 19.2 %copy-start.23 = (f32[8,512]{1,0:T(8,128)S(1)}, f32[8,512]{1,0:T(8,128)}, u32[]{:S(2)}) copy-start(f32[8,512]{1,0:T(8,128)} %copy-done.22) | copy-start | bytes 49156
  456.5 19.8 %copy-start.41 = (f32[1,512]{1,0:T(1,128)S(1)}, f32[1,512]{1,0:T(1,128)}, u32[]{:S(2)}) copy-start(f32[1,512]{1,0:T(1,128)} %copy-done.40) | copy-start | bytes 6148
  460.2 15.3 %all-to-all-start.22 = ((bf16[8,32,512]{2,1,0:T(8,128)(2,1)}), bf16[8,32,512]{2,1,0:T(8,128)(2,1)S(1)}, u32[]{:S(2)}, u32[]{:S(2)}) async-start(bf16[8,32,512]{2,1,0:T(8,128)(2,1)} %broadcast_in_dim.138), calls=%async_computation.22 | async-start | bytes 524288 | tf_op jit(solution)/shard_map/all_to_all | solution.py:54
  480.6 15.3 %all-to-all-start.23 = ((bf16[8,32,512]{2,1,0:T(8,128)(2,1)}), bf16[8,32,512]{2,1,0:T(8,128)(2,1)S(1)}, u32[]{:S(2)}, u32[]{:S(2)}) async-start(bf16[8,32,512]{2,1,0:T(8,128)(2,1)} %broadcast_in_dim.139), calls=%async_computation.23 | async-start | bytes 524288 | tf_op jit(solution)/shard_map/all_to_all | solution.py:54
  486.1 27.3 %copy-start.20 = (f32[8,512]{1,0:T(8,128)S(1)}, f32[8,512]{1,0:T(8,128)}, u32[]{:S(2)}) copy-start(f32[8,512]{1,0:T(8,128)} %copy-done.19) | copy-start | bytes 49156
  499.6 13.0 %all-to-all-start.24 = ((bf16[8,32,512]{2,1,0:T(8,128)(2,1)}), bf16[8,32,512]{2,1,0:T(8,128)(2,1)S(1)}, u32[]{:S(2)}, u32[]{:S(2)}) async-start(bf16[8,32,512]{2,1,0:T(8,128)(2,1)} %broadcast_in_dim.140), calls=%async_computation.24 | async-start | bytes 524288 | tf_op jit(solution)/shard_map/all_to_all | solution.py:54
  504.9 16.4 %collective-permute-start.8 = (bf16[2,32,4096]{2,1,0:T(8,128)(2,1)}, bf16[2,32,4096]{2,1,0:T(8,128)(2,1)}, u32[]{:S(2)}, u32[]{:S(2)}) collective-permute-start(bf16[2,32,4096]{2,1,0:T(8,128)(2,1)} %slice_bitcast_fusion.25), channel_id=1, source_target_pairs={{0,64},{32,96},{64,0},{96,32},{128,192},{160,224},{192,128},{224,1... | collective-permute-start | bytes 1572872 | tf_op jit(solution)/shard_map/ppermute | solution.py:58
  517.9 13.1 %all-to-all-start.25 = ((bf16[8,32,512]{2,1,0:T(8,128)(2,1)}), bf16[8,32,512]{2,1,0:T(8,128)(2,1)S(1)}, u32[]{:S(2)}, u32[]{:S(2)}) async-start(bf16[8,32,512]{2,1,0:T(8,128)(2,1)} %broadcast_in_dim.141), calls=%async_computation.25 | async-start | bytes 524288 | tf_op jit(solution)/shard_map/all_to_all | solution.py:54
  534.1 21.6 %copy-start.46 = (f32[1,512]{1,0:T(1,128)S(1)}, f32[1,512]{1,0:T(1,128)}, u32[]{:S(2)}) copy-start(f32[1,512]{1,0:T(1,128)} %copy-done.45) | copy-start | bytes 6148
  534.1 6.1 collective-permute-start.7
  540.9 14.4 %all-to-all-start.26 = ((bf16[8,32,512]{2,1,0:T(8,128)(2,1)}), bf16[8,32,512]{2,1,0:T(8,128)(2,1)S(1)}, u32[]{:S(2)}, u32[]{:S(2)}) async-start(bf16[8,32,512]{2,1,0:T(8,128)(2,1)} %broadcast_in_dim.142), calls=%async_computation.26 | async-start | bytes 524288 | tf_op jit(solution)/shard_map/all_to_all | solution.py:54
  560.0 13.0 %all-to-all-start.27 = ((bf16[8,32,512]{2,1,0:T(8,128)(2,1)}), bf16[8,32,512]{2,1,0:T(8,128)(2,1)S(1)}, u32[]{:S(2)}, u32[]{:S(2)}) async-start(bf16[8,32,512]{2,1,0:T(8,128)(2,1)} %broadcast_in_dim.143), calls=%async_computation.27 | async-start | bytes 524288 | tf_op jit(solution)/shard_map/all_to_all | solution.py:54
  573.1 16.6 %copy-start.18 = (f32[8,512]{1,0:T(8,128)S(1)}, f32[8,512]{1,0:T(8,128)}, u32[]{:S(2)}) copy-start(f32[8,512]{1,0:T(8,128)} %copy-done.17) | copy-start | bytes 49156
  573.1 16.8 %copy-start.44 = (f32[1,512]{1,0:T(1,128)S(1)}, f32[1,512]{1,0:T(1,128)}, u32[]{:S(2)}) copy-start(f32[1,512]{1,0:T(1,128)} %copy-done.43) | copy-start | bytes 6148
  576.1 17.4 %copy-start.51 = (bf16[32,512]{1,0:T(8,128)(2,1)}, bf16[32,512]{1,0:T(8,128)(2,1)S(1)}, u32[]{:S(2)}) copy-start(bf16[32,512]{1,0:T(8,128)(2,1)S(1)} %add_convert_fusion.3) | copy-start | bytes 98308
  576.9 12.7 %all-to-all-start.28 = ((bf16[8,32,512]{2,1,0:T(8,128)(2,1)}), bf16[8,32,512]{2,1,0:T(8,128)(2,1)S(1)}, u32[]{:S(2)}, u32[]{:S(2)}) async-start(bf16[8,32,512]{2,1,0:T(8,128)(2,1)} %broadcast_in_dim.144), calls=%async_computation.28 | async-start | bytes 524288 | tf_op jit(solution)/shard_map/all_to_all | solution.py:54
  594.3 12.7 %all-to-all-start.29 = ((bf16[8,32,512]{2,1,0:T(8,128)(2,1)}), bf16[8,32,512]{2,1,0:T(8,128)(2,1)S(1)}, u32[]{:S(2)}, u32[]{:S(2)}) async-start(bf16[8,32,512]{2,1,0:T(8,128)(2,1)} %broadcast_in_dim.145), calls=%async_computation.29 | async-start | bytes 524288 | tf_op jit(solution)/shard_map/all_to_all | solution.py:54
  607.0 16.6 %copy-start.24 = (f32[8,512]{1,0:T(8,128)S(1)}, f32[8,512]{1,0:T(8,128)}, u32[]{:S(2)}) copy-start(f32[8,512]{1,0:T(8,128)} %copy-done.22) | copy-start | bytes 49156
  607.0 16.8 %copy-start.42 = (f32[1,512]{1,0:T(1,128)S(1)}, f32[1,512]{1,0:T(1,128)}, u32[]{:S(2)}) copy-start(f32[1,512]{1,0:T(1,128)} %copy-done.40) | copy-start | bytes 6148
  610.0 13.8 %copy-start.50 = (bf16[32,512]{1,0:T(8,128)(2,1)}, bf16[32,512]{1,0:T(8,128)(2,1)S(1)}, u32[]{:S(2)}) copy-start(bf16[32,512]{1,0:T(8,128)(2,1)S(1)} %add_convert_fusion.2) | copy-start | bytes 98308
  610.7 12.7 %all-to-all-start.30 = ((bf16[8,32,512]{2,1,0:T(8,128)(2,1)}), bf16[8,32,512]{2,1,0:T(8,128)(2,1)S(1)}, u32[]{:S(2)}, u32[]{:S(2)}) async-start(bf16[8,32,512]{2,1,0:T(8,128)(2,1)} %broadcast_in_dim.146), calls=%async_computation.30 | async-start | bytes 524288 | tf_op jit(solution)/shard_map/all_to_all | solution.py:54
  628.1 12.7 %all-to-all-start.31 = ((bf16[8,32,512]{2,1,0:T(8,128)(2,1)}), bf16[8,32,512]{2,1,0:T(8,128)(2,1)S(1)}, u32[]{:S(2)}, u32[]{:S(2)}) async-start(bf16[8,32,512]{2,1,0:T(8,128)(2,1)} %broadcast_in_dim.147), calls=%async_computation.31 | async-start | bytes 524288 | tf_op jit(solution)/shard_map/all_to_all | solution.py:54
  631.7 16.3 %copy-start.3 = (f32[8,4,8,512]{3,2,0,1:T(8,128)S(1)}, f32[8,4,8,512]{3,2,0,1:T(8,128)}, u32[]{:S(2)}) copy-start(f32[8,4,8,512]{3,2,0,1:T(8,128)} %copy.215) | copy-start | bytes 1572868
  631.7 16.3 %copy-start.38 = (f32[1,4096]{1,0:T(1,128)S(1)}, f32[1,4096]{1,0:T(1,128)}, u32[]{:S(2)}) copy-start(f32[1,4096]{1,0:T(1,128)} %get-tuple-element.24) | copy-start | bytes 49156
  644.6 12.7 %all-to-all-start.32 = ((bf16[8,32,512]{2,1,0:T(8,128)(2,1)}), bf16[8,32,512]{2,1,0:T(8,128)(2,1)S(1)}, u32[]{:S(2)}, u32[]{:S(2)}) async-start(bf16[8,32,512]{2,1,0:T(8,128)(2,1)} %broadcast_in_dim.148), calls=%async_computation.32 | async-start | bytes 524288 | tf_op jit(solution)/shard_map/all_to_all | solution.py:54
  662.4 13.4 %all-to-all-start.33 = ((bf16[4,16,64,128]{3,2,1,0:T(8,128)(2,1)}), bf16[4,16,64,128]{3,2,1,0:T(8,128)(2,1)S(1)}, u32[]{:S(2)}, u32[]{:S(2)}) async-start(bf16[4,16,64,128]{3,2,1,0:T(8,128)(2,1)} %copy.167), calls=%async_computation.33 | async-start | bytes 2097152 | tf_op jit(solution)/shard_map/all_to_all | solution.py:160
  676.6 10.4 %all-to-all-start.34 = ((bf16[4,128,512]{2,1,0:T(8,128)(2,1)}), bf16[4,128,512]{2,1,0:T(8,128)(2,1)S(1)}, u32[]{:S(2)}, u32[]{:S(2)}) async-start(bf16[4,128,512]{2,1,0:T(8,128)(2,1)} %broadcast_in_dim.153), calls=%async_computation.34 | async-start | bytes 1048576 | tf_op jit(solution)/shard_map/all_to_all | solution.py:54
  689.7 61.7 %collective-permute-start.10 = (bf16[8,64,512]{2,1,0:T(8,128)(2,1)S(1)}, bf16[8,64,512]{2,1,0:T(8,128)(2,1)S(1)}, u32[]{:S(2)}, u32[]{:S(2)}) collective-permute-start(bf16[8,64,512]{2,1,0:T(8,128)(2,1)S(1)} %fusion.67), channel_id=1, source_target_pairs={{0,32},{32,0},{64,96},{96,64},{128,160},{160,128},{192,224},{224,1... | collective-permute-start | bytes 1572872 | tf_op jit(solution)/shard_map/ppermute | solution.py:58
  733.9 3.9 collective-permute-start.11
  738.4 7.4 all-to-all-start.36
  (41 other events, 218.1 us)

commit v3 on v2

v3 whole, which is shorter than its diff:
```python
import math

import jax
import jax.numpy as jnp
from jax import lax
from jax.experimental import pallas as pl
from jax.experimental.pallas import tpu as pltpu
from jax.sharding import PartitionSpec as P

D = 4096
GROUP = 128
STAGE = 4

norm_eps = 1e-05
full_turn = 2.0 * math.pi

SIN_TERMS = (3.141592653536291, -5.167712764624543, 2.5501633189471025,
             -0.5992521978250058, 0.08205040181365181, -0.007028386419353805)
COS_TERMS = (0.9999999997799043, -4.934802137078827, 4.058709159556301,
             -1.3352120030506605, 0.23493731381815505, -0.024396324355626643)


def horner(terms, square):
    total = jnp.full_like(square, terms[-1])
    for term in terms[-2::-1]:
        total = total * square + term
    return total


def half_turn(ratio):
    part = ratio - jnp.round(ratio)
    square = part * part
    return part * horner(SIN_TERMS, square), horner(COS_TERMS, square)


def quantize(values, scale):
    ratio = values / scale
    sine, cosine = half_turn(ratio)
    return scale * jnp.clip(ratio - sine * cosine / math.pi, -8.0, 7.0)


def level_and_slope(values, scale):
    ratio = values / scale
    sine, cosine = half_turn(ratio)
    stair = ratio - sine * cosine / math.pi
    inside = (stair > -8.0) & (stair < 7.0)
    level = scale * jnp.clip(stair, -8.0, 7.0)
    return level, jnp.where(inside, 2.0 * sine * sine, 0.0)


def copies_of(value, count):
    return jnp.broadcast_to(value[None], (count,) + value.shape)


def exchange(copies, axis):
    return lax.all_to_all(copies, axis, 0, 0, tiled=True)


def gather(value, axis):
    return exchange(copies_of(value, lax.axis_size(axis)), axis)


def crossed(value, mask):
    return lax.ppermute(value, "section", [(i, i ^ mask) for i in range(lax.axis_size("section"))])


VMEM = pl.BlockSpec(memory_space=pltpu.VMEM)
PARAMS = pltpu.CompilerParams(vmem_limit_bytes=8 * 1024 * 1024)


def load_kernel(place_ref, own, by1, by2, by3, *rest):
    outs, sems = rest[:STAGE], rest[STAGE]
    sources = (own, by1, by2, by3)
    place = place_ref[0]
    for layer in range(STAGE):
        for mask in range(STAGE):
            @pl.when((place ^ layer) == mask)
            def _():
                pltpu.make_async_copy(sources[mask], outs[layer], sems.at[layer]).start()
    for layer in range(STAGE):
        pltpu.make_async_copy(own, outs[layer], sems.at[layer]).wait()


def load_weights(place, own, by1, by2, by3):
    far = pl.BlockSpec(memory_space=pl.ANY)
    return pl.pallas_call(
        load_kernel,
        out_shape=[jax.ShapeDtypeStruct(own.shape, own.dtype)] * STAGE,
        in_specs=[pl.BlockSpec(memory_space=pltpu.SMEM)] + [far] * 4,
        out_specs=[VMEM] * STAGE,
        scratch_shapes=[pltpu.SemaphoreType.DMA((STAGE,))],
        compiler_params=PARAMS,
        name="load_weights",
    )(place, own, by1, by2, by3)


def rotate_kernel(rows_ref, gain_ref, rot_ref, scale_ref, normed_ref, rotated_ref, *copies):
    count, _, part = rows_ref.shape
    total = None
    for k in range(count):
        rows = rows_ref[k].astype(jnp.float32)
        square = jnp.sum(rows * rows, axis=-1, keepdims=True)
        total = square if total is None else total + square
    factor = lax.rsqrt(total / (count * part) + norm_eps)
    for k in range(count):
        cols = slice(k * part, (k + 1) * part)
        rows = rows_ref[k].astype(jnp.float32)
        normed_ref[:, cols] = (rows * factor * gain_ref[:, cols]).astype(jnp.bfloat16)
    rotated = jnp.dot(normed_ref[...], rot_ref[...], preferred_element_type=jnp.float32)
    rotated_ref[...] = rotated
    if copies:
        quantized = quantize(rotated, scale_ref[...]).astype(jnp.bfloat16)
        for k in range(count):
            copies[0][k] = quantized


def rotate(rows, gain, rot_cols, scale, last):
    count, tok_rows, part = rows.shape
    shapes = [
        jax.ShapeDtypeStruct((tok_rows, count * part), jnp.bfloat16),
        jax.ShapeDtypeStruct((tok_rows, part), jnp.float32),
        jax.ShapeDtypeStruct(rows.shape, jnp.bfloat16),
    ][: 2 if last else 3]
    return pl.pallas_call(
        rotate_kernel,
        out_shape=shapes,
        in_specs=[VMEM] * 4,
        out_specs=[VMEM] * len(shapes),
        compiler_params=PARAMS,
        name="rotate",
    )(rows, gain, rot_cols, scale)


def project_kernel(quant_ref, weight_ref, stream_ref, out_ref):
    count, tok_rows, part = quant_ref.shape
    total = stream_ref[0].astype(jnp.float32)
    for k in range(count):
        total = total + jnp.dot(
            quant_ref[k], weight_ref[k * part : (k + 1) * part, :], preferred_element_type=jnp.float32
        )
    stream = total.astype(jnp.bfloat16)
    for k in range(count):
        out_ref[k] = stream


def project(quant_rows, weight, copies):
    return pl.pallas_call(
        project_kernel,
        out_shape=jax.ShapeDtypeStruct(copies.shape, jnp.bfloat16),
        in_specs=[VMEM] * 3,
        out_specs=VMEM,
        compiler_params=PARAMS,
        name="project",
    )(quant_rows, weight, copies)


def local(hidden_in, rotation, proj, norm_gain, quant_exp):
    sections = lax.axis_size("section")
    replicas = lax.axis_size("dp")
    tensor = lax.axis_size("tp")
    section_pos = lax.axis_index("section")
    micro_count, tok_rows, part_cols = hidden_in.shape
    stages = sections // STAGE
    planes = sections // 2
    stage_pos = section_pos // STAGE
    place = section_pos % STAGE
    core = section_pos % 2
    same_core = [[2 * z + c for z in range(planes)] for c in range(2)]
    row_block = rotation.shape[0]

    own = proj[0]
    by2 = crossed(own, 2)
    by1 = crossed(own, 1)

    along_z = lax.all_to_all(
        copies_of(rotation, planes), "section", 0, 0, axis_index_groups=same_core, tiled=True
    )
    scale_row = jnp.repeat(jnp.exp2(quant_exp.astype(jnp.float32) * 0.25) * 0.125, GROUP, axis=1)
    params = jnp.concatenate([norm_gain, scale_row], axis=1)
    groups = [[STAGE * g + i for i in range(STAGE)] for g in range(stages)]
    params = lax.all_gather(params, "section", axis=0, tiled=True, axis_index_groups=groups)
    along_z, params = lax.optimization_barrier((along_z, params))
    gains, scales = params[:, :D], params[:, D:]
    along_x = gather(along_z, "dp")
    other_rows = crossed(along_x, 1)
    even_rows = jnp.where(core == 0, along_x, other_rows)
    odd_rows = jnp.where(core == 0, other_rows, along_x)
    rot_cols = jnp.stack([even_rows, odd_rows]).transpose(2, 0, 1, 3, 4).reshape(D, part_cols)

    copies = copies_of(lax.dynamic_index_in_dim(hidden_in, place, 0, keepdims=False), tensor)
    kept_normed = kept_rotated = None
    for stage in range(stages):
        normed_list, rotated_list = [], []
        for layer in range(STAGE):
            last = stage == stages - 1 and layer == STAGE - 1
            rows = exchange(copies, "tp")
            normed, rotated, *quant = rotate(
                rows, gains[layer : layer + 1], rot_cols, scales[layer : layer + 1], last
            )
            normed_list.append(normed)
            rotated_list.append(rotated)
            if stage == 0 and layer == 0:
                by2, _ = lax.optimization_barrier((by2, quant[0]))
                by3 = crossed(by2, 1)
                weights = load_weights(place[None].astype(jnp.int32), own, by1, by2, by3)
            if not last:
                copies = project(exchange(quant[0], "tp"), weights[layer], copies)
        normed_now = jnp.concatenate(normed_list, axis=0)
        rotated_now = jnp.concatenate(rotated_list, axis=0)
        if stage == 0:
            kept_normed, kept_rotated = normed_now, rotated_now
        else:
            valid = stage_pos == stage
            kept_normed = jnp.where(valid, normed_now, kept_normed)
            kept_rotated = jnp.where(valid, rotated_now, kept_rotated)
        if stage < stages - 1:
            stream = lax.ppermute(
                copies[0], "section", [(i, i + STAGE) for i in range(sections - STAGE)]
            )
            copies = copies_of(stream, tensor)

    all_rows = STAGE * tok_rows
    turned = lax.optimization_barrier(kept_normed.T)
    turned = turned.reshape(sections, replicas, row_block, all_rows).transpose(1, 0, 2, 3)
    turned = exchange(turned, "dp")
    turned = turned.transpose(1, 2, 0, 3).reshape(sections * row_block, replicas * all_rows)
    row_scales = jnp.repeat(scales, tok_rows, axis=0)
    level, slope = level_and_slope(kept_rotated, row_scales)
    error_part = level - kept_rotated
    grad_rot = (error_part * (slope - 1.0)).astype(jnp.bfloat16)
    loss = jnp.full((8, 128), jnp.sum(error_part * error_part), jnp.float32)
    losses = exchange(copies_of(loss, replicas * tensor), ("dp", "tp"))
    grad_all = gather(grad_rot, "dp").reshape(replicas * all_rows, part_cols)
    grad_all, losses = lax.optimization_barrier((grad_all, losses))
    terms = jnp.dot(turned, grad_all, preferred_element_type=jnp.float32)
    loss = jnp.sum(losses[:, 0], axis=0, keepdims=True)

    halves = terms.reshape(planes, 2, row_block, part_cols)
    mine = lax.dynamic_index_in_dim(halves, core, 1, keepdims=False)
    other = lax.dynamic_index_in_dim(halves, 1 - core, 1, keepdims=False).astype(jnp.bfloat16)
    pair_sum = (mine + crossed(other, 1).astype(jnp.float32)).astype(jnp.bfloat16)
    loss = (loss + crossed(loss, 1))[0, 0]
    high = lax.reduce_precision(loss, 8, 7)
    middle = lax.reduce_precision(loss - high, 8, 7)
    low = loss - high - middle
    lane = lax.broadcasted_iota(jnp.int32, (16, part_cols), 1)
    tail_rows = jnp.where(lane == 0, high, jnp.where(lane == 1, middle, jnp.where(lane == 2, low, 0.0)))
    tail_rows = tail_rows.astype(jnp.bfloat16)
    sent = jnp.concatenate([pair_sum, copies_of(tail_rows, planes)], axis=1)
    parts = lax.all_to_all(sent, "section", 0, 0, axis_index_groups=same_core, tiled=True)
    sums = jnp.sum(parts.astype(jnp.float32), axis=0)
    factor = 1.0 / math.sqrt(sections * all_rows * replicas)
    norm_count = all_rows * replicas * D
    return (sums[:row_block] * factor, jnp.sum(sums[row_block, :3]) / norm_count)


def solution(mesh):
    placed = (
        P(None, "dp", "tp"),
        P(("section", "dp"), "tp"),
        P("section", None, "tp"),
        P("section", None),
        P("section", "tp"),
    )
    return jax.shard_map(
        local,
        mesh=mesh,
        in_specs=placed,
        out_specs=(P(("section", "dp"), "tp"), P()),
        check_vma=False,
    )
```

time: 789 us -> 701 us (0.89)
  blocking collectives: 225 us -> 389 us
  waiting for transfers between devices: 205 us -> 91.7 us
  matrix products: 90.7 us -> 2.05 us
  starting transfers between devices: 162 us -> 122 us
  Pallas kernels: 0 us -> 35.4 us
  local copies, waits for them, and re-layouts: 69.5 us -> 38.5 us
  other arithmetic: 23.6 us -> 13.3 us
    all_to_all x14 -> x28, blocking collectives: 191 us -> 345 us  [exchange(): return lax.all_to_all(copies, axis, 0, 0, tiled=True)]
    all_to_all x23 -> x8, waiting for transfers between devices: 196 us -> 48.6 us  [the longest x7 46.7 us: exchange(): return lax.all_to_all(copies, axis, 0, 0, tiled=True)]
    dot_general x31 -> x0, matrix products: 89 us -> none  [the longest x15 45 us: project(): jnp.dot(quant_full, weights[layer], preferred_element_type=jnp.float32)]
    all_to_all x23 -> x8, starting transfers between devices: 90.1 us -> 44.9 us  [the longest x7 34 us: exchange(): return lax.all_to_all(copies, axis, 0, 0, tiled=True)]
    pallas_call x0 -> x32, Pallas kernels: none -> 35.4 us  [the longest x16 16.3 us: rotate(): pl.pallas_call(rotate_kernel, out_shape=shapes, in_specs=[VMEM] * 4, out_...]
    ppermute x9 -> x6, waiting for transfers between devices: 6.64 us -> 40.1 us  [crossed(): lax.ppermute(value, 'section', [(i, i ^ mask) for i in range(lax.axis_siz...]
    unnamed x141 -> x99, local copies, waits for them, and re-layouts: 5.3 us -> 22.2 us
    dynamic_update_slice x4 -> x0, local copies, waits for them, and re-layouts: 15.7 us -> none  [the longest x1 4.57 us: local(): weights = lax.dynamic_update_index_in_dim(weights, by3, place ^ 3, 0)]
  transfers between devices with their start and end apart: 35 -> 17, of which waited for: 27 -> 11; matrix products, arithmetic and copies ran while one was open for 12% -> 3% of each run, Pallas kernels for 0% -> 1%
where the time goes in v3:
time: 701 us; the launch traced here: 698 us
  blocking collectives  389 us (55%)
  starting transfers between devices  122 us (17%)
  waiting for transfers between devices  91.7 us (13%)
  local copies, waits for them, and re-layouts  38.5 us (5%)
  Pallas kernels  35.4 us (5%)
  other arithmetic  13.3 us (2%)
    all_to_all x28, blocking collectives, exchange(): return lax.all_to_all(copies, axis, 0, 0, tiled=True)  345 us
    ppermute x6, starting transfers between devices, crossed(): lax.ppermute(value, 'section', [(i, i ^ mask) for i in range(lax.axis_siz...  63.1 us
    all_to_all x7, waiting for transfers between devices, exchange(): return lax.all_to_all(copies, axis, 0, 0, tiled=True)  46.7 us
    ppermute x6, waiting for transfers between devices, crossed(): lax.ppermute(value, 'section', [(i, i ^ mask) for i in range(lax.axis_siz...  40.1 us
    all_to_all x7, starting transfers between devices, exchange(): return lax.all_to_all(copies, axis, 0, 0, tiled=True)  34 us
    all_to_all x1, blocking collectives, local(): lax.all_to_all(sent, 'section', 0, 0, axis_index_groups=same_core, tiled=...  30.5 us
    unnamed x99, local copies, waits for them, and re-layouts  22.2 us
    pallas_call x16, Pallas kernels, rotate(): pl.pallas_call(rotate_kernel, out_shape=shapes, in_specs=[VMEM] * 4, out_...  16.3 us
  transfers between devices with their start and end apart: 17, of which 11 were waited for; matrix products, arithmetic and copies ran while one was open for 3% of the time, Pallas kernels for 1%

profile of v3, /device:TPU:1, one launch (start us, length us, event | category | flops | bytes accessed | tf_op | source)
XLA Modules:
  0.0 698.2 jit_solution(5754373837240649366)
XLA Ops:
  2.4 10.9 %all-to-all-start.1 = ((bf16[8,64,512]{2,1,0:T(8,128)(2,1)}), bf16[8,64,512]{2,1,0:T(8,128)(2,1)S(1)}, u32[]{:S(2)}, u32[]{:S(2)}) async-start(bf16[8,64,512]{2,1,0:T(8,128)(2,1)} %broadcast_in_dim.91), calls=%async_computation.1 | async-start | bytes 1048576 | tf_op jit(solution)/shard_map/all_to_all | solution.py:175
  14.7 13.9 %all-gather = f32[4,1,4608]{2,1,0:T(1,128)S(1)} all-gather(f32[1,1,4608]{2,1,0:T(1,128)S(1)} %maximum_bitcast_fusion.1), channel_id=1, replica_groups={{0,32,64,96},{128,160,192,224},{256,288,320,352},{384,416,448,480},{1,3..., dimensions={0}, use_global_device_ids=true | all-gather | bytes 92160 | tf_op jit(solution)/shard_map/all_gather | solution.py:181
  28.7 2.0 all-to-all-done.1
  32.3 4.5 all-to-all-start.2
  38.7 23.4 %all-to-all-done.2 = bf16[4,8,64,512]{3,2,1,0:T(8,128)(2,1)} async-done(((bf16[4,8,64,512]{3,2,1,0:T(8,128)(2,1)}), bf16[4,8,64,512]{3,2,1,0:T(8,128)(2,1)}, u32[]{:S(2)}, u32[]{:S(2)}) %all-to-all-start.2) | async-done | bytes 2097184 | tf_op jit(solution)/shard_map/all_to_all | solution.py:56
  62.0 4.0 collective-permute-start
  68.7 6.8 all-to-all-start
  75.6 2.5 select_bitcast_fusion.1
  78.5 2.5 copy.20
  81.0 5.2 all-to-all-done.rows_ref
  86.2 2.2 copy-done.2
  90.1 39.8 %collective-permute-done.2.by2 = bf16[4096,512]{1,0:T(8,128)(2,1)} collective-permute-done((bf16[4096,512]{1,0:T(8,128)(2,1)}, bf16[4096,512]{1,0:T(8,128)(2,1)}, u32[]{:S(2)}, u32[]{:S(2)}) %collective-permute-start.2) | collective-permute-done | bytes 4194336 | tf_op jit(solution)/shard_map/ppermute | solution.py:64
  129.9 4.0 collective-permute-start.3
  133.8 6.8 all-to-all-start.3
  140.9 2.2 copy-done.14
  143.1 4.8 load_weights.1
  147.9 2.1 copy-done.5
  150.0 2.0 copy-done.7
  152.0 2.0 copy-done.9
  154.0 1.9 copy-done.12
  156.0 2.2 copy-done.10
  160.1 17.2 %all_to_all.185.rows_ref = bf16[8,32,512]{2,1,0:T(8,128)(2,1)S(1)} all-to-all(bf16[8,32,512]{2,1,0:T(8,128)(2,1)S(1)} %project.15.stream_ref), channel_id=1, replica_groups=mesh['section'=16,'dp'=4,'tp'=8] {'tp'}, dimensions={0} | all-to-all | bytes 524288 | tf_op jit(solution)/shard_map/all_to_all | solution.py:56
  178.3 12.1 %all_to_all.186.quant_ref = bf16[8,32,512]{2,1,0:T(8,128)(2,1)S(1)} all-to-all(bf16[8,32,512]{2,1,0:T(8,128)(2,1)S(1)} %get-tuple-element.63), channel_id=1, replica_groups=mesh['section'=16,'dp'=4,'tp'=8] {'tp'}, dimensions={0} | all-to-all | bytes 524288 | tf_op jit(solution)/shard_map/all_to_all | solution.py:56
  191.2 11.8 %all_to_all.187.rows_ref = bf16[8,32,512]{2,1,0:T(8,128)(2,1)S(1)} all-to-all(bf16[8,32,512]{2,1,0:T(8,128)(2,1)S(1)} %project.16.stream_ref), channel_id=1, replica_groups=mesh['section'=16,'dp'=4,'tp'=8] {'tp'}, dimensions={0} | all-to-all | bytes 524288 | tf_op jit(solution)/shard_map/all_to_all | solution.py:56
  204.0 11.9 %all_to_all.188.quant_ref = bf16[8,32,512]{2,1,0:T(8,128)(2,1)S(1)} all-to-all(bf16[8,32,512]{2,1,0:T(8,128)(2,1)S(1)} %get-tuple-element.65), channel_id=1, replica_groups=mesh['section'=16,'dp'=4,'tp'=8] {'tp'}, dimensions={0} | all-to-all | bytes 524288 | tf_op jit(solution)/shard_map/all_to_all | solution.py:56
  216.7 11.7 %all_to_all.189.rows_ref = bf16[8,32,512]{2,1,0:T(8,128)(2,1)S(1)} all-to-all(bf16[8,32,512]{2,1,0:T(8,128)(2,1)S(1)} %project.17.stream_ref), channel_id=1, replica_groups=mesh['section'=16,'dp'=4,'tp'=8] {'tp'}, dimensions={0} | all-to-all | bytes 524288 | tf_op jit(solution)/shard_map/all_to_all | solution.py:56
  229.5 11.9 %all_to_all.190.quant_ref = bf16[8,32,512]{2,1,0:T(8,128)(2,1)S(1)} all-to-all(bf16[8,32,512]{2,1,0:T(8,128)(2,1)S(1)} %get-tuple-element.67), channel_id=1, replica_groups=mesh['section'=16,'dp'=4,'tp'=8] {'tp'}, dimensions={0} | all-to-all | bytes 524288 | tf_op jit(solution)/shard_map/all_to_all | solution.py:56
  244.5 11.7 %all_to_all.191.rows_ref = bf16[8,32,512]{2,1,0:T(8,128)(2,1)S(1)} all-to-all(bf16[8,32,512]{2,1,0:T(8,128)(2,1)S(1)} %broadcast_in_dim.96.stream_ref), channel_id=1, replica_groups=mesh['section'=16,'dp'=4,'tp'=8] {'tp'}, dimensions={0} | all-to-all | bytes 524288 | tf_op jit(solution)/shard_map/all_to_all | solution.py:56
  257.3 11.9 %all_to_all.192.quant_ref = bf16[8,32,512]{2,1,0:T(8,128)(2,1)S(1)} all-to-all(bf16[8,32,512]{2,1,0:T(8,128)(2,1)S(1)} %get-tuple-element.69), channel_id=1, replica_groups=mesh['section'=16,'dp'=4,'tp'=8] {'tp'}, dimensions={0} | all-to-all | bytes 524288 | tf_op jit(solution)/shard_map/all_to_all | solution.py:56
  270.0 12.3 %all_to_all.193.rows_ref = bf16[8,32,512]{2,1,0:T(8,128)(2,1)S(1)} all-to-all(bf16[8,32,512]{2,1,0:T(8,128)(2,1)S(1)} %project.19.stream_ref), channel_id=1, replica_groups=mesh['section'=16,'dp'=4,'tp'=8] {'tp'}, dimensions={0} | all-to-all | bytes 524288 | tf_op jit(solution)/shard_map/all_to_all | solution.py:56
  283.9 12.4 %all_to_all.194.quant_ref = bf16[8,32,512]{2,1,0:T(8,128)(2,1)S(1)} all-to-all(bf16[8,32,512]{2,1,0:T(8,128)(2,1)S(1)} %get-tuple-element.70), channel_id=1, replica_groups=mesh['section'=16,'dp'=4,'tp'=8] {'tp'}, dimensions={0} | all-to-all | bytes 524288 | tf_op jit(solution)/shard_map/all_to_all | solution.py:56
  297.1 14.0 %all_to_all.195.rows_ref = bf16[8,32,512]{2,1,0:T(8,128)(2,1)S(1)} all-to-all(bf16[8,32,512]{2,1,0:T(8,128)(2,1)S(1)} %project.20.stream_ref), channel_id=1, replica_groups=mesh['section'=16,'dp'=4,'tp'=8] {'tp'}, dimensions={0} | all-to-all | bytes 524288 | tf_op jit(solution)/shard_map/all_to_all | solution.py:56
  312.7 14.8 %all_to_all.196.quant_ref = bf16[8,32,512]{2,1,0:T(8,128)(2,1)S(1)} all-to-all(bf16[8,32,512]{2,1,0:T(8,128)(2,1)S(1)} %get-tuple-element.71), channel_id=1, replica_groups=mesh['section'=16,'dp'=4,'tp'=8] {'tp'}, dimensions={0} | all-to-all | bytes 524288 | tf_op jit(solution)/shard_map/all_to_all | solution.py:56
  328.4 12.9 %all_to_all.197.rows_ref = bf16[8,32,512]{2,1,0:T(8,128)(2,1)S(1)} all-to-all(bf16[8,32,512]{2,1,0:T(8,128)(2,1)S(1)} %project.21.stream_ref), channel_id=1, replica_groups=mesh['section'=16,'dp'=4,'tp'=8] {'tp'}, dimensions={0} | all-to-all | bytes 524288 | tf_op jit(solution)/shard_map/all_to_all | solution.py:56
  342.3 12.0 %all_to_all.198.quant_ref = bf16[8,32,512]{2,1,0:T(8,128)(2,1)S(1)} all-to-all(bf16[8,32,512]{2,1,0:T(8,128)(2,1)S(1)} %get-tuple-element.72), channel_id=1, replica_groups=mesh['section'=16,'dp'=4,'tp'=8] {'tp'}, dimensions={0} | all-to-all | bytes 524288 | tf_op jit(solution)/shard_map/all_to_all | solution.py:56
  355.1 6.4 collective-permute-start.5
  362.6 11.7 %all_to_all.199.rows_ref = bf16[8,32,512]{2,1,0:T(8,128)(2,1)S(1)} all-to-all(bf16[8,32,512]{2,1,0:T(8,128)(2,1)S(1)} %broadcast_in_dim.97.stream_ref), channel_id=1, replica_groups=mesh['section'=16,'dp'=4,'tp'=8] {'tp'}, dimensions={0} | all-to-all | bytes 524288 | tf_op jit(solution)/shard_map/all_to_all | solution.py:56
  375.9 11.7 %all_to_all.200.quant_ref = bf16[8,32,512]{2,1,0:T(8,128)(2,1)S(1)} all-to-all(bf16[8,32,512]{2,1,0:T(8,128)(2,1)S(1)} %get-tuple-element.73), channel_id=1, replica_groups=mesh['section'=16,'dp'=4,'tp'=8] {'tp'}, dimensions={0} | all-to-all | bytes 524288 | tf_op jit(solution)/shard_map/all_to_all | solution.py:56
  388.5 11.7 %all_to_all.201.rows_ref = bf16[8,32,512]{2,1,0:T(8,128)(2,1)S(1)} all-to-all(bf16[8,32,512]{2,1,0:T(8,128)(2,1)S(1)} %project.23.stream_ref), channel_id=1, replica_groups=mesh['section'=16,'dp'=4,'tp'=8] {'tp'}, dimensions={0} | all-to-all | bytes 524288 | tf_op jit(solution)/shard_map/all_to_all | solution.py:56
  401.9 11.7 %all_to_all.202.quant_ref = bf16[8,32,512]{2,1,0:T(8,128)(2,1)S(1)} all-to-all(bf16[8,32,512]{2,1,0:T(8,128)(2,1)S(1)} %get-tuple-element.74), channel_id=1, replica_groups=mesh['section'=16,'dp'=4,'tp'=8] {'tp'}, dimensions={0} | all-to-all | bytes 524288 | tf_op jit(solution)/shard_map/all_to_all | solution.py:56
  414.4 11.7 %all_to_all.203.rows_ref = bf16[8,32,512]{2,1,0:T(8,128)(2,1)S(1)} all-to-all(bf16[8,32,512]{2,1,0:T(8,128)(2,1)S(1)} %project.24.stream_ref), channel_id=1, replica_groups=mesh['section'=16,'dp'=4,'tp'=8] {'tp'}, dimensions={0} | all-to-all | bytes 524288 | tf_op jit(solution)/shard_map/all_to_all | solution.py:56
  427.8 11.7 %all_to_all.204.quant_ref = bf16[8,32,512]{2,1,0:T(8,128)(2,1)S(1)} all-to-all(bf16[8,32,512]{2,1,0:T(8,128)(2,1)S(1)} %get-tuple-element.75), channel_id=1, replica_groups=mesh['section'=16,'dp'=4,'tp'=8] {'tp'}, dimensions={0} | all-to-all | bytes 524288 | tf_op jit(solution)/shard_map/all_to_all | solution.py:56
  440.3 12.3 %all_to_all.205.rows_ref = bf16[8,32,512]{2,1,0:T(8,128)(2,1)S(1)} all-to-all(bf16[8,32,512]{2,1,0:T(8,128)(2,1)S(1)} %project.25.stream_ref), channel_id=1, replica_groups=mesh['section'=16,'dp'=4,'tp'=8] {'tp'}, dimensions={0} | all-to-all | bytes 524288 | tf_op jit(solution)/shard_map/all_to_all | solution.py:56
  454.3 13.0 %all_to_all.206.quant_ref = bf16[8,32,512]{2,1,0:T(8,128)(2,1)S(1)} all-to-all(bf16[8,32,512]{2,1,0:T(8,128)(2,1)S(1)} %get-tuple-element.76), channel_id=1, replica_groups=mesh['section'=16,'dp'=4,'tp'=8] {'tp'}, dimensions={0} | all-to-all | bytes 524288 | tf_op jit(solution)/shard_map/all_to_all | solution.py:56
  468.2 6.6 collective-permute-start.6
  475.8 11.7 %all_to_all.207.rows_ref = bf16[8,32,512]{2,1,0:T(8,128)(2,1)S(1)} all-to-all(bf16[8,32,512]{2,1,0:T(8,128)(2,1)S(1)} %broadcast_in_dim.98.stream_ref), channel_id=1, replica_groups=mesh['section'=16,'dp'=4,'tp'=8] {'tp'}, dimensions={0} | all-to-all | bytes 524288 | tf_op jit(solution)/shard_map/all_to_all | solution.py:56
  488.5 11.7 %all_to_all.208.quant_ref = bf16[8,32,512]{2,1,0:T(8,128)(2,1)S(1)} all-to-all(bf16[8,32,512]{2,1,0:T(8,128)(2,1)S(1)} %get-tuple-element.78), channel_id=1, replica_groups=mesh['section'=16,'dp'=4,'tp'=8] {'tp'}, dimensions={0} | all-to-all | bytes 524288 | tf_op jit(solution)/shard_map/all_to_all | solution.py:56
  501.1 11.8 %all_to_all.209.rows_ref = bf16[8,32,512]{2,1,0:T(8,128)(2,1)S(1)} all-to-all(bf16[8,32,512]{2,1,0:T(8,128)(2,1)S(1)} %project.27.stream_ref), channel_id=1, replica_groups=mesh['section'=16,'dp'=4,'tp'=8] {'tp'}, dimensions={0} | all-to-all | bytes 524288 | tf_op jit(solution)/shard_map/all_to_all | solution.py:56
  514.0 11.7 %all_to_all.210.quant_ref = bf16[8,32,512]{2,1,0:T(8,128)(2,1)S(1)} all-to-all(bf16[8,32,512]{2,1,0:T(8,128)(2,1)S(1)} %get-tuple-element.80), channel_id=1, replica_groups=mesh['section'=16,'dp'=4,'tp'=8] {'tp'}, dimensions={0} | all-to-all | bytes 524288 | tf_op jit(solution)/shard_map/all_to_all | solution.py:56
  526.6 11.7 %all_to_all.211.rows_ref = bf16[8,32,512]{2,1,0:T(8,128)(2,1)S(1)} all-to-all(bf16[8,32,512]{2,1,0:T(8,128)(2,1)S(1)} %project.28.stream_ref), channel_id=1, replica_groups=mesh['section'=16,'dp'=4,'tp'=8] {'tp'}, dimensions={0} | all-to-all | bytes 524288 | tf_op jit(solution)/shard_map/all_to_all | solution.py:56
  540.0 11.7 %all_to_all.212.quant_ref = bf16[8,32,512]{2,1,0:T(8,128)(2,1)S(1)} all-to-all(bf16[8,32,512]{2,1,0:T(8,128)(2,1)S(1)} %get-tuple-element.82), channel_id=1, replica_groups=mesh['section'=16,'dp'=4,'tp'=8] {'tp'}, dimensions={0} | all-to-all | bytes 524288 | tf_op jit(solution)/shard_map/all_to_all | solution.py:56
  553.3 3.4 all-to-all-start.32
  557.4 8.5 %all-to-all-done.32.rows_ref = bf16[8,32,512]{2,1,0:T(8,128)(2,1)S(1)} async-done(((bf16[8,32,512]{2,1,0:T(8,128)(2,1)}), bf16[8,32,512]{2,1,0:T(8,128)(2,1)S(1)}, u32[]{:S(2)}, u32[]{:S(2)}) %all-to-all-start.32) | async-done | bytes 262176 | tf_op jit(solution)/shard_map/all_to_all | solution.py:56
  565.9 2.2 copy-done.4
  572.9 4.8 all-to-all-start.35
  577.7 1.9 fusion.8
  579.6 7.9 %all-to-all-done.35 = f32[32,8,128]{2,1,0:T(8,128)} async-done(((f32[32,8,128]{2,1,0:T(8,128)}), f32[32,8,128]{2,1,0:T(8,128)}, u32[]{:S(2)}, u32[]{:S(2)}) %all-to-all-start.35) | async-done | bytes 131104 | tf_op jit(solution)/shard_map/all_to_all | solution.py:56
  589.2 4.1 all-to-all-start.34
  593.4 2.6 fusion
  600.4 3.5 all-to-all-start.33
  604.9 41.5 %collective-permute-start.8 = (f32[1,128]{1,0:T(1,128)S(1)}, f32[1,128]{1,0:T(1,128)S(1)}, u32[]{:S(2)}, u32[]{:S(2)}) collective-permute-start(f32[1,128]{1,0:T(1,128)S(1)} %bitcast.96), channel_id=1, source_target_pairs={{0,32},{32,0},{64,96},{96,64},{128,160},{160,128},{192,224},{224,1... | collective-permute-start | bytes 1544 | tf_op jit(solution)/shard_map/ppermute | solution.py:64
  648.5 2.1 fusion.3
  650.7 9.9 %collective-permute-start.7 = (bf16[8,64,512]{2,1,0:T(8,128)(2,1)S(1)}, bf16[8,64,512]{2,1,0:T(8,128)(2,1)S(1)}, u32[]{:S(2)}, u32[]{:S(2)}) collective-permute-start(bf16[8,64,512]{2,1,0:T(8,128)(2,1)S(1)} %fusion.2), channel_id=1, source_target_pairs={{0,32},{32,0},{64,96},{96,64},{128,160},{160,128},{192,224},{224,1... | collective-permute-start | bytes 1572872 | tf_op jit(solution)/shard_map/ppermute | solution.py:64
  664.6 30.5 %all_to_all.213 = bf16[8,80,512]{2,1,0:T(8,128)(2,1)S(1)} all-to-all(bf16[8,80,512]{2,1,0:T(8,128)(2,1)S(1)} %pad_maximum_fusion), channel_id=1, replica_groups={{0,64,128,192,256,320,384,448},{32,96,160,224,288,352,416,480},{1,65,12..., dimensions={0} | all-to-all | bytes 1310720 | tf_op jit(solution)/shard_map/all_to_all | solution.py:250
  (173 shorter events, 66.2 us)
Async XLA Ops:
  0.6 67.3 %copy-start = (bf16[4,32,512]{2,1,0:T(8,128)(2,1)S(1)}, bf16[4,32,512]{2,1,0:T(8,128)(2,1)}, u32[]{:S(2)}) copy-start(bf16[4,32,512]{2,1,0:T(8,128)(2,1)} %param.5) | copy-start | bytes 393220
  2.4 28.3 %all-to-all-start.1 = ((bf16[8,64,512]{2,1,0:T(8,128)(2,1)}), bf16[8,64,512]{2,1,0:T(8,128)(2,1)S(1)}, u32[]{:S(2)}, u32[]{:S(2)}) async-start(bf16[8,64,512]{2,1,0:T(8,128)(2,1)} %broadcast_in_dim.91), calls=%async_computation.1 | async-start | bytes 1048576 | tf_op jit(solution)/shard_map/all_to_all | solution.py:175
  28.7 46.8 %copy-start.48 = (f32[4,1,4608]{2,0,1:T(4,128)}, f32[4,1,4608]{2,0,1:T(4,128)S(1)}, u32[]{:S(2)}) copy-start(f32[4,1,4608]{2,0,1:T(4,128)S(1)} %copy.28) | copy-start | bytes 221188
  32.3 29.8 %all-to-all-start.2 = ((bf16[4,8,64,512]{3,2,1,0:T(8,128)(2,1)}), bf16[4,8,64,512]{3,2,1,0:T(8,128)(2,1)}, u32[]{:S(2)}, u32[]{:S(2)}) async-start(bf16[4,8,64,512]{3,2,1,0:T(8,128)(2,1)} %broadcast_in_dim.94), calls=%async_computation.2 | async-start | bytes 4194304 | tf_op jit(solution)/shard_map/all_to_all | solution.py:56
  36.7 93.1 %collective-permute-start.2 = (bf16[4096,512]{1,0:T(8,128)(2,1)}, bf16[4096,512]{1,0:T(8,128)(2,1)}, u32[]{:S(2)}, u32[]{:S(2)}) collective-permute-start(bf16[4096,512]{1,0:T(8,128)(2,1)} %bitcast.86), channel_id=1, source_target_pairs={{0,64},{32,96},{64,0},{96,32},{128,192},{160,224},{192,128},{224,1... | collective-permute-start | bytes 12582920 | tf_op jit(solution)/shard_map/ppermute | solution.py:64
  62.0 13.6 %collective-permute-start = (bf16[4,8,64,512]{3,2,1,0:T(8,128)(2,1)}, bf16[4,8,64,512]{3,2,1,0:T(8,128)(2,1)}, u32[]{:S(2)}, u32[]{:S(2)}) collective-permute-start(bf16[4,8,64,512]{3,2,1,0:T(8,128)(2,1)} %all-to-all-done.2), channel_id=1, source_target_pairs={{0,32},{32,0},{64,96},{96,64},{128,160},{160,128},{192,224},{224,1... | collective-permute-start | bytes 6291464 | tf_op jit(solution)/shard_map/ppermute | solution.py:64
  66.0 74.7 %collective-permute-start.1 = (bf16[4096,512]{1,0:T(8,128)(2,1)}, bf16[4096,512]{1,0:T(8,128)(2,1)}, u32[]{:S(2)}, u32[]{:S(2)}) collective-permute-start(bf16[4096,512]{1,0:T(8,128)(2,1)} %bitcast.87), channel_id=1, source_target_pairs={{0,32},{32,0},{64,96},{96,64},{128,160},{160,128},{192,224},{224,1... | collective-permute-start | bytes 12582920 | tf_op jit(solution)/shard_map/ppermute | solution.py:64
  68.7 17.5 %all-to-all-start = ((bf16[8,32,512]{2,1,0:T(8,128)(2,1)}), bf16[8,32,512]{2,1,0:T(8,128)(2,1)S(1)}, u32[]{:S(2)}, u32[]{:S(2)}) async-start(bf16[8,32,512]{2,1,0:T(8,128)(2,1)} %broadcast_in_dim.90.stream_ref), calls=%async_computation | async-start | bytes 524288 | tf_op jit(solution)/shard_map/all_to_all | solution.py:56
  86.2 2.2 copy-start.2
  129.9 11.1 %collective-permute-start.3 = (bf16[4096,512]{1,0:T(8,128)(2,1)}, bf16[4096,512]{1,0:T(8,128)(2,1)}, u32[]{:S(2)}, u32[]{:S(2)}) collective-permute-start(bf16[4096,512]{1,0:T(8,128)(2,1)} %collective-permute-done.2.by2), channel_id=1, source_target_pairs={{0,32},{32,0},{64,96},{96,64},{128,160},{160,128},{192,224},{224,1... | collective-permute-start | bytes 12582920 | tf_op jit(solution)/shard_map/ppermute | solution.py:64
  133.8 22.2 %all-to-all-start.3 = ((bf16[8,32,512]{2,1,0:T(8,128)(2,1)}), bf16[8,32,512]{2,1,0:T(8,128)(2,1)S(1)}, u32[]{:S(2)}, u32[]{:S(2)}) async-start(bf16[8,32,512]{2,1,0:T(8,128)(2,1)} %get-tuple-element.60), calls=%async_computation.3 | async-start | bytes 524288 | tf_op jit(solution)/shard_map/all_to_all | solution.py:56
  140.9 2.2 copy-start.14
  147.9 2.1 copy-start.5
  150.0 2.0 copy-start.7
  152.0 2.0 copy-start.9
  154.0 1.9 copy-start.12
  156.0 2.2 copy-start.10
  158.2 19.1 %copy-start.3 = (bf16[8,2,4,64,512]{4,3,2,1,0:T(8,128)(2,1)S(1)}, bf16[8,2,4,64,512]{4,3,2,1,0:T(8,128)(2,1)}, u32[]{:S(2)}) copy-start(bf16[8,2,4,64,512]{4,3,2,1,0:T(8,128)(2,1)} %copy.20) | copy-start | bytes 12582916
  177.3 13.1 %copy-start.8 = (bf16[4096,512]{1,0:T(8,128)(2,1)S(1)}, bf16[4096,512]{1,0:T(8,128)(2,1)}, u32[]{:S(2)}) copy-start(bf16[4096,512]{1,0:T(8,128)(2,1)} %copy-done.7) | copy-start | bytes 12582916
  178.3 12.9 %copy-start.20 = (f32[32,512]{1,0:T(8,128)}, f32[32,512]{1,0:T(8,128)S(1)}, u32[]{:S(2)}) copy-start(f32[32,512]{1,0:T(8,128)S(1)} %get-tuple-element.109) | copy-start | bytes 196612
  203.0 12.9 %copy-start.6 = (bf16[4096,512]{1,0:T(8,128)(2,1)S(1)}, bf16[4096,512]{1,0:T(8,128)(2,1)}, u32[]{:S(2)}) copy-start(bf16[4096,512]{1,0:T(8,128)(2,1)} %copy-done.5) | copy-start | bytes 12582916
  204.0 12.7 %copy-start.22 = (f32[32,512]{1,0:T(8,128)}, f32[32,512]{1,0:T(8,128)S(1)}, u32[]{:S(2)}) copy-start(f32[32,512]{1,0:T(8,128)S(1)} %get-tuple-element.110) | copy-start | bytes 196612
  228.5 12.9 %copy-start.13 = (bf16[4096,512]{1,0:T(8,128)(2,1)S(1)}, bf16[4096,512]{1,0:T(8,128)(2,1)}, u32[]{:S(2)}) copy-start(bf16[4096,512]{1,0:T(8,128)(2,1)} %copy-done.12) | copy-start | bytes 12582916
  229.5 12.7 %copy-start.24 = (f32[32,512]{1,0:T(8,128)}, f32[32,512]{1,0:T(8,128)S(1)}, u32[]{:S(2)}) copy-start(f32[32,512]{1,0:T(8,128)S(1)} %get-tuple-element.111) | copy-start | bytes 196612
  242.2 2.3 collective-permute-start.4
  256.3 12.9 %copy-start.11 = (bf16[4096,512]{1,0:T(8,128)(2,1)S(1)}, bf16[4096,512]{1,0:T(8,128)(2,1)}, u32[]{:S(2)}) copy-start(bf16[4096,512]{1,0:T(8,128)(2,1)} %copy-done.9) | copy-start | bytes 12582916
  257.3 12.7 %copy-start.26 = (f32[32,512]{1,0:T(8,128)}, f32[32,512]{1,0:T(8,128)S(1)}, u32[]{:S(2)}) copy-start(f32[32,512]{1,0:T(8,128)S(1)} %get-tuple-element.104) | copy-start | bytes 196612
  283.3 0.6 copy-start.28
  342.3 12.0 %copy-start.32 = (f32[32,512]{1,0:T(8,128)}, f32[32,512]{1,0:T(8,128)S(1)}, u32[]{:S(2)}) copy-start(f32[32,512]{1,0:T(8,128)S(1)} %get-tuple-element.107) | copy-start | bytes 196612
  355.1 7.4 %collective-permute-start.5 = (bf16[32,512]{1,0:T(8,128)(2,1)S(1)}, bf16[32,512]{1,0:T(8,128)(2,1)S(1)}, u32[]{:S(2)}, u32[]{:S(2)}) collective-permute-start(bf16[32,512]{1,0:T(8,128)(2,1)S(1)} %slice_bitcast_fusion.1), channel_id=1, source_target_pairs={{0,128},{32,160},{64,192},{96,224},{128,256},{160,288},{192,320},{... | collective-permute-start | bytes 98312 | tf_op jit(solution)/shard_map/ppermute | solution.py:217
  375.3 0.6 copy-start.34
  427.1 0.6 copy-start.38
  453.6 0.7 copy-start.15
  454.3 13.0 %copy-start.40 = (f32[32,512]{1,0:T(8,128)}, f32[32,512]{1,0:T(8,128)S(1)}, u32[]{:S(2)}) copy-start(f32[32,512]{1,0:T(8,128)S(1)} %get-tuple-element.103) | copy-start | bytes 196612
  468.2 7.6 %collective-permute-start.6 = (bf16[32,512]{1,0:T(8,128)(2,1)S(1)}, bf16[32,512]{1,0:T(8,128)(2,1)S(1)}, u32[]{:S(2)}, u32[]{:S(2)}) collective-permute-start(bf16[32,512]{1,0:T(8,128)(2,1)S(1)} %slice_bitcast_fusion), channel_id=1, source_target_pairs={{0,128},{32,160},{64,192},{96,224},{128,256},{160,288},{192,320},{... | collective-permute-start | bytes 98312 | tf_op jit(solution)/shard_map/ppermute | solution.py:217
  488.5 12.6 %copy-start.42 = (f32[32,512]{1,0:T(8,128)}, f32[32,512]{1,0:T(8,128)S(1)}, u32[]{:S(2)}) copy-start(f32[32,512]{1,0:T(8,128)S(1)} %get-tuple-element.96) | copy-start | bytes 196612
  513.9 12.6 %copy-start.17 = (bf16[32,4096]{1,0:T(8,128)(2,1)}, bf16[32,4096]{1,0:T(8,128)(2,1)S(1)}, u32[]{:S(2)}) copy-start(bf16[32,4096]{1,0:T(8,128)(2,1)S(1)} %get-tuple-element.79) | copy-start | bytes 786436
  513.9 12.6 %copy-start.44 = (f32[32,512]{1,0:T(8,128)}, f32[32,512]{1,0:T(8,128)S(1)}, u32[]{:S(2)}) copy-start(f32[32,512]{1,0:T(8,128)S(1)} %get-tuple-element.97) | copy-start | bytes 196612
  539.3 0.7 copy-start.18
  540.0 13.3 %copy-start.46 = (f32[32,512]{1,0:T(8,128)}, f32[32,512]{1,0:T(8,128)S(1)}, u32[]{:S(2)}) copy-start(f32[32,512]{1,0:T(8,128)S(1)} %get-tuple-element.98) | copy-start | bytes 196612
  553.3 12.7 %all-to-all-start.32 = ((bf16[8,32,512]{2,1,0:T(8,128)(2,1)}), bf16[8,32,512]{2,1,0:T(8,128)(2,1)S(1)}, u32[]{:S(2)}, u32[]{:S(2)}) async-start(bf16[8,32,512]{2,1,0:T(8,128)(2,1)} %project.29), calls=%async_computation.32 | async-start | bytes 524288 | tf_op jit(solution)/shard_map/all_to_all | solution.py:56
  565.9 2.2 copy-start.4
  568.1 1.7 copy-start.21
  568.1 1.7 copy-start.23
  568.1 1.7 copy-start.25
  568.1 1.7 copy-start.27
  568.1 1.7 copy-start.29
  568.1 1.7 copy-start.31
  568.1 1.7 copy-start.33
  568.2 1.7 copy-start.35
  568.2 1.7 copy-start.37
  568.2 1.7 copy-start.39
  568.2 1.7 copy-start.41
  568.2 1.7 copy-start.43
  568.2 1.7 copy-start.45
  568.2 1.7 copy-start.47
  569.1 0.7 copy-start.19
  569.8 23.6 %copy-start.16 = (bf16[32,4096]{1,0:T(8,128)(2,1)S(1)}, bf16[32,4096]{1,0:T(8,128)(2,1)}, u32[]{:S(2)}) copy-start(bf16[32,4096]{1,0:T(8,128)(2,1)} %copy-done.15) | copy-start | bytes 786436
  572.9 14.6 %all-to-all-start.35 = ((f32[32,8,128]{2,1,0:T(8,128)}), f32[32,8,128]{2,1,0:T(8,128)}, u32[]{:S(2)}, u32[]{:S(2)}) async-start(f32[32,8,128]{2,1,0:T(8,128)} %broadcast_in_dim_broadcast_in_dim_broadcast_in_dim.3), calls=%async_computation.35 | async-start | bytes 262144 | tf_op jit(solution)/shard_map/all_to_all | solution.py:56
  589.2 11.1 %all-to-all-start.34 = ((bf16[4,128,512]{2,1,0:T(8,128)(2,1)}), bf16[4,128,512]{2,1,0:T(8,128)(2,1)}, u32[]{:S(2)}, u32[]{:S(2)}) async-start(bf16[4,128,512]{2,1,0:T(8,128)(2,1)} %broadcast_in_dim.103), calls=%async_computation.34 | async-start | bytes 1048576 | tf_op jit(solution)/shard_map/all_to_all | solution.py:56
  600.4 46.0 %all-to-all-start.33 = ((bf16[4,16,64,128]{3,2,1,0:T(8,128)(2,1)}), bf16[4,16,64,128]{3,2,1,0:T(8,128)(2,1)S(1)}, u32[]{:S(2)}, u32[]{:S(2)}) async-start(bf16[4,16,64,128]{3,2,1,0:T(8,128)(2,1)} %copy.22), calls=%async_computation.33 | async-start | bytes 2097152 | tf_op jit(solution)/shard_map/all_to_all | solution.py:56
  604.9 55.7 %collective-permute-start.8 = (f32[1,128]{1,0:T(1,128)S(1)}, f32[1,128]{1,0:T(1,128)S(1)}, u32[]{:S(2)}, u32[]{:S(2)}) collective-permute-start(f32[1,128]{1,0:T(1,128)S(1)} %bitcast.96), channel_id=1, source_target_pairs={{0,32},{32,0},{64,96},{96,64},{128,160},{160,128},{192,224},{224,1... | collective-permute-start | bytes 1544 | tf_op jit(solution)/shard_map/ppermute | solution.py:64
  650.7 13.6 %collective-permute-start.7 = (bf16[8,64,512]{2,1,0:T(8,128)(2,1)S(1)}, bf16[8,64,512]{2,1,0:T(8,128)(2,1)S(1)}, u32[]{:S(2)}, u32[]{:S(2)}) collective-permute-start(bf16[8,64,512]{2,1,0:T(8,128)(2,1)S(1)} %fusion.2), channel_id=1, source_target_pairs={{0,32},{32,0},{64,96},{96,64},{128,160},{160,128},{192,224},{224,1... | collective-permute-start | bytes 1572872 | tf_op jit(solution)/shard_map/ppermute | solution.py:64
  664.3 32.8 %copy-start.1 = (bf16[4,32,512]{2,1,0:T(8,128)(2,1)S(1)}, bf16[4,32,512]{2,1,0:T(8,128)(2,1)}, u32[]{:S(2)}) copy-start(bf16[4,32,512]{2,1,0:T(8,128)(2,1)} %param.5) | copy-start | bytes 393220
  (2 other events, 1.2 us)

commit v4 on v3

--- a/solution.py
+++ b/solution.py
@@ -1,3 +1,4 @@
+import functools
 import math
 
 import jax
@@ -68,30 +69,84 @@
 PARAMS = pltpu.CompilerParams(vmem_limit_bytes=8 * 1024 * 1024)
 
 
-def load_kernel(place_ref, own, by1, by2, by3, *rest):
-    outs, sems = rest[:STAGE], rest[STAGE]
-    sources = (own, by1, by2, by3)
-    place = place_ref[0]
-    for layer in range(STAGE):
-        for mask in range(STAGE):
-            @pl.when((place ^ layer) == mask)
-            def _():
-                pltpu.make_async_copy(sources[mask], outs[layer], sems.at[layer]).start()
-    for layer in range(STAGE):
-        pltpu.make_async_copy(own, outs[layer], sems.at[layer]).wait()
-
-
-def load_weights(place, own, by1, by2, by3):
+def pieces_of(layer, place_ref, sources, chunk):
+    wanted = place_ref[0] ^ layer
+    for mask, pieces in enumerate(sources):
+        first = 0
+        for piece in pieces:
+            for start in range(0, piece.shape[0], chunk):
+                yield wanted == mask, (first + start) // chunk, piece.at[pl.ds(start, chunk)]
+            first += piece.shape[0]
+
+
+def start_load(layer, place_ref, refs, into, sems):
+    own, by1, by2_head, by2_rest, by3_head, by3_rest = refs
+    chunk = into.shape[0] // sems.shape[0]
+    sources = ([own], [by1], [by2_head, by2_rest], [by3_head, by3_rest])
+    for condition, index, rows in pieces_of(layer, place_ref, sources, chunk):
+        @pl.when(condition)
+        def _():
+            pltpu.make_async_copy(rows, into.at[pl.ds(index * chunk, chunk)], sems.at[index]).start()
+
+
+def wait_load(refs, into, sems, index):
+    chunk = into.shape[0] // sems.shape[0]
+    pltpu.make_async_copy(
+        refs[0].at[pl.ds(index * chunk, chunk)], into.at[pl.ds(index * chunk, chunk)], sems.at[index]
+    ).wait()
+
+
+def load_kernel(layer, place_ref, *args):
+    refs, (out, sems) = args[:6], args[6:]
+    start_load(layer, place_ref, refs, out, sems)
+    for index in range(sems.shape[0]):
+        wait_load(refs, out, sems, index)
+
+
+def load_weight(layer, place, sources):
     far = pl.BlockSpec(memory_space=pl.ANY)
-    return pl.pallas_call(
-        load_kernel,
-        out_shape=[jax.ShapeDtypeStruct(own.shape, own.dtype)] * STAGE,
-        in_specs=[pl.BlockSpec(memory_space=pltpu.SMEM)] + [far] * 4,
-        out_specs=[VMEM] * STAGE,
-        scratch_shapes=[pltpu.SemaphoreType.DMA((STAGE,))],
+    own = sources[0]
+    return pl.pallas_call(
+        functools.partial(load_kernel, layer),
+        out_shape=jax.ShapeDtypeStruct(own.shape, own.dtype),
+        in_specs=[pl.BlockSpec(memory_space=pltpu.SMEM)] + [far] * 6,
+        out_specs=VMEM,
+        scratch_shapes=[pltpu.SemaphoreType.DMA((8,))],
         compiler_params=PARAMS,
-        name="load_weights",
-    )(place, own, by1, by2, by3)
+        name="load_weight",
+    )(place, *sources)
+
+
+def project_from_kernel(layer, place_ref, *args):
+    refs, (quant_ref, stream_ref, out_ref, weight_ref, sems) = args[:6], args[6:]
+    start_load(layer, place_ref, refs, weight_ref, sems)
+    count, tok_rows, part = quant_ref.shape
+    total = stream_ref[0].astype(jnp.float32)
+    for k in range(count):
+        wait_load(refs, weight_ref, sems, k)
+        total = total + jnp.dot(
+            quant_ref[k], weight_ref[k * part : (k + 1) * part, :], preferred_element_type=jnp.float32
+        )
+    stream = total.astype(jnp.bfloat16)
+    for k in range(count):
+        out_ref[k] = stream
+
+
+def project_from(layer, place, sources, quant_rows, copies):
+    far = pl.BlockSpec(memory_space=pl.ANY)
+    own = sources[0]
+    return pl.pallas_call(
+        functools.partial(project_from_kernel, layer),
+        out_shape=jax.ShapeDtypeStruct(copies.shape, jnp.bfloat16),
+        in_specs=[pl.BlockSpec(memory_space=pltpu.SMEM)] + [far] * 6 + [VMEM] * 2,
+        out_specs=VMEM,
+        scratch_shapes=[
+            pltpu.VMEM(own.shape, own.dtype),
+            pltpu.SemaphoreType.DMA((quant_rows.shape[0],)),
+        ],
+        compiler_params=PARAMS,
+        name="project_from",
+    )(place, *sources, quant_rows, copies)
 
 
 def rotate_kernel(rows_ref, gain_ref, rot_ref, scale_ref, normed_ref, rotated_ref, *copies):
@@ -152,6 +207,39 @@
         compiler_params=PARAMS,
         name="project",
     )(quant_rows, weight, copies)
+
+
+def terms_kernel(part_rows, core_ref, parts_ref, mine_ref, other_ref):
+    sources, rows, lanes = parts_ref.shape
+    count, _, cols = mine_ref.shape
+    features = 2 * count * part_rows
+    left = jnp.concatenate([parts_ref[s, :features] for s in range(sources)], axis=1)
+    right = jnp.concatenate(
+        [
+            jnp.concatenate([parts_ref[s, pl.ds(k, lanes)] for k in range(features, rows, lanes)], axis=1)
+            for s in range(sources)
+        ],
+        axis=0,
+    )
+    terms = jnp.dot(left, right, preferred_element_type=jnp.float32)
+    lower = core_ref[0] == 0
+    for z in range(count):
+        even = terms[2 * z * part_rows : (2 * z + 1) * part_rows]
+        odd = terms[(2 * z + 1) * part_rows : (2 * z + 2) * part_rows]
+        mine_ref[z] = jnp.where(lower, even, odd)
+        other_ref[z] = jnp.where(lower, odd, even).astype(jnp.bfloat16)
+
+
+def terms_of(core, parts, planes, row_block, part_cols):
+    shape = (planes, row_block, part_cols)
+    return pl.pallas_call(
+        functools.partial(terms_kernel, row_block),
+        out_shape=[jax.ShapeDtypeStruct(shape, jnp.float32), jax.ShapeDtypeStruct(shape, jnp.bfloat16)],
+        in_specs=[pl.BlockSpec(memory_space=pltpu.SMEM), VMEM],
+        out_specs=[VMEM, VMEM],
+        compiler_params=pltpu.CompilerParams(vmem_limit_bytes=24 * 1024 * 1024),
+        name="terms",
+    )(core[None].astype(jnp.int32), parts)
 
 
 def local(hidden_in, rotation, proj, norm_gain, quant_exp):
@@ -169,8 +257,10 @@
     row_block = rotation.shape[0]
 
     own = proj[0]
-    by2 = crossed(own, 2)
     by1 = crossed(own, 1)
+    head = D // 4
+    by2_head = crossed(own[:head], 2)
+    by2_rest = crossed(own[head:], 2)
 
     along_z = lax.all_to_all(
         copies_of(rotation, planes), "section", 0, 0, axis_index_groups=same_core, tiled=True
@@ -179,7 +269,8 @@
     params = jnp.concatenate([norm_gain, scale_row], axis=1)
     groups = [[STAGE * g + i for i in range(STAGE)] for g in range(stages)]
     params = lax.all_gather(params, "section", axis=0, tiled=True, axis_index_groups=groups)
-    along_z, params = lax.optimization_barrier((along_z, params))
+    along_z, params, by2_head = lax.optimization_barrier((along_z, params, by2_head))
+    by3_head = crossed(by2_head, 1)
     gains, scales = params[:, :D], params[:, D:]
     along_x = gather(along_z, "dp")
     other_rows = crossed(along_x, 1)
@@ -189,6 +280,8 @@
 
     copies = copies_of(lax.dynamic_index_in_dim(hidden_in, place, 0, keepdims=False), tensor)
     kept_normed = kept_rotated = None
+    weights = []
+    where = place[None].astype(jnp.int32)
     for stage in range(stages):
         normed_list, rotated_list = [], []
         for layer in range(STAGE):
@@ -199,12 +292,19 @@
             )
             normed_list.append(normed)
             rotated_list.append(rotated)
+            if last:
+                break
             if stage == 0 and layer == 0:
-                by2, _ = lax.optimization_barrier((by2, quant[0]))
-                by3 = crossed(by2, 1)
-                weights = load_weights(place[None].astype(jnp.int32), own, by1, by2, by3)
-            if not last:
-                copies = project(exchange(quant[0], "tp"), weights[layer], copies)
+                by2_rest, _ = lax.optimization_barrier((by2_rest, quant[0]))
+                by3_rest = crossed(by2_rest, 1)
+                sources = (own, by1, by2_head, by2_rest, by3_head, by3_rest)
+            quant_rows = exchange(quant[0], "tp")
+            if stage == 0:
+                copies = project_from(layer, where, sources, quant_rows, copies)
+                later, _ = lax.optimization_barrier((where, copies))
+                weights.append(load_weight(layer, later, sources))
+            else:
+                copies = project(quant_rows, weights[layer], copies)
         normed_now = jnp.concatenate(normed_list, axis=0)
         rotated_now = jnp.concatenate(rotated_list, axis=0)
         if stage == 0:
@@ -220,24 +320,23 @@
             copies = copies_of(stream, tensor)
 
     all_rows = STAGE * tok_rows
+    lanes = all_rows
     turned = lax.optimization_barrier(kept_normed.T)
-    turned = turned.reshape(sections, replicas, row_block, all_rows).transpose(1, 0, 2, 3)
-    turned = exchange(turned, "dp")
-    turned = turned.transpose(1, 2, 0, 3).reshape(sections * row_block, replicas * all_rows)
+    turned = turned.reshape(sections, replicas, row_block, lanes).transpose(1, 0, 2, 3)
+    turned = turned.reshape(replicas, sections * row_block, lanes)
     row_scales = jnp.repeat(scales, tok_rows, axis=0)
     level, slope = level_and_slope(kept_rotated, row_scales)
     error_part = level - kept_rotated
     grad_rot = (error_part * (slope - 1.0)).astype(jnp.bfloat16)
+    grad_rot = grad_rot.reshape(all_rows, part_cols // lanes, lanes).transpose(1, 0, 2)
+    sent = jnp.concatenate([turned, copies_of(grad_rot.reshape(-1, lanes), replicas)], axis=1)
+    parts = exchange(sent, "dp")
+    mine, other = terms_of(core, parts, planes, row_block, part_cols)
     loss = jnp.full((8, 128), jnp.sum(error_part * error_part), jnp.float32)
+    loss, _ = lax.optimization_barrier((loss, parts))
     losses = exchange(copies_of(loss, replicas * tensor), ("dp", "tp"))
-    grad_all = gather(grad_rot, "dp").reshape(replicas * all_rows, part_cols)
-    grad_all, losses = lax.optimization_barrier((grad_all, losses))
-    terms = jnp.dot(turned, grad_all, preferred_element_type=jnp.float32)
     loss = jnp.sum(losses[:, 0], axis=0, keepdims=True)
 
-    halves = terms.reshape(planes, 2, row_block, part_cols)
-    mine = lax.dynamic_index_in_dim(halves, core, 1, keepdims=False)
-    other = lax.dynamic_index_in_dim(halves, 1 - core, 1, keepdims=False).astype(jnp.bfloat16)
     pair_sum = (mine + crossed(other, 1).astype(jnp.float32)).astype(jnp.bfloat16)
     loss = (loss + crossed(loss, 1))[0, 0]
     high = lax.reduce_precision(loss, 8, 7)

time: 701 us -> 736 us (1.050)
  blocking collectives: 389 us -> 320 us
  local copies, waits for them, and re-layouts: 38.5 us -> 80.4 us
  waiting for transfers between devices: 91.7 us -> 128 us
  starting transfers between devices: 122 us -> 141 us
  Pallas kernels: 35.4 us -> 47 us
    all_to_all x28 -> x22, blocking collectives: 345 us -> 269 us  [exchange(): return lax.all_to_all(copies, axis, 0, 0, tiled=True)]
    all_to_all x7 -> x12, waiting for transfers between devices: 46.7 us -> 100 us  [exchange(): return lax.all_to_all(copies, axis, 0, 0, tiled=True)]
    unnamed x99 -> x199, local copies, waits for them, and re-layouts: 22.2 us -> 58.8 us
    ppermute x6 -> x8, waiting for transfers between devices: 40.1 us -> 19 us  [crossed(): lax.ppermute(value, 'section', [(i, i ^ mask) for i in range(lax.axis_siz...]
    all_to_all x7 -> x12, starting transfers between devices: 34 us -> 51 us  [exchange(): return lax.all_to_all(copies, axis, 0, 0, tiled=True)]
    pallas_call x1 -> x9, Pallas kernels: 4.77 us -> 16.3 us  [the longest x4 9.51 us: project_from(): pl.pallas_call(functools.partial(project_from_kernel, layer), out_shape=j...]
    all_gather x1, blocking collectives: 13.9 us -> 23.9 us  [local(): lax.all_gather(params, 'section', axis=0, tiled=True, axis_index_groups=g...]
    ppermute x6 -> x8, starting transfers between devices: 63.1 us -> 65.3 us  [crossed(): lax.ppermute(value, 'section', [(i, i ^ mask) for i in range(lax.axis_siz...]
  transfers between devices with their start and end apart: 17 -> 24, of which waited for: 11 -> 17; matrix products, arithmetic and copies ran while one was open for 3% -> 3% of each run, Pallas kernels for 1% -> 1%
where the time goes in v4:
time: 736 us; the launch traced here: 732 us
  blocking collectives  320 us (43%)
  starting transfers between devices  141 us (19%)
  waiting for transfers between devices  128 us (17%)
  local copies, waits for them, and re-layouts  80.4 us (11%)
  Pallas kernels  47 us (6%)
  other arithmetic  9.88 us (1%)
    all_to_all x22, blocking collectives, exchange(): return lax.all_to_all(copies, axis, 0, 0, tiled=True)  269 us
    all_to_all x12, waiting for transfers between devices, exchange(): return lax.all_to_all(copies, axis, 0, 0, tiled=True)  100 us
    ppermute x8, starting transfers between devices, crossed(): lax.ppermute(value, 'section', [(i, i ^ mask) for i in range(lax.axis_siz...  65.3 us
    unnamed x199, local copies, waits for them, and re-layouts  58.8 us
    all_to_all x12, starting transfers between devices, exchange(): return lax.all_to_all(copies, axis, 0, 0, tiled=True)  51 us
    all_to_all x1, blocking collectives, local(): lax.all_to_all(sent, 'section', 0, 0, axis_index_groups=same_core, tiled=...  27.3 us
    all_gather x1, blocking collectives, local(): lax.all_gather(params, 'section', axis=0, tiled=True, axis_index_groups=g...  23.9 us
    ppermute x8, waiting for transfers between devices, crossed(): lax.ppermute(value, 'section', [(i, i ^ mask) for i in range(lax.axis_siz...  19 us
  transfers between devices with their start and end apart: 24, of which 17 were waited for; matrix products, arithmetic and copies ran while one was open for 3% of the time, Pallas kernels for 1%

profile of v4, /device:TPU:1, one launch (start us, length us, event | category | flops | bytes accessed | tf_op | source)
XLA Modules:
  0.0 732.2 jit_solution(2568306159427302901)
XLA Ops:
  2.0 4.8 collective-permute-start.1
  7.7 9.1 %all-to-all-start = ((bf16[8,64,512]{2,1,0:T(8,128)(2,1)}), bf16[8,64,512]{2,1,0:T(8,128)(2,1)S(1)}, u32[]{:S(2)}, u32[]{:S(2)}) async-start(bf16[8,64,512]{2,1,0:T(8,128)(2,1)} %broadcast_in_dim.110), calls=%async_computation | async-start | bytes 1048576 | tf_op jit(solution)/shard_map/all_to_all | solution.py:265
  17.0 23.9 %all-gather = f32[4,1,4608]{2,1,0:T(1,128)S(1)} all-gather(f32[1,1,4608]{2,1,0:T(1,128)S(1)} %maximum_bitcast_fusion.1), channel_id=1, replica_groups={{0,32,64,96},{128,160,192,224},{256,288,320,352},{384,416,448,480},{1,3..., dimensions={0}, use_global_device_ids=true | all-gather | bytes 92160 | tf_op jit(solution)/shard_map/all_gather | solution.py:271
  41.5 6.0 all-to-all-done
  49.1 4.4 all-to-all-start.2
  53.5 3.9 slice_bitcast_fusion
  59.3 17.8 %all-to-all-done.2 = bf16[4,8,64,512]{3,2,1,0:T(8,128)(2,1)} async-done(((bf16[4,8,64,512]{3,2,1,0:T(8,128)(2,1)}), bf16[4,8,64,512]{3,2,1,0:T(8,128)(2,1)}, u32[]{:S(2)}, u32[]{:S(2)}) %all-to-all-start.2) | async-done | bytes 2097184 | tf_op jit(solution)/shard_map/all_to_all | solution.py:57
  77.1 5.7 collective-permute-start.3
  83.6 6.8 all-to-all-start.1
  94.5 2.5 select_bitcast_fusion.1
  97.4 2.5 copy.47
  100.0 2.8 all-to-all-done.1.rows_ref
  107.3 18.9 %collective-permute-done.2.args_3_ = bf16[3072,512]{1,0:T(8,128)(2,1)S(1)} collective-permute-done((bf16[3072,512]{1,0:T(8,128)(2,1)}, bf16[3072,512]{1,0:T(8,128)(2,1)S(1)}, u32[]{:S(2)}, u32[]{:S(2)}) %collective-permute-start.2) | collective-permute-done | bytes 3145760 | tf_op jit(solution)/shard_map/ppermute | solution.py:65
  126.3 5.7 collective-permute-start.5
  133.9 6.8 all-to-all-start.3
  140.7 10.7 %all-to-all-done.3.args_6_ = bf16[8,32,512]{2,1,0:T(8,128)(2,1)S(1)} async-done(((bf16[8,32,512]{2,1,0:T(8,128)(2,1)}), bf16[8,32,512]{2,1,0:T(8,128)(2,1)S(1)}, u32[]{:S(2)}, u32[]{:S(2)}) %all-to-all-start.3) | async-done | bytes 262176 | tf_op jit(solution)/shard_map/all_to_all | solution.py:57
  153.6 3.8 project_from.4.args_7_
  157.4 13.2 %all_to_all.180.rows_ref = bf16[8,32,512]{2,1,0:T(8,128)(2,1)S(1)} all-to-all(bf16[8,32,512]{2,1,0:T(8,128)(2,1)S(1)} %project_from.4.args_7_), channel_id=1, replica_groups=mesh['section'=16,'dp'=4,'tp'=8] {'tp'}, dimensions={0} | all-to-all | bytes 524288 | tf_op jit(solution)/shard_map/all_to_all | solution.py:57
  172.9 11.6 %all_to_all.181.args_6_ = bf16[8,32,512]{2,1,0:T(8,128)(2,1)S(1)} all-to-all(bf16[8,32,512]{2,1,0:T(8,128)(2,1)S(1)} %get-tuple-element.65), channel_id=1, replica_groups=mesh['section'=16,'dp'=4,'tp'=8] {'tp'}, dimensions={0} | all-to-all | bytes 524288 | tf_op jit(solution)/shard_map/all_to_all | solution.py:57
  185.7 12.0 %all_to_all.182.rows_ref = bf16[8,32,512]{2,1,0:T(8,128)(2,1)S(1)} all-to-all(bf16[8,32,512]{2,1,0:T(8,128)(2,1)S(1)} %project_from.5.args_7_), channel_id=1, replica_groups=mesh['section'=16,'dp'=4,'tp'=8] {'tp'}, dimensions={0} | all-to-all | bytes 524288 | tf_op jit(solution)/shard_map/all_to_all | solution.py:57
  200.1 11.7 %all_to_all.183.args_6_ = bf16[8,32,512]{2,1,0:T(8,128)(2,1)S(1)} all-to-all(bf16[8,32,512]{2,1,0:T(8,128)(2,1)S(1)} %get-tuple-element.66), channel_id=1, replica_groups=mesh['section'=16,'dp'=4,'tp'=8] {'tp'}, dimensions={0} | all-to-all | bytes 524288 | tf_op jit(solution)/shard_map/all_to_all | solution.py:57
  211.8 2.4 project_from.6.args_7_
  214.2 11.7 %all_to_all.184.rows_ref = bf16[8,32,512]{2,1,0:T(8,128)(2,1)S(1)} all-to-all(bf16[8,32,512]{2,1,0:T(8,128)(2,1)S(1)} %project_from.6.args_7_), channel_id=1, replica_groups=mesh['section'=16,'dp'=4,'tp'=8] {'tp'}, dimensions={0} | all-to-all | bytes 524288 | tf_op jit(solution)/shard_map/all_to_all | solution.py:57
  228.3 11.7 %all_to_all.185.args_6_ = bf16[8,32,512]{2,1,0:T(8,128)(2,1)S(1)} all-to-all(bf16[8,32,512]{2,1,0:T(8,128)(2,1)S(1)} %get-tuple-element.67), channel_id=1, replica_groups=mesh['section'=16,'dp'=4,'tp'=8] {'tp'}, dimensions={0} | all-to-all | bytes 524288 | tf_op jit(solution)/shard_map/all_to_all | solution.py:57
  242.1 4.0 collective-permute-start.6
  247.1 11.7 %all_to_all.186.rows_ref = bf16[8,32,512]{2,1,0:T(8,128)(2,1)S(1)} all-to-all(bf16[8,32,512]{2,1,0:T(8,128)(2,1)S(1)} %broadcast_in_dim.116.stream_ref), channel_id=1, replica_groups=mesh['section'=16,'dp'=4,'tp'=8] {'tp'}, dimensions={0} | all-to-all | bytes 524288 | tf_op jit(solution)/shard_map/all_to_all | solution.py:57
  261.9 3.4 all-to-all-start.11
  271.8 2.8 all-to-all-done.11.quant_ref
  280.2 13.0 %all_to_all.187.rows_ref = bf16[8,32,512]{2,1,0:T(8,128)(2,1)S(1)} all-to-all(bf16[8,32,512]{2,1,0:T(8,128)(2,1)S(1)} %project.11.stream_ref), channel_id=1, replica_groups=mesh['section'=16,'dp'=4,'tp'=8] {'tp'}, dimensions={0} | all-to-all | bytes 524288 | tf_op jit(solution)/shard_map/all_to_all | solution.py:57
  296.3 4.0 all-to-all-start.13
  304.9 4.8 all-to-all-done.13.quant_ref
  313.8 11.7 %all_to_all.188.rows_ref = bf16[8,32,512]{2,1,0:T(8,128)(2,1)S(1)} all-to-all(bf16[8,32,512]{2,1,0:T(8,128)(2,1)S(1)} %project.12.stream_ref), channel_id=1, replica_groups=mesh['section'=16,'dp'=4,'tp'=8] {'tp'}, dimensions={0} | all-to-all | bytes 524288 | tf_op jit(solution)/shard_map/all_to_all | solution.py:57
  328.5 3.4 all-to-all-start.15
  338.4 4.2 all-to-all-done.15.quant_ref
  348.2 12.1 %all_to_all.189.rows_ref = bf16[8,32,512]{2,1,0:T(8,128)(2,1)S(1)} all-to-all(bf16[8,32,512]{2,1,0:T(8,128)(2,1)S(1)} %project.13.stream_ref), channel_id=1, replica_groups=mesh['section'=16,'dp'=4,'tp'=8] {'tp'}, dimensions={0} | all-to-all | bytes 524288 | tf_op jit(solution)/shard_map/all_to_all | solution.py:57
  363.3 4.0 all-to-all-start.17
  372.9 6.6 all-to-all-done.17.quant_ref
  383.7 4.8 collective-permute-start.7
  389.5 11.7 %all_to_all.190.rows_ref = bf16[8,32,512]{2,1,0:T(8,128)(2,1)S(1)} all-to-all(bf16[8,32,512]{2,1,0:T(8,128)(2,1)S(1)} %broadcast_in_dim.117.stream_ref), channel_id=1, replica_groups=mesh['section'=16,'dp'=4,'tp'=8] {'tp'}, dimensions={0} | all-to-all | bytes 524288 | tf_op jit(solution)/shard_map/all_to_all | solution.py:57
  402.3 11.9 %all_to_all.191.quant_ref = bf16[8,32,512]{2,1,0:T(8,128)(2,1)S(1)} all-to-all(bf16[8,32,512]{2,1,0:T(8,128)(2,1)S(1)} %get-tuple-element.76), channel_id=1, replica_groups=mesh['section'=16,'dp'=4,'tp'=8] {'tp'}, dimensions={0} | all-to-all | bytes 524288 | tf_op jit(solution)/shard_map/all_to_all | solution.py:57
  415.0 11.7 %all_to_all.192.rows_ref = bf16[8,32,512]{2,1,0:T(8,128)(2,1)S(1)} all-to-all(bf16[8,32,512]{2,1,0:T(8,128)(2,1)S(1)} %project.15.stream_ref), channel_id=1, replica_groups=mesh['section'=16,'dp'=4,'tp'=8] {'tp'}, dimensions={0} | all-to-all | bytes 524288 | tf_op jit(solution)/shard_map/all_to_all | solution.py:57
  427.7 11.9 %all_to_all.193.quant_ref = bf16[8,32,512]{2,1,0:T(8,128)(2,1)S(1)} all-to-all(bf16[8,32,512]{2,1,0:T(8,128)(2,1)S(1)} %get-tuple-element.77), channel_id=1, replica_groups=mesh['section'=16,'dp'=4,'tp'=8] {'tp'}, dimensions={0} | all-to-all | bytes 524288 | tf_op jit(solution)/shard_map/all_to_all | solution.py:57
  440.4 11.7 %all_to_all.194.rows_ref = bf16[8,32,512]{2,1,0:T(8,128)(2,1)S(1)} all-to-all(bf16[8,32,512]{2,1,0:T(8,128)(2,1)S(1)} %project.16.stream_ref), channel_id=1, replica_groups=mesh['section'=16,'dp'=4,'tp'=8] {'tp'}, dimensions={0} | all-to-all | bytes 524288 | tf_op jit(solution)/shard_map/all_to_all | solution.py:57
  453.1 12.7 %all_to_all.195.quant_ref = bf16[8,32,512]{2,1,0:T(8,128)(2,1)S(1)} all-to-all(bf16[8,32,512]{2,1,0:T(8,128)(2,1)S(1)} %get-tuple-element.78), channel_id=1, replica_groups=mesh['section'=16,'dp'=4,'tp'=8] {'tp'}, dimensions={0} | all-to-all | bytes 524288 | tf_op jit(solution)/shard_map/all_to_all | solution.py:57
  466.6 13.9 %all_to_all.196.rows_ref = bf16[8,32,512]{2,1,0:T(8,128)(2,1)S(1)} all-to-all(bf16[8,32,512]{2,1,0:T(8,128)(2,1)S(1)} %project.17.stream_ref), channel_id=1, replica_groups=mesh['section'=16,'dp'=4,'tp'=8] {'tp'}, dimensions={0} | all-to-all | bytes 524288 | tf_op jit(solution)/shard_map/all_to_all | solution.py:57
  481.5 14.9 %all_to_all.197.quant_ref = bf16[8,32,512]{2,1,0:T(8,128)(2,1)S(1)} all-to-all(bf16[8,32,512]{2,1,0:T(8,128)(2,1)S(1)} %get-tuple-element.79), channel_id=1, replica_groups=mesh['section'=16,'dp'=4,'tp'=8] {'tp'}, dimensions={0} | all-to-all | bytes 524288 | tf_op jit(solution)/shard_map/all_to_all | solution.py:57
  497.3 6.5 collective-permute-start.8
  504.8 11.7 %all_to_all.198.rows_ref = bf16[8,32,512]{2,1,0:T(8,128)(2,1)S(1)} all-to-all(bf16[8,32,512]{2,1,0:T(8,128)(2,1)S(1)} %broadcast_in_dim.118.stream_ref), channel_id=1, replica_groups=mesh['section'=16,'dp'=4,'tp'=8] {'tp'}, dimensions={0} | all-to-all | bytes 524288 | tf_op jit(solution)/shard_map/all_to_all | solution.py:57
  517.5 11.7 %all_to_all.199.quant_ref = bf16[8,32,512]{2,1,0:T(8,128)(2,1)S(1)} all-to-all(bf16[8,32,512]{2,1,0:T(8,128)(2,1)S(1)} %get-tuple-element.81), channel_id=1, replica_groups=mesh['section'=16,'dp'=4,'tp'=8] {'tp'}, dimensions={0} | all-to-all | bytes 524288 | tf_op jit(solution)/shard_map/all_to_all | solution.py:57
  530.1 11.7 %all_to_all.200.rows_ref = bf16[8,32,512]{2,1,0:T(8,128)(2,1)S(1)} all-to-all(bf16[8,32,512]{2,1,0:T(8,128)(2,1)S(1)} %project.19.stream_ref), channel_id=1, replica_groups=mesh['section'=16,'dp'=4,'tp'=8] {'tp'}, dimensions={0} | all-to-all | bytes 524288 | tf_op jit(solution)/shard_map/all_to_all | solution.py:57
  543.5 3.4 all-to-all-start.29
  549.1 7.2 all-to-all-done.29.quant_ref
  560.0 3.4 all-to-all-start.30
  564.8 9.9 %all-to-all-done.30.rows_ref = bf16[8,32,512]{2,1,0:T(8,128)(2,1)S(1)} async-done(((bf16[8,32,512]{2,1,0:T(8,128)(2,1)}), bf16[8,32,512]{2,1,0:T(8,128)(2,1)S(1)}, u32[]{:S(2)}, u32[]{:S(2)}) %all-to-all-start.30) | async-done | bytes 262176 | tf_op jit(solution)/shard_map/all_to_all | solution.py:57
  578.5 3.4 all-to-all-start.31
  583.3 10.8 %all-to-all-done.31.quant_ref = bf16[8,32,512]{2,1,0:T(8,128)(2,1)S(1)} async-done(((bf16[8,32,512]{2,1,0:T(8,128)(2,1)}), bf16[8,32,512]{2,1,0:T(8,128)(2,1)S(1)}, u32[]{:S(2)}, u32[]{:S(2)}) %all-to-all-start.31) | async-done | bytes 262176 | tf_op jit(solution)/shard_map/all_to_all | solution.py:57
  596.3 2.5 project.21
  598.8 3.4 all-to-all-start.32
  603.5 10.9 %all-to-all-done.32.rows_ref = bf16[8,32,512]{2,1,0:T(8,128)(2,1)S(1)} async-done(((bf16[8,32,512]{2,1,0:T(8,128)(2,1)}), bf16[8,32,512]{2,1,0:T(8,128)(2,1)S(1)}, u32[]{:S(2)}, u32[]{:S(2)}) %all-to-all-start.32) | async-done | bytes 262176 | tf_op jit(solution)/shard_map/all_to_all | solution.py:57
  623.5 4.4 all-to-all-start.33
  628.8 11.6 %all-to-all-done.33.parts_ref = bf16[4,1536,128]{2,1,0:T(8,128)(2,1)S(1)} async-done(((bf16[4,1536,128]{2,1,0:T(8,128)(2,1)}), bf16[4,1536,128]{2,1,0:T(8,128)(2,1)S(1)}, u32[]{:S(2)}, u32[]{:S(2)}) %all-to-all-start.33) | async-done | bytes 1572896 | tf_op jit(solution)/shard_map/all_to_all | solution.py:57
  641.1 12.7 %all_to_all.201 = f32[32,8,128]{2,1,0:T(8,128)S(1)} all-to-all(f32[32,8,128]{2,1,0:T(8,128)S(1)} %broadcast_in_dim.129), channel_id=1, replica_groups=mesh['section'=16,'dp'=4,'tp'=8] {'dp','tp'}, dimensions={0} | all-to-all | bytes 262144 | tf_op jit(solution)/shard_map/all_to_all | solution.py:57
  653.8 41.2 %collective-permute-start.10 = (f32[1,128]{1,0:T(1,128)S(1)}, f32[1,128]{1,0:T(1,128)S(1)}, u32[]{:S(2)}, u32[]{:S(2)}) collective-permute-start(f32[1,128]{1,0:T(1,128)S(1)} %bitcast.168), channel_id=1, source_target_pairs={{0,32},{32,0},{64,96},{96,64},{128,160},{160,128},{192,224},{224,1... | collective-permute-start | bytes 1544 | tf_op jit(solution)/shard_map/ppermute | solution.py:65
  701.8 27.3 %all_to_all.202 = bf16[8,80,512]{2,1,0:T(8,128)(2,1)S(1)} all-to-all(bf16[8,80,512]{2,1,0:T(8,128)(2,1)S(1)} %pad_maximum_fusion.1), channel_id=1, replica_groups={{0,64,128,192,256,320,384,448},{32,96,160,224,288,352,416,480},{1,65,12..., dimensions={0} | all-to-all | bytes 1310720 | tf_op jit(solution)/shard_map/all_to_all | solution.py:349
  (295 shorter events, 130.6 us)
Async XLA Ops:
  0.6 82.2 %copy-start = (bf16[4,32,512]{2,1,0:T(8,128)(2,1)S(1)}, bf16[4,32,512]{2,1,0:T(8,128)(2,1)}, u32[]{:S(2)}) copy-start(bf16[4,32,512]{2,1,0:T(8,128)(2,1)} %param.5) | copy-start | bytes 393220
  0.6 6.2 copy-start.96
  0.7 16.2 %copy-start.98 = (s32[1,4]{1,0:T(1,128)S(1)}, s32[1,4]{1,0:T(1,128)}, u32[]{:S(2)}) copy-start(s32[1,4]{1,0:T(1,128)} %param.9) | copy-start | bytes 52
  0.7 16.3 %copy-start.97 = (f32[1,4096]{1,0:T(1,128)S(1)}, f32[1,4096]{1,0:T(1,128)}, u32[]{:S(2)}) copy-start(f32[1,4096]{1,0:T(1,128)} %param.8) | copy-start | bytes 49156
  2.0 45.5 %collective-permute-start.1 = (bf16[1024,512]{1,0:T(8,128)(2,1)S(1)}, bf16[1024,512]{1,0:T(8,128)(2,1)}, u32[]{:S(2)}, u32[]{:S(2)}) collective-permute-start(bf16[1024,512]{1,0:T(8,128)(2,1)S(1)} %slice_bitcast_fusion.1), channel_id=1, source_target_pairs={{0,64},{32,96},{64,0},{96,32},{128,192},{160,224},{192,128},{224,1... | collective-permute-start | bytes 3145736 | tf_op jit(solution)/shard_map/ppermute | solution.py:65
  7.7 39.8 %all-to-all-start = ((bf16[8,64,512]{2,1,0:T(8,128)(2,1)}), bf16[8,64,512]{2,1,0:T(8,128)(2,1)S(1)}, u32[]{:S(2)}, u32[]{:S(2)}) async-start(bf16[8,64,512]{2,1,0:T(8,128)(2,1)} %broadcast_in_dim.110), calls=%async_computation | async-start | bytes 1048576 | tf_op jit(solution)/shard_map/all_to_all | solution.py:265
  49.1 28.0 %all-to-all-start.2 = ((bf16[4,8,64,512]{3,2,1,0:T(8,128)(2,1)}), bf16[4,8,64,512]{3,2,1,0:T(8,128)(2,1)}, u32[]{:S(2)}, u32[]{:S(2)}) async-start(bf16[4,8,64,512]{3,2,1,0:T(8,128)(2,1)} %broadcast_in_dim.115), calls=%async_computation.2 | async-start | bytes 4194304 | tf_op jit(solution)/shard_map/all_to_all | solution.py:57
  57.4 68.8 %collective-permute-start.2 = (bf16[3072,512]{1,0:T(8,128)(2,1)}, bf16[3072,512]{1,0:T(8,128)(2,1)S(1)}, u32[]{:S(2)}, u32[]{:S(2)}) collective-permute-start(bf16[3072,512]{1,0:T(8,128)(2,1)} %slice_bitcast_fusion), channel_id=1, source_target_pairs={{0,64},{32,96},{64,0},{96,32},{128,192},{160,224},{192,128},{224,1... | collective-permute-start | bytes 9437192 | tf_op jit(solution)/shard_map/ppermute | solution.py:65
  77.1 17.4 %collective-permute-start.3 = (bf16[4,8,64,512]{3,2,1,0:T(8,128)(2,1)}, bf16[4,8,64,512]{3,2,1,0:T(8,128)(2,1)}, u32[]{:S(2)}, u32[]{:S(2)}) collective-permute-start(bf16[4,8,64,512]{3,2,1,0:T(8,128)(2,1)} %all-to-all-done.2), channel_id=1, source_target_pairs={{0,32},{32,0},{64,96},{96,64},{128,160},{160,128},{192,224},{224,1... | collective-permute-start | bytes 6291464 | tf_op jit(solution)/shard_map/ppermute | solution.py:65
  83.6 19.2 %all-to-all-start.1 = ((bf16[8,32,512]{2,1,0:T(8,128)(2,1)}), bf16[8,32,512]{2,1,0:T(8,128)(2,1)S(1)}, u32[]{:S(2)}, u32[]{:S(2)}) async-start(bf16[8,32,512]{2,1,0:T(8,128)(2,1)} %broadcast_in_dim.114.args_7_), calls=%async_computation.1 | async-start | bytes 524288 | tf_op jit(solution)/shard_map/all_to_all | solution.py:57
  90.4 50.3 %collective-permute-start = (bf16[4096,512]{1,0:T(8,128)(2,1)}, bf16[4096,512]{1,0:T(8,128)(2,1)}, u32[]{:S(2)}, u32[]{:S(2)}) collective-permute-start(bf16[4096,512]{1,0:T(8,128)(2,1)} %bitcast.151), channel_id=1, source_target_pairs={{0,32},{32,0},{64,96},{96,64},{128,160},{160,128},{192,224},{224,1... | collective-permute-start | bytes 12582920 | tf_op jit(solution)/shard_map/ppermute | solution.py:65
  102.8 2.2 copy-start.2
  107.3 44.1 %copy-start.58 = (f32[32,512]{1,0:T(8,128)}, f32[32,512]{1,0:T(8,128)S(1)}, u32[]{:S(2)}) copy-start(f32[32,512]{1,0:T(8,128)S(1)} %get-tuple-element.111) | copy-start | bytes 196612
  126.3 25.1 %collective-permute-start.5 = (bf16[3072,512]{1,0:T(8,128)(2,1)S(1)}, bf16[3072,512]{1,0:T(8,128)(2,1)}, u32[]{:S(2)}, u32[]{:S(2)}) collective-permute-start(bf16[3072,512]{1,0:T(8,128)(2,1)S(1)} %collective-permute-done.2.args_3_), channel_id=1, source_target_pairs={{0,32},{32,0},{64,96},{96,64},{128,160},{160,128},{192,224},{224,1... | collective-permute-start | bytes 9437192 | tf_op jit(solution)/shard_map/ppermute | solution.py:65
  131.9 8.8 %collective-permute-start.4 = (bf16[1024,512]{1,0:T(8,128)(2,1)}, bf16[1024,512]{1,0:T(8,128)(2,1)}, u32[]{:S(2)}, u32[]{:S(2)}) collective-permute-start(bf16[1024,512]{1,0:T(8,128)(2,1)} %collective-permute-done.1.args_2_), channel_id=1, source_target_pairs={{0,32},{32,0},{64,96},{96,64},{128,160},{160,128},{192,224},{224,1... | collective-permute-start | bytes 3145736 | tf_op jit(solution)/shard_map/ppermute | solution.py:65
  133.9 17.5 %all-to-all-start.3 = ((bf16[8,32,512]{2,1,0:T(8,128)(2,1)}), bf16[8,32,512]{2,1,0:T(8,128)(2,1)S(1)}, u32[]{:S(2)}, u32[]{:S(2)}) async-start(bf16[8,32,512]{2,1,0:T(8,128)(2,1)} %copy-done.53), calls=%async_computation.3 | async-start | bytes 524288 | tf_op jit(solution)/shard_map/all_to_all | solution.py:57
  151.4 2.2 copy-start.10
  153.6 17.0 %copy-start.3 = (bf16[8,2,4,64,512]{4,3,2,1,0:T(8,128)(2,1)S(1)}, bf16[8,2,4,64,512]{4,3,2,1,0:T(8,128)(2,1)}, u32[]{:S(2)}) copy-start(bf16[8,2,4,64,512]{4,3,2,1,0:T(8,128)(2,1)} %copy.47) | copy-start | bytes 12582916
  242.1 5.0 collective-permute-start.6
  247.1 12.7 %copy-start.31 = (bf16[8,32,512]{2,1,0:T(8,128)(2,1)}, bf16[8,32,512]{2,1,0:T(8,128)(2,1)S(1)}, u32[]{:S(2)}) copy-start(bf16[8,32,512]{2,1,0:T(8,128)(2,1)S(1)} %broadcast_in_dim.116.stream_ref) | copy-start | bytes 786436
  261.9 12.7 %all-to-all-start.11 = ((bf16[8,32,512]{2,1,0:T(8,128)(2,1)}), bf16[8,32,512]{2,1,0:T(8,128)(2,1)S(1)}, u32[]{:S(2)}, u32[]{:S(2)}) async-start(bf16[8,32,512]{2,1,0:T(8,128)(2,1)} %copy-done.55), calls=%async_computation.11 | async-start | bytes 524288 | tf_op jit(solution)/shard_map/all_to_all | solution.py:57
  265.3 2.2 copy-start.11
  279.4 13.9 %copy-start.4 = (bf16[8,2,4,64,512]{4,3,2,1,0:T(8,128)(2,1)S(1)}, bf16[8,2,4,64,512]{4,3,2,1,0:T(8,128)(2,1)}, u32[]{:S(2)}) copy-start(bf16[8,2,4,64,512]{4,3,2,1,0:T(8,128)(2,1)} %copy.47) | copy-start | bytes 12582916
  296.3 13.4 %all-to-all-start.13 = ((bf16[8,32,512]{2,1,0:T(8,128)(2,1)}), bf16[8,32,512]{2,1,0:T(8,128)(2,1)}, u32[]{:S(2)}, u32[]{:S(2)}) async-start(bf16[8,32,512]{2,1,0:T(8,128)(2,1)} %copy-done.56), calls=%async_computation.13 | async-start | bytes 524288 | tf_op jit(solution)/shard_map/all_to_all | solution.py:57
  300.3 2.2 copy-start.12
  309.6 2.2 copy-start.20
  311.8 13.7 %copy-start.5 = (bf16[8,2,4,64,512]{4,3,2,1,0:T(8,128)(2,1)S(1)}, bf16[8,2,4,64,512]{4,3,2,1,0:T(8,128)(2,1)}, u32[]{:S(2)}) copy-start(bf16[8,2,4,64,512]{4,3,2,1,0:T(8,128)(2,1)} %copy.47) | copy-start | bytes 12582916
  313.8 12.7 %copy-start.29 = (bf16[8,32,512]{2,1,0:T(8,128)(2,1)}, bf16[8,32,512]{2,1,0:T(8,128)(2,1)S(1)}, u32[]{:S(2)}) copy-start(bf16[8,32,512]{2,1,0:T(8,128)(2,1)S(1)} %project.12.stream_ref) | copy-start | bytes 786436
  328.5 14.1 %all-to-all-start.15 = ((bf16[8,32,512]{2,1,0:T(8,128)(2,1)}), bf16[8,32,512]{2,1,0:T(8,128)(2,1)S(1)}, u32[]{:S(2)}, u32[]{:S(2)}) async-start(bf16[8,32,512]{2,1,0:T(8,128)(2,1)} %copy-done.57), calls=%async_computation.15 | async-start | bytes 524288 | tf_op jit(solution)/shard_map/all_to_all | solution.py:57
  331.9 2.2 copy-start.13
  347.4 12.9 %copy-start.6 = (bf16[8,2,4,64,512]{4,3,2,1,0:T(8,128)(2,1)S(1)}, bf16[8,2,4,64,512]{4,3,2,1,0:T(8,128)(2,1)}, u32[]{:S(2)}) copy-start(bf16[8,2,4,64,512]{4,3,2,1,0:T(8,128)(2,1)} %copy.47) | copy-start | bytes 12582916
  363.3 16.2 %all-to-all-start.17 = ((bf16[8,32,512]{2,1,0:T(8,128)(2,1)}), bf16[8,32,512]{2,1,0:T(8,128)(2,1)}, u32[]{:S(2)}, u32[]{:S(2)}) async-start(bf16[8,32,512]{2,1,0:T(8,128)(2,1)} %copy-done.54), calls=%async_computation.17 | async-start | bytes 524288 | tf_op jit(solution)/shard_map/all_to_all | solution.py:57
  367.4 2.2 copy-start.14
  381.7 19.6 %copy-start.7 = (bf16[8,2,4,64,512]{4,3,2,1,0:T(8,128)(2,1)S(1)}, bf16[8,2,4,64,512]{4,3,2,1,0:T(8,128)(2,1)}, u32[]{:S(2)}) copy-start(bf16[8,2,4,64,512]{4,3,2,1,0:T(8,128)(2,1)} %copy.47) | copy-start | bytes 12582916
  383.7 5.8 collective-permute-start.7
  401.3 12.9 %copy-start.25 = (bf16[4096,512]{1,0:T(8,128)(2,1)S(1)}, bf16[4096,512]{1,0:T(8,128)(2,1)}, u32[]{:S(2)}) copy-start(bf16[4096,512]{1,0:T(8,128)(2,1)} %copy-done.23) | copy-start | bytes 12582916
  426.7 12.9 %copy-start.21 = (bf16[4096,512]{1,0:T(8,128)(2,1)S(1)}, bf16[4096,512]{1,0:T(8,128)(2,1)}, u32[]{:S(2)}) copy-start(bf16[4096,512]{1,0:T(8,128)(2,1)} %copy-done.19) | copy-start | bytes 12582916
  452.2 13.6 %copy-start.17 = (bf16[4096,512]{1,0:T(8,128)(2,1)S(1)}, bf16[4096,512]{1,0:T(8,128)(2,1)}, u32[]{:S(2)}) copy-start(bf16[4096,512]{1,0:T(8,128)(2,1)} %copy-done.15) | copy-start | bytes 12582916
  480.5 15.9 %copy-start.28 = (bf16[4096,512]{1,0:T(8,128)(2,1)S(1)}, bf16[4096,512]{1,0:T(8,128)(2,1)}, u32[]{:S(2)}) copy-start(bf16[4096,512]{1,0:T(8,128)(2,1)} %copy-done.26) | copy-start | bytes 12582916
  497.3 7.5 %collective-permute-start.8 = (bf16[32,512]{1,0:T(8,128)(2,1)S(1)}, bf16[32,512]{1,0:T(8,128)(2,1)S(1)}, u32[]{:S(2)}, u32[]{:S(2)}) collective-permute-start(bf16[32,512]{1,0:T(8,128)(2,1)S(1)} %slice_bitcast_fusion.2), channel_id=1, source_target_pairs={{0,128},{32,160},{64,192},{96,224},{128,256},{160,288},{192,320},{... | collective-permute-start | bytes 98312 | tf_op jit(solution)/shard_map/ppermute | solution.py:317
  517.5 85.3 %copy-start.74 = (f32[32,512]{1,0:T(8,128)}, f32[32,512]{1,0:T(8,128)S(1)}, u32[]{:S(2)}) copy-start(f32[32,512]{1,0:T(8,128)S(1)} %get-tuple-element.99) | copy-start | bytes 196612
  541.8 6.7 copy-start.59
  541.8 6.7 copy-start.61
  543.5 59.4 %copy-start.76 = (f32[32,512]{1,0:T(8,128)}, f32[32,512]{1,0:T(8,128)S(1)}, u32[]{:S(2)}) copy-start(f32[32,512]{1,0:T(8,128)S(1)} %get-tuple-element.100) | copy-start | bytes 196612
  543.5 12.8 %all-to-all-start.29 = ((bf16[8,32,512]{2,1,0:T(8,128)(2,1)}), bf16[8,32,512]{2,1,0:T(8,128)(2,1)S(1)}, u32[]{:S(2)}, u32[]{:S(2)}) async-start(bf16[8,32,512]{2,1,0:T(8,128)(2,1)} %get-tuple-element.83), calls=%async_computation.29 | async-start | bytes 524288 | tf_op jit(solution)/shard_map/all_to_all | solution.py:57
  558.5 5.0 copy-start.63
  558.5 5.0 copy-start.65
  558.5 5.6 copy-start.67
  558.5 5.6 copy-start.69
  560.0 14.6 %all-to-all-start.30 = ((bf16[8,32,512]{2,1,0:T(8,128)(2,1)}), bf16[8,32,512]{2,1,0:T(8,128)(2,1)S(1)}, u32[]{:S(2)}, u32[]{:S(2)}) async-start(bf16[8,32,512]{2,1,0:T(8,128)(2,1)} %project.20.stream_ref), calls=%async_computation.30 | async-start | bytes 524288 | tf_op jit(solution)/shard_map/all_to_all | solution.py:57
  576.8 5.1 copy-start.71
  576.8 5.1 copy-start.73
  578.5 43.0 %copy-start.78 = (f32[32,512]{1,0:T(8,128)}, f32[32,512]{1,0:T(8,128)S(1)}, u32[]{:S(2)}) copy-start(f32[32,512]{1,0:T(8,128)S(1)} %get-tuple-element.101) | copy-start | bytes 196612
  578.5 15.6 %all-to-all-start.31 = ((bf16[8,32,512]{2,1,0:T(8,128)(2,1)}), bf16[8,32,512]{2,1,0:T(8,128)(2,1)S(1)}, u32[]{:S(2)}, u32[]{:S(2)}) async-start(bf16[8,32,512]{2,1,0:T(8,128)(2,1)} %get-tuple-element.85), calls=%async_computation.31 | async-start | bytes 524288 | tf_op jit(solution)/shard_map/all_to_all | solution.py:57
  598.8 15.7 %all-to-all-start.32 = ((bf16[8,32,512]{2,1,0:T(8,128)(2,1)}), bf16[8,32,512]{2,1,0:T(8,128)(2,1)S(1)}, u32[]{:S(2)}, u32[]{:S(2)}) async-start(bf16[8,32,512]{2,1,0:T(8,128)(2,1)} %project.21), calls=%async_computation.32 | async-start | bytes 524288 | tf_op jit(solution)/shard_map/all_to_all | solution.py:57
  617.6 4.0 copy-start.80
  623.4 4.4 copy-start.75
  623.4 4.4 copy-start.77
  623.4 4.4 copy-start.79
  623.5 4.4 copy-start.81
  623.5 16.9 %all-to-all-start.33 = ((bf16[4,1536,128]{2,1,0:T(8,128)(2,1)}), bf16[4,1536,128]{2,1,0:T(8,128)(2,1)S(1)}, u32[]{:S(2)}, u32[]{:S(2)}) async-start(bf16[4,1536,128]{2,1,0:T(8,128)(2,1)} %pad_maximum_fusion), calls=%async_computation.33 | async-start | bytes 3145728 | tf_op jit(solution)/shard_map/all_to_all | solution.py:57
  653.8 43.9 %collective-permute-start.10 = (f32[1,128]{1,0:T(1,128)S(1)}, f32[1,128]{1,0:T(1,128)S(1)}, u32[]{:S(2)}, u32[]{:S(2)}) collective-permute-start(f32[1,128]{1,0:T(1,128)S(1)} %bitcast.168), channel_id=1, source_target_pairs={{0,32},{32,0},{64,96},{96,64},{128,160},{160,128},{192,224},{224,1... | collective-permute-start | bytes 1544 | tf_op jit(solution)/shard_map/ppermute | solution.py:65
  695.8 5.7 collective-permute-start.9
  701.5 29.6 %copy-start.1 = (bf16[4,32,512]{2,1,0:T(8,128)(2,1)S(1)}, bf16[4,32,512]{2,1,0:T(8,128)(2,1)}, u32[]{:S(2)}) copy-start(bf16[4,32,512]{2,1,0:T(8,128)(2,1)} %param.5) | copy-start | bytes 393220
  (59 other events, 79.6 us)

commit v5 on v4

v5 whole, which is shorter than its diff:
```python
import functools
import math

import jax
import jax.numpy as jnp
from jax import lax
from jax.experimental import pallas as pl
from jax.experimental.pallas import tpu as pltpu
from jax.sharding import PartitionSpec as P

D = 4096
GROUP = 128
STAGE = 4

norm_eps = 1e-05
full_turn = 2.0 * math.pi

SIN_TERMS = (3.141592653536291, -5.167712764624543, 2.5501633189471025,
             -0.5992521978250058, 0.08205040181365181, -0.007028386419353805)
COS_TERMS = (0.9999999997799043, -4.934802137078827, 4.058709159556301,
             -1.3352120030506605, 0.23493731381815505, -0.024396324355626643)


def horner(terms, square):
    total = jnp.full_like(square, terms[-1])
    for term in terms[-2::-1]:
        total = total * square + term
    return total


def half_turn(ratio):
    part = ratio - jnp.round(ratio)
    square = part * part
    return part * horner(SIN_TERMS, square), horner(COS_TERMS, square)


def quantize(values, scale):
    ratio = values / scale
    sine, cosine = half_turn(ratio)
    return scale * jnp.clip(ratio - sine * cosine / math.pi, -8.0, 7.0)


def level_and_slope(values, scale):
    ratio = values / scale
    sine, cosine = half_turn(ratio)
    stair = ratio - sine * cosine / math.pi
    inside = (stair > -8.0) & (stair < 7.0)
    level = scale * jnp.clip(stair, -8.0, 7.0)
    return level, jnp.where(inside, 2.0 * sine * sine, 0.0)


def copies_of(value, count):
    return jnp.broadcast_to(value[None], (count,) + value.shape)


def exchange(copies, axis):
    return lax.all_to_all(copies, axis, 0, 0, tiled=True)


def gather(value, axis):
    return exchange(copies_of(value, lax.axis_size(axis)), axis)


def crossed(value, mask):
    return lax.ppermute(value, "section", [(i, i ^ mask) for i in range(lax.axis_size("section"))])


VMEM = pl.BlockSpec(memory_space=pltpu.VMEM)
SMEM = pl.BlockSpec(memory_space=pltpu.SMEM)
FAR = pl.BlockSpec(memory_space=pl.ANY)
PARAMS = pltpu.CompilerParams(vmem_limit_bytes=8 * 1024 * 1024)


def start_load(layer, place_ref, refs, into, sems):
    chunks = sems.shape[0]
    chunk = into.shape[0] // chunks
    plane, core = place_ref[0] // 2, place_ref[0] % 2
    own, by1, even_mine, even_other, odd_mine, odd_other = refs
    mine, other = (odd_mine, odd_other) if layer % 2 else (even_mine, even_other)
    here, same = plane == layer // 2, core == layer % 2
    away, differs = jnp.logical_not(here), jnp.logical_not(same)
    for wanted, source in (
        (here & same, own), (here & differs, by1), (away & same, mine), (away & differs, other)
    ):
        @pl.when(wanted)
        def _():
            for index in range(chunks):
                rows = pl.ds(index * chunk, chunk)
                pltpu.make_async_copy(source.at[rows], into.at[rows], sems.at[index]).start()


def project_kernel(layer, place_ref, *args):
    refs, (quant_ref, stream_ref, copies_ref, out_ref, weight_ref, sems) = args[:6], args[6:]
    start_load(layer, place_ref, refs, weight_ref, sems)
    count, tok_rows, part = quant_ref.shape
    total = stream_ref[...].astype(jnp.float32)
    for k in range(count):
        rows = pl.ds(k * part, part)
        pltpu.make_async_copy(refs[0].at[rows], weight_ref.at[rows], sems.at[k]).wait()
        total = total + jnp.dot(quant_ref[k], weight_ref[rows], preferred_element_type=jnp.float32)
    stream = total.astype(jnp.bfloat16)
    out_ref[...] = stream
    for k in range(count):
        copies_ref[k] = stream


def project(layer, place, sources, quant_rows, stream):
    own = sources[0]
    return pl.pallas_call(
        functools.partial(project_kernel, layer),
        out_shape=[
            jax.ShapeDtypeStruct(quant_rows.shape, jnp.bfloat16),
            jax.ShapeDtypeStruct(stream.shape, jnp.bfloat16),
        ],
        in_specs=[SMEM] + [FAR] * 6 + [VMEM] * 2,
        out_specs=[VMEM] * 2,
        scratch_shapes=[
            pltpu.VMEM(own.shape, own.dtype),
            pltpu.SemaphoreType.DMA((quant_rows.shape[0],)),
        ],
        compiler_params=pltpu.CompilerParams(vmem_limit_bytes=56 * 1024 * 1024),
        name="project",
    )(place, *sources, quant_rows, stream)


def rotate_kernel(layer, last, keep_ref, rows_ref, gain_ref, rot_ref, scale_ref, _, __, *rest):
    (kept_normed, kept_rotated), rest = rest[:2], rest[2:]
    copies, (normed_ref, rotated_ref, sems) = rest[:-3], rest[-3:]
    count, tok_rows, part = rows_ref.shape
    place = pl.ds(layer * tok_rows, tok_rows)
    keep = keep_ref[0] == 1
    keep_normed = pltpu.make_async_copy(normed_ref, kept_normed.at[place], sems.at[0])
    keep_rotated = pltpu.make_async_copy(rotated_ref, kept_rotated.at[place], sems.at[1])
    total = None
    for k in range(count):
        rows = rows_ref[k].astype(jnp.float32)
        square = jnp.sum(rows * rows, axis=-1, keepdims=True)
        total = square if total is None else total + square
    factor = lax.rsqrt(total / (count * part) + norm_eps)
    for k in range(count):
        cols = slice(k * part, (k + 1) * part)
        rows = rows_ref[k].astype(jnp.float32)
        normed_ref[:, cols] = (rows * factor * gain_ref[:, cols]).astype(jnp.bfloat16)
    pl.when(keep)(keep_normed.start)
    rotated = jnp.dot(normed_ref[...], rot_ref[...], preferred_element_type=jnp.float32)
    rotated_ref[...] = rotated
    pl.when(keep)(keep_rotated.start)
    if not last:
        quantized = quantize(rotated, scale_ref[...]).astype(jnp.bfloat16)
        for k in range(count):
            copies[0][k] = quantized

    @pl.when(keep)
    def _():
        keep_normed.wait()
        keep_rotated.wait()


def rotate(layer, last, keep, rows, gain, rot_cols, scale, kept):
    count, tok_rows, part = rows.shape
    shapes = [jax.ShapeDtypeStruct(k.shape, k.dtype) for k in kept]
    if not last:
        shapes.append(jax.ShapeDtypeStruct(rows.shape, jnp.bfloat16))
    return pl.pallas_call(
        functools.partial(rotate_kernel, layer, last),
        out_shape=shapes,
        in_specs=[SMEM] + [VMEM] * 4 + [FAR] * 2,
        out_specs=[FAR] * 2 + [VMEM] * (len(shapes) - 2),
        input_output_aliases={5: 0, 6: 1},
        scratch_shapes=[
            pltpu.VMEM((tok_rows, count * part), jnp.bfloat16),
            pltpu.VMEM((tok_rows, part), jnp.float32),
            pltpu.SemaphoreType.DMA((2,)),
        ],
        compiler_params=PARAMS,
        name="rotate",
    )(keep, rows, gain, rot_cols, scale, *kept)


def terms_kernel(part_rows, core_ref, parts_ref, mine_ref, other_ref):
    sources, rows, lanes = parts_ref.shape
    count, _, cols = mine_ref.shape
    features = 2 * count * part_rows
    left = jnp.concatenate([parts_ref[s, :features] for s in range(sources)], axis=1)
    right = jnp.concatenate(
        [
            jnp.concatenate([parts_ref[s, pl.ds(k, lanes)] for k in range(features, rows, lanes)], axis=1)
            for s in range(sources)
        ],
        axis=0,
    )
    terms = jnp.dot(left, right, preferred_element_type=jnp.float32)
    lower = core_ref[0] == 0
    for z in range(count):
        even = terms[2 * z * part_rows : (2 * z + 1) * part_rows]
        odd = terms[(2 * z + 1) * part_rows : (2 * z + 2) * part_rows]
        mine_ref[z] = jnp.where(lower, even, odd)
        other_ref[z] = jnp.where(lower, odd, even).astype(jnp.bfloat16)


def terms_of(core, parts, planes, row_block, part_cols):
    shape = (planes, row_block, part_cols)
    return pl.pallas_call(
        functools.partial(terms_kernel, row_block),
        out_shape=[jax.ShapeDtypeStruct(shape, jnp.float32), jax.ShapeDtypeStruct(shape, jnp.bfloat16)],
        in_specs=[pl.BlockSpec(memory_space=pltpu.SMEM), VMEM],
        out_specs=[VMEM, VMEM],
        compiler_params=pltpu.CompilerParams(vmem_limit_bytes=24 * 1024 * 1024),
        name="terms",
    )(core[None].astype(jnp.int32), parts)


def local(hidden_in, rotation, proj, norm_gain, quant_exp):
    sections = lax.axis_size("section")
    replicas = lax.axis_size("dp")
    tensor = lax.axis_size("tp")
    section_pos = lax.axis_index("section")
    micro_count, tok_rows, part_cols = hidden_in.shape
    stages = sections // STAGE
    planes = sections // 2
    stage_pos = section_pos // STAGE
    place = section_pos % STAGE
    core = section_pos % 2
    same_core = [[2 * z + c for z in range(planes)] for c in range(2)]
    row_block = rotation.shape[0]

    own = proj[0]
    by1 = crossed(own, 1)
    even_mine = lax.ppermute(own, "section", [(i, i ^ 2) for i in range(0, sections, 2)])

    scale_row = jnp.repeat(jnp.exp2(quant_exp.astype(jnp.float32) * 0.25) * 0.125, GROUP, axis=1)
    params = jnp.concatenate([norm_gain, scale_row], axis=1)
    params_by1 = crossed(params, 1)
    params_by2 = crossed(jnp.concatenate([params, params_by1], axis=0), 2)
    found = jnp.concatenate([params, params_by1, params_by2], axis=0)
    params = jnp.stack([lax.dynamic_index_in_dim(found, place ^ k, 0, False) for k in range(STAGE)])
    gains, scales = params[:, :D], params[:, D:]

    along_z = lax.all_to_all(
        copies_of(rotation, planes), "section", 0, 0, axis_index_groups=same_core, tiled=True
    )
    along_x = gather(along_z, "dp")
    other_rows = crossed(along_x, 1)
    own_later, _ = lax.optimization_barrier((own, other_rows))
    odd_mine = lax.ppermute(own_later, "section", [(i, i ^ 2) for i in range(1, sections, 2)])
    even_rows = jnp.where(core == 0, along_x, other_rows)
    odd_rows = jnp.where(core == 0, other_rows, along_x)
    rot_cols = jnp.stack([even_rows, odd_rows]).transpose(2, 0, 1, 3, 4).reshape(D, part_cols)

    where = place[None].astype(jnp.int32)
    all_rows = STAGE * tok_rows
    stream = lax.dynamic_index_in_dim(hidden_in, place, 0, keepdims=False)
    copies = copies_of(stream, tensor)
    kept = (jnp.zeros((all_rows, D), jnp.bfloat16), jnp.zeros((all_rows, part_cols), jnp.float32))
    for stage in range(stages):
        keep = jnp.full((1,), 1, jnp.int32) if stage == 0 else (stage_pos == stage).astype(jnp.int32)[None]
        for layer in range(STAGE):
            last = stage == stages - 1 and layer == STAGE - 1
            gain, scale = gains[layer : layer + 1], scales[layer : layer + 1]
            results = rotate(layer, last, keep, exchange(copies, "tp"), gain, rot_cols, scale, kept)
            kept = results[:2]
            if last:
                break
            quant = results[2]
            if stage == 0 and layer == 0:
                even_mine, _ = lax.optimization_barrier((even_mine, quant))
                even_other = lax.ppermute(even_mine, "section", [(i, i + 1) for i in range(0, sections, 2)])
                sources = (own, by1, even_mine, even_other, even_mine, even_other)
            if stage == 0 and layer == 1:
                odd_mine, _ = lax.optimization_barrier((odd_mine, quant))
                odd_other = lax.ppermute(odd_mine, "section", [(i + 1, i) for i in range(0, sections, 2)])
                sources = (own, by1, even_mine, even_other, odd_mine, odd_other)
            copies, stream = project(layer, where, sources, exchange(quant, "tp"), stream)
        if stage < stages - 1:
            stream = lax.ppermute(
                stream, "section", [(i, i + STAGE) for i in range(sections - STAGE)]
            )
            copies = copies_of(stream, tensor)
    kept_normed, kept_rotated = kept

    lanes = all_rows
    turned = lax.optimization_barrier(kept_normed.T)
    turned = turned.reshape(sections, replicas, row_block, lanes).transpose(1, 0, 2, 3)
    turned = turned.reshape(replicas, sections * row_block, lanes)
    row_scales = jnp.repeat(scales, tok_rows, axis=0)
    level, slope = level_and_slope(kept_rotated, row_scales)
    error_part = level - kept_rotated
    grad_rot = (error_part * (slope - 1.0)).astype(jnp.bfloat16)
    grad_rot = grad_rot.reshape(all_rows, part_cols // lanes, lanes).transpose(1, 0, 2)
    sent = jnp.concatenate([turned, copies_of(grad_rot.reshape(-1, lanes), replicas)], axis=1)
    parts = exchange(sent, "dp")
    mine, other = terms_of(core, parts, planes, row_block, part_cols)
    loss = jnp.full((8, 128), jnp.sum(error_part * error_part), jnp.float32)
    loss = loss + crossed(loss, 1)
    loss, _ = lax.optimization_barrier((loss, other))
    losses = exchange(copies_of(loss, replicas * tensor), ("dp", "tp"))
    loss = jnp.sum(losses[:, 0, 0])

    pair_sum = (mine + crossed(other, 1).astype(jnp.float32)).astype(jnp.bfloat16)
    high = lax.reduce_precision(loss, 8, 7)
    middle = lax.reduce_precision(loss - high, 8, 7)
    low = loss - high - middle
    lane = lax.broadcasted_iota(jnp.int32, (16, part_cols), 1)
    tail_rows = jnp.where(lane == 0, high, jnp.where(lane == 1, middle, jnp.where(lane == 2, low, 0.0)))
    tail_rows = tail_rows.astype(jnp.bfloat16)
    sent = jnp.concatenate([pair_sum, copies_of(tail_rows, planes)], axis=1)
    parts = lax.all_to_all(sent, "section", 0, 0, axis_index_groups=same_core, tiled=True)
    sums = jnp.sum(parts.astype(jnp.float32), axis=0)
    factor = 1.0 / math.sqrt(sections * all_rows * replicas)
    norm_count = all_rows * replicas * D
    return (sums[:row_block] * factor, jnp.sum(sums[row_block, :3]) / norm_count)


def solution(mesh):
    placed = (
        P(None, "dp", "tp"),
        P(("section", "dp"), "tp"),
        P("section", None, "tp"),
        P("section", None),
        P("section", "tp"),
    )
    return jax.shard_map(
        local,
        mesh=mesh,
        in_specs=placed,
        out_specs=(P(("section", "dp"), "tp"), P()),
        check_vma=False,
    )
```

time: 736 us -> 715 us (0.971)
  local copies, waits for them, and re-layouts: 80.4 us -> 22.2 us
  blocking collectives: 320 us -> 372 us
  Pallas kernels: 47 us -> 82.4 us
  waiting for transfers between devices: 128 us -> 95.3 us
  starting transfers between devices: 141 us -> 116 us
    all_to_all x22 -> x25, blocking collectives: 269 us -> 324 us  [exchange(): return lax.all_to_all(copies, axis, 0, 0, tiled=True)]
    unnamed x199 -> x36, local copies, waits for them, and re-layouts: 58.8 us -> 11.7 us
    pallas_call x35 -> x31, Pallas kernels: 46.3 us -> 81.7 us  [the longest x15 63.1 us: project(): pl.pallas_call(functools.partial(project_kernel, layer), out_shape=[jax.S...]
    all_to_all x0 -> x1, blocking collectives: none -> 26.7 us  [local(): lax.all_to_all(copies_of(rotation, planes), 'section', 0, 0, axis_index_g...]
    all_to_all x12 -> x9, waiting for transfers between devices: 100 us -> 75.4 us  [exchange(): return lax.all_to_all(copies, axis, 0, 0, tiled=True)]
    all_gather x1 -> x0, blocking collectives: 23.9 us -> none  [local(): lax.all_gather(params, 'section', axis=0, tiled=True, axis_index_groups=g...]
    ppermute x8 -> x6, waiting for transfers between devices: 19 us -> 0.81 us  [crossed(): lax.ppermute(value, 'section', [(i, i ^ mask) for i in range(lax.axis_siz...]
    ppermute x3 -> x7, waiting for transfers between devices: 3.01 us -> 19.1 us  [the longest x1 15.1 us: local(): lax.ppermute(own_later, 'section', [(i, i ^ 2) for i in range(1, sections...]
  transfers between devices with their start and end apart: 24 -> 22, of which waited for: 17 -> 12; matrix products, arithmetic and copies ran while one was open for 3% -> 1% of each run, Pallas kernels for 1% -> 1%
where the time goes in v5:
time: 715 us; the launch traced here: 704 us
  blocking collectives  372 us (52%)
  starting transfers between devices  116 us (16%)
  waiting for transfers between devices  95.3 us (13%)
  Pallas kernels  82.4 us (12%)
  local copies, waits for them, and re-layouts  22.2 us (3%)
  other arithmetic  9.43 us (1%)
    all_to_all x25, blocking collectives, exchange(): return lax.all_to_all(copies, axis, 0, 0, tiled=True)  324 us
    all_to_all x9, waiting for transfers between devices, exchange(): return lax.all_to_all(copies, axis, 0, 0, tiled=True)  75.4 us
    pallas_call x15, Pallas kernels, project(): pl.pallas_call(functools.partial(project_kernel, layer), out_shape=[jax.S...  63.1 us
    ppermute x6, starting transfers between devices, crossed(): lax.ppermute(value, 'section', [(i, i ^ mask) for i in range(lax.axis_siz...  54.7 us
    all_to_all x9, starting transfers between devices, exchange(): return lax.all_to_all(copies, axis, 0, 0, tiled=True)  38.3 us
    all_to_all x1, blocking collectives, local(): lax.all_to_all(copies_of(rotation, planes), 'section', 0, 0, axis_index_g...  26.7 us
    all_to_all x1, blocking collectives, local(): lax.all_to_all(sent, 'section', 0, 0, axis_index_groups=same_core, tiled=...  21.6 us
    pallas_call x16, Pallas kernels, rotate(): pl.pallas_call(functools.partial(rotate_kernel, layer, last), out_shape=s...  18.6 us
  transfers between devices with their start and end apart: 22, of which 12 were waited for; matrix products, arithmetic and copies ran while one was open for 1% of the time, Pallas kernels for 1%

profile of v5, /device:TPU:1, one launch (start us, length us, event | category | flops | bytes accessed | tf_op | source)
XLA Modules:
  0.0 704.0 jit_solution(739453535848868048)
XLA Ops:
  1.6 26.7 %all_to_all.180 = bf16[8,64,512]{2,1,0:T(8,128)(2,1)S(1)} all-to-all(bf16[8,64,512]{2,1,0:T(8,128)(2,1)S(1)} %broadcast_in_dim.126), channel_id=1, replica_groups={{0,64,128,192,256,320,384,448},{32,96,160,224,288,352,416,480},{1,65,12..., dimensions={0} | all-to-all | bytes 1048576 | tf_op jit(solution)/shard_map/all_to_all | solution.py:239
  29.9 4.6 all-to-all-start.2
  37.1 21.3 %all-to-all-done.2 = bf16[4,8,64,512]{3,2,1,0:T(8,128)(2,1)} async-done(((bf16[4,8,64,512]{3,2,1,0:T(8,128)(2,1)}), bf16[4,8,64,512]{3,2,1,0:T(8,128)(2,1)}, u32[]{:S(2)}, u32[]{:S(2)}) %all-to-all-start.2) | async-done | bytes 2097184 | tf_op jit(solution)/shard_map/all_to_all | solution.py:57
  58.5 5.3 collective-permute-start.4
  70.9 6.8 all-to-all-start
  83.4 6.7 all-to-all-done.rows_ref
  98.4 3.4 all-to-all-start.3
  101.8 9.2 %all-to-all-done.3.args_6_ = bf16[8,32,512]{2,1,0:T(8,128)(2,1)S(1)} async-done(((bf16[8,32,512]{2,1,0:T(8,128)(2,1)}), bf16[8,32,512]{2,1,0:T(8,128)(2,1)S(1)}, u32[]{:S(2)}, u32[]{:S(2)}) %all-to-all-start.3) | async-done | bytes 262176 | tf_op jit(solution)/shard_map/all_to_all | solution.py:57
  111.8 4.5 project.15
  116.3 12.7 %all_to_all.181.rows_ref = bf16[8,32,512]{2,1,0:T(8,128)(2,1)S(1)} all-to-all(bf16[8,32,512]{2,1,0:T(8,128)(2,1)} %get-tuple-element.84), channel_id=1, replica_groups=mesh['section'=16,'dp'=4,'tp'=8] {'tp'}, dimensions={0} | all-to-all | bytes 524288 | tf_op jit(solution)/shard_map/all_to_all | solution.py:57
  130.1 15.1 %collective-permute-done.6.args_4_ = bf16[4096,512]{1,0:T(8,128)(2,1)} collective-permute-done((bf16[4096,512]{1,0:T(8,128)(2,1)}, bf16[4096,512]{1,0:T(8,128)(2,1)}, u32[]{:S(2)}, u32[]{:S(2)}) %collective-permute-start.6) | collective-permute-done | bytes 4194336 | tf_op jit(solution)/shard_map/ppermute | solution.py:245
  148.5 12.4 %all_to_all.182.args_6_ = bf16[8,32,512]{2,1,0:T(8,128)(2,1)} all-to-all(bf16[8,32,512]{2,1,0:T(8,128)(2,1)S(1)} %get-tuple-element.87), channel_id=1, replica_groups=mesh['section'=16,'dp'=4,'tp'=8] {'tp'}, dimensions={0} | all-to-all | bytes 524288 | tf_op jit(solution)/shard_map/all_to_all | solution.py:57
  160.9 4.1 project.16
  165.0 12.7 %all_to_all.183.rows_ref = bf16[8,32,512]{2,1,0:T(8,128)(2,1)S(1)} all-to-all(bf16[8,32,512]{2,1,0:T(8,128)(2,1)} %get-tuple-element.90), channel_id=1, replica_groups=mesh['section'=16,'dp'=4,'tp'=8] {'tp'}, dimensions={0} | all-to-all | bytes 524288 | tf_op jit(solution)/shard_map/all_to_all | solution.py:57
  178.9 12.9 %all_to_all.184.args_6_ = bf16[8,32,512]{2,1,0:T(8,128)(2,1)} all-to-all(bf16[8,32,512]{2,1,0:T(8,128)(2,1)S(1)} %get-tuple-element.93), channel_id=1, replica_groups=mesh['section'=16,'dp'=4,'tp'=8] {'tp'}, dimensions={0} | all-to-all | bytes 524288 | tf_op jit(solution)/shard_map/all_to_all | solution.py:57
  191.8 4.1 project.17
  195.9 13.9 %all_to_all.185.rows_ref = bf16[8,32,512]{2,1,0:T(8,128)(2,1)S(1)} all-to-all(bf16[8,32,512]{2,1,0:T(8,128)(2,1)} %get-tuple-element.95), channel_id=1, replica_groups=mesh['section'=16,'dp'=4,'tp'=8] {'tp'}, dimensions={0} | all-to-all | bytes 524288 | tf_op jit(solution)/shard_map/all_to_all | solution.py:57
  211.0 14.4 %all_to_all.186.args_6_ = bf16[8,32,512]{2,1,0:T(8,128)(2,1)} all-to-all(bf16[8,32,512]{2,1,0:T(8,128)(2,1)S(1)} %get-tuple-element.98), channel_id=1, replica_groups=mesh['section'=16,'dp'=4,'tp'=8] {'tp'}, dimensions={0} | all-to-all | bytes 524288 | tf_op jit(solution)/shard_map/all_to_all | solution.py:57
  225.4 4.1 project.18
  233.2 3.4 all-to-all-start.10
  236.7 10.5 %all-to-all-done.10.rows_ref = bf16[8,32,512]{2,1,0:T(8,128)(2,1)S(1)} async-done(((bf16[8,32,512]{2,1,0:T(8,128)(2,1)}), bf16[8,32,512]{2,1,0:T(8,128)(2,1)S(1)}, u32[]{:S(2)}, u32[]{:S(2)}) %all-to-all-start.10) | async-done | bytes 262176 | tf_op jit(solution)/shard_map/all_to_all | solution.py:57
  250.5 12.6 %all_to_all.187.args_6_ = bf16[8,32,512]{2,1,0:T(8,128)(2,1)} all-to-all(bf16[8,32,512]{2,1,0:T(8,128)(2,1)S(1)} %get-tuple-element.103), channel_id=1, replica_groups=mesh['section'=16,'dp'=4,'tp'=8] {'tp'}, dimensions={0} | all-to-all | bytes 524288 | tf_op jit(solution)/shard_map/all_to_all | solution.py:57
  263.1 4.5 project.19
  267.6 12.8 %all_to_all.188.rows_ref = bf16[8,32,512]{2,1,0:T(8,128)(2,1)S(1)} all-to-all(bf16[8,32,512]{2,1,0:T(8,128)(2,1)} %get-tuple-element.104), channel_id=1, replica_groups=mesh['section'=16,'dp'=4,'tp'=8] {'tp'}, dimensions={0} | all-to-all | bytes 524288 | tf_op jit(solution)/shard_map/all_to_all | solution.py:57
  281.5 12.4 %all_to_all.189.args_6_ = bf16[8,32,512]{2,1,0:T(8,128)(2,1)} all-to-all(bf16[8,32,512]{2,1,0:T(8,128)(2,1)S(1)} %get-tuple-element.107), channel_id=1, replica_groups=mesh['section'=16,'dp'=4,'tp'=8] {'tp'}, dimensions={0} | all-to-all | bytes 524288 | tf_op jit(solution)/shard_map/all_to_all | solution.py:57
  293.9 4.1 project.20
  298.0 12.7 %all_to_all.190.rows_ref = bf16[8,32,512]{2,1,0:T(8,128)(2,1)S(1)} all-to-all(bf16[8,32,512]{2,1,0:T(8,128)(2,1)} %get-tuple-element.109), channel_id=1, replica_groups=mesh['section'=16,'dp'=4,'tp'=8] {'tp'}, dimensions={0} | all-to-all | bytes 524288 | tf_op jit(solution)/shard_map/all_to_all | solution.py:57
  311.8 12.4 %all_to_all.191.args_6_ = bf16[8,32,512]{2,1,0:T(8,128)(2,1)} all-to-all(bf16[8,32,512]{2,1,0:T(8,128)(2,1)S(1)} %get-tuple-element.112), channel_id=1, replica_groups=mesh['section'=16,'dp'=4,'tp'=8] {'tp'}, dimensions={0} | all-to-all | bytes 524288 | tf_op jit(solution)/shard_map/all_to_all | solution.py:57
  324.2 4.1 project.21
  328.3 12.7 %all_to_all.192.rows_ref = bf16[8,32,512]{2,1,0:T(8,128)(2,1)S(1)} all-to-all(bf16[8,32,512]{2,1,0:T(8,128)(2,1)} %get-tuple-element.114), channel_id=1, replica_groups=mesh['section'=16,'dp'=4,'tp'=8] {'tp'}, dimensions={0} | all-to-all | bytes 524288 | tf_op jit(solution)/shard_map/all_to_all | solution.py:57
  342.1 12.3 %all_to_all.193.args_6_ = bf16[8,32,512]{2,1,0:T(8,128)(2,1)} all-to-all(bf16[8,32,512]{2,1,0:T(8,128)(2,1)S(1)} %get-tuple-element.117), channel_id=1, replica_groups=mesh['section'=16,'dp'=4,'tp'=8] {'tp'}, dimensions={0} | all-to-all | bytes 524288 | tf_op jit(solution)/shard_map/all_to_all | solution.py:57
  354.4 4.1 project.22
  358.5 4.5 collective-permute-start.9
  365.0 3.4 all-to-all-start.18
  368.5 9.2 %all-to-all-done.18.rows_ref = bf16[8,32,512]{2,1,0:T(8,128)(2,1)S(1)} async-done(((bf16[8,32,512]{2,1,0:T(8,128)(2,1)}), bf16[8,32,512]{2,1,0:T(8,128)(2,1)S(1)}, u32[]{:S(2)}, u32[]{:S(2)}) %all-to-all-start.18) | async-done | bytes 262176 | tf_op jit(solution)/shard_map/all_to_all | solution.py:57
  381.0 12.4 %all_to_all.194.args_6_ = bf16[8,32,512]{2,1,0:T(8,128)(2,1)} all-to-all(bf16[8,32,512]{2,1,0:T(8,128)(2,1)S(1)} %get-tuple-element.122), channel_id=1, replica_groups=mesh['section'=16,'dp'=4,'tp'=8] {'tp'}, dimensions={0} | all-to-all | bytes 524288 | tf_op jit(solution)/shard_map/all_to_all | solution.py:57
  393.4 4.5 project.23
  397.9 12.7 %all_to_all.195.rows_ref = bf16[8,32,512]{2,1,0:T(8,128)(2,1)S(1)} all-to-all(bf16[8,32,512]{2,1,0:T(8,128)(2,1)} %get-tuple-element.123), channel_id=1, replica_groups=mesh['section'=16,'dp'=4,'tp'=8] {'tp'}, dimensions={0} | all-to-all | bytes 524288 | tf_op jit(solution)/shard_map/all_to_all | solution.py:57
  411.7 14.6 %all_to_all.196.args_6_ = bf16[8,32,512]{2,1,0:T(8,128)(2,1)} all-to-all(bf16[8,32,512]{2,1,0:T(8,128)(2,1)S(1)} %get-tuple-element.126), channel_id=1, replica_groups=mesh['section'=16,'dp'=4,'tp'=8] {'tp'}, dimensions={0} | all-to-all | bytes 524288 | tf_op jit(solution)/shard_map/all_to_all | solution.py:57
  426.3 4.1 project.24
  430.4 13.8 %all_to_all.197.rows_ref = bf16[8,32,512]{2,1,0:T(8,128)(2,1)S(1)} all-to-all(bf16[8,32,512]{2,1,0:T(8,128)(2,1)} %get-tuple-element.128), channel_id=1, replica_groups=mesh['section'=16,'dp'=4,'tp'=8] {'tp'}, dimensions={0} | all-to-all | bytes 524288 | tf_op jit(solution)/shard_map/all_to_all | solution.py:57
  445.2 12.5 %all_to_all.198.args_6_ = bf16[8,32,512]{2,1,0:T(8,128)(2,1)} all-to-all(bf16[8,32,512]{2,1,0:T(8,128)(2,1)S(1)} %get-tuple-element.131), channel_id=1, replica_groups=mesh['section'=16,'dp'=4,'tp'=8] {'tp'}, dimensions={0} | all-to-all | bytes 524288 | tf_op jit(solution)/shard_map/all_to_all | solution.py:57
  457.8 4.1 project.25
  461.9 15.8 %all_to_all.199.rows_ref = bf16[8,32,512]{2,1,0:T(8,128)(2,1)S(1)} all-to-all(bf16[8,32,512]{2,1,0:T(8,128)(2,1)} %get-tuple-element.133), channel_id=1, replica_groups=mesh['section'=16,'dp'=4,'tp'=8] {'tp'}, dimensions={0} | all-to-all | bytes 524288 | tf_op jit(solution)/shard_map/all_to_all | solution.py:57
  478.9 12.5 %all_to_all.200.args_6_ = bf16[8,32,512]{2,1,0:T(8,128)(2,1)} all-to-all(bf16[8,32,512]{2,1,0:T(8,128)(2,1)S(1)} %get-tuple-element.136), channel_id=1, replica_groups=mesh['section'=16,'dp'=4,'tp'=8] {'tp'}, dimensions={0} | all-to-all | bytes 524288 | tf_op jit(solution)/shard_map/all_to_all | solution.py:57
  491.4 4.1 project.26
  495.5 6.8 collective-permute-start.10
  504.4 3.4 all-to-all-start.26
  507.8 9.2 %all-to-all-done.26.rows_ref = bf16[8,32,512]{2,1,0:T(8,128)(2,1)S(1)} async-done(((bf16[8,32,512]{2,1,0:T(8,128)(2,1)}), bf16[8,32,512]{2,1,0:T(8,128)(2,1)S(1)}, u32[]{:S(2)}, u32[]{:S(2)}) %all-to-all-start.26) | async-done | bytes 262176 | tf_op jit(solution)/shard_map/all_to_all | solution.py:57
  520.3 12.5 %all_to_all.201.args_6_ = bf16[8,32,512]{2,1,0:T(8,128)(2,1)} all-to-all(bf16[8,32,512]{2,1,0:T(8,128)(2,1)S(1)} %get-tuple-element.141), channel_id=1, replica_groups=mesh['section'=16,'dp'=4,'tp'=8] {'tp'}, dimensions={0} | all-to-all | bytes 524288 | tf_op jit(solution)/shard_map/all_to_all | solution.py:57
  532.8 4.5 project.27
  537.3 12.7 %all_to_all.202.rows_ref = bf16[8,32,512]{2,1,0:T(8,128)(2,1)S(1)} all-to-all(bf16[8,32,512]{2,1,0:T(8,128)(2,1)} %get-tuple-element.142), channel_id=1, replica_groups=mesh['section'=16,'dp'=4,'tp'=8] {'tp'}, dimensions={0} | all-to-all | bytes 524288 | tf_op jit(solution)/shard_map/all_to_all | solution.py:57
  551.2 12.4 %all_to_all.203.args_6_ = bf16[8,32,512]{2,1,0:T(8,128)(2,1)} all-to-all(bf16[8,32,512]{2,1,0:T(8,128)(2,1)S(1)} %get-tuple-element.145), channel_id=1, replica_groups=mesh['section'=16,'dp'=4,'tp'=8] {'tp'}, dimensions={0} | all-to-all | bytes 524288 | tf_op jit(solution)/shard_map/all_to_all | solution.py:57
  563.6 4.1 project.28
  567.7 12.7 %all_to_all.204.rows_ref = bf16[8,32,512]{2,1,0:T(8,128)(2,1)S(1)} all-to-all(bf16[8,32,512]{2,1,0:T(8,128)(2,1)} %get-tuple-element.147), channel_id=1, replica_groups=mesh['section'=16,'dp'=4,'tp'=8] {'tp'}, dimensions={0} | all-to-all | bytes 524288 | tf_op jit(solution)/shard_map/all_to_all | solution.py:57
  581.4 12.4 %all_to_all.205.args_6_ = bf16[8,32,512]{2,1,0:T(8,128)(2,1)} all-to-all(bf16[8,32,512]{2,1,0:T(8,128)(2,1)S(1)} %get-tuple-element.150), channel_id=1, replica_groups=mesh['section'=16,'dp'=4,'tp'=8] {'tp'}, dimensions={0} | all-to-all | bytes 524288 | tf_op jit(solution)/shard_map/all_to_all | solution.py:57
  593.8 4.1 project.29
  597.9 3.6 all-to-all-start.32
  601.7 9.1 %all-to-all-done.32.rows_ref = bf16[8,32,512]{2,1,0:T(8,128)(2,1)S(1)} async-done(((bf16[8,32,512]{2,1,0:T(8,128)(2,1)}), bf16[8,32,512]{2,1,0:T(8,128)(2,1)S(1)}, u32[]{:S(2)}, u32[]{:S(2)}) %all-to-all-start.32) | async-done | bytes 262176 | tf_op jit(solution)/shard_map/all_to_all | solution.py:57
  617.2 4.6 all-to-all-start.33
  622.5 32.7 %collective-permute-start.12 = (f32[8,128]{1,0:T(8,128)S(1)}, f32[8,128]{1,0:T(8,128)S(1)}, u32[]{:S(2)}, u32[]{:S(2)}) collective-permute-start(f32[8,128]{1,0:T(8,128)S(1)} %broadcast_in_dim.142), channel_id=1, source_target_pairs={{0,32},{32,0},{64,96},{96,64},{128,160},{160,128},{192,224},{224,1... | collective-permute-start | bytes 12296 | tf_op jit(solution)/shard_map/ppermute | solution.py:65
  658.0 4.9 all-to-all-start.34
  662.9 10.5 %collective-permute-start.11 = (bf16[8,64,512]{2,1,0:T(8,128)(2,1)S(1)}, bf16[8,64,512]{2,1,0:T(8,128)(2,1)S(1)}, u32[]{:S(2)}, u32[]{:S(2)}) collective-permute-start(bf16[8,64,512]{2,1,0:T(8,128)(2,1)S(1)} %get-tuple-element.158), channel_id=1, source_target_pairs={{0,32},{32,0},{64,96},{96,64},{128,160},{160,128},{192,224},{224,1... | collective-permute-start | bytes 1572872 | tf_op jit(solution)/shard_map/ppermute | solution.py:65
  679.3 21.6 %all_to_all.206 = bf16[8,80,512]{2,1,0:T(8,128)(2,1)S(1)} all-to-all(bf16[8,80,512]{2,1,0:T(8,128)(2,1)S(1)} %pad_maximum_fusion.1), channel_id=1, replica_groups={{0,64,128,192,256,320,384,448},{32,96,160,224,288,352,416,480},{1,65,12..., dimensions={0} | all-to-all | bytes 1310720 | tf_op jit(solution)/shard_map/all_to_all | solution.py:307
  (116 shorter events, 73.7 us)
Async XLA Ops:
  0.6 69.6 %copy-start = (bf16[4,32,512]{2,1,0:T(8,128)(2,1)S(1)}, bf16[4,32,512]{2,1,0:T(8,128)(2,1)}, u32[]{:S(2)}) copy-start(bf16[4,32,512]{2,1,0:T(8,128)(2,1)} %param.5) | copy-start | bytes 393220
  29.9 7.3 %copy-start.17 = (s32[1,4]{1,0:T(1,128)S(1)}, s32[1,4]{1,0:T(1,128)}, u32[]{:S(2)}) copy-start(s32[1,4]{1,0:T(1,128)} %param.9) | copy-start | bytes 52
  29.9 33.9 %copy-start.13 = (f32[1,4096]{1,0:T(1,128)S(1)}, f32[1,4096]{1,0:T(1,128)}, u32[]{:S(2)}) copy-start(f32[1,4096]{1,0:T(1,128)} %param.8) | copy-start | bytes 49156
  29.9 28.6 %all-to-all-start.2 = ((bf16[4,8,64,512]{3,2,1,0:T(8,128)(2,1)}), bf16[4,8,64,512]{3,2,1,0:T(8,128)(2,1)}, u32[]{:S(2)}, u32[]{:S(2)}) async-start(bf16[4,8,64,512]{3,2,1,0:T(8,128)(2,1)} %broadcast_in_dim.127), calls=%async_computation.2 | async-start | bytes 4194304 | tf_op jit(solution)/shard_map/all_to_all | solution.py:57
  34.5 59.9 %collective-permute-start.1 = (bf16[4096,512]{1,0:T(8,128)(2,1)}, bf16[4096,512]{1,0:T(8,128)(2,1)}, u32[]{:S(2)}, u32[]{:S(2)}) collective-permute-start(bf16[4096,512]{1,0:T(8,128)(2,1)} %bitcast.3.args_0_), channel_id=1, source_target_pairs={{0,64},{64,0},{128,192},{192,128},{256,320},{320,256},{384,448},{4... | collective-permute-start | bytes 12582920 | tf_op jit(solution)/shard_map/ppermute | solution.py:229
  58.5 19.5 %collective-permute-start.4 = (bf16[4,8,64,512]{3,2,1,0:T(8,128)(2,1)}, bf16[4,8,64,512]{3,2,1,0:T(8,128)(2,1)}, u32[]{:S(2)}, u32[]{:S(2)}) collective-permute-start(bf16[4,8,64,512]{3,2,1,0:T(8,128)(2,1)} %all-to-all-done.2), channel_id=1, source_target_pairs={{0,32},{32,0},{64,96},{96,64},{128,160},{160,128},{192,224},{224,1... | collective-permute-start | bytes 6291464 | tf_op jit(solution)/shard_map/ppermute | solution.py:65
  63.8 4.4 collective-permute-start.2
  65.8 36.1 %collective-permute-start = (bf16[4096,512]{1,0:T(8,128)(2,1)}, bf16[4096,512]{1,0:T(8,128)(2,1)}, u32[]{:S(2)}, u32[]{:S(2)}) collective-permute-start(bf16[4096,512]{1,0:T(8,128)(2,1)} %bitcast.3.args_0_), channel_id=1, source_target_pairs={{0,32},{32,0},{64,96},{96,64},{128,160},{160,128},{192,224},{224,1... | collective-permute-start | bytes 12582920 | tf_op jit(solution)/shard_map/ppermute | solution.py:65
  68.3 9.5 %collective-permute-start.3 = (f32[2,4608]{1,0:T(2,128)S(1)}, f32[2,4608]{1,0:T(2,128)S(1)}, u32[]{:S(2)}, u32[]{:S(2)}) collective-permute-start(f32[2,4608]{1,0:T(2,128)S(1)} %pad_maximum_fusion.3), channel_id=1, source_target_pairs={{0,64},{32,96},{64,0},{96,32},{128,192},{160,224},{192,128},{224,1... | collective-permute-start | bytes 110600 | tf_op jit(solution)/shard_map/ppermute | solution.py:65
  70.2 10.3 %copy-start.12 = (bf16[32,512]{1,0:T(8,128)(2,1)}, bf16[32,512]{1,0:T(8,128)(2,1)S(1)}, u32[]{:S(2)}) copy-start(bf16[32,512]{1,0:T(8,128)(2,1)S(1)} %dynamic-slice_bitcast_fusion.args_7_) | copy-start | bytes 98308
  70.9 19.2 %all-to-all-start = ((bf16[8,32,512]{2,1,0:T(8,128)(2,1)}), bf16[8,32,512]{2,1,0:T(8,128)(2,1)S(1)}, u32[]{:S(2)}, u32[]{:S(2)}) async-start(bf16[8,32,512]{2,1,0:T(8,128)(2,1)} %broadcast_in_dim.123), calls=%async_computation | async-start | bytes 524288 | tf_op jit(solution)/shard_map/all_to_all | solution.py:57
  90.3 2.2 copy-start.2
  94.4 16.7 %collective-permute-start.5 = (bf16[4096,512]{1,0:T(8,128)(2,1)}, bf16[4096,512]{1,0:T(8,128)(2,1)}, u32[]{:S(2)}, u32[]{:S(2)}) collective-permute-start(bf16[4096,512]{1,0:T(8,128)(2,1)} %collective-permute-done.1.args_2_.args_4_), channel_id=1, source_target_pairs={{0,32},{64,96},{128,160},{192,224},{256,288},{320,352},{384,416},{... | collective-permute-start | bytes 12582920 | tf_op jit(solution)/shard_map/ppermute | solution.py:267
  95.7 49.6 %collective-permute-start.6 = (bf16[4096,512]{1,0:T(8,128)(2,1)}, bf16[4096,512]{1,0:T(8,128)(2,1)}, u32[]{:S(2)}, u32[]{:S(2)}) collective-permute-start(bf16[4096,512]{1,0:T(8,128)(2,1)} %bitcast.3.args_0_), channel_id=1, source_target_pairs={{32,96},{96,32},{160,224},{224,160},{288,352},{352,288},{416,480},... | collective-permute-start | bytes 12582920 | tf_op jit(solution)/shard_map/ppermute | solution.py:245
  98.4 12.7 %all-to-all-start.3 = ((bf16[8,32,512]{2,1,0:T(8,128)(2,1)}), bf16[8,32,512]{2,1,0:T(8,128)(2,1)S(1)}, u32[]{:S(2)}, u32[]{:S(2)}) async-start(bf16[8,32,512]{2,1,0:T(8,128)(2,1)} %get-tuple-element.81), calls=%async_computation.3 | async-start | bytes 524288 | tf_op jit(solution)/shard_map/all_to_all | solution.py:57
  111.1 0.7 copy-start.11
  111.8 17.2 %copy-start.3 = (bf16[8,2,4,64,512]{4,3,2,1,0:T(8,128)(2,1)S(1)}, bf16[8,2,4,64,512]{4,3,2,1,0:T(8,128)(2,1)}, u32[]{:S(2)}) copy-start(bf16[8,2,4,64,512]{4,3,2,1,0:T(8,128)(2,1)} %copy.54) | copy-start | bytes 12582916
  145.2 15.7 %collective-permute-start.7 = (bf16[4096,512]{1,0:T(8,128)(2,1)}, bf16[4096,512]{1,0:T(8,128)(2,1)}, u32[]{:S(2)}, u32[]{:S(2)}) collective-permute-start(bf16[4096,512]{1,0:T(8,128)(2,1)} %collective-permute-done.6.args_4_), channel_id=1, source_target_pairs={{32,0},{96,64},{160,128},{224,192},{288,256},{352,320},{416,384},{... | collective-permute-start | bytes 12582920 | tf_op jit(solution)/shard_map/ppermute | solution.py:271
  229.5 3.0 collective-permute-start.8
  232.5 18.0 %copy-start.14 = (bf16[32,512]{1,0:T(8,128)(2,1)}, bf16[32,512]{1,0:T(8,128)(2,1)S(1)}, u32[]{:S(2)}) copy-start(bf16[32,512]{1,0:T(8,128)(2,1)S(1)} %collective-permute-done.8.args_7_) | copy-start | bytes 98308
  233.2 14.0 %all-to-all-start.10 = ((bf16[8,32,512]{2,1,0:T(8,128)(2,1)}), bf16[8,32,512]{2,1,0:T(8,128)(2,1)S(1)}, u32[]{:S(2)}, u32[]{:S(2)}) async-start(bf16[8,32,512]{2,1,0:T(8,128)(2,1)} %broadcast_in_dim.134), calls=%async_computation.10 | async-start | bytes 524288 | tf_op jit(solution)/shard_map/all_to_all | solution.py:57
  247.2 2.2 copy-start.4
  263.1 17.3 %copy-start.5 = (bf16[8,2,4,64,512]{4,3,2,1,0:T(8,128)(2,1)S(1)}, bf16[8,2,4,64,512]{4,3,2,1,0:T(8,128)(2,1)}, u32[]{:S(2)}) copy-start(bf16[8,2,4,64,512]{4,3,2,1,0:T(8,128)(2,1)} %copy.54) | copy-start | bytes 12582916
  358.5 5.8 collective-permute-start.9
  364.3 16.7 %copy-start.16 = (bf16[32,512]{1,0:T(8,128)(2,1)}, bf16[32,512]{1,0:T(8,128)(2,1)S(1)}, u32[]{:S(2)}) copy-start(bf16[32,512]{1,0:T(8,128)(2,1)S(1)} %collective-permute-done.9.args_7_) | copy-start | bytes 98308
  365.0 12.7 %all-to-all-start.18 = ((bf16[8,32,512]{2,1,0:T(8,128)(2,1)}), bf16[8,32,512]{2,1,0:T(8,128)(2,1)S(1)}, u32[]{:S(2)}, u32[]{:S(2)}) async-start(bf16[8,32,512]{2,1,0:T(8,128)(2,1)} %broadcast_in_dim.135), calls=%async_computation.18 | async-start | bytes 524288 | tf_op jit(solution)/shard_map/all_to_all | solution.py:57
  377.7 2.2 copy-start.6
  393.4 17.2 %copy-start.7 = (bf16[8,2,4,64,512]{4,3,2,1,0:T(8,128)(2,1)S(1)}, bf16[8,2,4,64,512]{4,3,2,1,0:T(8,128)(2,1)}, u32[]{:S(2)}) copy-start(bf16[8,2,4,64,512]{4,3,2,1,0:T(8,128)(2,1)} %copy.54) | copy-start | bytes 12582916
  495.5 8.2 %collective-permute-start.10 = (bf16[32,512]{1,0:T(8,128)(2,1)}, bf16[32,512]{1,0:T(8,128)(2,1)S(1)}, u32[]{:S(2)}, u32[]{:S(2)}) collective-permute-start(bf16[32,512]{1,0:T(8,128)(2,1)} %get-tuple-element.138), channel_id=1, source_target_pairs={{0,128},{32,160},{64,192},{96,224},{128,256},{160,288},{192,320},{... | collective-permute-start | bytes 98312 | tf_op jit(solution)/shard_map/ppermute | solution.py:275
  503.6 16.7 %copy-start.15 = (bf16[32,512]{1,0:T(8,128)(2,1)}, bf16[32,512]{1,0:T(8,128)(2,1)S(1)}, u32[]{:S(2)}) copy-start(bf16[32,512]{1,0:T(8,128)(2,1)S(1)} %collective-permute-done.10.args_7_) | copy-start | bytes 98308
  504.4 12.7 %all-to-all-start.26 = ((bf16[8,32,512]{2,1,0:T(8,128)(2,1)}), bf16[8,32,512]{2,1,0:T(8,128)(2,1)S(1)}, u32[]{:S(2)}, u32[]{:S(2)}) async-start(bf16[8,32,512]{2,1,0:T(8,128)(2,1)} %broadcast_in_dim.136), calls=%async_computation.26 | async-start | bytes 524288 | tf_op jit(solution)/shard_map/all_to_all | solution.py:57
  517.0 2.2 copy-start.8
  532.8 17.2 %copy-start.9 = (bf16[8,2,4,64,512]{4,3,2,1,0:T(8,128)(2,1)S(1)}, bf16[8,2,4,64,512]{4,3,2,1,0:T(8,128)(2,1)}, u32[]{:S(2)}) copy-start(bf16[8,2,4,64,512]{4,3,2,1,0:T(8,128)(2,1)} %copy.54) | copy-start | bytes 12582916
  597.9 12.9 %all-to-all-start.32 = ((bf16[8,32,512]{2,1,0:T(8,128)(2,1)}), bf16[8,32,512]{2,1,0:T(8,128)(2,1)S(1)}, u32[]{:S(2)}, u32[]{:S(2)}) async-start(bf16[8,32,512]{2,1,0:T(8,128)(2,1)} %get-tuple-element.152), calls=%async_computation.32 | async-start | bytes 524288 | tf_op jit(solution)/shard_map/all_to_all | solution.py:57
  610.8 2.2 copy-start.10
  617.2 39.4 %all-to-all-start.33 = ((bf16[4,1536,128]{2,1,0:T(8,128)(2,1)}), bf16[4,1536,128]{2,1,0:T(8,128)(2,1)S(1)}, u32[]{:S(2)}, u32[]{:S(2)}) async-start(bf16[4,1536,128]{2,1,0:T(8,128)(2,1)} %pad_maximum_fusion), calls=%async_computation.33 | async-start | bytes 3145728 | tf_op jit(solution)/shard_map/all_to_all | solution.py:57
  622.5 33.5 %collective-permute-start.12 = (f32[8,128]{1,0:T(8,128)S(1)}, f32[8,128]{1,0:T(8,128)S(1)}, u32[]{:S(2)}, u32[]{:S(2)}) collective-permute-start(f32[8,128]{1,0:T(8,128)S(1)} %broadcast_in_dim.142), channel_id=1, source_target_pairs={{0,32},{32,0},{64,96},{96,64},{128,160},{160,128},{192,224},{224,1... | collective-permute-start | bytes 12296 | tf_op jit(solution)/shard_map/ppermute | solution.py:65
  658.0 15.5 %all-to-all-start.34 = ((f32[32,8,128]{2,1,0:T(8,128)}), f32[32,8,128]{2,1,0:T(8,128)S(1)}, u32[]{:S(2)}, u32[]{:S(2)}) async-start(f32[32,8,128]{2,1,0:T(8,128)} %broadcast_in_dim.143), calls=%async_computation.34 | async-start | bytes 262144 | tf_op jit(solution)/shard_map/all_to_all | solution.py:57
  662.9 16.1 %collective-permute-start.11 = (bf16[8,64,512]{2,1,0:T(8,128)(2,1)S(1)}, bf16[8,64,512]{2,1,0:T(8,128)(2,1)S(1)}, u32[]{:S(2)}, u32[]{:S(2)}) collective-permute-start(bf16[8,64,512]{2,1,0:T(8,128)(2,1)S(1)} %get-tuple-element.158), channel_id=1, source_target_pairs={{0,32},{32,0},{64,96},{96,64},{128,160},{160,128},{192,224},{224,1... | collective-permute-start | bytes 1572872 | tf_op jit(solution)/shard_map/ppermute | solution.py:65
  679.0 23.8 %copy-start.1 = (bf16[4,32,512]{2,1,0:T(8,128)(2,1)S(1)}, bf16[4,32,512]{2,1,0:T(8,128)(2,1)}, u32[]{:S(2)}) copy-start(bf16[4,32,512]{2,1,0:T(8,128)(2,1)} %param.5) | copy-start | bytes 393220

commit v6 on v5

--- a/solution.py
+++ b/solution.py
@@ -89,7 +89,7 @@
                 pltpu.make_async_copy(source.at[rows], into.at[rows], sems.at[index]).start()
 
 
-def project_kernel(layer, place_ref, *args):
+def project_from_kernel(layer, place_ref, *args):
     refs, (quant_ref, stream_ref, copies_ref, out_ref, weight_ref, sems) = args[:6], args[6:]
     start_load(layer, place_ref, refs, weight_ref, sems)
     count, tok_rows, part = quant_ref.shape
@@ -104,10 +104,10 @@
         copies_ref[k] = stream
 
 
-def project(layer, place, sources, quant_rows, stream):
+def project_from(layer, place, sources, quant_rows, stream):
     own = sources[0]
     return pl.pallas_call(
-        functools.partial(project_kernel, layer),
+        functools.partial(project_from_kernel, layer),
         out_shape=[
             jax.ShapeDtypeStruct(quant_rows.shape, jnp.bfloat16),
             jax.ShapeDtypeStruct(stream.shape, jnp.bfloat16),
@@ -118,9 +118,35 @@
             pltpu.VMEM(own.shape, own.dtype),
             pltpu.SemaphoreType.DMA((quant_rows.shape[0],)),
         ],
-        compiler_params=pltpu.CompilerParams(vmem_limit_bytes=56 * 1024 * 1024),
+        compiler_params=PARAMS,
+        name="project_from",
+    )(place, *sources, quant_rows, stream)
+
+
+def project_kernel(quant_ref, weight_ref, stream_ref, copies_ref, out_ref):
+    count, tok_rows, part = quant_ref.shape
+    total = stream_ref[...].astype(jnp.float32)
+    for k in range(count):
+        rows = pl.ds(k * part, part)
+        total = total + jnp.dot(quant_ref[k], weight_ref[rows], preferred_element_type=jnp.float32)
+    stream = total.astype(jnp.bfloat16)
+    out_ref[...] = stream
+    for k in range(count):
+        copies_ref[k] = stream
+
+
+def project(quant_rows, weight, stream):
+    return pl.pallas_call(
+        project_kernel,
+        out_shape=[
+            jax.ShapeDtypeStruct(quant_rows.shape, jnp.bfloat16),
+            jax.ShapeDtypeStruct(stream.shape, jnp.bfloat16),
+        ],
+        in_specs=[VMEM] * 3,
+        out_specs=[VMEM] * 2,
+        compiler_params=PARAMS,
         name="project",
-    )(place, *sources, quant_rows, stream)
+    )(quant_rows, weight, stream)
 
 
 def rotate_kernel(layer, last, keep_ref, rows_ref, gain_ref, rot_ref, scale_ref, _, __, *rest):
@@ -239,6 +265,7 @@
     along_z = lax.all_to_all(
         copies_of(rotation, planes), "section", 0, 0, axis_index_groups=same_core, tiled=True
     )
+    along_z, gains, scales = lax.optimization_barrier((along_z, gains, scales))
     along_x = gather(along_z, "dp")
     other_rows = crossed(along_x, 1)
     own_later, _ = lax.optimization_barrier((own, other_rows))
@@ -252,12 +279,22 @@
     stream = lax.dynamic_index_in_dim(hidden_in, place, 0, keepdims=False)
     copies = copies_of(stream, tensor)
     kept = (jnp.zeros((all_rows, D), jnp.bfloat16), jnp.zeros((all_rows, part_cols), jnp.float32))
+    weights = []
     for stage in range(stages):
         keep = jnp.full((1,), 1, jnp.int32) if stage == 0 else (stage_pos == stage).astype(jnp.int32)[None]
         for layer in range(STAGE):
             last = stage == stages - 1 and layer == STAGE - 1
             gain, scale = gains[layer : layer + 1], scales[layer : layer + 1]
-            results = rotate(layer, last, keep, exchange(copies, "tp"), gain, rot_cols, scale, kept)
+            rows = exchange(copies, "tp")
+            if stage == 0 and layer > 0 or stage == 1 and layer == 0:
+                done = (layer - 1) % STAGE
+                mine, other = sources[4:] if done % 2 else sources[2:4]
+                weight = jnp.where(core == done % 2, mine, other)
+                near = jnp.where(core == done % 2, own, by1)
+                weight = jnp.where(place // 2 == done // 2, near, weight)
+                rows, weight = lax.optimization_barrier((rows, weight))
+                weights.append(weight)
+            results = rotate(layer, last, keep, rows, gain, rot_cols, scale, kept)
             kept = results[:2]
             if last:
                 break
@@ -270,7 +307,11 @@
                 odd_mine, _ = lax.optimization_barrier((odd_mine, quant))
                 odd_other = lax.ppermute(odd_mine, "section", [(i + 1, i) for i in range(0, sections, 2)])
                 sources = (own, by1, even_mine, even_other, odd_mine, odd_other)
-            copies, stream = project(layer, where, sources, exchange(quant, "tp"), stream)
+            quant_rows = exchange(quant, "tp")
+            if stage == 0:
+                copies, stream = project_from(layer, where, sources, quant_rows, stream)
+            else:
+                copies, stream = project(quant_rows, weights[layer], stream)
         if stage < stages - 1:
             stream = lax.ppermute(
                 stream, "section", [(i, i + STAGE) for i in range(sections - STAGE)]
@@ -288,11 +329,21 @@
     grad_rot = (error_part * (slope - 1.0)).astype(jnp.bfloat16)
     grad_rot = grad_rot.reshape(all_rows, part_cols // lanes, lanes).transpose(1, 0, 2)
     sent = jnp.concatenate([turned, copies_of(grad_rot.reshape(-1, lanes), replicas)], axis=1)
-    parts = exchange(sent, "dp")
+    dp_pos = lax.axis_index("dp")
+
+    def block(step):
+        return lax.dynamic_index_in_dim(sent, lax.rem(dp_pos + step, replicas), 0, keepdims=False)
+
+    parts = jnp.stack(
+        [block(0)]
+        + [
+            lax.ppermute(block(k), "dp", [(i, (i + k) % replicas) for i in range(replicas)])
+            for k in range(1, replicas)
+        ]
+    )
     mine, other = terms_of(core, parts, planes, row_block, part_cols)
     loss = jnp.full((8, 128), jnp.sum(error_part * error_part), jnp.float32)
     loss = loss + crossed(loss, 1)
-    loss, _ = lax.optimization_barrier((loss, other))
     losses = exchange(copies_of(loss, replicas * tensor), ("dp", "tp"))
     loss = jnp.sum(losses[:, 0, 0])
 

time: 715 us -> 671 us (0.938)
  blocking collectives: 372 us -> 305 us
  Pallas kernels: 82.4 us -> 43.4 us
  waiting for transfers between devices: 95.3 us -> 134 us
  other arithmetic: 9.43 us -> 25.4 us
  starting transfers between devices: 116 us -> 124 us
    all_to_all x25 -> x22, blocking collectives: 324 us -> 277 us  [exchange(): return lax.all_to_all(copies, axis, 0, 0, tiled=True)]
    pallas_call x15, Pallas kernels: 63.1 us -> 23.4 us  [the longest x4 12 us: project_from(): pl.pallas_call(functools.partial(project_from_kernel, layer), out_shape=[...]
    all_to_all x1 -> x0, blocking collectives: 26.7 us -> none  [local(): lax.all_to_all(copies_of(rotation, planes), 'section', 0, 0, axis_index_g...]
    all_to_all x9 -> x11, waiting for transfers between devices: 75.4 us -> 96.9 us  [exchange(): return lax.all_to_all(copies, axis, 0, 0, tiled=True)]
    all_to_all x0 -> x1, waiting for transfers between devices: none -> 17 us  [local(): lax.all_to_all(copies_of(rotation, planes), 'section', 0, 0, axis_index_g...]
    select_n x0 -> x2, other arithmetic: none -> 14.1 us  [local(): weight = jnp.where(place // 2 == done // 2, near, weight)]
    ppermute x0 -> x3, starting transfers between devices: none -> 7.4 us  [local(): lax.ppermute(block(k), 'dp', [(i, (i + k) % replicas) for i in range(repl...]
    all_to_all x9 -> x11, starting transfers between devices: 38.3 us -> 43.9 us  [exchange(): return lax.all_to_all(copies, axis, 0, 0, tiled=True)]
  transfers between devices with their start and end apart: 22 -> 28, of which waited for: 12 -> 18; matrix products, arithmetic and copies ran while one was open for 1% -> 4% of each run, Pallas kernels for 1% -> 1%
where the time goes in v6:
time: 671 us; the launch traced here: 665 us
  blocking collectives  305 us (45%)
  waiting for transfers between devices  134 us (20%)
  starting transfers between devices  124 us (18%)
  Pallas kernels  43.4 us (6%)
  local copies, waits for them, and re-layouts  26.6 us (4%)
  other arithmetic  25.4 us (4%)
  between operations  6.88 us (1%)
    all_to_all x22, blocking collectives, exchange(): return lax.all_to_all(copies, axis, 0, 0, tiled=True)  277 us
    all_to_all x11, waiting for transfers between devices, exchange(): return lax.all_to_all(copies, axis, 0, 0, tiled=True)  96.9 us
    ppermute x6, starting transfers between devices, crossed(): lax.ppermute(value, 'section', [(i, i ^ mask) for i in range(lax.axis_siz...  47.6 us
    all_to_all x11, starting transfers between devices, exchange(): return lax.all_to_all(copies, axis, 0, 0, tiled=True)  43.9 us
    all_to_all x1, blocking collectives, local(): lax.all_to_all(sent, 'section', 0, 0, axis_index_groups=same_core, tiled=...  28 us
    pallas_call x16, Pallas kernels, rotate(): pl.pallas_call(functools.partial(rotate_kernel, layer, last), out_shape=s...  19.3 us
    all_to_all x1, waiting for transfers between devices, local(): lax.all_to_all(copies_of(rotation, planes), 'section', 0, 0, axis_index_g...  17 us
    unnamed x48, local copies, waits for them, and re-layouts  15.4 us
  transfers between devices with their start and end apart: 28, of which 18 were waited for; matrix products, arithmetic and copies ran while one was open for 4% of the time, Pallas kernels for 1%

profile of v6, /device:TPU:1, one launch (start us, length us, event | category | flops | bytes accessed | tf_op | source)
XLA Modules:
  0.0 665.2 jit_solution(7607945115178618627)
XLA Ops:
  2.2 8.8 %collective-permute-start.2 = (f32[1,4608]{1,0:T(1,128)S(1)}, f32[1,4608]{1,0:T(1,128)S(1)}, u32[]{:S(2)}, u32[]{:S(2)}) collective-permute-start(f32[1,4608]{1,0:T(1,128)S(1)} %pad_maximum_fusion.5), channel_id=1, source_target_pairs={{0,32},{32,0},{64,96},{96,64},{128,160},{160,128},{192,224},{224,1... | collective-permute-start | bytes 55304 | tf_op jit(solution)/shard_map/ppermute | solution.py:65
  16.1 5.8 all-to-all-start.1
  23.0 17.0 %all-to-all-done.1 = bf16[8,64,512]{2,1,0:T(8,128)(2,1)S(1)} async-done(((bf16[8,64,512]{2,1,0:T(8,128)(2,1)}), bf16[8,64,512]{2,1,0:T(8,128)(2,1)S(1)}, u32[]{:S(2)}, u32[]{:S(2)}) %all-to-all-start.1) | async-done | bytes 524320 | tf_op jit(solution)/shard_map/all_to_all | solution.py:265
  41.5 4.5 all-to-all-start.2
  46.0 2.6 collective-permute-start.1
  48.6 23.4 %all-to-all-done.2 = bf16[4,8,64,512]{3,2,1,0:T(8,128)(2,1)} async-done(((bf16[4,8,64,512]{3,2,1,0:T(8,128)(2,1)}), bf16[4,8,64,512]{3,2,1,0:T(8,128)(2,1)}, u32[]{:S(2)}, u32[]{:S(2)}) %all-to-all-start.2) | async-done | bytes 2097184 | tf_op jit(solution)/shard_map/all_to_all | solution.py:57
  72.0 3.2 collective-permute-start.4
  77.9 6.8 %all-to-all-start = ((bf16[8,32,512]{2,1,0:T(8,128)(2,1)}), bf16[8,32,512]{2,1,0:T(8,128)(2,1)S(1)}, u32[]{:S(2)}, u32[]{:S(2)}) async-start(bf16[8,32,512]{2,1,0:T(8,128)(2,1)} %broadcast_in_dim.127), calls=%async_computation | async-start | bytes 524288 | tf_op jit(solution)/shard_map/all_to_all | solution.py:57
  84.8 2.5 select_bitcast_fusion.1
  87.7 2.5 copy.54
  90.3 5.2 all-to-all-done.rows_ref
  102.9 3.4 all-to-all-start.3
  106.4 9.2 %all-to-all-done.3.args_6_ = bf16[8,32,512]{2,1,0:T(8,128)(2,1)S(1)} async-done(((bf16[8,32,512]{2,1,0:T(8,128)(2,1)}), bf16[8,32,512]{2,1,0:T(8,128)(2,1)S(1)}, u32[]{:S(2)}, u32[]{:S(2)}) %all-to-all-start.3) | async-done | bytes 262176 | tf_op jit(solution)/shard_map/all_to_all | solution.py:57
  115.6 3.2 project_from.4
  118.8 3.4 all-to-all-start.4
  122.2 8.0 %broadcast_select_fusion.1 = (bf16[4096,512]{1,0:T(8,128)(2,1)}, bf16[4096,512]{1,0:T(8,128)(2,1)}) fusion(pred[]{:T(512)S(6)} %eq.61, bf16[4096,512]{1,0:T(8,128)(2,1)} %collective-permute-done.args_1_, pred[]{:T(512)S(6)} %eq.58, bf16[4096,512]{1,0:T(8,128)(2,1)} %collective-permute-done.1.args_2_.args_4_, ...), kind=kLoop, calls=%fused_computation.2 | loop fusion | flops 8388608 | bytes 25165828 | tf_op jit(solution)/shard_map/jit(_where)/select_n | solution.py:294
  135.6 15.2 %collective-permute-done.6.args_4_ = bf16[4096,512]{1,0:T(8,128)(2,1)} collective-permute-done((bf16[4096,512]{1,0:T(8,128)(2,1)}, bf16[4096,512]{1,0:T(8,128)(2,1)}, u32[]{:S(2)}, u32[]{:S(2)}) %collective-permute-start.6) | collective-permute-done | bytes 4194336 | tf_op jit(solution)/shard_map/ppermute | solution.py:272
  150.8 3.2 collective-permute-start.7
  154.0 3.4 all-to-all-start.5
  157.4 9.2 %all-to-all-done.5.args_6_ = bf16[8,32,512]{2,1,0:T(8,128)(2,1)S(1)} async-done(((bf16[8,32,512]{2,1,0:T(8,128)(2,1)}), bf16[8,32,512]{2,1,0:T(8,128)(2,1)S(1)}, u32[]{:S(2)}, u32[]{:S(2)}) %all-to-all-start.5) | async-done | bytes 262176 | tf_op jit(solution)/shard_map/all_to_all | solution.py:57
  166.7 3.2 project_from.5
  169.8 3.4 all-to-all-start.6
  173.3 6.0 broadcast_select_fusion
  179.3 3.2 all-to-all-done.6.rows_ref
  185.9 12.5 %all_to_all.175.args_6_ = bf16[8,32,512]{2,1,0:T(8,128)(2,1)S(1)} all-to-all(bf16[8,32,512]{2,1,0:T(8,128)(2,1)S(1)} %get-tuple-element.108), channel_id=1, replica_groups=mesh['section'=16,'dp'=4,'tp'=8] {'tp'}, dimensions={0} | all-to-all | bytes 524288 | tf_op jit(solution)/shard_map/all_to_all | solution.py:57
  198.4 2.6 project_from.6
  201.0 11.8 %all_to_all.176.rows_ref = bf16[8,32,512]{2,1,0:T(8,128)(2,1)S(1)} all-to-all(bf16[8,32,512]{2,1,0:T(8,128)(2,1)S(1)} %get-tuple-element.110), channel_id=1, replica_groups=mesh['section'=16,'dp'=4,'tp'=8] {'tp'}, dimensions={0} | all-to-all | bytes 524288 | tf_op jit(solution)/shard_map/all_to_all | solution.py:57
  213.9 13.0 %all_to_all.177.args_6_ = bf16[8,32,512]{2,1,0:T(8,128)(2,1)S(1)} all-to-all(bf16[8,32,512]{2,1,0:T(8,128)(2,1)S(1)} %get-tuple-element.114), channel_id=1, replica_groups=mesh['section'=16,'dp'=4,'tp'=8] {'tp'}, dimensions={0} | all-to-all | bytes 524288 | tf_op jit(solution)/shard_map/all_to_all | solution.py:57
  227.0 3.2 project_from.7
  233.2 3.4 all-to-all-start.10
  236.6 12.1 %all-to-all-done.10.rows_ref = bf16[8,32,512]{2,1,0:T(8,128)(2,1)S(1)} async-done(((bf16[8,32,512]{2,1,0:T(8,128)(2,1)}), bf16[8,32,512]{2,1,0:T(8,128)(2,1)S(1)}, u32[]{:S(2)}, u32[]{:S(2)}) %all-to-all-start.10) | async-done | bytes 262176 | tf_op jit(solution)/shard_map/all_to_all | solution.py:57
  252.0 14.9 %all_to_all.178.quant_ref = bf16[8,32,512]{2,1,0:T(8,128)(2,1)S(1)} all-to-all(bf16[8,32,512]{2,1,0:T(8,128)(2,1)S(1)} %get-tuple-element.120), channel_id=1, replica_groups=mesh['section'=16,'dp'=4,'tp'=8] {'tp'}, dimensions={0} | all-to-all | bytes 524288 | tf_op jit(solution)/shard_map/all_to_all | solution.py:57
  267.7 14.6 %all_to_all.179.rows_ref = bf16[8,32,512]{2,1,0:T(8,128)(2,1)S(1)} all-to-all(bf16[8,32,512]{2,1,0:T(8,128)(2,1)S(1)} %get-tuple-element.122), channel_id=1, replica_groups=mesh['section'=16,'dp'=4,'tp'=8] {'tp'}, dimensions={0} | all-to-all | bytes 524288 | tf_op jit(solution)/shard_map/all_to_all | solution.py:57
  283.5 13.5 %all_to_all.180.quant_ref = bf16[8,32,512]{2,1,0:T(8,128)(2,1)S(1)} all-to-all(bf16[8,32,512]{2,1,0:T(8,128)(2,1)S(1)} %get-tuple-element.125), channel_id=1, replica_groups=mesh['section'=16,'dp'=4,'tp'=8] {'tp'}, dimensions={0} | all-to-all | bytes 524288 | tf_op jit(solution)/shard_map/all_to_all | solution.py:57
  297.8 11.6 %all_to_all.181.rows_ref = bf16[8,32,512]{2,1,0:T(8,128)(2,1)S(1)} all-to-all(bf16[8,32,512]{2,1,0:T(8,128)(2,1)S(1)} %get-tuple-element.128), channel_id=1, replica_groups=mesh['section'=16,'dp'=4,'tp'=8] {'tp'}, dimensions={0} | all-to-all | bytes 524288 | tf_op jit(solution)/shard_map/all_to_all | solution.py:57
  310.5 12.2 %all_to_all.182.quant_ref = bf16[8,32,512]{2,1,0:T(8,128)(2,1)S(1)} all-to-all(bf16[8,32,512]{2,1,0:T(8,128)(2,1)S(1)} %get-tuple-element.131), channel_id=1, replica_groups=mesh['section'=16,'dp'=4,'tp'=8] {'tp'}, dimensions={0} | all-to-all | bytes 524288 | tf_op jit(solution)/shard_map/all_to_all | solution.py:57
  323.6 11.8 %all_to_all.183.rows_ref = bf16[8,32,512]{2,1,0:T(8,128)(2,1)S(1)} all-to-all(bf16[8,32,512]{2,1,0:T(8,128)(2,1)S(1)} %get-tuple-element.134), channel_id=1, replica_groups=mesh['section'=16,'dp'=4,'tp'=8] {'tp'}, dimensions={0} | all-to-all | bytes 524288 | tf_op jit(solution)/shard_map/all_to_all | solution.py:57
  336.5 11.9 %all_to_all.184.quant_ref = bf16[8,32,512]{2,1,0:T(8,128)(2,1)S(1)} all-to-all(bf16[8,32,512]{2,1,0:T(8,128)(2,1)S(1)} %get-tuple-element.137), channel_id=1, replica_groups=mesh['section'=16,'dp'=4,'tp'=8] {'tp'}, dimensions={0} | all-to-all | bytes 524288 | tf_op jit(solution)/shard_map/all_to_all | solution.py:57
  349.9 4.6 collective-permute-start.9
  356.3 3.4 all-to-all-start.18
  359.7 9.2 %all-to-all-done.18.rows_ref = bf16[8,32,512]{2,1,0:T(8,128)(2,1)S(1)} async-done(((bf16[8,32,512]{2,1,0:T(8,128)(2,1)}), bf16[8,32,512]{2,1,0:T(8,128)(2,1)S(1)}, u32[]{:S(2)}, u32[]{:S(2)}) %all-to-all-start.18) | async-done | bytes 262176 | tf_op jit(solution)/shard_map/all_to_all | solution.py:57
  372.3 11.9 %all_to_all.185.quant_ref = bf16[8,32,512]{2,1,0:T(8,128)(2,1)S(1)} all-to-all(bf16[8,32,512]{2,1,0:T(8,128)(2,1)S(1)} %get-tuple-element.143), channel_id=1, replica_groups=mesh['section'=16,'dp'=4,'tp'=8] {'tp'}, dimensions={0} | all-to-all | bytes 524288 | tf_op jit(solution)/shard_map/all_to_all | solution.py:57
  385.0 11.9 %all_to_all.186.rows_ref = bf16[8,32,512]{2,1,0:T(8,128)(2,1)S(1)} all-to-all(bf16[8,32,512]{2,1,0:T(8,128)(2,1)S(1)} %get-tuple-element.144), channel_id=1, replica_groups=mesh['section'=16,'dp'=4,'tp'=8] {'tp'}, dimensions={0} | all-to-all | bytes 524288 | tf_op jit(solution)/shard_map/all_to_all | solution.py:57
  398.0 12.1 %all_to_all.187.quant_ref = bf16[8,32,512]{2,1,0:T(8,128)(2,1)S(1)} all-to-all(bf16[8,32,512]{2,1,0:T(8,128)(2,1)S(1)} %get-tuple-element.147), channel_id=1, replica_groups=mesh['section'=16,'dp'=4,'tp'=8] {'tp'}, dimensions={0} | all-to-all | bytes 524288 | tf_op jit(solution)/shard_map/all_to_all | solution.py:57
  410.9 13.6 %all_to_all.188.rows_ref = bf16[8,32,512]{2,1,0:T(8,128)(2,1)S(1)} all-to-all(bf16[8,32,512]{2,1,0:T(8,128)(2,1)S(1)} %get-tuple-element.149), channel_id=1, replica_groups=mesh['section'=16,'dp'=4,'tp'=8] {'tp'}, dimensions={0} | all-to-all | bytes 524288 | tf_op jit(solution)/shard_map/all_to_all | solution.py:57
  425.7 14.9 %all_to_all.189.quant_ref = bf16[8,32,512]{2,1,0:T(8,128)(2,1)S(1)} all-to-all(bf16[8,32,512]{2,1,0:T(8,128)(2,1)S(1)} %get-tuple-element.152), channel_id=1, replica_groups=mesh['section'=16,'dp'=4,'tp'=8] {'tp'}, dimensions={0} | all-to-all | bytes 524288 | tf_op jit(solution)/shard_map/all_to_all | solution.py:57
  441.4 13.1 %all_to_all.190.rows_ref = bf16[8,32,512]{2,1,0:T(8,128)(2,1)S(1)} all-to-all(bf16[8,32,512]{2,1,0:T(8,128)(2,1)S(1)} %get-tuple-element.154), channel_id=1, replica_groups=mesh['section'=16,'dp'=4,'tp'=8] {'tp'}, dimensions={0} | all-to-all | bytes 524288 | tf_op jit(solution)/shard_map/all_to_all | solution.py:57
  455.6 12.2 %all_to_all.191.quant_ref = bf16[8,32,512]{2,1,0:T(8,128)(2,1)S(1)} all-to-all(bf16[8,32,512]{2,1,0:T(8,128)(2,1)S(1)} %get-tuple-element.157), channel_id=1, replica_groups=mesh['section'=16,'dp'=4,'tp'=8] {'tp'}, dimensions={0} | all-to-all | bytes 524288 | tf_op jit(solution)/shard_map/all_to_all | solution.py:57
  469.4 4.6 collective-permute-start.10
  475.8 3.4 all-to-all-start.26
  479.2 9.2 %all-to-all-done.26.rows_ref = bf16[8,32,512]{2,1,0:T(8,128)(2,1)S(1)} async-done(((bf16[8,32,512]{2,1,0:T(8,128)(2,1)}), bf16[8,32,512]{2,1,0:T(8,128)(2,1)S(1)}, u32[]{:S(2)}, u32[]{:S(2)}) %all-to-all-start.26) | async-done | bytes 262176 | tf_op jit(solution)/shard_map/all_to_all | solution.py:57
  491.7 12.0 %all_to_all.192.quant_ref = bf16[8,32,512]{2,1,0:T(8,128)(2,1)S(1)} all-to-all(bf16[8,32,512]{2,1,0:T(8,128)(2,1)S(1)} %get-tuple-element.162), channel_id=1, replica_groups=mesh['section'=16,'dp'=4,'tp'=8] {'tp'}, dimensions={0} | all-to-all | bytes 524288 | tf_op jit(solution)/shard_map/all_to_all | solution.py:57
  504.6 11.9 %all_to_all.193.rows_ref = bf16[8,32,512]{2,1,0:T(8,128)(2,1)S(1)} all-to-all(bf16[8,32,512]{2,1,0:T(8,128)(2,1)S(1)} %get-tuple-element.163), channel_id=1, replica_groups=mesh['section'=16,'dp'=4,'tp'=8] {'tp'}, dimensions={0} | all-to-all | bytes 524288 | tf_op jit(solution)/shard_map/all_to_all | solution.py:57
  517.5 11.9 %all_to_all.194.quant_ref = bf16[8,32,512]{2,1,0:T(8,128)(2,1)S(1)} all-to-all(bf16[8,32,512]{2,1,0:T(8,128)(2,1)S(1)} %get-tuple-element.166), channel_id=1, replica_groups=mesh['section'=16,'dp'=4,'tp'=8] {'tp'}, dimensions={0} | all-to-all | bytes 524288 | tf_op jit(solution)/shard_map/all_to_all | solution.py:57
  530.3 11.7 %all_to_all.195.rows_ref = bf16[8,32,512]{2,1,0:T(8,128)(2,1)S(1)} all-to-all(bf16[8,32,512]{2,1,0:T(8,128)(2,1)S(1)} %get-tuple-element.168), channel_id=1, replica_groups=mesh['section'=16,'dp'=4,'tp'=8] {'tp'}, dimensions={0} | all-to-all | bytes 524288 | tf_op jit(solution)/shard_map/all_to_all | solution.py:57
  543.1 11.9 %all_to_all.196.quant_ref = bf16[8,32,512]{2,1,0:T(8,128)(2,1)S(1)} all-to-all(bf16[8,32,512]{2,1,0:T(8,128)(2,1)S(1)} %get-tuple-element.171), channel_id=1, replica_groups=mesh['section'=16,'dp'=4,'tp'=8] {'tp'}, dimensions={0} | all-to-all | bytes 524288 | tf_op jit(solution)/shard_map/all_to_all | solution.py:57
  556.5 3.4 all-to-all-start.32
  560.0 9.2 %all-to-all-done.32.rows_ref = bf16[8,32,512]{2,1,0:T(8,128)(2,1)S(1)} async-done(((bf16[8,32,512]{2,1,0:T(8,128)(2,1)}), bf16[8,32,512]{2,1,0:T(8,128)(2,1)S(1)}, u32[]{:S(2)}, u32[]{:S(2)}) %all-to-all-start.32) | async-done | bytes 262176 | tf_op jit(solution)/shard_map/all_to_all | solution.py:57
  576.3 3.6 collective-permute-start.12
  582.5 29.2 %collective-permute-start.15 = (f32[8,128]{1,0:T(8,128)S(1)}, f32[8,128]{1,0:T(8,128)S(1)}, u32[]{:S(2)}, u32[]{:S(2)}) collective-permute-start(f32[8,128]{1,0:T(8,128)S(1)} %broadcast_in_dim.142), channel_id=1, source_target_pairs={{0,32},{32,0},{64,96},{96,64},{128,160},{160,128},{192,224},{224,1... | collective-permute-start | bytes 12296 | tf_op jit(solution)/shard_map/ppermute | solution.py:65
  613.8 5.3 all-to-all-start.33
  620.1 2.5 collective-permute-start.14
  622.6 5.6 all-to-all-done.33
  634.1 28.0 %all_to_all.197 = bf16[8,80,512]{2,1,0:T(8,128)(2,1)S(1)} all-to-all(bf16[8,80,512]{2,1,0:T(8,128)(2,1)S(1)} %pad_maximum_fusion.1), channel_id=1, replica_groups={{0,64,128,192,256,320,384,448},{32,96,160,224,288,352,416,480},{1,65,12..., dimensions={0} | all-to-all | bytes 1310720 | tf_op jit(solution)/shard_map/all_to_all | solution.py:358
  (141 shorter events, 82.4 us)
Async XLA Ops:
  0.6 76.6 %copy-start = (bf16[4,32,512]{2,1,0:T(8,128)(2,1)S(1)}, bf16[4,32,512]{2,1,0:T(8,128)(2,1)}, u32[]{:S(2)}) copy-start(bf16[4,32,512]{2,1,0:T(8,128)(2,1)} %param.5) | copy-start | bytes 393220
  2.2 9.6 %collective-permute-start.2 = (f32[1,4608]{1,0:T(1,128)S(1)}, f32[1,4608]{1,0:T(1,128)S(1)}, u32[]{:S(2)}, u32[]{:S(2)}) collective-permute-start(f32[1,4608]{1,0:T(1,128)S(1)} %pad_maximum_fusion.5), channel_id=1, source_target_pairs={{0,32},{32,0},{64,96},{96,64},{128,160},{160,128},{192,224},{224,1... | collective-permute-start | bytes 55304 | tf_op jit(solution)/shard_map/ppermute | solution.py:65
  12.5 9.5 %collective-permute-start.3 = (f32[2,4608]{1,0:T(2,128)S(1)}, f32[2,4608]{1,0:T(2,128)S(1)}, u32[]{:S(2)}, u32[]{:S(2)}) collective-permute-start(f32[2,4608]{1,0:T(2,128)S(1)} %pad_maximum_fusion.4), channel_id=1, source_target_pairs={{0,64},{32,96},{64,0},{96,32},{128,192},{160,224},{192,128},{224,1... | collective-permute-start | bytes 110600 | tf_op jit(solution)/shard_map/ppermute | solution.py:65
  16.1 23.8 %all-to-all-start.1 = ((bf16[8,64,512]{2,1,0:T(8,128)(2,1)}), bf16[8,64,512]{2,1,0:T(8,128)(2,1)S(1)}, u32[]{:S(2)}, u32[]{:S(2)}) async-start(bf16[8,64,512]{2,1,0:T(8,128)(2,1)} %broadcast_in_dim.128), calls=%async_computation.1 | async-start | bytes 1048576 | tf_op jit(solution)/shard_map/all_to_all | solution.py:265
  41.5 30.5 %all-to-all-start.2 = ((bf16[4,8,64,512]{3,2,1,0:T(8,128)(2,1)}), bf16[4,8,64,512]{3,2,1,0:T(8,128)(2,1)}, u32[]{:S(2)}, u32[]{:S(2)}) async-start(bf16[4,8,64,512]{3,2,1,0:T(8,128)(2,1)} %broadcast_in_dim.131), calls=%async_computation.2 | async-start | bytes 4194304 | tf_op jit(solution)/shard_map/all_to_all | solution.py:57
  46.0 53.7 %collective-permute-start.1 = (bf16[4096,512]{1,0:T(8,128)(2,1)}, bf16[4096,512]{1,0:T(8,128)(2,1)}, u32[]{:S(2)}, u32[]{:S(2)}) collective-permute-start(bf16[4096,512]{1,0:T(8,128)(2,1)} %bitcast.5.args_0_), channel_id=1, source_target_pairs={{0,64},{64,0},{128,192},{192,128},{256,320},{320,256},{384,448},{4... | collective-permute-start | bytes 12582920 | tf_op jit(solution)/shard_map/ppermute | solution.py:255
  72.0 12.8 %collective-permute-start.4 = (bf16[4,8,64,512]{3,2,1,0:T(8,128)(2,1)}, bf16[4,8,64,512]{3,2,1,0:T(8,128)(2,1)}, u32[]{:S(2)}, u32[]{:S(2)}) collective-permute-start(bf16[4,8,64,512]{3,2,1,0:T(8,128)(2,1)} %all-to-all-done.2), channel_id=1, source_target_pairs={{0,32},{32,0},{64,96},{96,64},{128,160},{160,128},{192,224},{224,1... | collective-permute-start | bytes 6291464 | tf_op jit(solution)/shard_map/ppermute | solution.py:65
  75.2 31.1 %collective-permute-start = (bf16[4096,512]{1,0:T(8,128)(2,1)}, bf16[4096,512]{1,0:T(8,128)(2,1)}, u32[]{:S(2)}, u32[]{:S(2)}) collective-permute-start(bf16[4096,512]{1,0:T(8,128)(2,1)} %bitcast.5.args_0_), channel_id=1, source_target_pairs={{0,32},{32,0},{64,96},{96,64},{128,160},{160,128},{192,224},{224,1... | collective-permute-start | bytes 12582920 | tf_op jit(solution)/shard_map/ppermute | solution.py:65
  77.9 17.5 %all-to-all-start = ((bf16[8,32,512]{2,1,0:T(8,128)(2,1)}), bf16[8,32,512]{2,1,0:T(8,128)(2,1)S(1)}, u32[]{:S(2)}, u32[]{:S(2)}) async-start(bf16[8,32,512]{2,1,0:T(8,128)(2,1)} %broadcast_in_dim.127), calls=%async_computation | async-start | bytes 524288 | tf_op jit(solution)/shard_map/all_to_all | solution.py:57
  95.6 2.2 copy-start.2
  99.7 15.9 %collective-permute-start.5 = (bf16[4096,512]{1,0:T(8,128)(2,1)}, bf16[4096,512]{1,0:T(8,128)(2,1)}, u32[]{:S(2)}, u32[]{:S(2)}) collective-permute-start(bf16[4096,512]{1,0:T(8,128)(2,1)} %collective-permute-done.1.args_2_.args_4_), channel_id=1, source_target_pairs={{0,32},{64,96},{128,160},{192,224},{256,288},{320,352},{384,416},{... | collective-permute-start | bytes 12582920 | tf_op jit(solution)/shard_map/ppermute | solution.py:304
  101.0 49.8 %collective-permute-start.6 = (bf16[4096,512]{1,0:T(8,128)(2,1)}, bf16[4096,512]{1,0:T(8,128)(2,1)}, u32[]{:S(2)}, u32[]{:S(2)}) collective-permute-start(bf16[4096,512]{1,0:T(8,128)(2,1)} %bitcast.5.args_0_), channel_id=1, source_target_pairs={{32,96},{96,32},{160,224},{224,160},{288,352},{352,288},{416,480},... | collective-permute-start | bytes 12582920 | tf_op jit(solution)/shard_map/ppermute | solution.py:272
  102.9 12.7 %all-to-all-start.3 = ((bf16[8,32,512]{2,1,0:T(8,128)(2,1)}), bf16[8,32,512]{2,1,0:T(8,128)(2,1)S(1)}, u32[]{:S(2)}, u32[]{:S(2)}) async-start(bf16[8,32,512]{2,1,0:T(8,128)(2,1)} %get-tuple-element.94), calls=%async_computation.3 | async-start | bytes 524288 | tf_op jit(solution)/shard_map/all_to_all | solution.py:57
  118.8 12.7 %all-to-all-start.4 = ((bf16[8,32,512]{2,1,0:T(8,128)(2,1)}), bf16[8,32,512]{2,1,0:T(8,128)(2,1)S(1)}, u32[]{:S(2)}, u32[]{:S(2)}) async-start(bf16[8,32,512]{2,1,0:T(8,128)(2,1)} %get-tuple-element.97), calls=%async_computation.4 | async-start | bytes 524288 | tf_op jit(solution)/shard_map/all_to_all | solution.py:57
  131.5 2.2 copy-start.3
  150.8 15.9 %collective-permute-start.7 = (bf16[4096,512]{1,0:T(8,128)(2,1)}, bf16[4096,512]{1,0:T(8,128)(2,1)}, u32[]{:S(2)}, u32[]{:S(2)}) collective-permute-start(bf16[4096,512]{1,0:T(8,128)(2,1)} %collective-permute-done.6.args_4_), channel_id=1, source_target_pairs={{32,0},{96,64},{160,128},{224,192},{288,256},{352,320},{416,384},{... | collective-permute-start | bytes 12582920 | tf_op jit(solution)/shard_map/ppermute | solution.py:308
  154.0 12.7 %all-to-all-start.5 = ((bf16[8,32,512]{2,1,0:T(8,128)(2,1)}), bf16[8,32,512]{2,1,0:T(8,128)(2,1)S(1)}, u32[]{:S(2)}, u32[]{:S(2)}) async-start(bf16[8,32,512]{2,1,0:T(8,128)(2,1)} %get-tuple-element.101), calls=%async_computation.5 | async-start | bytes 524288 | tf_op jit(solution)/shard_map/all_to_all | solution.py:57
  169.8 12.7 %all-to-all-start.6 = ((bf16[8,32,512]{2,1,0:T(8,128)(2,1)}), bf16[8,32,512]{2,1,0:T(8,128)(2,1)S(1)}, u32[]{:S(2)}, u32[]{:S(2)}) async-start(bf16[8,32,512]{2,1,0:T(8,128)(2,1)} %get-tuple-element.104), calls=%async_computation.6 | async-start | bytes 524288 | tf_op jit(solution)/shard_map/all_to_all | solution.py:57
  182.5 2.2 copy-start.4
  198.4 14.4 %copy-start.5 = (bf16[8,2,4,64,512]{4,3,2,1,0:T(8,128)(2,1)S(1)}, bf16[8,2,4,64,512]{4,3,2,1,0:T(8,128)(2,1)}, u32[]{:S(2)}) copy-start(bf16[8,2,4,64,512]{4,3,2,1,0:T(8,128)(2,1)} %copy.54) | copy-start | bytes 12582916
  230.1 2.3 collective-permute-start.8
  233.2 15.5 %all-to-all-start.10 = ((bf16[8,32,512]{2,1,0:T(8,128)(2,1)}), bf16[8,32,512]{2,1,0:T(8,128)(2,1)S(1)}, u32[]{:S(2)}, u32[]{:S(2)}) async-start(bf16[8,32,512]{2,1,0:T(8,128)(2,1)} %broadcast_in_dim.134), calls=%async_computation.10 | async-start | bytes 524288 | tf_op jit(solution)/shard_map/all_to_all | solution.py:57
  248.7 2.2 copy-start.6
  250.9 16.0 %copy-start.16 = (bf16[4096,512]{1,0:T(8,128)(2,1)S(1)}, bf16[4096,512]{1,0:T(8,128)(2,1)}, u32[]{:S(2)}) copy-start(bf16[4096,512]{1,0:T(8,128)(2,1)} %get-tuple-element.121.weight_ref) | copy-start | bytes 12582916
  266.8 15.5 %copy-start.7 = (bf16[8,2,4,64,512]{4,3,2,1,0:T(8,128)(2,1)S(1)}, bf16[8,2,4,64,512]{4,3,2,1,0:T(8,128)(2,1)}, u32[]{:S(2)}) copy-start(bf16[8,2,4,64,512]{4,3,2,1,0:T(8,128)(2,1)} %copy.54) | copy-start | bytes 12582916
  282.3 14.6 %copy-start.19 = (bf16[4096,512]{1,0:T(8,128)(2,1)S(1)}, bf16[4096,512]{1,0:T(8,128)(2,1)}, u32[]{:S(2)}) copy-start(bf16[4096,512]{1,0:T(8,128)(2,1)} %get-tuple-element.126.weight_ref) | copy-start | bytes 12582916
  309.4 13.3 %copy-start.13 = (bf16[4096,512]{1,0:T(8,128)(2,1)S(1)}, bf16[4096,512]{1,0:T(8,128)(2,1)}, u32[]{:S(2)}) copy-start(bf16[4096,512]{1,0:T(8,128)(2,1)} %get-tuple-element.132.weight_ref) | copy-start | bytes 12582916
  335.4 13.0 %copy-start.22 = (bf16[4096,512]{1,0:T(8,128)(2,1)S(1)}, bf16[4096,512]{1,0:T(8,128)(2,1)}, u32[]{:S(2)}) copy-start(bf16[4096,512]{1,0:T(8,128)(2,1)} %get-tuple-element.138.weight_ref) | copy-start | bytes 12582916
  349.9 5.6 collective-permute-start.9
  356.3 12.7 %all-to-all-start.18 = ((bf16[8,32,512]{2,1,0:T(8,128)(2,1)}), bf16[8,32,512]{2,1,0:T(8,128)(2,1)S(1)}, u32[]{:S(2)}, u32[]{:S(2)}) async-start(bf16[8,32,512]{2,1,0:T(8,128)(2,1)} %broadcast_in_dim.135), calls=%async_computation.18 | async-start | bytes 524288 | tf_op jit(solution)/shard_map/all_to_all | solution.py:57
  369.0 2.2 copy-start.8
  371.1 13.0 %copy-start.17 = (bf16[4096,512]{1,0:T(8,128)(2,1)S(1)}, bf16[4096,512]{1,0:T(8,128)(2,1)}, u32[]{:S(2)}) copy-start(bf16[4096,512]{1,0:T(8,128)(2,1)} %get-tuple-element.121.weight_ref) | copy-start | bytes 12582916
  384.1 12.7 %copy-start.9 = (bf16[8,2,4,64,512]{4,3,2,1,0:T(8,128)(2,1)S(1)}, bf16[8,2,4,64,512]{4,3,2,1,0:T(8,128)(2,1)}, u32[]{:S(2)}) copy-start(bf16[8,2,4,64,512]{4,3,2,1,0:T(8,128)(2,1)} %copy.54) | copy-start | bytes 12582916
  396.8 13.3 %copy-start.20 = (bf16[4096,512]{1,0:T(8,128)(2,1)S(1)}, bf16[4096,512]{1,0:T(8,128)(2,1)}, u32[]{:S(2)}) copy-start(bf16[4096,512]{1,0:T(8,128)(2,1)} %get-tuple-element.126.weight_ref) | copy-start | bytes 12582916
  424.6 16.0 %copy-start.14 = (bf16[4096,512]{1,0:T(8,128)(2,1)S(1)}, bf16[4096,512]{1,0:T(8,128)(2,1)}, u32[]{:S(2)}) copy-start(bf16[4096,512]{1,0:T(8,128)(2,1)} %get-tuple-element.132.weight_ref) | copy-start | bytes 12582916
  454.5 13.3 %copy-start.23 = (bf16[4096,512]{1,0:T(8,128)(2,1)S(1)}, bf16[4096,512]{1,0:T(8,128)(2,1)}, u32[]{:S(2)}) copy-start(bf16[4096,512]{1,0:T(8,128)(2,1)} %get-tuple-element.138.weight_ref) | copy-start | bytes 12582916
  469.4 5.7 collective-permute-start.10
  475.8 12.7 %all-to-all-start.26 = ((bf16[8,32,512]{2,1,0:T(8,128)(2,1)}), bf16[8,32,512]{2,1,0:T(8,128)(2,1)S(1)}, u32[]{:S(2)}, u32[]{:S(2)}) async-start(bf16[8,32,512]{2,1,0:T(8,128)(2,1)} %broadcast_in_dim.136), calls=%async_computation.26 | async-start | bytes 524288 | tf_op jit(solution)/shard_map/all_to_all | solution.py:57
  488.4 2.2 copy-start.10
  490.6 13.1 %copy-start.18 = (bf16[4096,512]{1,0:T(8,128)(2,1)S(1)}, bf16[4096,512]{1,0:T(8,128)(2,1)}, u32[]{:S(2)}) copy-start(bf16[4096,512]{1,0:T(8,128)(2,1)} %get-tuple-element.121.weight_ref) | copy-start | bytes 12582916
  503.7 12.7 %copy-start.11 = (bf16[8,2,4,64,512]{4,3,2,1,0:T(8,128)(2,1)S(1)}, bf16[8,2,4,64,512]{4,3,2,1,0:T(8,128)(2,1)}, u32[]{:S(2)}) copy-start(bf16[8,2,4,64,512]{4,3,2,1,0:T(8,128)(2,1)} %copy.54) | copy-start | bytes 12582916
  516.4 13.0 %copy-start.21 = (bf16[4096,512]{1,0:T(8,128)(2,1)S(1)}, bf16[4096,512]{1,0:T(8,128)(2,1)}, u32[]{:S(2)}) copy-start(bf16[4096,512]{1,0:T(8,128)(2,1)} %get-tuple-element.126.weight_ref) | copy-start | bytes 12582916
  542.0 13.0 %copy-start.15 = (bf16[4096,512]{1,0:T(8,128)(2,1)S(1)}, bf16[4096,512]{1,0:T(8,128)(2,1)}, u32[]{:S(2)}) copy-start(bf16[4096,512]{1,0:T(8,128)(2,1)} %get-tuple-element.132.weight_ref) | copy-start | bytes 12582916
  556.5 12.7 %all-to-all-start.32 = ((bf16[8,32,512]{2,1,0:T(8,128)(2,1)}), bf16[8,32,512]{2,1,0:T(8,128)(2,1)S(1)}, u32[]{:S(2)}, u32[]{:S(2)}) async-start(bf16[8,32,512]{2,1,0:T(8,128)(2,1)} %get-tuple-element.173), calls=%async_computation.32 | async-start | bytes 524288 | tf_op jit(solution)/shard_map/all_to_all | solution.py:57
  569.2 2.2 copy-start.12
  574.4 44.7 %collective-permute-start.13 = (bf16[1536,128]{1,0:T(8,128)(2,1)S(1)}, bf16[1536,128]{1,0:T(8,128)(2,1)S(1)}, u32[]{:S(2)}, u32[]{:S(2)}) collective-permute-start(bf16[1536,128]{1,0:T(8,128)(2,1)S(1)} %get-tuple-element.189), channel_id=1, source_target_pairs={{0,24},{8,0},{16,8},{24,16},{1,25},{9,1},{17,9},{25,17},{2,26},{10... | collective-permute-start | bytes 1179656 | tf_op jit(solution)/shard_map/ppermute | solution.py:340
  576.3 42.8 %collective-permute-start.12 = (bf16[1536,128]{1,0:T(8,128)(2,1)S(1)}, bf16[1536,128]{1,0:T(8,128)(2,1)S(1)}, u32[]{:S(2)}, u32[]{:S(2)}) collective-permute-start(bf16[1536,128]{1,0:T(8,128)(2,1)S(1)} %get-tuple-element.188), channel_id=1, source_target_pairs={{0,16},{8,24},{16,0},{24,8},{1,17},{9,25},{17,1},{25,9},{2,18},{10... | collective-permute-start | bytes 1179656 | tf_op jit(solution)/shard_map/ppermute | solution.py:340
  579.9 39.2 %collective-permute-start.11 = (bf16[1536,128]{1,0:T(8,128)(2,1)S(1)}, bf16[1536,128]{1,0:T(8,128)(2,1)S(1)}, u32[]{:S(2)}, u32[]{:S(2)}) collective-permute-start(bf16[1536,128]{1,0:T(8,128)(2,1)S(1)} %get-tuple-element.187), channel_id=1, source_target_pairs={{0,8},{8,16},{16,24},{24,0},{1,9},{9,17},{17,25},{25,1},{2,10},{10... | collective-permute-start | bytes 1179656 | tf_op jit(solution)/shard_map/ppermute | solution.py:340
  582.5 30.0 %collective-permute-start.15 = (f32[8,128]{1,0:T(8,128)S(1)}, f32[8,128]{1,0:T(8,128)S(1)}, u32[]{:S(2)}, u32[]{:S(2)}) collective-permute-start(f32[8,128]{1,0:T(8,128)S(1)} %broadcast_in_dim.142), channel_id=1, source_target_pairs={{0,32},{32,0},{64,96},{96,64},{128,160},{160,128},{192,224},{224,1... | collective-permute-start | bytes 12296 | tf_op jit(solution)/shard_map/ppermute | solution.py:65
  613.8 14.4 %all-to-all-start.33 = ((f32[32,8,128]{2,1,0:T(8,128)}), f32[32,8,128]{2,1,0:T(8,128)S(1)}, u32[]{:S(2)}, u32[]{:S(2)}) async-start(f32[32,8,128]{2,1,0:T(8,128)} %broadcast_in_dim.143), calls=%async_computation.33 | async-start | bytes 262144 | tf_op jit(solution)/shard_map/all_to_all | solution.py:57
  620.1 13.8 %collective-permute-start.14 = (bf16[8,64,512]{2,1,0:T(8,128)(2,1)S(1)}, bf16[8,64,512]{2,1,0:T(8,128)(2,1)S(1)}, u32[]{:S(2)}, u32[]{:S(2)}) collective-permute-start(bf16[8,64,512]{2,1,0:T(8,128)(2,1)S(1)} %get-tuple-element.179), channel_id=1, source_target_pairs={{0,32},{32,0},{64,96},{96,64},{128,160},{160,128},{192,224},{224,1... | collective-permute-start | bytes 1572872 | tf_op jit(solution)/shard_map/ppermute | solution.py:65
  633.9 30.2 %copy-start.1 = (bf16[4,32,512]{2,1,0:T(8,128)(2,1)S(1)}, bf16[4,32,512]{2,1,0:T(8,128)(2,1)}, u32[]{:S(2)}) copy-start(bf16[4,32,512]{2,1,0:T(8,128)(2,1)} %param.5) | copy-start | bytes 393220

commit v7 on v6

--- a/solution.py
+++ b/solution.py
@@ -203,6 +203,22 @@
     )(keep, rows, gain, rot_cols, scale, *kept)
 
 
+def spread_kernel(stream_ref, copies_ref):
+    for k in range(copies_ref.shape[0]):
+        copies_ref[k] = stream_ref[...]
+
+
+def spread(stream, count):
+    return pl.pallas_call(
+        spread_kernel,
+        out_shape=jax.ShapeDtypeStruct((count,) + stream.shape, stream.dtype),
+        in_specs=[VMEM],
+        out_specs=VMEM,
+        compiler_params=PARAMS,
+        name="spread",
+    )(stream)
+
+
 def terms_kernel(part_rows, core_ref, parts_ref, mine_ref, other_ref):
     sources, rows, lanes = parts_ref.shape
     count, _, cols = mine_ref.shape
@@ -233,7 +249,7 @@
         out_specs=[VMEM, VMEM],
         compiler_params=pltpu.CompilerParams(vmem_limit_bytes=24 * 1024 * 1024),
         name="terms",
-    )(core[None].astype(jnp.int32), parts)
+    )(core, parts)
 
 
 def local(hidden_in, rotation, proj, norm_gain, quant_exp):
@@ -252,12 +268,13 @@
 
     own = proj[0]
     by1 = crossed(own, 1)
-    even_mine = lax.ppermute(own, "section", [(i, i ^ 2) for i in range(0, sections, 2)])
 
     scale_row = jnp.repeat(jnp.exp2(quant_exp.astype(jnp.float32) * 0.25) * 0.125, GROUP, axis=1)
     params = jnp.concatenate([norm_gain, scale_row], axis=1)
     params_by1 = crossed(params, 1)
     params_by2 = crossed(jnp.concatenate([params, params_by1], axis=0), 2)
+    own_now, _ = lax.optimization_barrier((own, params_by2))
+    even_mine = lax.ppermute(own_now, "section", [(i, i ^ 2) for i in range(0, sections, 2)])
     found = jnp.concatenate([params, params_by1, params_by2], axis=0)
     params = jnp.stack([lax.dynamic_index_in_dim(found, place ^ k, 0, False) for k in range(STAGE)])
     gains, scales = params[:, :D], params[:, D:]
@@ -265,7 +282,7 @@
     along_z = lax.all_to_all(
         copies_of(rotation, planes), "section", 0, 0, axis_index_groups=same_core, tiled=True
     )
-    along_z, gains, scales = lax.optimization_barrier((along_z, gains, scales))
+    along_z, by1 = lax.optimization_barrier((along_z, by1))
     along_x = gather(along_z, "dp")
     other_rows = crossed(along_x, 1)
     own_later, _ = lax.optimization_barrier((own, other_rows))
@@ -277,11 +294,17 @@
     where = place[None].astype(jnp.int32)
     all_rows = STAGE * tok_rows
     stream = lax.dynamic_index_in_dim(hidden_in, place, 0, keepdims=False)
-    copies = copies_of(stream, tensor)
+    copies = spread(stream, tensor)
     kept = (jnp.zeros((all_rows, D), jnp.bfloat16), jnp.zeros((all_rows, part_cols), jnp.float32))
     weights = []
+    keeps = [jnp.full((1,), 1, jnp.int32)]
+    keeps += [(stage_pos == stage).astype(jnp.int32)[None] for stage in range(1, stages)]
+    row_scales = jnp.repeat(scales, tok_rows, axis=0)
+    partners = [lax.rem(lax.axis_index("dp") + step, replicas) for step in range(replicas)]
+    which = core[None].astype(jnp.int32)
+    ahead = (keeps, row_scales, partners, which)
     for stage in range(stages):
-        keep = jnp.full((1,), 1, jnp.int32) if stage == 0 else (stage_pos == stage).astype(jnp.int32)[None]
+        keep = keeps[stage]
         for layer in range(STAGE):
             last = stage == stages - 1 and layer == STAGE - 1
             gain, scale = gains[layer : layer + 1], scales[layer : layer + 1]
@@ -292,7 +315,8 @@
                 weight = jnp.where(core == done % 2, mine, other)
                 near = jnp.where(core == done % 2, own, by1)
                 weight = jnp.where(place // 2 == done // 2, near, weight)
-                rows, weight = lax.optimization_barrier((rows, weight))
+                rows, weight, ahead = lax.optimization_barrier((rows, weight, ahead))
+                keeps, row_scales, partners, which = ahead
                 weights.append(weight)
             results = rotate(layer, last, keep, rows, gain, rot_cols, scale, kept)
             kept = results[:2]
@@ -316,23 +340,21 @@
             stream = lax.ppermute(
                 stream, "section", [(i, i + STAGE) for i in range(sections - STAGE)]
             )
-            copies = copies_of(stream, tensor)
+            copies = spread(stream, tensor)
     kept_normed, kept_rotated = kept
 
     lanes = all_rows
     turned = lax.optimization_barrier(kept_normed.T)
     turned = turned.reshape(sections, replicas, row_block, lanes).transpose(1, 0, 2, 3)
     turned = turned.reshape(replicas, sections * row_block, lanes)
-    row_scales = jnp.repeat(scales, tok_rows, axis=0)
     level, slope = level_and_slope(kept_rotated, row_scales)
     error_part = level - kept_rotated
     grad_rot = (error_part * (slope - 1.0)).astype(jnp.bfloat16)
     grad_rot = grad_rot.reshape(all_rows, part_cols // lanes, lanes).transpose(1, 0, 2)
     sent = jnp.concatenate([turned, copies_of(grad_rot.reshape(-1, lanes), replicas)], axis=1)
-    dp_pos = lax.axis_index("dp")
 
     def block(step):
-        return lax.dynamic_index_in_dim(sent, lax.rem(dp_pos + step, replicas), 0, keepdims=False)
+        return lax.dynamic_index_in_dim(sent, partners[step], 0, keepdims=False)
 
     parts = jnp.stack(
         [block(0)]
@@ -341,19 +363,19 @@
             for k in range(1, replicas)
         ]
     )
-    mine, other = terms_of(core, parts, planes, row_block, part_cols)
+    mine, other = terms_of(which, parts, planes, row_block, part_cols)
     loss = jnp.full((8, 128), jnp.sum(error_part * error_part), jnp.float32)
+    loss = jnp.sum(exchange(copies_of(loss, replicas * tensor), ("dp", "tp")), axis=0)
     loss = loss + crossed(loss, 1)
-    losses = exchange(copies_of(loss, replicas * tensor), ("dp", "tp"))
-    loss = jnp.sum(losses[:, 0, 0])
-
-    pair_sum = (mine + crossed(other, 1).astype(jnp.float32)).astype(jnp.bfloat16)
+    loss = jnp.concatenate([loss, loss], axis=0)
     high = lax.reduce_precision(loss, 8, 7)
     middle = lax.reduce_precision(loss - high, 8, 7)
     low = loss - high - middle
-    lane = lax.broadcasted_iota(jnp.int32, (16, part_cols), 1)
+    lane = lax.broadcasted_iota(jnp.int32, loss.shape, 1)
     tail_rows = jnp.where(lane == 0, high, jnp.where(lane == 1, middle, jnp.where(lane == 2, low, 0.0)))
-    tail_rows = tail_rows.astype(jnp.bfloat16)
+    tail_rows = jnp.tile(tail_rows.astype(jnp.bfloat16), (1, part_cols // lanes))
+
+    pair_sum = (mine + crossed(other, 1).astype(jnp.float32)).astype(jnp.bfloat16)
     sent = jnp.concatenate([pair_sum, copies_of(tail_rows, planes)], axis=1)
     parts = lax.all_to_all(sent, "section", 0, 0, axis_index_groups=same_core, tiled=True)
     sums = jnp.sum(parts.astype(jnp.float32), axis=0)

time: 671 us -> 663 us (0.988)
  blocking collectives: 305 us -> 345 us
  waiting for transfers between devices: 134 us -> 95.1 us
  starting transfers between devices: 124 us -> 134 us
  local copies, waits for them, and re-layouts: 26.6 us -> 17.2 us
    all_to_all x22 -> x25, blocking collectives: 277 us -> 317 us  [exchange(): return lax.all_to_all(copies, axis, 0, 0, tiled=True)]
    all_to_all x11 -> x8, waiting for transfers between devices: 96.9 us -> 61 us  [exchange(): return lax.all_to_all(copies, axis, 0, 0, tiled=True)]
    ppermute x6, starting transfers between devices: 47.6 us -> 58.7 us  [crossed(): lax.ppermute(value, 'section', [(i, i ^ mask) for i in range(lax.axis_siz...]
    all_to_all x11 -> x8, starting transfers between devices: 43.9 us -> 34.6 us  [exchange(): return lax.all_to_all(copies, axis, 0, 0, tiled=True)]
    unnamed x48 -> x25, local copies, waits for them, and re-layouts: 15.4 us -> 8.79 us
  transfers between devices with their start and end apart: 28 -> 25, of which waited for: 18 -> 15; matrix products, arithmetic and copies ran while one was open for 4% -> 4% of each run, Pallas kernels for 1% -> 1%
where the time goes in v7:
time: 663 us; the launch traced here: 661 us
  blocking collectives  345 us (52%)
  starting transfers between devices  134 us (20%)
  waiting for transfers between devices  95.1 us (14%)
  Pallas kernels  44.1 us (7%)
  other arithmetic  21.3 us (3%)
  local copies, waits for them, and re-layouts  17.2 us (3%)
    all_to_all x25, blocking collectives, exchange(): return lax.all_to_all(copies, axis, 0, 0, tiled=True)  317 us
    all_to_all x8, waiting for transfers between devices, exchange(): return lax.all_to_all(copies, axis, 0, 0, tiled=True)  61 us
    ppermute x6, starting transfers between devices, crossed(): lax.ppermute(value, 'section', [(i, i ^ mask) for i in range(lax.axis_siz...  58.7 us
    all_to_all x8, starting transfers between devices, exchange(): return lax.all_to_all(copies, axis, 0, 0, tiled=True)  34.6 us
    all_to_all x1, blocking collectives, local(): lax.all_to_all(sent, 'section', 0, 0, axis_index_groups=same_core, tiled=...  28.4 us
    pallas_call x16, Pallas kernels, rotate(): pl.pallas_call(functools.partial(rotate_kernel, layer, last), out_shape=s...  19.3 us
    all_to_all x1, waiting for transfers between devices, local(): lax.all_to_all(copies_of(rotation, planes), 'section', 0, 0, axis_index_g...  14.3 us
    select_n x2, other arithmetic, local(): weight = jnp.where(place // 2 == done // 2, near, weight)  14 us
  transfers between devices with their start and end apart: 25, of which 15 were waited for; matrix products, arithmetic and copies ran while one was open for 4% of the time, Pallas kernels for 1%

profile of v7, /device:TPU:1, one launch (start us, length us, event | category | flops | bytes accessed | tf_op | source)
XLA Modules:
  0.0 660.5 jit_solution(15943697188751470292)
XLA Ops:
  0.6 8.9 %collective-permute-start = (bf16[4096,512]{1,0:T(8,128)(2,1)}, bf16[4096,512]{1,0:T(8,128)(2,1)}, u32[]{:S(2)}, u32[]{:S(2)}) collective-permute-start(bf16[4096,512]{1,0:T(8,128)(2,1)} %bitcast.1.args_0_), channel_id=1, source_target_pairs={{0,32},{32,0},{64,96},{96,64},{128,160},{160,128},{192,224},{224,1... | collective-permute-start | bytes 12582920 | tf_op jit(solution)/shard_map/ppermute | solution.py:65
  11.3 4.7 all-to-all-start
  19.6 14.3 %all-to-all-done = bf16[8,64,512]{2,1,0:T(8,128)(2,1)S(1)} async-done(((bf16[8,64,512]{2,1,0:T(8,128)(2,1)}), bf16[8,64,512]{2,1,0:T(8,128)(2,1)S(1)}, u32[]{:S(2)}, u32[]{:S(2)}) %all-to-all-start) | async-done | bytes 524320 | tf_op jit(solution)/shard_map/all_to_all | solution.py:282
  35.6 4.6 all-to-all-start.2
  42.2 3.2 collective-permute-done.2
  45.3 2.7 collective-permute-start.3
  48.1 18.1 %all-to-all-done.2 = bf16[4,8,64,512]{3,2,1,0:T(8,128)(2,1)} async-done(((bf16[4,8,64,512]{3,2,1,0:T(8,128)(2,1)}), bf16[4,8,64,512]{3,2,1,0:T(8,128)(2,1)}, u32[]{:S(2)}, u32[]{:S(2)}) %all-to-all-start.2) | async-done | bytes 2097184 | tf_op jit(solution)/shard_map/all_to_all | solution.py:57
  66.2 3.2 collective-permute-start.4
  70.2 6.8 %all-to-all-start.1 = ((bf16[8,32,512]{2,1,0:T(8,128)(2,1)}), bf16[8,32,512]{2,1,0:T(8,128)(2,1)S(1)}, u32[]{:S(2)}, u32[]{:S(2)}) async-start(bf16[8,32,512]{2,1,0:T(8,128)(2,1)} %spread.4), calls=%async_computation.1 | async-start | bytes 524288 | tf_op jit(solution)/shard_map/all_to_all | solution.py:57
  77.2 2.5 select_bitcast_fusion.1
  80.1 2.5 copy.50
  82.6 6.8 %all-to-all-done.1.rows_ref = bf16[8,32,512]{2,1,0:T(8,128)(2,1)S(1)} async-done(((bf16[8,32,512]{2,1,0:T(8,128)(2,1)}), bf16[8,32,512]{2,1,0:T(8,128)(2,1)S(1)}, u32[]{:S(2)}, u32[]{:S(2)}) %all-to-all-start.1) | async-done | bytes 262176 | tf_op jit(solution)/shard_map/all_to_all | solution.py:57
  96.9 3.4 all-to-all-start.3
  100.4 9.1 %all-to-all-done.3.args_6_ = bf16[8,32,512]{2,1,0:T(8,128)(2,1)S(1)} async-done(((bf16[8,32,512]{2,1,0:T(8,128)(2,1)}), bf16[8,32,512]{2,1,0:T(8,128)(2,1)S(1)}, u32[]{:S(2)}, u32[]{:S(2)}) %all-to-all-start.3) | async-done | bytes 262176 | tf_op jit(solution)/shard_map/all_to_all | solution.py:57
  109.6 3.1 project_from.4
  112.7 5.7 all-to-all-start.4
  118.4 8.0 %broadcast_select_fusion.1 = (bf16[4096,512]{1,0:T(8,128)(2,1)}, bf16[4096,512]{1,0:T(8,128)(2,1)}) fusion(pred[]{:T(512)S(6)} %eq.61, bf16[4096,512]{1,0:T(8,128)(2,1)} %collective-permute-done.args_1_, pred[]{:T(512)S(6)} %eq.55, bf16[4096,512]{1,0:T(8,128)(2,1)} %collective-permute-done.3.args_2_.args_4_, ...), kind=kLoop, calls=%fused_computation.2 | loop fusion | flops 8388608 | bytes 25165828 | tf_op jit(solution)/shard_map/jit(_where)/select_n | solution.py:317
  131.8 12.6 %collective-permute-done.6.args_4_ = bf16[4096,512]{1,0:T(8,128)(2,1)} collective-permute-done((bf16[4096,512]{1,0:T(8,128)(2,1)}, bf16[4096,512]{1,0:T(8,128)(2,1)}, u32[]{:S(2)}, u32[]{:S(2)}) %collective-permute-start.6) | collective-permute-done | bytes 4194336 | tf_op jit(solution)/shard_map/ppermute | solution.py:289
  144.5 4.3 collective-permute-start.7
  148.8 3.4 all-to-all-start.5
  152.2 9.8 %all-to-all-done.5.args_6_ = bf16[8,32,512]{2,1,0:T(8,128)(2,1)S(1)} async-done(((bf16[8,32,512]{2,1,0:T(8,128)(2,1)}), bf16[8,32,512]{2,1,0:T(8,128)(2,1)S(1)}, u32[]{:S(2)}, u32[]{:S(2)}) %all-to-all-start.5) | async-done | bytes 262176 | tf_op jit(solution)/shard_map/all_to_all | solution.py:57
  162.0 3.1 project_from.5
  165.2 3.4 all-to-all-start.6
  168.6 6.0 broadcast_select_fusion
  174.6 4.5 all-to-all-done.6.rows_ref
  182.5 14.8 %all_to_all.175.args_6_ = bf16[8,32,512]{2,1,0:T(8,128)(2,1)S(1)} all-to-all(bf16[8,32,512]{2,1,0:T(8,128)(2,1)S(1)} %get-tuple-element.152), channel_id=1, replica_groups=mesh['section'=16,'dp'=4,'tp'=8] {'tp'}, dimensions={0} | all-to-all | bytes 524288 | tf_op jit(solution)/shard_map/all_to_all | solution.py:57
  197.3 2.6 project_from.6
  199.9 14.7 %all_to_all.176.rows_ref = bf16[8,32,512]{2,1,0:T(8,128)(2,1)S(1)} all-to-all(bf16[8,32,512]{2,1,0:T(8,128)(2,1)S(1)} %get-tuple-element.154), channel_id=1, replica_groups=mesh['section'=16,'dp'=4,'tp'=8] {'tp'}, dimensions={0} | all-to-all | bytes 524288 | tf_op jit(solution)/shard_map/all_to_all | solution.py:57
  215.8 14.2 %all_to_all.177.args_6_ = bf16[8,32,512]{2,1,0:T(8,128)(2,1)S(1)} all-to-all(bf16[8,32,512]{2,1,0:T(8,128)(2,1)S(1)} %get-tuple-element.167), channel_id=1, replica_groups=mesh['section'=16,'dp'=4,'tp'=8] {'tp'}, dimensions={0} | all-to-all | bytes 524288 | tf_op jit(solution)/shard_map/all_to_all | solution.py:57
  230.0 3.1 project_from.7
  233.1 3.0 collective-permute-start.8
  237.2 11.6 %all_to_all.178.rows_ref = bf16[8,32,512]{2,1,0:T(8,128)(2,1)S(1)} all-to-all(bf16[8,32,512]{2,1,0:T(8,128)(2,1)S(1)} %spread.5), channel_id=1, replica_groups=mesh['section'=16,'dp'=4,'tp'=8] {'tp'}, dimensions={0} | all-to-all | bytes 524288 | tf_op jit(solution)/shard_map/all_to_all | solution.py:57
  249.9 12.7 %all_to_all.179.quant_ref = bf16[8,32,512]{2,1,0:T(8,128)(2,1)S(1)} all-to-all(bf16[8,32,512]{2,1,0:T(8,128)(2,1)S(1)} %get-tuple-element.185), channel_id=1, replica_groups=mesh['section'=16,'dp'=4,'tp'=8] {'tp'}, dimensions={0} | all-to-all | bytes 524288 | tf_op jit(solution)/shard_map/all_to_all | solution.py:57
  263.4 11.8 %all_to_all.180.rows_ref = bf16[8,32,512]{2,1,0:T(8,128)(2,1)S(1)} all-to-all(bf16[8,32,512]{2,1,0:T(8,128)(2,1)S(1)} %get-tuple-element.187), channel_id=1, replica_groups=mesh['section'=16,'dp'=4,'tp'=8] {'tp'}, dimensions={0} | all-to-all | bytes 524288 | tf_op jit(solution)/shard_map/all_to_all | solution.py:57
  276.3 11.9 %all_to_all.181.quant_ref = bf16[8,32,512]{2,1,0:T(8,128)(2,1)S(1)} all-to-all(bf16[8,32,512]{2,1,0:T(8,128)(2,1)S(1)} %get-tuple-element.190), channel_id=1, replica_groups=mesh['section'=16,'dp'=4,'tp'=8] {'tp'}, dimensions={0} | all-to-all | bytes 524288 | tf_op jit(solution)/shard_map/all_to_all | solution.py:57
  289.0 11.7 %all_to_all.182.rows_ref = bf16[8,32,512]{2,1,0:T(8,128)(2,1)S(1)} all-to-all(bf16[8,32,512]{2,1,0:T(8,128)(2,1)S(1)} %get-tuple-element.193), channel_id=1, replica_groups=mesh['section'=16,'dp'=4,'tp'=8] {'tp'}, dimensions={0} | all-to-all | bytes 524288 | tf_op jit(solution)/shard_map/all_to_all | solution.py:57
  301.8 11.9 %all_to_all.183.quant_ref = bf16[8,32,512]{2,1,0:T(8,128)(2,1)S(1)} all-to-all(bf16[8,32,512]{2,1,0:T(8,128)(2,1)S(1)} %get-tuple-element.196), channel_id=1, replica_groups=mesh['section'=16,'dp'=4,'tp'=8] {'tp'}, dimensions={0} | all-to-all | bytes 524288 | tf_op jit(solution)/shard_map/all_to_all | solution.py:57
  314.6 11.7 %all_to_all.184.rows_ref = bf16[8,32,512]{2,1,0:T(8,128)(2,1)S(1)} all-to-all(bf16[8,32,512]{2,1,0:T(8,128)(2,1)S(1)} %get-tuple-element.199), channel_id=1, replica_groups=mesh['section'=16,'dp'=4,'tp'=8] {'tp'}, dimensions={0} | all-to-all | bytes 524288 | tf_op jit(solution)/shard_map/all_to_all | solution.py:57
  327.4 11.9 %all_to_all.185.quant_ref = bf16[8,32,512]{2,1,0:T(8,128)(2,1)S(1)} all-to-all(bf16[8,32,512]{2,1,0:T(8,128)(2,1)S(1)} %get-tuple-element.202), channel_id=1, replica_groups=mesh['section'=16,'dp'=4,'tp'=8] {'tp'}, dimensions={0} | all-to-all | bytes 524288 | tf_op jit(solution)/shard_map/all_to_all | solution.py:57
  340.8 4.5 collective-permute-start.9
  346.4 11.7 %all_to_all.186.rows_ref = bf16[8,32,512]{2,1,0:T(8,128)(2,1)S(1)} all-to-all(bf16[8,32,512]{2,1,0:T(8,128)(2,1)S(1)} %spread.6), channel_id=1, replica_groups=mesh['section'=16,'dp'=4,'tp'=8] {'tp'}, dimensions={0} | all-to-all | bytes 524288 | tf_op jit(solution)/shard_map/all_to_all | solution.py:57
  359.2 14.8 %all_to_all.187.quant_ref = bf16[8,32,512]{2,1,0:T(8,128)(2,1)S(1)} all-to-all(bf16[8,32,512]{2,1,0:T(8,128)(2,1)S(1)} %get-tuple-element.208), channel_id=1, replica_groups=mesh['section'=16,'dp'=4,'tp'=8] {'tp'}, dimensions={0} | all-to-all | bytes 524288 | tf_op jit(solution)/shard_map/all_to_all | solution.py:57
  374.9 13.4 %all_to_all.188.rows_ref = bf16[8,32,512]{2,1,0:T(8,128)(2,1)S(1)} all-to-all(bf16[8,32,512]{2,1,0:T(8,128)(2,1)S(1)} %get-tuple-element.209), channel_id=1, replica_groups=mesh['section'=16,'dp'=4,'tp'=8] {'tp'}, dimensions={0} | all-to-all | bytes 524288 | tf_op jit(solution)/shard_map/all_to_all | solution.py:57
  389.4 12.2 %all_to_all.189.quant_ref = bf16[8,32,512]{2,1,0:T(8,128)(2,1)S(1)} all-to-all(bf16[8,32,512]{2,1,0:T(8,128)(2,1)S(1)} %get-tuple-element.212), channel_id=1, replica_groups=mesh['section'=16,'dp'=4,'tp'=8] {'tp'}, dimensions={0} | all-to-all | bytes 524288 | tf_op jit(solution)/shard_map/all_to_all | solution.py:57
  402.5 12.2 %all_to_all.190.rows_ref = bf16[8,32,512]{2,1,0:T(8,128)(2,1)S(1)} all-to-all(bf16[8,32,512]{2,1,0:T(8,128)(2,1)S(1)} %get-tuple-element.214), channel_id=1, replica_groups=mesh['section'=16,'dp'=4,'tp'=8] {'tp'}, dimensions={0} | all-to-all | bytes 524288 | tf_op jit(solution)/shard_map/all_to_all | solution.py:57
  415.8 11.9 %all_to_all.191.quant_ref = bf16[8,32,512]{2,1,0:T(8,128)(2,1)S(1)} all-to-all(bf16[8,32,512]{2,1,0:T(8,128)(2,1)S(1)} %get-tuple-element.217), channel_id=1, replica_groups=mesh['section'=16,'dp'=4,'tp'=8] {'tp'}, dimensions={0} | all-to-all | bytes 524288 | tf_op jit(solution)/shard_map/all_to_all | solution.py:57
  428.6 11.7 %all_to_all.192.rows_ref = bf16[8,32,512]{2,1,0:T(8,128)(2,1)S(1)} all-to-all(bf16[8,32,512]{2,1,0:T(8,128)(2,1)S(1)} %get-tuple-element.219), channel_id=1, replica_groups=mesh['section'=16,'dp'=4,'tp'=8] {'tp'}, dimensions={0} | all-to-all | bytes 524288 | tf_op jit(solution)/shard_map/all_to_all | solution.py:57
  441.4 11.7 %all_to_all.193.quant_ref = bf16[8,32,512]{2,1,0:T(8,128)(2,1)S(1)} all-to-all(bf16[8,32,512]{2,1,0:T(8,128)(2,1)S(1)} %get-tuple-element.222), channel_id=1, replica_groups=mesh['section'=16,'dp'=4,'tp'=8] {'tp'}, dimensions={0} | all-to-all | bytes 524288 | tf_op jit(solution)/shard_map/all_to_all | solution.py:57
  454.7 4.8 collective-permute-start.10
  460.6 13.6 %all_to_all.194.rows_ref = bf16[8,32,512]{2,1,0:T(8,128)(2,1)S(1)} all-to-all(bf16[8,32,512]{2,1,0:T(8,128)(2,1)S(1)} %spread.7), channel_id=1, replica_groups=mesh['section'=16,'dp'=4,'tp'=8] {'tp'}, dimensions={0} | all-to-all | bytes 524288 | tf_op jit(solution)/shard_map/all_to_all | solution.py:57
  475.3 11.7 %all_to_all.195.quant_ref = bf16[8,32,512]{2,1,0:T(8,128)(2,1)S(1)} all-to-all(bf16[8,32,512]{2,1,0:T(8,128)(2,1)S(1)} %get-tuple-element.227), channel_id=1, replica_groups=mesh['section'=16,'dp'=4,'tp'=8] {'tp'}, dimensions={0} | all-to-all | bytes 524288 | tf_op jit(solution)/shard_map/all_to_all | solution.py:57
  487.9 11.7 %all_to_all.196.rows_ref = bf16[8,32,512]{2,1,0:T(8,128)(2,1)S(1)} all-to-all(bf16[8,32,512]{2,1,0:T(8,128)(2,1)S(1)} %get-tuple-element.228), channel_id=1, replica_groups=mesh['section'=16,'dp'=4,'tp'=8] {'tp'}, dimensions={0} | all-to-all | bytes 524288 | tf_op jit(solution)/shard_map/all_to_all | solution.py:57
  500.7 12.5 %all_to_all.197.quant_ref = bf16[8,32,512]{2,1,0:T(8,128)(2,1)S(1)} all-to-all(bf16[8,32,512]{2,1,0:T(8,128)(2,1)S(1)} %get-tuple-element.231), channel_id=1, replica_groups=mesh['section'=16,'dp'=4,'tp'=8] {'tp'}, dimensions={0} | all-to-all | bytes 524288 | tf_op jit(solution)/shard_map/all_to_all | solution.py:57
  514.1 13.7 %all_to_all.198.rows_ref = bf16[8,32,512]{2,1,0:T(8,128)(2,1)S(1)} all-to-all(bf16[8,32,512]{2,1,0:T(8,128)(2,1)S(1)} %get-tuple-element.233), channel_id=1, replica_groups=mesh['section'=16,'dp'=4,'tp'=8] {'tp'}, dimensions={0} | all-to-all | bytes 524288 | tf_op jit(solution)/shard_map/all_to_all | solution.py:57
  528.8 14.8 %all_to_all.199.quant_ref = bf16[8,32,512]{2,1,0:T(8,128)(2,1)S(1)} all-to-all(bf16[8,32,512]{2,1,0:T(8,128)(2,1)S(1)} %get-tuple-element.236), channel_id=1, replica_groups=mesh['section'=16,'dp'=4,'tp'=8] {'tp'}, dimensions={0} | all-to-all | bytes 524288 | tf_op jit(solution)/shard_map/all_to_all | solution.py:57
  545.2 3.4 all-to-all-start.32
  548.7 11.3 %all-to-all-done.32.rows_ref = bf16[8,32,512]{2,1,0:T(8,128)(2,1)S(1)} async-done(((bf16[8,32,512]{2,1,0:T(8,128)(2,1)}), bf16[8,32,512]{2,1,0:T(8,128)(2,1)S(1)}, u32[]{:S(2)}, u32[]{:S(2)}) %all-to-all-start.32) | async-done | bytes 262176 | tf_op jit(solution)/shard_map/all_to_all | solution.py:57
  565.1 5.0 collective-permute-start.11
  570.1 4.9 collective-permute-start.12
  575.0 4.0 collective-permute-start.13
  580.3 3.9 all-to-all-start.33
  585.3 33.3 %collective-permute-start.14 = (bf16[8,64,512]{2,1,0:T(8,128)(2,1)S(1)}, bf16[8,64,512]{2,1,0:T(8,128)(2,1)S(1)}, u32[]{:S(2)}, u32[]{:S(2)}) collective-permute-start(bf16[8,64,512]{2,1,0:T(8,128)(2,1)S(1)} %get-tuple-element.249), channel_id=1, source_target_pairs={{0,32},{32,0},{64,96},{96,64},{128,160},{160,128},{192,224},{224,1... | collective-permute-start | bytes 1572872 | tf_op jit(solution)/shard_map/ppermute | solution.py:65
  618.7 9.1 %collective-permute-start.15 = (f32[8,128]{1,0:T(8,128)S(1)}, f32[8,128]{1,0:T(8,128)S(1)}, u32[]{:S(2)}, u32[]{:S(2)}) collective-permute-start(f32[8,128]{1,0:T(8,128)S(1)} %reduce_sum.37), channel_id=1, source_target_pairs={{0,32},{32,0},{64,96},{96,64},{128,160},{160,128},{192,224},{224,1... | collective-permute-start | bytes 12296 | tf_op jit(solution)/shard_map/ppermute | solution.py:65
  628.9 28.4 %all_to_all.200 = bf16[8,80,512]{2,1,0:T(8,128)(2,1)S(1)} all-to-all(bf16[8,80,512]{2,1,0:T(8,128)(2,1)S(1)} %pad_maximum_fusion.1), channel_id=1, replica_groups={{0,64,128,192,256,320,384,448},{32,96,160,224,288,352,416,480},{1,65,12..., dimensions={0} | all-to-all | bytes 1310720 | tf_op jit(solution)/shard_map/all_to_all | solution.py:380
  (114 shorter events, 64.2 us)
Async XLA Ops:
  0.6 68.8 %copy-start = (bf16[4,32,512]{2,1,0:T(8,128)(2,1)S(1)}, bf16[4,32,512]{2,1,0:T(8,128)(2,1)}, u32[]{:S(2)}) copy-start(bf16[4,32,512]{2,1,0:T(8,128)(2,1)} %param.5) | copy-start | bytes 393220
  0.6 33.3 %collective-permute-start = (bf16[4096,512]{1,0:T(8,128)(2,1)}, bf16[4096,512]{1,0:T(8,128)(2,1)}, u32[]{:S(2)}, u32[]{:S(2)}) collective-permute-start(bf16[4096,512]{1,0:T(8,128)(2,1)} %bitcast.1.args_0_), channel_id=1, source_target_pairs={{0,32},{32,0},{64,96},{96,64},{128,160},{160,128},{192,224},{224,1... | collective-permute-start | bytes 12582920 | tf_op jit(solution)/shard_map/ppermute | solution.py:65
  11.3 22.7 %all-to-all-start = ((bf16[8,64,512]{2,1,0:T(8,128)(2,1)}), bf16[8,64,512]{2,1,0:T(8,128)(2,1)S(1)}, u32[]{:S(2)}, u32[]{:S(2)}) async-start(bf16[8,64,512]{2,1,0:T(8,128)(2,1)} %broadcast_in_dim.75), calls=%async_computation | async-start | bytes 1048576 | tf_op jit(solution)/shard_map/all_to_all | solution.py:282
  17.4 22.8 %collective-permute-start.1 = (f32[1,4608]{1,0:T(1,128)S(1)}, f32[1,4608]{1,0:T(1,128)S(1)}, u32[]{:S(2)}, u32[]{:S(2)}) collective-permute-start(f32[1,4608]{1,0:T(1,128)S(1)} %pad_maximum_fusion.4), channel_id=1, source_target_pairs={{0,32},{32,0},{64,96},{96,64},{128,160},{160,128},{192,224},{224,1... | collective-permute-start | bytes 55304 | tf_op jit(solution)/shard_map/ppermute | solution.py:65
  35.6 4.6 copy-start.11
  35.6 30.6 %all-to-all-start.2 = ((bf16[4,8,64,512]{3,2,1,0:T(8,128)(2,1)}), bf16[4,8,64,512]{3,2,1,0:T(8,128)(2,1)}, u32[]{:S(2)}, u32[]{:S(2)}) async-start(bf16[4,8,64,512]{3,2,1,0:T(8,128)(2,1)} %broadcast_in_dim.78), calls=%async_computation.2 | async-start | bytes 4194304 | tf_op jit(solution)/shard_map/all_to_all | solution.py:57
  40.2 5.1 collective-permute-start.2
  45.3 48.2 %collective-permute-start.3 = (bf16[4096,512]{1,0:T(8,128)(2,1)}, bf16[4096,512]{1,0:T(8,128)(2,1)}, u32[]{:S(2)}, u32[]{:S(2)}) collective-permute-start(bf16[4096,512]{1,0:T(8,128)(2,1)} %bitcast.1.args_0_), channel_id=1, source_target_pairs={{0,64},{64,0},{128,192},{192,128},{256,320},{320,256},{384,448},{4... | collective-permute-start | bytes 12582920 | tf_op jit(solution)/shard_map/ppermute | solution.py:277
  66.2 11.0 %collective-permute-start.4 = (bf16[4,8,64,512]{3,2,1,0:T(8,128)(2,1)}, bf16[4,8,64,512]{3,2,1,0:T(8,128)(2,1)}, u32[]{:S(2)}, u32[]{:S(2)}) collective-permute-start(bf16[4,8,64,512]{3,2,1,0:T(8,128)(2,1)} %all-to-all-done.2), channel_id=1, source_target_pairs={{0,32},{32,0},{64,96},{96,64},{128,160},{160,128},{192,224},{224,1... | collective-permute-start | bytes 6291464 | tf_op jit(solution)/shard_map/ppermute | solution.py:65
  70.2 19.2 %all-to-all-start.1 = ((bf16[8,32,512]{2,1,0:T(8,128)(2,1)}), bf16[8,32,512]{2,1,0:T(8,128)(2,1)S(1)}, u32[]{:S(2)}, u32[]{:S(2)}) async-start(bf16[8,32,512]{2,1,0:T(8,128)(2,1)} %spread.4), calls=%async_computation.1 | async-start | bytes 524288 | tf_op jit(solution)/shard_map/all_to_all | solution.py:57
  89.5 2.2 copy-start.2
  93.6 16.0 %collective-permute-start.5 = (bf16[4096,512]{1,0:T(8,128)(2,1)}, bf16[4096,512]{1,0:T(8,128)(2,1)}, u32[]{:S(2)}, u32[]{:S(2)}) collective-permute-start(bf16[4096,512]{1,0:T(8,128)(2,1)} %collective-permute-done.3.args_2_.args_4_), channel_id=1, source_target_pairs={{0,32},{64,96},{128,160},{192,224},{256,288},{320,352},{384,416},{... | collective-permute-start | bytes 12582920 | tf_op jit(solution)/shard_map/ppermute | solution.py:328
  94.9 49.6 %collective-permute-start.6 = (bf16[4096,512]{1,0:T(8,128)(2,1)}, bf16[4096,512]{1,0:T(8,128)(2,1)}, u32[]{:S(2)}, u32[]{:S(2)}) collective-permute-start(bf16[4096,512]{1,0:T(8,128)(2,1)} %bitcast.1.args_0_), channel_id=1, source_target_pairs={{32,96},{96,32},{160,224},{224,160},{288,352},{352,288},{416,480},... | collective-permute-start | bytes 12582920 | tf_op jit(solution)/shard_map/ppermute | solution.py:289
  96.9 12.7 %all-to-all-start.3 = ((bf16[8,32,512]{2,1,0:T(8,128)(2,1)}), bf16[8,32,512]{2,1,0:T(8,128)(2,1)S(1)}, u32[]{:S(2)}, u32[]{:S(2)}) async-start(bf16[8,32,512]{2,1,0:T(8,128)(2,1)} %get-tuple-element.129), calls=%async_computation.3 | async-start | bytes 524288 | tf_op jit(solution)/shard_map/all_to_all | solution.py:57
  112.7 15.0 %all-to-all-start.4 = ((bf16[8,32,512]{2,1,0:T(8,128)(2,1)}), bf16[8,32,512]{2,1,0:T(8,128)(2,1)S(1)}, u32[]{:S(2)}, u32[]{:S(2)}) async-start(bf16[8,32,512]{2,1,0:T(8,128)(2,1)} %get-tuple-element.132), calls=%async_computation.4 | async-start | bytes 524288 | tf_op jit(solution)/shard_map/all_to_all | solution.py:57
  127.8 2.2 copy-start.3
  144.5 17.6 %collective-permute-start.7 = (bf16[4096,512]{1,0:T(8,128)(2,1)}, bf16[4096,512]{1,0:T(8,128)(2,1)}, u32[]{:S(2)}, u32[]{:S(2)}) collective-permute-start(bf16[4096,512]{1,0:T(8,128)(2,1)} %collective-permute-done.6.args_4_), channel_id=1, source_target_pairs={{32,0},{96,64},{160,128},{224,192},{288,256},{352,320},{416,384},{... | collective-permute-start | bytes 12582920 | tf_op jit(solution)/shard_map/ppermute | solution.py:332
  148.8 13.3 %all-to-all-start.5 = ((bf16[8,32,512]{2,1,0:T(8,128)(2,1)}), bf16[8,32,512]{2,1,0:T(8,128)(2,1)S(1)}, u32[]{:S(2)}, u32[]{:S(2)}) async-start(bf16[8,32,512]{2,1,0:T(8,128)(2,1)} %get-tuple-element.136), calls=%async_computation.5 | async-start | bytes 524288 | tf_op jit(solution)/shard_map/all_to_all | solution.py:57
  165.2 13.9 %all-to-all-start.6 = ((bf16[8,32,512]{2,1,0:T(8,128)(2,1)}), bf16[8,32,512]{2,1,0:T(8,128)(2,1)S(1)}, u32[]{:S(2)}, u32[]{:S(2)}) async-start(bf16[8,32,512]{2,1,0:T(8,128)(2,1)} %get-tuple-element.139), calls=%async_computation.6 | async-start | bytes 524288 | tf_op jit(solution)/shard_map/all_to_all | solution.py:57
  179.1 2.2 copy-start.4
  197.3 17.3 %copy-start.5 = (bf16[8,2,4,64,512]{4,3,2,1,0:T(8,128)(2,1)S(1)}, bf16[8,2,4,64,512]{4,3,2,1,0:T(8,128)(2,1)}, u32[]{:S(2)}) copy-start(bf16[8,2,4,64,512]{4,3,2,1,0:T(8,128)(2,1)} %copy.50) | copy-start | bytes 12582916
  233.1 4.0 collective-permute-start.8
  248.8 13.8 %copy-start.8 = (bf16[4096,512]{1,0:T(8,128)(2,1)S(1)}, bf16[4096,512]{1,0:T(8,128)(2,1)}, u32[]{:S(2)}) copy-start(bf16[4096,512]{1,0:T(8,128)(2,1)} %get-tuple-element.186.weight_ref) | copy-start | bytes 12582916
  275.2 13.0 %copy-start.9 = (bf16[4096,512]{1,0:T(8,128)(2,1)S(1)}, bf16[4096,512]{1,0:T(8,128)(2,1)}, u32[]{:S(2)}) copy-start(bf16[4096,512]{1,0:T(8,128)(2,1)} %get-tuple-element.191.weight_ref) | copy-start | bytes 12582916
  300.7 13.0 %copy-start.7 = (bf16[4096,512]{1,0:T(8,128)(2,1)S(1)}, bf16[4096,512]{1,0:T(8,128)(2,1)}, u32[]{:S(2)}) copy-start(bf16[4096,512]{1,0:T(8,128)(2,1)} %get-tuple-element.197.weight_ref) | copy-start | bytes 12582916
  326.3 13.0 %copy-start.10 = (bf16[4096,512]{1,0:T(8,128)(2,1)S(1)}, bf16[4096,512]{1,0:T(8,128)(2,1)}, u32[]{:S(2)}) copy-start(bf16[4096,512]{1,0:T(8,128)(2,1)} %get-tuple-element.203.weight_ref) | copy-start | bytes 12582916
  340.8 5.5 collective-permute-start.9
  454.7 5.8 collective-permute-start.10
  545.2 14.7 %all-to-all-start.32 = ((bf16[8,32,512]{2,1,0:T(8,128)(2,1)}), bf16[8,32,512]{2,1,0:T(8,128)(2,1)S(1)}, u32[]{:S(2)}, u32[]{:S(2)}) async-start(bf16[8,32,512]{2,1,0:T(8,128)(2,1)} %get-tuple-element.238), calls=%async_computation.32 | async-start | bytes 524288 | tf_op jit(solution)/shard_map/all_to_all | solution.py:57
  559.9 2.2 copy-start.6
  565.1 19.1 %collective-permute-start.11 = (bf16[1536,128]{1,0:T(8,128)(2,1)S(1)}, bf16[1536,128]{1,0:T(8,128)(2,1)S(1)}, u32[]{:S(2)}, u32[]{:S(2)}) collective-permute-start(bf16[1536,128]{1,0:T(8,128)(2,1)S(1)} %get-tuple-element.257), channel_id=1, source_target_pairs={{0,8},{8,16},{16,24},{24,0},{1,9},{9,17},{17,25},{25,1},{2,10},{10... | collective-permute-start | bytes 1179656 | tf_op jit(solution)/shard_map/ppermute | solution.py:362
  570.1 14.1 %collective-permute-start.12 = (bf16[1536,128]{1,0:T(8,128)(2,1)S(1)}, bf16[1536,128]{1,0:T(8,128)(2,1)S(1)}, u32[]{:S(2)}, u32[]{:S(2)}) collective-permute-start(bf16[1536,128]{1,0:T(8,128)(2,1)S(1)} %get-tuple-element.258), channel_id=1, source_target_pairs={{0,16},{8,24},{16,0},{24,8},{1,17},{9,25},{17,1},{25,9},{2,18},{10... | collective-permute-start | bytes 1179656 | tf_op jit(solution)/shard_map/ppermute | solution.py:362
  575.0 9.3 %collective-permute-start.13 = (bf16[1536,128]{1,0:T(8,128)(2,1)S(1)}, bf16[1536,128]{1,0:T(8,128)(2,1)S(1)}, u32[]{:S(2)}, u32[]{:S(2)}) collective-permute-start(bf16[1536,128]{1,0:T(8,128)(2,1)S(1)} %get-tuple-element.259), channel_id=1, source_target_pairs={{0,24},{8,0},{16,8},{24,16},{1,25},{9,1},{17,9},{25,17},{2,26},{10... | collective-permute-start | bytes 1179656 | tf_op jit(solution)/shard_map/ppermute | solution.py:362
  580.3 38.3 %all-to-all-start.33 = ((f32[32,8,128]{2,1,0:T(8,128)}), f32[32,8,128]{2,1,0:T(8,128)S(1)}, u32[]{:S(2)}, u32[]{:S(2)}) async-start(f32[32,8,128]{2,1,0:T(8,128)} %broadcast_in_dim_broadcast_in_dim_broadcast_in_dim.3), calls=%async_computation.33 | async-start | bytes 262144 | tf_op jit(solution)/shard_map/all_to_all | solution.py:57
  585.3 43.4 %collective-permute-start.14 = (bf16[8,64,512]{2,1,0:T(8,128)(2,1)S(1)}, bf16[8,64,512]{2,1,0:T(8,128)(2,1)S(1)}, u32[]{:S(2)}, u32[]{:S(2)}) collective-permute-start(bf16[8,64,512]{2,1,0:T(8,128)(2,1)S(1)} %get-tuple-element.249), channel_id=1, source_target_pairs={{0,32},{32,0},{64,96},{96,64},{128,160},{160,128},{192,224},{224,1... | collective-permute-start | bytes 1572872 | tf_op jit(solution)/shard_map/ppermute | solution.py:65
  618.7 10.0 %collective-permute-start.15 = (f32[8,128]{1,0:T(8,128)S(1)}, f32[8,128]{1,0:T(8,128)S(1)}, u32[]{:S(2)}, u32[]{:S(2)}) collective-permute-start(f32[8,128]{1,0:T(8,128)S(1)} %reduce_sum.37), channel_id=1, source_target_pairs={{0,32},{32,0},{64,96},{96,64},{128,160},{160,128},{192,224},{224,1... | collective-permute-start | bytes 12296 | tf_op jit(solution)/shard_map/ppermute | solution.py:65
  628.7 30.7 %copy-start.1 = (bf16[4,32,512]{2,1,0:T(8,128)(2,1)S(1)}, bf16[4,32,512]{2,1,0:T(8,128)(2,1)}, u32[]{:S(2)}) copy-start(bf16[4,32,512]{2,1,0:T(8,128)(2,1)} %param.5) | copy-start | bytes 393220

commit v8 on v7

--- a/solution.py
+++ b/solution.py
@@ -272,17 +272,18 @@
     scale_row = jnp.repeat(jnp.exp2(quant_exp.astype(jnp.float32) * 0.25) * 0.125, GROUP, axis=1)
     params = jnp.concatenate([norm_gain, scale_row], axis=1)
     params_by1 = crossed(params, 1)
-    params_by2 = crossed(jnp.concatenate([params, params_by1], axis=0), 2)
-    own_now, _ = lax.optimization_barrier((own, params_by2))
-    even_mine = lax.ppermute(own_now, "section", [(i, i ^ 2) for i in range(0, sections, 2)])
-    found = jnp.concatenate([params, params_by1, params_by2], axis=0)
-    params = jnp.stack([lax.dynamic_index_in_dim(found, place ^ k, 0, False) for k in range(STAGE)])
-    gains, scales = params[:, :D], params[:, D:]
-
+    params_by2 = crossed(params, 2)
     along_z = lax.all_to_all(
         copies_of(rotation, planes), "section", 0, 0, axis_index_groups=same_core, tiled=True
     )
-    along_z, by1 = lax.optimization_barrier((along_z, by1))
+    along_z, by1, params_by2 = lax.optimization_barrier((along_z, by1, params_by2))
+    params_by3 = crossed(params_by2, 1)
+    own_now, _ = lax.optimization_barrier((own, params_by2))
+    even_mine = lax.ppermute(own_now, "section", [(i, i ^ 2) for i in range(0, sections, 2)])
+    found = jnp.concatenate([params, params_by1, params_by2, params_by3], axis=0)
+    params = jnp.stack([lax.dynamic_index_in_dim(found, place ^ k, 0, False) for k in range(STAGE)])
+    gains, scales = params[:, :D], params[:, D:]
+
     along_x = gather(along_z, "dp")
     other_rows = crossed(along_x, 1)
     own_later, _ = lax.optimization_barrier((own, other_rows))
@@ -300,7 +301,8 @@
     keeps = [jnp.full((1,), 1, jnp.int32)]
     keeps += [(stage_pos == stage).astype(jnp.int32)[None] for stage in range(1, stages)]
     row_scales = jnp.repeat(scales, tok_rows, axis=0)
-    partners = [lax.rem(lax.axis_index("dp") + step, replicas) for step in range(replicas)]
+    dp_pos = lax.axis_index("dp").astype(jnp.uint32)
+    partners = [lax.rem(dp_pos + jnp.uint32(step), jnp.uint32(replicas)) for step in range(replicas)]
     which = core[None].astype(jnp.int32)
     ahead = (keeps, row_scales, partners, which)
     for stage in range(stages):
@@ -309,15 +311,15 @@
             last = stage == stages - 1 and layer == STAGE - 1
             gain, scale = gains[layer : layer + 1], scales[layer : layer + 1]
             rows = exchange(copies, "tp")
-            if stage == 0 and layer > 0 or stage == 1 and layer == 0:
-                done = (layer - 1) % STAGE
-                mine, other = sources[4:] if done % 2 else sources[2:4]
-                weight = jnp.where(core == done % 2, mine, other)
-                near = jnp.where(core == done % 2, own, by1)
-                weight = jnp.where(place // 2 == done // 2, near, weight)
-                rows, weight, ahead = lax.optimization_barrier((rows, weight, ahead))
+            if stage == 0 and layer in (1, 2):
+                odd = layer - 1
+                mine, other = sources[4:] if odd else sources[2:4]
+                far = jnp.where(core == odd, mine, other)
+                near = jnp.where(core == odd, own, by1)
+                pair = jnp.where(place // 2 == 0, near, far), jnp.where(place // 2 == 0, far, near)
+                rows, pair, ahead = lax.optimization_barrier((rows, pair, ahead))
+                weights.append(pair)
                 keeps, row_scales, partners, which = ahead
-                weights.append(weight)
             results = rotate(layer, last, keep, rows, gain, rot_cols, scale, kept)
             kept = results[:2]
             if last:
@@ -332,10 +334,10 @@
                 odd_other = lax.ppermute(odd_mine, "section", [(i + 1, i) for i in range(0, sections, 2)])
                 sources = (own, by1, even_mine, even_other, odd_mine, odd_other)
             quant_rows = exchange(quant, "tp")
-            if stage == 0:
+            if stage == 0 and layer < 2:
                 copies, stream = project_from(layer, where, sources, quant_rows, stream)
             else:
-                copies, stream = project(quant_rows, weights[layer], stream)
+                copies, stream = project(quant_rows, weights[layer % 2][layer // 2], stream)
         if stage < stages - 1:
             stream = lax.ppermute(
                 stream, "section", [(i, i + STAGE) for i in range(sections - STAGE)]

time: 663 us -> 644 us (0.971)
  starting transfers between devices: 134 us -> 120 us
  blocking collectives: 345 us -> 353 us
  waiting for transfers between devices: 95.1 us -> 87.4 us
    all_to_all x1, waiting for transfers between devices: 14.3 us -> 4.59 us  [local(): lax.all_to_all(copies_of(rotation, planes), 'section', 0, 0, axis_index_g...]
    all_to_all x25 -> x26, blocking collectives: 317 us -> 326 us  [exchange(): return lax.all_to_all(copies, axis, 0, 0, tiled=True)]
    all_to_all x8 -> x7, waiting for transfers between devices: 61 us -> 52.7 us  [exchange(): return lax.all_to_all(copies, axis, 0, 0, tiled=True)]
    all_to_all x8 -> x7, starting transfers between devices: 34.6 us -> 30 us  [exchange(): return lax.all_to_all(copies, axis, 0, 0, tiled=True)]
    pallas_call x11 -> x13, Pallas kernels: 11.3 us -> 13.6 us  [project(): pl.pallas_call(project_kernel, out_shape=[jax.ShapeDtypeStruct(quant_rows...]
    ppermute x6 -> x7, starting transfers between devices: 58.7 us -> 56.8 us  [crossed(): lax.ppermute(value, 'section', [(i, i ^ mask) for i in range(lax.axis_siz...]
  transfers between devices with their start and end apart: 25 -> 25, of which waited for: 15 -> 14; matrix products, arithmetic and copies ran while one was open for 4% -> 4% of each run, Pallas kernels for 1% -> 1%
where the time goes in v8:
time: 644 us; the launch traced here: 642 us
  blocking collectives  353 us (55%)
  starting transfers between devices  120 us (19%)
  waiting for transfers between devices  87.4 us (14%)
  Pallas kernels  40.7 us (6%)
  other arithmetic  21.5 us (3%)
  local copies, waits for them, and re-layouts  15.1 us (2%)
    all_to_all x26, blocking collectives, exchange(): return lax.all_to_all(copies, axis, 0, 0, tiled=True)  326 us
    ppermute x7, starting transfers between devices, crossed(): lax.ppermute(value, 'section', [(i, i ^ mask) for i in range(lax.axis_siz...  56.8 us
    all_to_all x7, waiting for transfers between devices, exchange(): return lax.all_to_all(copies, axis, 0, 0, tiled=True)  52.7 us
    all_to_all x7, starting transfers between devices, exchange(): return lax.all_to_all(copies, axis, 0, 0, tiled=True)  30 us
    all_to_all x1, blocking collectives, local(): lax.all_to_all(sent, 'section', 0, 0, axis_index_groups=same_core, tiled=...  27.7 us
    pallas_call x16, Pallas kernels, rotate(): pl.pallas_call(functools.partial(rotate_kernel, layer, last), out_shape=s...  19.3 us
    ppermute x1, waiting for transfers between devices, local(): lax.ppermute(own_later, 'section', [(i, i ^ 2) for i in range(1, sections...  14.8 us
    select_n x2, other arithmetic, local(): jnp.where(place // 2 == 0, far, near)  14.2 us
  transfers between devices with their start and end apart: 25, of which 14 were waited for; matrix products, arithmetic and copies ran while one was open for 4% of the time, Pallas kernels for 1%

profile of v8, /device:TPU:1, one launch (start us, length us, event | category | flops | bytes accessed | tf_op | source)
XLA Modules:
  0.0 641.5 jit_solution(14161748205243414443)
XLA Ops:
  0.6 8.9 %collective-permute-start = (bf16[4096,512]{1,0:T(8,128)(2,1)}, bf16[4096,512]{1,0:T(8,128)(2,1)}, u32[]{:S(2)}, u32[]{:S(2)}) collective-permute-start(bf16[4096,512]{1,0:T(8,128)(2,1)} %bitcast.1.args_0_), channel_id=1, source_target_pairs={{0,32},{32,0},{64,96},{96,64},{128,160},{160,128},{192,224},{224,1... | collective-permute-start | bytes 12582920 | tf_op jit(solution)/shard_map/ppermute | solution.py:65
  11.3 4.7 all-to-all-start
  17.4 3.4 collective-permute-start.1
  20.8 8.6 %collective-permute-done.1 = f32[1,4608]{1,0:T(1,128)S(1)} collective-permute-done((f32[1,4608]{1,0:T(1,128)S(1)}, f32[1,4608]{1,0:T(1,128)S(1)}, u32[]{:S(2)}, u32[]{:S(2)}) %collective-permute-start.1) | collective-permute-done | bytes 18464 | tf_op jit(solution)/shard_map/ppermute | solution.py:65
  29.4 4.6 all-to-all-done
  35.6 4.6 all-to-all-start.2
  40.2 2.7 collective-permute-start.2
  43.0 23.2 %all-to-all-done.2 = bf16[4,8,64,512]{3,2,1,0:T(8,128)(2,1)} async-done(((bf16[4,8,64,512]{3,2,1,0:T(8,128)(2,1)}), bf16[4,8,64,512]{3,2,1,0:T(8,128)(2,1)}, u32[]{:S(2)}, u32[]{:S(2)}) %all-to-all-start.2) | async-done | bytes 2097184 | tf_op jit(solution)/shard_map/all_to_all | solution.py:57
  66.2 3.3 collective-permute-start.5
  71.4 2.4 collective-permute-start.4
  74.6 6.8 %all-to-all-start.1 = ((bf16[8,32,512]{2,1,0:T(8,128)(2,1)}), bf16[8,32,512]{2,1,0:T(8,128)(2,1)S(1)}, u32[]{:S(2)}, u32[]{:S(2)}) async-start(bf16[8,32,512]{2,1,0:T(8,128)(2,1)} %spread.4), calls=%async_computation.1 | async-start | bytes 524288 | tf_op jit(solution)/shard_map/all_to_all | solution.py:57
  81.7 2.5 select_bitcast_fusion.1
  84.6 2.5 copy.50
  87.1 6.7 %all-to-all-done.1.rows_ref = bf16[8,32,512]{2,1,0:T(8,128)(2,1)S(1)} async-done(((bf16[8,32,512]{2,1,0:T(8,128)(2,1)}), bf16[8,32,512]{2,1,0:T(8,128)(2,1)S(1)}, u32[]{:S(2)}, u32[]{:S(2)}) %all-to-all-start.1) | async-done | bytes 262176 | tf_op jit(solution)/shard_map/all_to_all | solution.py:57
  93.9 2.2 copy-done.2
  101.3 3.4 all-to-all-start.3
  104.8 9.3 %all-to-all-done.3.args_6_ = bf16[8,32,512]{2,1,0:T(8,128)(2,1)S(1)} async-done(((bf16[8,32,512]{2,1,0:T(8,128)(2,1)}), bf16[8,32,512]{2,1,0:T(8,128)(2,1)S(1)}, u32[]{:S(2)}, u32[]{:S(2)}) %all-to-all-start.3) | async-done | bytes 262176 | tf_op jit(solution)/shard_map/all_to_all | solution.py:57
  114.1 3.1 project_from.2
  117.3 3.4 all-to-all-start.4
  120.7 8.0 %broadcast_select_fusion.6 = (bf16[4096,512]{1,0:T(8,128)(2,1)}, bf16[4096,512]{1,0:T(8,128)(2,1)}) fusion(pred[]{:T(512)S(6)} %eq.50, bf16[4096,512]{1,0:T(8,128)(2,1)} %collective-permute-done.args_1_, pred[]{:T(512)S(6)} %eq.49, bf16[4096,512]{1,0:T(8,128)(2,1)} %collective-permute-done.2.args_2_.args_4_, ...), kind=kLoop, calls=%fused_computation.7 | loop fusion | flops 8388608 | bytes 25165826 | tf_op jit(solution)/shard_map/jit(_where)/select_n | solution.py:319
  134.1 14.8 %collective-permute-done.7.args_4_ = bf16[4096,512]{1,0:T(8,128)(2,1)} collective-permute-done((bf16[4096,512]{1,0:T(8,128)(2,1)}, bf16[4096,512]{1,0:T(8,128)(2,1)}, u32[]{:S(2)}, u32[]{:S(2)}) %collective-permute-start.7) | collective-permute-done | bytes 4194336 | tf_op jit(solution)/shard_map/ppermute | solution.py:290
  148.9 3.2 collective-permute-start.8
  152.1 3.4 all-to-all-start.5
  155.5 9.2 %all-to-all-done.5.args_6_ = bf16[8,32,512]{2,1,0:T(8,128)(2,1)S(1)} async-done(((bf16[8,32,512]{2,1,0:T(8,128)(2,1)}), bf16[8,32,512]{2,1,0:T(8,128)(2,1)S(1)}, u32[]{:S(2)}, u32[]{:S(2)}) %all-to-all-start.5) | async-done | bytes 262176 | tf_op jit(solution)/shard_map/all_to_all | solution.py:57
  164.8 3.1 project_from.3
  167.9 3.4 all-to-all-start.6
  171.3 6.3 broadcast_select_fusion.4
  177.6 3.0 all-to-all-done.6.rows_ref
  180.6 2.2 copy-done.4
  184.0 12.8 %all_to_all.175.quant_ref = bf16[8,32,512]{2,1,0:T(8,128)(2,1)S(1)} all-to-all(bf16[8,32,512]{2,1,0:T(8,128)(2,1)S(1)} %get-tuple-element.139), channel_id=1, replica_groups=mesh['section'=16,'dp'=4,'tp'=8] {'tp'}, dimensions={0} | all-to-all | bytes 524288 | tf_op jit(solution)/shard_map/all_to_all | solution.py:57
  197.7 11.9 %all_to_all.176.rows_ref = bf16[8,32,512]{2,1,0:T(8,128)(2,1)S(1)} all-to-all(bf16[8,32,512]{2,1,0:T(8,128)(2,1)S(1)} %get-tuple-element.142), channel_id=1, replica_groups=mesh['section'=16,'dp'=4,'tp'=8] {'tp'}, dimensions={0} | all-to-all | bytes 524288 | tf_op jit(solution)/shard_map/all_to_all | solution.py:57
  210.8 13.2 %all_to_all.177.quant_ref = bf16[8,32,512]{2,1,0:T(8,128)(2,1)S(1)} all-to-all(bf16[8,32,512]{2,1,0:T(8,128)(2,1)S(1)} %get-tuple-element.145), channel_id=1, replica_groups=mesh['section'=16,'dp'=4,'tp'=8] {'tp'}, dimensions={0} | all-to-all | bytes 524288 | tf_op jit(solution)/shard_map/all_to_all | solution.py:57
  227.8 14.8 %all_to_all.178.rows_ref = bf16[8,32,512]{2,1,0:T(8,128)(2,1)S(1)} all-to-all(bf16[8,32,512]{2,1,0:T(8,128)(2,1)S(1)} %spread.5), channel_id=1, replica_groups=mesh['section'=16,'dp'=4,'tp'=8] {'tp'}, dimensions={0} | all-to-all | bytes 524288 | tf_op jit(solution)/shard_map/all_to_all | solution.py:57
  243.8 14.8 %all_to_all.179.quant_ref = bf16[8,32,512]{2,1,0:T(8,128)(2,1)S(1)} all-to-all(bf16[8,32,512]{2,1,0:T(8,128)(2,1)S(1)} %get-tuple-element.151), channel_id=1, replica_groups=mesh['section'=16,'dp'=4,'tp'=8] {'tp'}, dimensions={0} | all-to-all | bytes 524288 | tf_op jit(solution)/shard_map/all_to_all | solution.py:57
  259.4 14.2 %all_to_all.180.rows_ref = bf16[8,32,512]{2,1,0:T(8,128)(2,1)S(1)} all-to-all(bf16[8,32,512]{2,1,0:T(8,128)(2,1)S(1)} %get-tuple-element.153), channel_id=1, replica_groups=mesh['section'=16,'dp'=4,'tp'=8] {'tp'}, dimensions={0} | all-to-all | bytes 524288 | tf_op jit(solution)/shard_map/all_to_all | solution.py:57
  274.8 12.9 %all_to_all.181.quant_ref = bf16[8,32,512]{2,1,0:T(8,128)(2,1)S(1)} all-to-all(bf16[8,32,512]{2,1,0:T(8,128)(2,1)S(1)} %get-tuple-element.156), channel_id=1, replica_groups=mesh['section'=16,'dp'=4,'tp'=8] {'tp'}, dimensions={0} | all-to-all | bytes 524288 | tf_op jit(solution)/shard_map/all_to_all | solution.py:57
  288.5 12.1 %all_to_all.182.rows_ref = bf16[8,32,512]{2,1,0:T(8,128)(2,1)S(1)} all-to-all(bf16[8,32,512]{2,1,0:T(8,128)(2,1)S(1)} %get-tuple-element.159), channel_id=1, replica_groups=mesh['section'=16,'dp'=4,'tp'=8] {'tp'}, dimensions={0} | all-to-all | bytes 524288 | tf_op jit(solution)/shard_map/all_to_all | solution.py:57
  301.8 11.8 %all_to_all.183.quant_ref = bf16[8,32,512]{2,1,0:T(8,128)(2,1)S(1)} all-to-all(bf16[8,32,512]{2,1,0:T(8,128)(2,1)S(1)} %get-tuple-element.162), channel_id=1, replica_groups=mesh['section'=16,'dp'=4,'tp'=8] {'tp'}, dimensions={0} | all-to-all | bytes 524288 | tf_op jit(solution)/shard_map/all_to_all | solution.py:57
  314.4 11.7 %all_to_all.184.rows_ref = bf16[8,32,512]{2,1,0:T(8,128)(2,1)S(1)} all-to-all(bf16[8,32,512]{2,1,0:T(8,128)(2,1)S(1)} %get-tuple-element.164), channel_id=1, replica_groups=mesh['section'=16,'dp'=4,'tp'=8] {'tp'}, dimensions={0} | all-to-all | bytes 524288 | tf_op jit(solution)/shard_map/all_to_all | solution.py:57
  327.3 11.7 %all_to_all.185.quant_ref = bf16[8,32,512]{2,1,0:T(8,128)(2,1)S(1)} all-to-all(bf16[8,32,512]{2,1,0:T(8,128)(2,1)S(1)} %get-tuple-element.167), channel_id=1, replica_groups=mesh['section'=16,'dp'=4,'tp'=8] {'tp'}, dimensions={0} | all-to-all | bytes 524288 | tf_op jit(solution)/shard_map/all_to_all | solution.py:57
  340.6 4.7 collective-permute-start.10
  346.4 11.7 %all_to_all.186.rows_ref = bf16[8,32,512]{2,1,0:T(8,128)(2,1)S(1)} all-to-all(bf16[8,32,512]{2,1,0:T(8,128)(2,1)S(1)} %spread.6), channel_id=1, replica_groups=mesh['section'=16,'dp'=4,'tp'=8] {'tp'}, dimensions={0} | all-to-all | bytes 524288 | tf_op jit(solution)/shard_map/all_to_all | solution.py:57
  359.2 11.7 %all_to_all.187.quant_ref = bf16[8,32,512]{2,1,0:T(8,128)(2,1)S(1)} all-to-all(bf16[8,32,512]{2,1,0:T(8,128)(2,1)S(1)} %get-tuple-element.172), channel_id=1, replica_groups=mesh['section'=16,'dp'=4,'tp'=8] {'tp'}, dimensions={0} | all-to-all | bytes 524288 | tf_op jit(solution)/shard_map/all_to_all | solution.py:57
  371.8 11.7 %all_to_all.188.rows_ref = bf16[8,32,512]{2,1,0:T(8,128)(2,1)S(1)} all-to-all(bf16[8,32,512]{2,1,0:T(8,128)(2,1)S(1)} %get-tuple-element.173), channel_id=1, replica_groups=mesh['section'=16,'dp'=4,'tp'=8] {'tp'}, dimensions={0} | all-to-all | bytes 524288 | tf_op jit(solution)/shard_map/all_to_all | solution.py:57
  384.6 12.2 %all_to_all.189.quant_ref = bf16[8,32,512]{2,1,0:T(8,128)(2,1)S(1)} all-to-all(bf16[8,32,512]{2,1,0:T(8,128)(2,1)S(1)} %get-tuple-element.176), channel_id=1, replica_groups=mesh['section'=16,'dp'=4,'tp'=8] {'tp'}, dimensions={0} | all-to-all | bytes 524288 | tf_op jit(solution)/shard_map/all_to_all | solution.py:57
  397.7 13.3 %all_to_all.190.rows_ref = bf16[8,32,512]{2,1,0:T(8,128)(2,1)S(1)} all-to-all(bf16[8,32,512]{2,1,0:T(8,128)(2,1)S(1)} %get-tuple-element.178), channel_id=1, replica_groups=mesh['section'=16,'dp'=4,'tp'=8] {'tp'}, dimensions={0} | all-to-all | bytes 524288 | tf_op jit(solution)/shard_map/all_to_all | solution.py:57
  412.1 14.8 %all_to_all.191.quant_ref = bf16[8,32,512]{2,1,0:T(8,128)(2,1)S(1)} all-to-all(bf16[8,32,512]{2,1,0:T(8,128)(2,1)S(1)} %get-tuple-element.181), channel_id=1, replica_groups=mesh['section'=16,'dp'=4,'tp'=8] {'tp'}, dimensions={0} | all-to-all | bytes 524288 | tf_op jit(solution)/shard_map/all_to_all | solution.py:57
  427.7 13.4 %all_to_all.192.rows_ref = bf16[8,32,512]{2,1,0:T(8,128)(2,1)S(1)} all-to-all(bf16[8,32,512]{2,1,0:T(8,128)(2,1)S(1)} %get-tuple-element.183), channel_id=1, replica_groups=mesh['section'=16,'dp'=4,'tp'=8] {'tp'}, dimensions={0} | all-to-all | bytes 524288 | tf_op jit(solution)/shard_map/all_to_all | solution.py:57
  442.3 12.2 %all_to_all.193.quant_ref = bf16[8,32,512]{2,1,0:T(8,128)(2,1)S(1)} all-to-all(bf16[8,32,512]{2,1,0:T(8,128)(2,1)S(1)} %get-tuple-element.186), channel_id=1, replica_groups=mesh['section'=16,'dp'=4,'tp'=8] {'tp'}, dimensions={0} | all-to-all | bytes 524288 | tf_op jit(solution)/shard_map/all_to_all | solution.py:57
  456.0 5.6 collective-permute-start.11
  462.7 12.2 %all_to_all.194.rows_ref = bf16[8,32,512]{2,1,0:T(8,128)(2,1)S(1)} all-to-all(bf16[8,32,512]{2,1,0:T(8,128)(2,1)S(1)} %spread.7), channel_id=1, replica_groups=mesh['section'=16,'dp'=4,'tp'=8] {'tp'}, dimensions={0} | all-to-all | bytes 524288 | tf_op jit(solution)/shard_map/all_to_all | solution.py:57
  476.0 11.7 %all_to_all.195.quant_ref = bf16[8,32,512]{2,1,0:T(8,128)(2,1)S(1)} all-to-all(bf16[8,32,512]{2,1,0:T(8,128)(2,1)S(1)} %get-tuple-element.191), channel_id=1, replica_groups=mesh['section'=16,'dp'=4,'tp'=8] {'tp'}, dimensions={0} | all-to-all | bytes 524288 | tf_op jit(solution)/shard_map/all_to_all | solution.py:57
  488.5 11.7 %all_to_all.196.rows_ref = bf16[8,32,512]{2,1,0:T(8,128)(2,1)S(1)} all-to-all(bf16[8,32,512]{2,1,0:T(8,128)(2,1)S(1)} %get-tuple-element.192), channel_id=1, replica_groups=mesh['section'=16,'dp'=4,'tp'=8] {'tp'}, dimensions={0} | all-to-all | bytes 524288 | tf_op jit(solution)/shard_map/all_to_all | solution.py:57
  501.4 11.7 %all_to_all.197.quant_ref = bf16[8,32,512]{2,1,0:T(8,128)(2,1)S(1)} all-to-all(bf16[8,32,512]{2,1,0:T(8,128)(2,1)S(1)} %get-tuple-element.195), channel_id=1, replica_groups=mesh['section'=16,'dp'=4,'tp'=8] {'tp'}, dimensions={0} | all-to-all | bytes 524288 | tf_op jit(solution)/shard_map/all_to_all | solution.py:57
  514.0 11.7 %all_to_all.198.rows_ref = bf16[8,32,512]{2,1,0:T(8,128)(2,1)S(1)} all-to-all(bf16[8,32,512]{2,1,0:T(8,128)(2,1)S(1)} %get-tuple-element.197), channel_id=1, replica_groups=mesh['section'=16,'dp'=4,'tp'=8] {'tp'}, dimensions={0} | all-to-all | bytes 524288 | tf_op jit(solution)/shard_map/all_to_all | solution.py:57
  526.8 11.6 %all_to_all.199.quant_ref = bf16[8,32,512]{2,1,0:T(8,128)(2,1)S(1)} all-to-all(bf16[8,32,512]{2,1,0:T(8,128)(2,1)S(1)} %get-tuple-element.200), channel_id=1, replica_groups=mesh['section'=16,'dp'=4,'tp'=8] {'tp'}, dimensions={0} | all-to-all | bytes 524288 | tf_op jit(solution)/shard_map/all_to_all | solution.py:57
  539.9 11.7 %all_to_all.200.rows_ref = bf16[8,32,512]{2,1,0:T(8,128)(2,1)S(1)} all-to-all(bf16[8,32,512]{2,1,0:T(8,128)(2,1)S(1)} %get-tuple-element.202), channel_id=1, replica_groups=mesh['section'=16,'dp'=4,'tp'=8] {'tp'}, dimensions={0} | all-to-all | bytes 524288 | tf_op jit(solution)/shard_map/all_to_all | solution.py:57
  554.6 2.7 collective-permute-start.14
  557.4 3.1 collective-permute-start.13
  563.7 4.9 all-to-all-start.33
  568.6 2.9 collective-permute-done.12
  572.5 30.3 %collective-permute-start.15 = (bf16[8,64,512]{2,1,0:T(8,128)(2,1)S(1)}, bf16[8,64,512]{2,1,0:T(8,128)(2,1)S(1)}, u32[]{:S(2)}, u32[]{:S(2)}) collective-permute-start(bf16[8,64,512]{2,1,0:T(8,128)(2,1)S(1)} %get-tuple-element.213), channel_id=1, source_target_pairs={{0,32},{32,0},{64,96},{96,64},{128,160},{160,128},{192,224},{224,1... | collective-permute-start | bytes 1572872 | tf_op jit(solution)/shard_map/ppermute | solution.py:65
  602.9 6.6 %collective-permute-start.16 = (f32[8,128]{1,0:T(8,128)S(1)}, f32[8,128]{1,0:T(8,128)S(1)}, u32[]{:S(2)}, u32[]{:S(2)}) collective-permute-start(f32[8,128]{1,0:T(8,128)S(1)} %reduce_sum.37), channel_id=1, source_target_pairs={{0,32},{32,0},{64,96},{96,64},{128,160},{160,128},{192,224},{224,1... | collective-permute-start | bytes 12296 | tf_op jit(solution)/shard_map/ppermute | solution.py:65
  610.6 27.7 %all_to_all.201 = bf16[8,80,512]{2,1,0:T(8,128)(2,1)S(1)} all-to-all(bf16[8,80,512]{2,1,0:T(8,128)(2,1)S(1)} %pad_maximum_fusion.1), channel_id=1, replica_groups={{0,64,128,192,256,320,384,448},{32,96,160,224,288,352,416,480},{1,65,12..., dimensions={0} | all-to-all | bytes 1310720 | tf_op jit(solution)/shard_map/all_to_all | solution.py:382
  (112 shorter events, 60.8 us)
Async XLA Ops:
  0.6 73.2 %copy-start = (bf16[4,32,512]{2,1,0:T(8,128)(2,1)S(1)}, bf16[4,32,512]{2,1,0:T(8,128)(2,1)}, u32[]{:S(2)}) copy-start(bf16[4,32,512]{2,1,0:T(8,128)(2,1)} %param.5) | copy-start | bytes 393220
  0.6 33.3 %collective-permute-start = (bf16[4096,512]{1,0:T(8,128)(2,1)}, bf16[4096,512]{1,0:T(8,128)(2,1)}, u32[]{:S(2)}, u32[]{:S(2)}) collective-permute-start(bf16[4096,512]{1,0:T(8,128)(2,1)} %bitcast.1.args_0_), channel_id=1, source_target_pairs={{0,32},{32,0},{64,96},{96,64},{128,160},{160,128},{192,224},{224,1... | collective-permute-start | bytes 12582920 | tf_op jit(solution)/shard_map/ppermute | solution.py:65
  11.3 22.7 %all-to-all-start = ((bf16[8,64,512]{2,1,0:T(8,128)(2,1)}), bf16[8,64,512]{2,1,0:T(8,128)(2,1)S(1)}, u32[]{:S(2)}, u32[]{:S(2)}) async-start(bf16[8,64,512]{2,1,0:T(8,128)(2,1)} %broadcast_in_dim.75), calls=%async_computation | async-start | bytes 1048576 | tf_op jit(solution)/shard_map/all_to_all | solution.py:276
  17.4 12.0 %collective-permute-start.1 = (f32[1,4608]{1,0:T(1,128)S(1)}, f32[1,4608]{1,0:T(1,128)S(1)}, u32[]{:S(2)}, u32[]{:S(2)}) collective-permute-start(f32[1,4608]{1,0:T(1,128)S(1)} %pad_maximum_fusion.3), channel_id=1, source_target_pairs={{0,64},{32,96},{64,0},{96,32},{128,192},{160,224},{192,128},{224,1... | collective-permute-start | bytes 55304 | tf_op jit(solution)/shard_map/ppermute | solution.py:65
  35.6 45.8 %copy-start.10 = (f32[1,4096]{1,0:T(1,128)S(1)}, f32[1,4096]{1,0:T(1,128)}, u32[]{:S(2)}) copy-start(f32[1,4096]{1,0:T(1,128)} %param.8) | copy-start | bytes 49156
  35.6 30.6 %all-to-all-start.2 = ((bf16[4,8,64,512]{3,2,1,0:T(8,128)(2,1)}), bf16[4,8,64,512]{3,2,1,0:T(8,128)(2,1)}, u32[]{:S(2)}, u32[]{:S(2)}) async-start(bf16[4,8,64,512]{3,2,1,0:T(8,128)(2,1)} %broadcast_in_dim.78), calls=%async_computation.2 | async-start | bytes 4194304 | tf_op jit(solution)/shard_map/all_to_all | solution.py:57
  40.2 57.8 %collective-permute-start.2 = (bf16[4096,512]{1,0:T(8,128)(2,1)}, bf16[4096,512]{1,0:T(8,128)(2,1)}, u32[]{:S(2)}, u32[]{:S(2)}) collective-permute-start(bf16[4096,512]{1,0:T(8,128)(2,1)} %bitcast.1.args_0_), channel_id=1, source_target_pairs={{0,64},{64,0},{128,192},{192,128},{256,320},{320,256},{384,448},{4... | collective-permute-start | bytes 12582920 | tf_op jit(solution)/shard_map/ppermute | solution.py:282
  66.2 15.5 %collective-permute-start.5 = (bf16[4,8,64,512]{3,2,1,0:T(8,128)(2,1)}, bf16[4,8,64,512]{3,2,1,0:T(8,128)(2,1)}, u32[]{:S(2)}, u32[]{:S(2)}) collective-permute-start(bf16[4,8,64,512]{3,2,1,0:T(8,128)(2,1)} %all-to-all-done.2), channel_id=1, source_target_pairs={{0,32},{32,0},{64,96},{96,64},{128,160},{160,128},{192,224},{224,1... | collective-permute-start | bytes 6291464 | tf_op jit(solution)/shard_map/ppermute | solution.py:65
  69.5 11.9 %collective-permute-start.3 = (f32[1,4608]{1,0:T(1,128)S(1)}, f32[1,4608]{1,0:T(1,128)S(1)}, u32[]{:S(2)}, u32[]{:S(2)}) collective-permute-start(f32[1,4608]{1,0:T(1,128)S(1)} %pad_maximum_fusion.3), channel_id=1, source_target_pairs={{0,32},{32,0},{64,96},{96,64},{128,160},{160,128},{192,224},{224,1... | collective-permute-start | bytes 55304 | tf_op jit(solution)/shard_map/ppermute | solution.py:65
  71.4 10.0 %collective-permute-start.4 = (f32[1,4608]{1,0:T(1,128)S(1)}, f32[1,4608]{1,0:T(1,128)S(1)}, u32[]{:S(2)}, u32[]{:S(2)}) collective-permute-start(f32[1,4608]{1,0:T(1,128)S(1)} %collective-permute-done.1), channel_id=1, source_target_pairs={{0,32},{32,0},{64,96},{96,64},{128,160},{160,128},{192,224},{224,1... | collective-permute-start | bytes 55304 | tf_op jit(solution)/shard_map/ppermute | solution.py:65
  74.6 19.2 %all-to-all-start.1 = ((bf16[8,32,512]{2,1,0:T(8,128)(2,1)}), bf16[8,32,512]{2,1,0:T(8,128)(2,1)S(1)}, u32[]{:S(2)}, u32[]{:S(2)}) async-start(bf16[8,32,512]{2,1,0:T(8,128)(2,1)} %spread.4), calls=%async_computation.1 | async-start | bytes 524288 | tf_op jit(solution)/shard_map/all_to_all | solution.py:57
  93.9 2.2 copy-start.2
  98.0 16.1 %collective-permute-start.6 = (bf16[4096,512]{1,0:T(8,128)(2,1)}, bf16[4096,512]{1,0:T(8,128)(2,1)}, u32[]{:S(2)}, u32[]{:S(2)}) collective-permute-start(bf16[4096,512]{1,0:T(8,128)(2,1)} %collective-permute-done.2.args_2_.args_4_), channel_id=1, source_target_pairs={{0,32},{64,96},{128,160},{192,224},{256,288},{320,352},{384,416},{... | collective-permute-start | bytes 12582920 | tf_op jit(solution)/shard_map/ppermute | solution.py:330
  99.3 49.6 %collective-permute-start.7 = (bf16[4096,512]{1,0:T(8,128)(2,1)}, bf16[4096,512]{1,0:T(8,128)(2,1)}, u32[]{:S(2)}, u32[]{:S(2)}) collective-permute-start(bf16[4096,512]{1,0:T(8,128)(2,1)} %bitcast.1.args_0_), channel_id=1, source_target_pairs={{32,96},{96,32},{160,224},{224,160},{288,352},{352,288},{416,480},... | collective-permute-start | bytes 12582920 | tf_op jit(solution)/shard_map/ppermute | solution.py:290
  101.3 12.8 %all-to-all-start.3 = ((bf16[8,32,512]{2,1,0:T(8,128)(2,1)}), bf16[8,32,512]{2,1,0:T(8,128)(2,1)S(1)}, u32[]{:S(2)}, u32[]{:S(2)}) async-start(bf16[8,32,512]{2,1,0:T(8,128)(2,1)} %get-tuple-element.112), calls=%async_computation.3 | async-start | bytes 524288 | tf_op jit(solution)/shard_map/all_to_all | solution.py:57
  117.3 12.7 %all-to-all-start.4 = ((bf16[8,32,512]{2,1,0:T(8,128)(2,1)}), bf16[8,32,512]{2,1,0:T(8,128)(2,1)S(1)}, u32[]{:S(2)}, u32[]{:S(2)}) async-start(bf16[8,32,512]{2,1,0:T(8,128)(2,1)} %get-tuple-element.115), calls=%async_computation.4 | async-start | bytes 524288 | tf_op jit(solution)/shard_map/all_to_all | solution.py:57
  130.0 2.2 copy-start.3
  148.9 15.9 %collective-permute-start.8 = (bf16[4096,512]{1,0:T(8,128)(2,1)}, bf16[4096,512]{1,0:T(8,128)(2,1)}, u32[]{:S(2)}, u32[]{:S(2)}) collective-permute-start(bf16[4096,512]{1,0:T(8,128)(2,1)} %collective-permute-done.7.args_4_), channel_id=1, source_target_pairs={{32,0},{96,64},{160,128},{224,192},{288,256},{352,320},{416,384},{... | collective-permute-start | bytes 12582920 | tf_op jit(solution)/shard_map/ppermute | solution.py:334
  152.1 12.7 %all-to-all-start.5 = ((bf16[8,32,512]{2,1,0:T(8,128)(2,1)}), bf16[8,32,512]{2,1,0:T(8,128)(2,1)S(1)}, u32[]{:S(2)}, u32[]{:S(2)}) async-start(bf16[8,32,512]{2,1,0:T(8,128)(2,1)} %get-tuple-element.119), calls=%async_computation.5 | async-start | bytes 524288 | tf_op jit(solution)/shard_map/all_to_all | solution.py:57
  167.9 12.7 %all-to-all-start.6 = ((bf16[8,32,512]{2,1,0:T(8,128)(2,1)}), bf16[8,32,512]{2,1,0:T(8,128)(2,1)S(1)}, u32[]{:S(2)}, u32[]{:S(2)}) async-start(bf16[8,32,512]{2,1,0:T(8,128)(2,1)} %get-tuple-element.122), calls=%async_computation.6 | async-start | bytes 524288 | tf_op jit(solution)/shard_map/all_to_all | solution.py:57
  180.6 2.2 copy-start.4
  182.8 14.0 %copy-start.6 = (bf16[4096,512]{1,0:T(8,128)(2,1)S(1)}, bf16[4096,512]{1,0:T(8,128)(2,1)}, u32[]{:S(2)}) copy-start(bf16[4096,512]{1,0:T(8,128)(2,1)} %get-tuple-element.140.weight_ref) | copy-start | bytes 12582916
  196.8 12.8 %copy-start.5 = (bf16[8,2,4,64,512]{4,3,2,1,0:T(8,128)(2,1)S(1)}, bf16[8,2,4,64,512]{4,3,2,1,0:T(8,128)(2,1)}, u32[]{:S(2)}) copy-start(bf16[8,2,4,64,512]{4,3,2,1,0:T(8,128)(2,1)} %copy.50) | copy-start | bytes 12582916
  209.6 14.4 %copy-start.9 = (bf16[4096,512]{1,0:T(8,128)(2,1)S(1)}, bf16[4096,512]{1,0:T(8,128)(2,1)}, u32[]{:S(2)}) copy-start(bf16[4096,512]{1,0:T(8,128)(2,1)} %get-tuple-element.146.weight_ref) | copy-start | bytes 12582916
  225.5 2.3 collective-permute-start.9
  242.6 15.9 %copy-start.7 = (bf16[4096,512]{1,0:T(8,128)(2,1)S(1)}, bf16[4096,512]{1,0:T(8,128)(2,1)}, u32[]{:S(2)}) copy-start(bf16[4096,512]{1,0:T(8,128)(2,1)} %get-tuple-element.152.weight_ref) | copy-start | bytes 12582916
  273.6 14.0 %copy-start.8 = (bf16[4096,512]{1,0:T(8,128)(2,1)S(1)}, bf16[4096,512]{1,0:T(8,128)(2,1)}, u32[]{:S(2)}) copy-start(bf16[4096,512]{1,0:T(8,128)(2,1)} %get-tuple-element.157.weight_ref) | copy-start | bytes 12582916
  340.6 5.8 collective-permute-start.10
  456.0 6.6 %collective-permute-start.11 = (bf16[32,512]{1,0:T(8,128)(2,1)S(1)}, bf16[32,512]{1,0:T(8,128)(2,1)S(1)}, u32[]{:S(2)}, u32[]{:S(2)}) collective-permute-start(bf16[32,512]{1,0:T(8,128)(2,1)S(1)} %get-tuple-element.188), channel_id=1, source_target_pairs={{0,128},{32,160},{64,192},{96,224},{128,256},{160,288},{192,320},{... | collective-permute-start | bytes 98312 | tf_op jit(solution)/shard_map/ppermute | solution.py:342
  554.6 14.0 %collective-permute-start.14 = (bf16[1536,128]{1,0:T(8,128)(2,1)S(1)}, bf16[1536,128]{1,0:T(8,128)(2,1)S(1)}, u32[]{:S(2)}, u32[]{:S(2)}) collective-permute-start(bf16[1536,128]{1,0:T(8,128)(2,1)S(1)} %get-tuple-element.223), channel_id=1, source_target_pairs={{0,24},{8,0},{16,8},{24,16},{1,25},{9,1},{17,9},{25,17},{2,26},{10... | collective-permute-start | bytes 1179656 | tf_op jit(solution)/shard_map/ppermute | solution.py:364
  557.4 11.3 %collective-permute-start.13 = (bf16[1536,128]{1,0:T(8,128)(2,1)S(1)}, bf16[1536,128]{1,0:T(8,128)(2,1)S(1)}, u32[]{:S(2)}, u32[]{:S(2)}) collective-permute-start(bf16[1536,128]{1,0:T(8,128)(2,1)S(1)} %get-tuple-element.222), channel_id=1, source_target_pairs={{0,16},{8,24},{16,0},{24,8},{1,17},{9,25},{17,1},{25,9},{2,18},{10... | collective-permute-start | bytes 1179656 | tf_op jit(solution)/shard_map/ppermute | solution.py:364
  560.5 11.1 %collective-permute-start.12 = (bf16[1536,128]{1,0:T(8,128)(2,1)S(1)}, bf16[1536,128]{1,0:T(8,128)(2,1)S(1)}, u32[]{:S(2)}, u32[]{:S(2)}) collective-permute-start(bf16[1536,128]{1,0:T(8,128)(2,1)S(1)} %get-tuple-element.221), channel_id=1, source_target_pairs={{0,8},{8,16},{16,24},{24,0},{1,9},{9,17},{17,25},{25,1},{2,10},{10... | collective-permute-start | bytes 1179656 | tf_op jit(solution)/shard_map/ppermute | solution.py:364
  563.7 39.1 %all-to-all-start.33 = ((f32[32,8,128]{2,1,0:T(8,128)}), f32[32,8,128]{2,1,0:T(8,128)S(1)}, u32[]{:S(2)}, u32[]{:S(2)}) async-start(f32[32,8,128]{2,1,0:T(8,128)} %broadcast_in_dim_broadcast_in_dim_broadcast_in_dim.3), calls=%async_computation.33 | async-start | bytes 262144 | tf_op jit(solution)/shard_map/all_to_all | solution.py:57
  572.5 37.9 %collective-permute-start.15 = (bf16[8,64,512]{2,1,0:T(8,128)(2,1)S(1)}, bf16[8,64,512]{2,1,0:T(8,128)(2,1)S(1)}, u32[]{:S(2)}, u32[]{:S(2)}) collective-permute-start(bf16[8,64,512]{2,1,0:T(8,128)(2,1)S(1)} %get-tuple-element.213), channel_id=1, source_target_pairs={{0,32},{32,0},{64,96},{96,64},{128,160},{160,128},{192,224},{224,1... | collective-permute-start | bytes 1572872 | tf_op jit(solution)/shard_map/ppermute | solution.py:65
  602.9 7.5 %collective-permute-start.16 = (f32[8,128]{1,0:T(8,128)S(1)}, f32[8,128]{1,0:T(8,128)S(1)}, u32[]{:S(2)}, u32[]{:S(2)}) collective-permute-start(f32[8,128]{1,0:T(8,128)S(1)} %reduce_sum.37), channel_id=1, source_target_pairs={{0,32},{32,0},{64,96},{96,64},{128,160},{160,128},{192,224},{224,1... | collective-permute-start | bytes 12296 | tf_op jit(solution)/shard_map/ppermute | solution.py:65
  610.4 30.0 %copy-start.1 = (bf16[4,32,512]{2,1,0:T(8,128)(2,1)S(1)}, bf16[4,32,512]{2,1,0:T(8,128)(2,1)}, u32[]{:S(2)}) copy-start(bf16[4,32,512]{2,1,0:T(8,128)(2,1)} %param.5) | copy-start | bytes 393220

commit v9 on v8

--- a/solution.py
+++ b/solution.py
@@ -285,6 +285,9 @@
     gains, scales = params[:, :D], params[:, D:]
 
     along_x = gather(along_z, "dp")
+    stream = lax.dynamic_index_in_dim(hidden_in, place, 0, keepdims=False)
+    copies = spread(stream, tensor)
+    along_x, gains, scales, stream, copies = lax.optimization_barrier((along_x, gains, scales, stream, copies))
     other_rows = crossed(along_x, 1)
     own_later, _ = lax.optimization_barrier((own, other_rows))
     odd_mine = lax.ppermute(own_later, "section", [(i, i ^ 2) for i in range(1, sections, 2)])
@@ -294,8 +297,6 @@
 
     where = place[None].astype(jnp.int32)
     all_rows = STAGE * tok_rows
-    stream = lax.dynamic_index_in_dim(hidden_in, place, 0, keepdims=False)
-    copies = spread(stream, tensor)
     kept = (jnp.zeros((all_rows, D), jnp.bfloat16), jnp.zeros((all_rows, part_cols), jnp.float32))
     weights = []
     keeps = [jnp.full((1,), 1, jnp.int32)]
@@ -367,9 +368,10 @@
     )
     mine, other = terms_of(which, parts, planes, row_block, part_cols)
     loss = jnp.full((8, 128), jnp.sum(error_part * error_part), jnp.float32)
-    loss = jnp.sum(exchange(copies_of(loss, replicas * tensor), ("dp", "tp")), axis=0)
+    losses = exchange(copies_of(loss, replicas * tensor), ("dp", "tp"))
+    losses, _ = lax.optimization_barrier((losses, other))
+    loss = jnp.sum(losses, axis=0)
     loss = loss + crossed(loss, 1)
-    loss = jnp.concatenate([loss, loss], axis=0)
     high = lax.reduce_precision(loss, 8, 7)
     middle = lax.reduce_precision(loss - high, 8, 7)
     low = loss - high - middle

time: 644 us -> 644 us (level)
  no operation moved by 1% of the time
where the time goes in v9:
time: 644 us; the launch traced here: 642 us
  blocking collectives  353 us (55%)
  starting transfers between devices  120 us (19%)
  waiting for transfers between devices  88 us (14%)
  Pallas kernels  40.7 us (6%)
  other arithmetic  21.6 us (3%)
  local copies, waits for them, and re-layouts  15 us (2%)
    all_to_all x26, blocking collectives, exchange(): return lax.all_to_all(copies, axis, 0, 0, tiled=True)  326 us
    ppermute x7, starting transfers between devices, crossed(): lax.ppermute(value, 'section', [(i, i ^ mask) for i in range(lax.axis_siz...  56.9 us
    all_to_all x7, waiting for transfers between devices, exchange(): return lax.all_to_all(copies, axis, 0, 0, tiled=True)  56.2 us
    all_to_all x7, starting transfers between devices, exchange(): return lax.all_to_all(copies, axis, 0, 0, tiled=True)  29.8 us
    all_to_all x1, blocking collectives, local(): lax.all_to_all(sent, 'section', 0, 0, axis_index_groups=same_core, tiled=...  27.2 us
    pallas_call x16, Pallas kernels, rotate(): pl.pallas_call(functools.partial(rotate_kernel, layer, last), out_shape=s...  19.3 us
    ppermute x1, waiting for transfers between devices, local(): lax.ppermute(own_later, 'section', [(i, i ^ 2) for i in range(1, sections...  14.4 us
    select_n x2, other arithmetic, local(): jnp.where(place // 2 == 0, far, near)  14.2 us
  transfers between devices with their start and end apart: 25, of which 14 were waited for; matrix products, arithmetic and copies ran while one was open for 4% of the time, Pallas kernels for 1%

profile of v9, /device:TPU:1, one launch (start us, length us, event | category | flops | bytes accessed | tf_op | source)
XLA Modules:
  0.0 641.7 jit_solution(16580622305003650741)
XLA Ops:
  0.6 8.9 %collective-permute-start = (bf16[4096,512]{1,0:T(8,128)(2,1)}, bf16[4096,512]{1,0:T(8,128)(2,1)}, u32[]{:S(2)}, u32[]{:S(2)}) collective-permute-start(bf16[4096,512]{1,0:T(8,128)(2,1)} %bitcast.1.args_0_), channel_id=1, source_target_pairs={{0,32},{32,0},{64,96},{96,64},{128,160},{160,128},{192,224},{224,1... | collective-permute-start | bytes 12582920 | tf_op jit(solution)/shard_map/ppermute | solution.py:65
  11.3 4.7 all-to-all-start
  17.4 3.4 collective-permute-start.1
  20.8 2.8 collective-permute-start.3
  23.6 5.8 collective-permute-done.1
  29.4 4.6 all-to-all-done
  34.0 2.4 collective-permute-start.4
  37.2 2.7 collective-permute-start.2
  41.6 4.6 all-to-all-start.1
  46.5 26.3 %all-to-all-done.1 = bf16[4,8,64,512]{3,2,1,0:T(8,128)(2,1)} async-done(((bf16[4,8,64,512]{3,2,1,0:T(8,128)(2,1)}), bf16[4,8,64,512]{3,2,1,0:T(8,128)(2,1)}, u32[]{:S(2)}, u32[]{:S(2)}) %all-to-all-start.1) | async-done | bytes 2097184 | tf_op jit(solution)/shard_map/all_to_all | solution.py:57
  72.8 2.6 collective-permute-start.5
  75.4 6.8 %all-to-all-start.2 = ((bf16[8,32,512]{2,1,0:T(8,128)(2,1)}), bf16[8,32,512]{2,1,0:T(8,128)(2,1)S(1)}, u32[]{:S(2)}, u32[]{:S(2)}) async-start(bf16[8,32,512]{2,1,0:T(8,128)(2,1)} %spread.4), calls=%async_computation.2 | async-start | bytes 524288 | tf_op jit(solution)/shard_map/all_to_all | solution.py:57
  82.3 2.5 select_bitcast_fusion.1
  85.2 2.5 copy.46
  87.8 6.9 %all-to-all-done.2.rows_ref = bf16[8,32,512]{2,1,0:T(8,128)(2,1)S(1)} async-done(((bf16[8,32,512]{2,1,0:T(8,128)(2,1)}), bf16[8,32,512]{2,1,0:T(8,128)(2,1)S(1)}, u32[]{:S(2)}, u32[]{:S(2)}) %all-to-all-start.2) | async-done | bytes 262176 | tf_op jit(solution)/shard_map/all_to_all | solution.py:57
  100.2 2.3 collective-permute-start.7
  102.4 3.4 all-to-all-start.3
  105.9 9.4 %all-to-all-done.3.args_6_ = bf16[8,32,512]{2,1,0:T(8,128)(2,1)S(1)} async-done(((bf16[8,32,512]{2,1,0:T(8,128)(2,1)}), bf16[8,32,512]{2,1,0:T(8,128)(2,1)S(1)}, u32[]{:S(2)}, u32[]{:S(2)}) %all-to-all-start.3) | async-done | bytes 262176 | tf_op jit(solution)/shard_map/all_to_all | solution.py:57
  115.3 3.1 project_from.2
  118.5 3.4 all-to-all-start.4
  121.9 8.0 %broadcast_select_fusion.6 = (bf16[4096,512]{1,0:T(8,128)(2,1)}, bf16[4096,512]{1,0:T(8,128)(2,1)}) fusion(pred[]{:T(512)S(6)} %eq.50, bf16[4096,512]{1,0:T(8,128)(2,1)} %collective-permute-done.args_1_, pred[]{:T(512)S(6)} %eq.49, bf16[4096,512]{1,0:T(8,128)(2,1)} %collective-permute-done.2.args_2_.args_4_, ...), kind=kLoop, calls=%fused_computation.7 | loop fusion | flops 8388608 | bytes 25165826 | tf_op jit(solution)/shard_map/jit(_where)/select_n | solution.py:320
  135.4 14.4 %collective-permute-done.7.args_4_ = bf16[4096,512]{1,0:T(8,128)(2,1)} collective-permute-done((bf16[4096,512]{1,0:T(8,128)(2,1)}, bf16[4096,512]{1,0:T(8,128)(2,1)}, u32[]{:S(2)}, u32[]{:S(2)}) %collective-permute-start.7) | collective-permute-done | bytes 4194336 | tf_op jit(solution)/shard_map/ppermute | solution.py:293
  149.7 3.2 collective-permute-start.8
  153.0 3.4 all-to-all-start.5
  156.4 9.2 %all-to-all-done.5.args_6_ = bf16[8,32,512]{2,1,0:T(8,128)(2,1)S(1)} async-done(((bf16[8,32,512]{2,1,0:T(8,128)(2,1)}), bf16[8,32,512]{2,1,0:T(8,128)(2,1)S(1)}, u32[]{:S(2)}, u32[]{:S(2)}) %all-to-all-start.5) | async-done | bytes 262176 | tf_op jit(solution)/shard_map/all_to_all | solution.py:57
  165.6 3.1 project_from.3
  168.8 3.4 all-to-all-start.6
  172.2 6.3 broadcast_select_fusion.4
  178.5 3.0 all-to-all-done.6.rows_ref
  184.8 12.8 %all_to_all.175.quant_ref = bf16[8,32,512]{2,1,0:T(8,128)(2,1)S(1)} all-to-all(bf16[8,32,512]{2,1,0:T(8,128)(2,1)S(1)} %get-tuple-element.150), channel_id=1, replica_groups=mesh['section'=16,'dp'=4,'tp'=8] {'tp'}, dimensions={0} | all-to-all | bytes 524288 | tf_op jit(solution)/shard_map/all_to_all | solution.py:57
  198.5 11.9 %all_to_all.176.rows_ref = bf16[8,32,512]{2,1,0:T(8,128)(2,1)S(1)} all-to-all(bf16[8,32,512]{2,1,0:T(8,128)(2,1)S(1)} %get-tuple-element.153), channel_id=1, replica_groups=mesh['section'=16,'dp'=4,'tp'=8] {'tp'}, dimensions={0} | all-to-all | bytes 524288 | tf_op jit(solution)/shard_map/all_to_all | solution.py:57
  211.6 13.2 %all_to_all.177.quant_ref = bf16[8,32,512]{2,1,0:T(8,128)(2,1)S(1)} all-to-all(bf16[8,32,512]{2,1,0:T(8,128)(2,1)S(1)} %get-tuple-element.156), channel_id=1, replica_groups=mesh['section'=16,'dp'=4,'tp'=8] {'tp'}, dimensions={0} | all-to-all | bytes 524288 | tf_op jit(solution)/shard_map/all_to_all | solution.py:57
  228.7 14.8 %all_to_all.178.rows_ref = bf16[8,32,512]{2,1,0:T(8,128)(2,1)S(1)} all-to-all(bf16[8,32,512]{2,1,0:T(8,128)(2,1)S(1)} %spread.5), channel_id=1, replica_groups=mesh['section'=16,'dp'=4,'tp'=8] {'tp'}, dimensions={0} | all-to-all | bytes 524288 | tf_op jit(solution)/shard_map/all_to_all | solution.py:57
  244.6 14.8 %all_to_all.179.quant_ref = bf16[8,32,512]{2,1,0:T(8,128)(2,1)S(1)} all-to-all(bf16[8,32,512]{2,1,0:T(8,128)(2,1)S(1)} %get-tuple-element.162), channel_id=1, replica_groups=mesh['section'=16,'dp'=4,'tp'=8] {'tp'}, dimensions={0} | all-to-all | bytes 524288 | tf_op jit(solution)/shard_map/all_to_all | solution.py:57
  260.3 14.2 %all_to_all.180.rows_ref = bf16[8,32,512]{2,1,0:T(8,128)(2,1)S(1)} all-to-all(bf16[8,32,512]{2,1,0:T(8,128)(2,1)S(1)} %get-tuple-element.164), channel_id=1, replica_groups=mesh['section'=16,'dp'=4,'tp'=8] {'tp'}, dimensions={0} | all-to-all | bytes 524288 | tf_op jit(solution)/shard_map/all_to_all | solution.py:57
  275.6 12.9 %all_to_all.181.quant_ref = bf16[8,32,512]{2,1,0:T(8,128)(2,1)S(1)} all-to-all(bf16[8,32,512]{2,1,0:T(8,128)(2,1)S(1)} %get-tuple-element.167), channel_id=1, replica_groups=mesh['section'=16,'dp'=4,'tp'=8] {'tp'}, dimensions={0} | all-to-all | bytes 524288 | tf_op jit(solution)/shard_map/all_to_all | solution.py:57
  289.4 12.1 %all_to_all.182.rows_ref = bf16[8,32,512]{2,1,0:T(8,128)(2,1)S(1)} all-to-all(bf16[8,32,512]{2,1,0:T(8,128)(2,1)S(1)} %get-tuple-element.170), channel_id=1, replica_groups=mesh['section'=16,'dp'=4,'tp'=8] {'tp'}, dimensions={0} | all-to-all | bytes 524288 | tf_op jit(solution)/shard_map/all_to_all | solution.py:57
  302.6 11.8 %all_to_all.183.quant_ref = bf16[8,32,512]{2,1,0:T(8,128)(2,1)S(1)} all-to-all(bf16[8,32,512]{2,1,0:T(8,128)(2,1)S(1)} %get-tuple-element.173), channel_id=1, replica_groups=mesh['section'=16,'dp'=4,'tp'=8] {'tp'}, dimensions={0} | all-to-all | bytes 524288 | tf_op jit(solution)/shard_map/all_to_all | solution.py:57
  315.3 11.7 %all_to_all.184.rows_ref = bf16[8,32,512]{2,1,0:T(8,128)(2,1)S(1)} all-to-all(bf16[8,32,512]{2,1,0:T(8,128)(2,1)S(1)} %get-tuple-element.175), channel_id=1, replica_groups=mesh['section'=16,'dp'=4,'tp'=8] {'tp'}, dimensions={0} | all-to-all | bytes 524288 | tf_op jit(solution)/shard_map/all_to_all | solution.py:57
  328.1 11.7 %all_to_all.185.quant_ref = bf16[8,32,512]{2,1,0:T(8,128)(2,1)S(1)} all-to-all(bf16[8,32,512]{2,1,0:T(8,128)(2,1)S(1)} %get-tuple-element.178), channel_id=1, replica_groups=mesh['section'=16,'dp'=4,'tp'=8] {'tp'}, dimensions={0} | all-to-all | bytes 524288 | tf_op jit(solution)/shard_map/all_to_all | solution.py:57
  341.4 4.7 collective-permute-start.10
  347.2 11.7 %all_to_all.186.rows_ref = bf16[8,32,512]{2,1,0:T(8,128)(2,1)S(1)} all-to-all(bf16[8,32,512]{2,1,0:T(8,128)(2,1)S(1)} %spread.6), channel_id=1, replica_groups=mesh['section'=16,'dp'=4,'tp'=8] {'tp'}, dimensions={0} | all-to-all | bytes 524288 | tf_op jit(solution)/shard_map/all_to_all | solution.py:57
  360.0 11.7 %all_to_all.187.quant_ref = bf16[8,32,512]{2,1,0:T(8,128)(2,1)S(1)} all-to-all(bf16[8,32,512]{2,1,0:T(8,128)(2,1)S(1)} %get-tuple-element.183), channel_id=1, replica_groups=mesh['section'=16,'dp'=4,'tp'=8] {'tp'}, dimensions={0} | all-to-all | bytes 524288 | tf_op jit(solution)/shard_map/all_to_all | solution.py:57
  372.6 11.7 %all_to_all.188.rows_ref = bf16[8,32,512]{2,1,0:T(8,128)(2,1)S(1)} all-to-all(bf16[8,32,512]{2,1,0:T(8,128)(2,1)S(1)} %get-tuple-element.184), channel_id=1, replica_groups=mesh['section'=16,'dp'=4,'tp'=8] {'tp'}, dimensions={0} | all-to-all | bytes 524288 | tf_op jit(solution)/shard_map/all_to_all | solution.py:57
  385.5 12.2 %all_to_all.189.quant_ref = bf16[8,32,512]{2,1,0:T(8,128)(2,1)S(1)} all-to-all(bf16[8,32,512]{2,1,0:T(8,128)(2,1)S(1)} %get-tuple-element.187), channel_id=1, replica_groups=mesh['section'=16,'dp'=4,'tp'=8] {'tp'}, dimensions={0} | all-to-all | bytes 524288 | tf_op jit(solution)/shard_map/all_to_all | solution.py:57
  398.5 13.3 %all_to_all.190.rows_ref = bf16[8,32,512]{2,1,0:T(8,128)(2,1)S(1)} all-to-all(bf16[8,32,512]{2,1,0:T(8,128)(2,1)S(1)} %get-tuple-element.189), channel_id=1, replica_groups=mesh['section'=16,'dp'=4,'tp'=8] {'tp'}, dimensions={0} | all-to-all | bytes 524288 | tf_op jit(solution)/shard_map/all_to_all | solution.py:57
  413.0 14.8 %all_to_all.191.quant_ref = bf16[8,32,512]{2,1,0:T(8,128)(2,1)S(1)} all-to-all(bf16[8,32,512]{2,1,0:T(8,128)(2,1)S(1)} %get-tuple-element.192), channel_id=1, replica_groups=mesh['section'=16,'dp'=4,'tp'=8] {'tp'}, dimensions={0} | all-to-all | bytes 524288 | tf_op jit(solution)/shard_map/all_to_all | solution.py:57
  428.6 13.4 %all_to_all.192.rows_ref = bf16[8,32,512]{2,1,0:T(8,128)(2,1)S(1)} all-to-all(bf16[8,32,512]{2,1,0:T(8,128)(2,1)S(1)} %get-tuple-element.194), channel_id=1, replica_groups=mesh['section'=16,'dp'=4,'tp'=8] {'tp'}, dimensions={0} | all-to-all | bytes 524288 | tf_op jit(solution)/shard_map/all_to_all | solution.py:57
  443.1 12.2 %all_to_all.193.quant_ref = bf16[8,32,512]{2,1,0:T(8,128)(2,1)S(1)} all-to-all(bf16[8,32,512]{2,1,0:T(8,128)(2,1)S(1)} %get-tuple-element.197), channel_id=1, replica_groups=mesh['section'=16,'dp'=4,'tp'=8] {'tp'}, dimensions={0} | all-to-all | bytes 524288 | tf_op jit(solution)/shard_map/all_to_all | solution.py:57
  456.9 5.6 collective-permute-start.11
  463.5 12.2 %all_to_all.194.rows_ref = bf16[8,32,512]{2,1,0:T(8,128)(2,1)S(1)} all-to-all(bf16[8,32,512]{2,1,0:T(8,128)(2,1)S(1)} %spread.7), channel_id=1, replica_groups=mesh['section'=16,'dp'=4,'tp'=8] {'tp'}, dimensions={0} | all-to-all | bytes 524288 | tf_op jit(solution)/shard_map/all_to_all | solution.py:57
  476.8 11.8 %all_to_all.195.quant_ref = bf16[8,32,512]{2,1,0:T(8,128)(2,1)S(1)} all-to-all(bf16[8,32,512]{2,1,0:T(8,128)(2,1)S(1)} %get-tuple-element.202), channel_id=1, replica_groups=mesh['section'=16,'dp'=4,'tp'=8] {'tp'}, dimensions={0} | all-to-all | bytes 524288 | tf_op jit(solution)/shard_map/all_to_all | solution.py:57
  489.4 11.7 %all_to_all.196.rows_ref = bf16[8,32,512]{2,1,0:T(8,128)(2,1)S(1)} all-to-all(bf16[8,32,512]{2,1,0:T(8,128)(2,1)S(1)} %get-tuple-element.203), channel_id=1, replica_groups=mesh['section'=16,'dp'=4,'tp'=8] {'tp'}, dimensions={0} | all-to-all | bytes 524288 | tf_op jit(solution)/shard_map/all_to_all | solution.py:57
  502.3 11.7 %all_to_all.197.quant_ref = bf16[8,32,512]{2,1,0:T(8,128)(2,1)S(1)} all-to-all(bf16[8,32,512]{2,1,0:T(8,128)(2,1)S(1)} %get-tuple-element.206), channel_id=1, replica_groups=mesh['section'=16,'dp'=4,'tp'=8] {'tp'}, dimensions={0} | all-to-all | bytes 524288 | tf_op jit(solution)/shard_map/all_to_all | solution.py:57
  514.8 11.7 %all_to_all.198.rows_ref = bf16[8,32,512]{2,1,0:T(8,128)(2,1)S(1)} all-to-all(bf16[8,32,512]{2,1,0:T(8,128)(2,1)S(1)} %get-tuple-element.208), channel_id=1, replica_groups=mesh['section'=16,'dp'=4,'tp'=8] {'tp'}, dimensions={0} | all-to-all | bytes 524288 | tf_op jit(solution)/shard_map/all_to_all | solution.py:57
  527.7 11.6 %all_to_all.199.quant_ref = bf16[8,32,512]{2,1,0:T(8,128)(2,1)S(1)} all-to-all(bf16[8,32,512]{2,1,0:T(8,128)(2,1)S(1)} %get-tuple-element.211), channel_id=1, replica_groups=mesh['section'=16,'dp'=4,'tp'=8] {'tp'}, dimensions={0} | all-to-all | bytes 524288 | tf_op jit(solution)/shard_map/all_to_all | solution.py:57
  540.7 11.7 %all_to_all.200.rows_ref = bf16[8,32,512]{2,1,0:T(8,128)(2,1)S(1)} all-to-all(bf16[8,32,512]{2,1,0:T(8,128)(2,1)S(1)} %get-tuple-element.213), channel_id=1, replica_groups=mesh['section'=16,'dp'=4,'tp'=8] {'tp'}, dimensions={0} | all-to-all | bytes 524288 | tf_op jit(solution)/shard_map/all_to_all | solution.py:57
  555.5 2.8 collective-permute-start.14
  558.2 3.0 collective-permute-start.13
  564.6 4.7 all-to-all-start.33
  569.3 3.2 collective-permute-done.12
  573.4 30.1 %collective-permute-start.15 = (bf16[8,64,512]{2,1,0:T(8,128)(2,1)S(1)}, bf16[8,64,512]{2,1,0:T(8,128)(2,1)S(1)}, u32[]{:S(2)}, u32[]{:S(2)}) collective-permute-start(bf16[8,64,512]{2,1,0:T(8,128)(2,1)S(1)} %get-tuple-element.224), channel_id=1, source_target_pairs={{0,32},{32,0},{64,96},{96,64},{128,160},{160,128},{192,224},{224,1... | collective-permute-start | bytes 1572872 | tf_op jit(solution)/shard_map/ppermute | solution.py:65
  603.5 6.8 %collective-permute-start.16 = (f32[8,128]{1,0:T(8,128)S(1)}, f32[8,128]{1,0:T(8,128)S(1)}, u32[]{:S(2)}, u32[]{:S(2)}) collective-permute-start(f32[8,128]{1,0:T(8,128)S(1)} %reduce_sum.37), channel_id=1, source_target_pairs={{0,32},{32,0},{64,96},{96,64},{128,160},{160,128},{192,224},{224,1... | collective-permute-start | bytes 12296 | tf_op jit(solution)/shard_map/ppermute | solution.py:65
  611.4 27.2 %all_to_all.201 = bf16[8,72,512]{2,1,0:T(8,128)(2,1)S(1)} all-to-all(bf16[8,72,512]{2,1,0:T(8,128)(2,1)S(1)} %pad_maximum_fusion.1), channel_id=1, replica_groups={{0,64,128,192,256,320,384,448},{32,96,160,224,288,352,416,480},{1,65,12..., dimensions={0} | all-to-all | bytes 1179648 | tf_op jit(solution)/shard_map/all_to_all | solution.py:384
  (112 shorter events, 61.4 us)
Async XLA Ops:
  0.6 35.8 %copy-start = (bf16[4,32,512]{2,1,0:T(8,128)(2,1)S(1)}, bf16[4,32,512]{2,1,0:T(8,128)(2,1)}, u32[]{:S(2)}) copy-start(bf16[4,32,512]{2,1,0:T(8,128)(2,1)} %param.5) | copy-start | bytes 393220
  0.6 33.3 %collective-permute-start = (bf16[4096,512]{1,0:T(8,128)(2,1)}, bf16[4096,512]{1,0:T(8,128)(2,1)}, u32[]{:S(2)}, u32[]{:S(2)}) collective-permute-start(bf16[4096,512]{1,0:T(8,128)(2,1)} %bitcast.1.args_0_), channel_id=1, source_target_pairs={{0,32},{32,0},{64,96},{96,64},{128,160},{160,128},{192,224},{224,1... | collective-permute-start | bytes 12582920 | tf_op jit(solution)/shard_map/ppermute | solution.py:65
  11.3 22.7 %all-to-all-start = ((bf16[8,64,512]{2,1,0:T(8,128)(2,1)}), bf16[8,64,512]{2,1,0:T(8,128)(2,1)S(1)}, u32[]{:S(2)}, u32[]{:S(2)}) async-start(bf16[8,64,512]{2,1,0:T(8,128)(2,1)} %broadcast_in_dim.75), calls=%async_computation | async-start | bytes 1048576 | tf_op jit(solution)/shard_map/all_to_all | solution.py:276
  17.4 12.0 %collective-permute-start.1 = (f32[1,4608]{1,0:T(1,128)S(1)}, f32[1,4608]{1,0:T(1,128)S(1)}, u32[]{:S(2)}, u32[]{:S(2)}) collective-permute-start(f32[1,4608]{1,0:T(1,128)S(1)} %pad_maximum_fusion.4), channel_id=1, source_target_pairs={{0,64},{32,96},{64,0},{96,32},{128,192},{160,224},{192,128},{224,1... | collective-permute-start | bytes 55304 | tf_op jit(solution)/shard_map/ppermute | solution.py:65
  20.8 25.4 %collective-permute-start.3 = (f32[1,4608]{1,0:T(1,128)S(1)}, f32[1,4608]{1,0:T(1,128)S(1)}, u32[]{:S(2)}, u32[]{:S(2)}) collective-permute-start(f32[1,4608]{1,0:T(1,128)S(1)} %pad_maximum_fusion.4), channel_id=1, source_target_pairs={{0,32},{32,0},{64,96},{96,64},{128,160},{160,128},{192,224},{224,1... | collective-permute-start | bytes 55304 | tf_op jit(solution)/shard_map/ppermute | solution.py:65
  34.0 12.2 %collective-permute-start.4 = (f32[1,4608]{1,0:T(1,128)S(1)}, f32[1,4608]{1,0:T(1,128)S(1)}, u32[]{:S(2)}, u32[]{:S(2)}) collective-permute-start(f32[1,4608]{1,0:T(1,128)S(1)} %collective-permute-done.1), channel_id=1, source_target_pairs={{0,32},{32,0},{64,96},{96,64},{128,160},{160,128},{192,224},{224,1... | collective-permute-start | bytes 55304 | tf_op jit(solution)/shard_map/ppermute | solution.py:65
  37.2 61.7 %collective-permute-start.2 = (bf16[4096,512]{1,0:T(8,128)(2,1)}, bf16[4096,512]{1,0:T(8,128)(2,1)}, u32[]{:S(2)}, u32[]{:S(2)}) collective-permute-start(bf16[4096,512]{1,0:T(8,128)(2,1)} %bitcast.1.args_0_), channel_id=1, source_target_pairs={{0,64},{64,0},{128,192},{192,128},{256,320},{320,256},{384,448},{4... | collective-permute-start | bytes 12582920 | tf_op jit(solution)/shard_map/ppermute | solution.py:282
  41.6 4.6 copy-start.10
  41.6 31.3 %all-to-all-start.1 = ((bf16[4,8,64,512]{3,2,1,0:T(8,128)(2,1)}), bf16[4,8,64,512]{3,2,1,0:T(8,128)(2,1)}, u32[]{:S(2)}, u32[]{:S(2)}) async-start(bf16[4,8,64,512]{3,2,1,0:T(8,128)(2,1)} %broadcast_in_dim.78), calls=%async_computation.1 | async-start | bytes 4194304 | tf_op jit(solution)/shard_map/all_to_all | solution.py:57
  72.8 9.5 %collective-permute-start.5 = (bf16[4,8,64,512]{3,2,1,0:T(8,128)(2,1)}, bf16[4,8,64,512]{3,2,1,0:T(8,128)(2,1)}, u32[]{:S(2)}, u32[]{:S(2)}) collective-permute-start(bf16[4,8,64,512]{3,2,1,0:T(8,128)(2,1)} %all-to-all-done.1), channel_id=1, source_target_pairs={{0,32},{32,0},{64,96},{96,64},{128,160},{160,128},{192,224},{224,1... | collective-permute-start | bytes 6291464 | tf_op jit(solution)/shard_map/ppermute | solution.py:65
  75.4 19.2 %all-to-all-start.2 = ((bf16[8,32,512]{2,1,0:T(8,128)(2,1)}), bf16[8,32,512]{2,1,0:T(8,128)(2,1)S(1)}, u32[]{:S(2)}, u32[]{:S(2)}) async-start(bf16[8,32,512]{2,1,0:T(8,128)(2,1)} %spread.4), calls=%async_computation.2 | async-start | bytes 524288 | tf_op jit(solution)/shard_map/all_to_all | solution.py:57
  94.8 2.2 copy-start.2
  98.9 16.5 %collective-permute-start.6 = (bf16[4096,512]{1,0:T(8,128)(2,1)}, bf16[4096,512]{1,0:T(8,128)(2,1)}, u32[]{:S(2)}, u32[]{:S(2)}) collective-permute-start(bf16[4096,512]{1,0:T(8,128)(2,1)} %collective-permute-done.2.args_2_.args_4_), channel_id=1, source_target_pairs={{0,32},{64,96},{128,160},{192,224},{256,288},{320,352},{384,416},{... | collective-permute-start | bytes 12582920 | tf_op jit(solution)/shard_map/ppermute | solution.py:331
  100.2 49.6 %collective-permute-start.7 = (bf16[4096,512]{1,0:T(8,128)(2,1)}, bf16[4096,512]{1,0:T(8,128)(2,1)}, u32[]{:S(2)}, u32[]{:S(2)}) collective-permute-start(bf16[4096,512]{1,0:T(8,128)(2,1)} %bitcast.1.args_0_), channel_id=1, source_target_pairs={{32,96},{96,32},{160,224},{224,160},{288,352},{352,288},{416,480},... | collective-permute-start | bytes 12582920 | tf_op jit(solution)/shard_map/ppermute | solution.py:293
  102.4 12.9 %all-to-all-start.3 = ((bf16[8,32,512]{2,1,0:T(8,128)(2,1)}), bf16[8,32,512]{2,1,0:T(8,128)(2,1)S(1)}, u32[]{:S(2)}, u32[]{:S(2)}) async-start(bf16[8,32,512]{2,1,0:T(8,128)(2,1)} %get-tuple-element.122), calls=%async_computation.3 | async-start | bytes 524288 | tf_op jit(solution)/shard_map/all_to_all | solution.py:57
  118.5 12.8 %all-to-all-start.4 = ((bf16[8,32,512]{2,1,0:T(8,128)(2,1)}), bf16[8,32,512]{2,1,0:T(8,128)(2,1)S(1)}, u32[]{:S(2)}, u32[]{:S(2)}) async-start(bf16[8,32,512]{2,1,0:T(8,128)(2,1)} %get-tuple-element.126), calls=%async_computation.4 | async-start | bytes 524288 | tf_op jit(solution)/shard_map/all_to_all | solution.py:57
  131.3 2.2 copy-start.3
  149.7 15.9 %collective-permute-start.8 = (bf16[4096,512]{1,0:T(8,128)(2,1)}, bf16[4096,512]{1,0:T(8,128)(2,1)}, u32[]{:S(2)}, u32[]{:S(2)}) collective-permute-start(bf16[4096,512]{1,0:T(8,128)(2,1)} %collective-permute-done.7.args_4_), channel_id=1, source_target_pairs={{32,0},{96,64},{160,128},{224,192},{288,256},{352,320},{416,384},{... | collective-permute-start | bytes 12582920 | tf_op jit(solution)/shard_map/ppermute | solution.py:335
  153.0 12.7 %all-to-all-start.5 = ((bf16[8,32,512]{2,1,0:T(8,128)(2,1)}), bf16[8,32,512]{2,1,0:T(8,128)(2,1)S(1)}, u32[]{:S(2)}, u32[]{:S(2)}) async-start(bf16[8,32,512]{2,1,0:T(8,128)(2,1)} %get-tuple-element.130), calls=%async_computation.5 | async-start | bytes 524288 | tf_op jit(solution)/shard_map/all_to_all | solution.py:57
  168.8 12.7 %all-to-all-start.6 = ((bf16[8,32,512]{2,1,0:T(8,128)(2,1)}), bf16[8,32,512]{2,1,0:T(8,128)(2,1)S(1)}, u32[]{:S(2)}, u32[]{:S(2)}) async-start(bf16[8,32,512]{2,1,0:T(8,128)(2,1)} %get-tuple-element.133), calls=%async_computation.6 | async-start | bytes 524288 | tf_op jit(solution)/shard_map/all_to_all | solution.py:57
  181.4 2.2 copy-start.4
  183.6 14.0 %copy-start.6 = (bf16[4096,512]{1,0:T(8,128)(2,1)S(1)}, bf16[4096,512]{1,0:T(8,128)(2,1)}, u32[]{:S(2)}) copy-start(bf16[4096,512]{1,0:T(8,128)(2,1)} %get-tuple-element.151.weight_ref) | copy-start | bytes 12582916
  197.7 12.8 %copy-start.5 = (bf16[8,2,4,64,512]{4,3,2,1,0:T(8,128)(2,1)S(1)}, bf16[8,2,4,64,512]{4,3,2,1,0:T(8,128)(2,1)}, u32[]{:S(2)}) copy-start(bf16[8,2,4,64,512]{4,3,2,1,0:T(8,128)(2,1)} %copy.46) | copy-start | bytes 12582916
  210.4 14.4 %copy-start.9 = (bf16[4096,512]{1,0:T(8,128)(2,1)S(1)}, bf16[4096,512]{1,0:T(8,128)(2,1)}, u32[]{:S(2)}) copy-start(bf16[4096,512]{1,0:T(8,128)(2,1)} %get-tuple-element.157.weight_ref) | copy-start | bytes 12582916
  226.4 2.3 collective-permute-start.9
  243.5 15.9 %copy-start.7 = (bf16[4096,512]{1,0:T(8,128)(2,1)S(1)}, bf16[4096,512]{1,0:T(8,128)(2,1)}, u32[]{:S(2)}) copy-start(bf16[4096,512]{1,0:T(8,128)(2,1)} %get-tuple-element.163.weight_ref) | copy-start | bytes 12582916
  274.5 14.0 %copy-start.8 = (bf16[4096,512]{1,0:T(8,128)(2,1)S(1)}, bf16[4096,512]{1,0:T(8,128)(2,1)}, u32[]{:S(2)}) copy-start(bf16[4096,512]{1,0:T(8,128)(2,1)} %get-tuple-element.168.weight_ref) | copy-start | bytes 12582916
  341.4 5.8 collective-permute-start.10
  456.9 6.6 %collective-permute-start.11 = (bf16[32,512]{1,0:T(8,128)(2,1)S(1)}, bf16[32,512]{1,0:T(8,128)(2,1)S(1)}, u32[]{:S(2)}, u32[]{:S(2)}) collective-permute-start(bf16[32,512]{1,0:T(8,128)(2,1)S(1)} %get-tuple-element.199), channel_id=1, source_target_pairs={{0,128},{32,160},{64,192},{96,224},{128,256},{160,288},{192,320},{... | collective-permute-start | bytes 98312 | tf_op jit(solution)/shard_map/ppermute | solution.py:343
  555.5 13.8 %collective-permute-start.14 = (bf16[1536,128]{1,0:T(8,128)(2,1)S(1)}, bf16[1536,128]{1,0:T(8,128)(2,1)S(1)}, u32[]{:S(2)}, u32[]{:S(2)}) collective-permute-start(bf16[1536,128]{1,0:T(8,128)(2,1)S(1)} %get-tuple-element.235), channel_id=1, source_target_pairs={{0,24},{8,0},{16,8},{24,16},{1,25},{9,1},{17,9},{25,17},{2,26},{10... | collective-permute-start | bytes 1179656 | tf_op jit(solution)/shard_map/ppermute | solution.py:365
  558.2 11.0 %collective-permute-start.13 = (bf16[1536,128]{1,0:T(8,128)(2,1)S(1)}, bf16[1536,128]{1,0:T(8,128)(2,1)S(1)}, u32[]{:S(2)}, u32[]{:S(2)}) collective-permute-start(bf16[1536,128]{1,0:T(8,128)(2,1)S(1)} %get-tuple-element.234), channel_id=1, source_target_pairs={{0,16},{8,24},{16,0},{24,8},{1,17},{9,25},{17,1},{25,9},{2,18},{10... | collective-permute-start | bytes 1179656 | tf_op jit(solution)/shard_map/ppermute | solution.py:365
  561.3 11.2 %collective-permute-start.12 = (bf16[1536,128]{1,0:T(8,128)(2,1)S(1)}, bf16[1536,128]{1,0:T(8,128)(2,1)S(1)}, u32[]{:S(2)}, u32[]{:S(2)}) collective-permute-start(bf16[1536,128]{1,0:T(8,128)(2,1)S(1)} %get-tuple-element.233), channel_id=1, source_target_pairs={{0,8},{8,16},{16,24},{24,0},{1,9},{9,17},{17,25},{25,1},{2,10},{10... | collective-permute-start | bytes 1179656 | tf_op jit(solution)/shard_map/ppermute | solution.py:365
  564.6 38.9 %all-to-all-start.33 = ((f32[32,8,128]{2,1,0:T(8,128)}), f32[32,8,128]{2,1,0:T(8,128)S(1)}, u32[]{:S(2)}, u32[]{:S(2)}) async-start(f32[32,8,128]{2,1,0:T(8,128)} %broadcast_in_dim_broadcast_in_dim_broadcast_in_dim.3), calls=%async_computation.33 | async-start | bytes 262144 | tf_op jit(solution)/shard_map/all_to_all | solution.py:57
  573.4 37.7 %collective-permute-start.15 = (bf16[8,64,512]{2,1,0:T(8,128)(2,1)S(1)}, bf16[8,64,512]{2,1,0:T(8,128)(2,1)S(1)}, u32[]{:S(2)}, u32[]{:S(2)}) collective-permute-start(bf16[8,64,512]{2,1,0:T(8,128)(2,1)S(1)} %get-tuple-element.224), channel_id=1, source_target_pairs={{0,32},{32,0},{64,96},{96,64},{128,160},{160,128},{192,224},{224,1... | collective-permute-start | bytes 1572872 | tf_op jit(solution)/shard_map/ppermute | solution.py:65
  603.5 7.6 %collective-permute-start.16 = (f32[8,128]{1,0:T(8,128)S(1)}, f32[8,128]{1,0:T(8,128)S(1)}, u32[]{:S(2)}, u32[]{:S(2)}) collective-permute-start(f32[8,128]{1,0:T(8,128)S(1)} %reduce_sum.37), channel_id=1, source_target_pairs={{0,32},{32,0},{64,96},{96,64},{128,160},{160,128},{192,224},{224,1... | collective-permute-start | bytes 12296 | tf_op jit(solution)/shard_map/ppermute | solution.py:65
  611.2 29.4 %copy-start.1 = (bf16[4,32,512]{2,1,0:T(8,128)(2,1)S(1)}, bf16[4,32,512]{2,1,0:T(8,128)(2,1)}, u32[]{:S(2)}) copy-start(bf16[4,32,512]{2,1,0:T(8,128)(2,1)} %param.5) | copy-start | bytes 393220

commit v10 on v9

--- a/solution.py
+++ b/solution.py
@@ -63,6 +63,17 @@
 
 def crossed(value, mask):
     return lax.ppermute(value, "section", [(i, i ^ mask) for i in range(lax.axis_size("section"))])
+
+
+def doubled(value):
+    count, position = lax.axis_size("tp"), lax.axis_index("tp")
+    value, mask = value[None], 1
+    while mask < count:
+        other = lax.ppermute(value, "tp", [(i, i ^ mask) for i in range(count)])
+        upper = position & mask != 0
+        value = jnp.concatenate([jnp.where(upper, other, value), jnp.where(upper, value, other)], axis=0)
+        mask *= 2
+    return value
 
 
 VMEM = pl.BlockSpec(memory_space=pltpu.VMEM)
@@ -276,8 +287,8 @@
     along_z = lax.all_to_all(
         copies_of(rotation, planes), "section", 0, 0, axis_index_groups=same_core, tiled=True
     )
-    along_z, by1, params_by2 = lax.optimization_barrier((along_z, by1, params_by2))
     params_by3 = crossed(params_by2, 1)
+    along_z, by1, params_by2, params_by3 = lax.optimization_barrier((along_z, by1, params_by2, params_by3))
     own_now, _ = lax.optimization_barrier((own, params_by2))
     even_mine = lax.ppermute(own_now, "section", [(i, i ^ 2) for i in range(0, sections, 2)])
     found = jnp.concatenate([params, params_by1, params_by2, params_by3], axis=0)
@@ -286,8 +297,11 @@
 
     along_x = gather(along_z, "dp")
     stream = lax.dynamic_index_in_dim(hidden_in, place, 0, keepdims=False)
-    copies = spread(stream, tensor)
-    along_x, gains, scales, stream, copies = lax.optimization_barrier((along_x, gains, scales, stream, copies))
+    stream, _ = lax.optimization_barrier((stream, along_z))
+    first_rows = doubled(stream)
+    along_x, gains, scales, stream, first_rows = lax.optimization_barrier(
+        (along_x, gains, scales, stream, first_rows)
+    )
     other_rows = crossed(along_x, 1)
     own_later, _ = lax.optimization_barrier((own, other_rows))
     odd_mine = lax.ppermute(own_later, "section", [(i, i ^ 2) for i in range(1, sections, 2)])
@@ -311,7 +325,7 @@
         for layer in range(STAGE):
             last = stage == stages - 1 and layer == STAGE - 1
             gain, scale = gains[layer : layer + 1], scales[layer : layer + 1]
-            rows = exchange(copies, "tp")
+            rows = exchange(copies, "tp") if stage or layer else first_rows
             if stage == 0 and layer in (1, 2):
                 odd = layer - 1
                 mine, other = sources[4:] if odd else sources[2:4]

time: 644 us -> 636 us (0.988)
  waiting for transfers between devices: 88 us -> 64 us
  starting transfers between devices: 120 us -> 141 us
    all_to_all x7 -> x6, waiting for transfers between devices: 56.2 us -> 26.9 us  [exchange(): return lax.all_to_all(copies, axis, 0, 0, tiled=True)]
    ppermute x0 -> x3, starting transfers between devices: none -> 15.6 us  [doubled(): other = lax.ppermute(value, 'tp', [(i, i ^ mask) for i in range(count)])]
    all_to_all x7 -> x6, starting transfers between devices: 29.8 us -> 29.2 us  [exchange(): return lax.all_to_all(copies, axis, 0, 0, tiled=True)]
  transfers between devices with their start and end apart: 25 -> 27, of which waited for: 14 -> 19; matrix products, arithmetic and copies ran while one was open for 4% -> 4% of each run, Pallas kernels for 1% -> 1%
where the time goes in v10:
time: 636 us; the launch traced here: 634 us
  blocking collectives  353 us (56%)
  starting transfers between devices  141 us (22%)
  waiting for transfers between devices  64 us (10%)
  Pallas kernels  40.1 us (6%)
  other arithmetic  21.7 us (3%)
  local copies, waits for them, and re-layouts  10.8 us (2%)
    all_to_all x26, blocking collectives, exchange(): return lax.all_to_all(copies, axis, 0, 0, tiled=True)  322 us
    ppermute x7, starting transfers between devices, crossed(): lax.ppermute(value, 'section', [(i, i ^ mask) for i in range(lax.axis_siz...  56.6 us
    all_to_all x1, blocking collectives, local(): lax.all_to_all(sent, 'section', 0, 0, axis_index_groups=same_core, tiled=...  30.3 us
    all_to_all x6, starting transfers between devices, exchange(): return lax.all_to_all(copies, axis, 0, 0, tiled=True)  29.2 us
    all_to_all x6, waiting for transfers between devices, exchange(): return lax.all_to_all(copies, axis, 0, 0, tiled=True)  26.9 us
    pallas_call x16, Pallas kernels, rotate(): pl.pallas_call(functools.partial(rotate_kernel, layer, last), out_shape=s...  19.4 us
    ppermute x3, starting transfers between devices, doubled(): other = lax.ppermute(value, 'tp', [(i, i ^ mask) for i in range(count)])  15.6 us
    select_n x2, other arithmetic, local(): jnp.where(place // 2 == 0, far, near)  14.3 us
  transfers between devices with their start and end apart: 27, of which 19 were waited for; matrix products, arithmetic and copies ran while one was open for 4% of the time, Pallas kernels for 1%

profile of v10, /device:TPU:1, one launch (start us, length us, event | category | flops | bytes accessed | tf_op | source)
XLA Modules:
  0.0 633.6 jit_solution(11913428216959848091)
XLA Ops:
  0.6 8.9 %collective-permute-start = (bf16[4096,512]{1,0:T(8,128)(2,1)}, bf16[4096,512]{1,0:T(8,128)(2,1)}, u32[]{:S(2)}, u32[]{:S(2)}) collective-permute-start(bf16[4096,512]{1,0:T(8,128)(2,1)} %bitcast.1.args_0_), channel_id=1, source_target_pairs={{0,32},{32,0},{64,96},{96,64},{128,160},{160,128},{192,224},{224,1... | collective-permute-start | bytes 12582920 | tf_op jit(solution)/shard_map/ppermute | solution.py:65
  11.3 4.7 all-to-all-start
  17.4 3.4 collective-permute-start.1
  20.8 2.8 collective-permute-start.4
  23.6 5.8 collective-permute-done.1
  29.4 3.4 collective-permute-start.2
  34.0 2.8 collective-permute-start.3
  38.4 4.6 all-to-all-start.1
  43.0 3.2 collective-permute-start.5
  48.1 4.2 collective-permute-start.6
  54.5 8.2 %collective-permute-start.7 = (bf16[4,32,512]{2,1,0:T(8,128)(2,1)S(1)}, bf16[4,32,512]{2,1,0:T(8,128)(2,1)S(1)}, u32[]{:S(2)}, u32[]{:S(2)}) collective-permute-start(bf16[4,32,512]{2,1,0:T(8,128)(2,1)S(1)} %pad_maximum_fusion.3), channel_id=1, source_target_pairs={{0,4},{1,5},{2,6},{3,7},{4,0},{5,1},{6,2},{7,3},{8,12},{9,13},{10,... | collective-permute-start | bytes 393224 | tf_op jit(solution)/shard_map/ppermute | solution.py:72
  62.7 2.3 collective-permute-done.7
  65.1 4.1 all-to-all-done.1
  69.2 3.1 collective-permute-start.8
  72.4 4.0 collective-permute-done.8
  76.4 2.5 select_bitcast_fusion.1
  85.2 6.8 %all-to-all-start.2 = ((bf16[8,32,512]{2,1,0:T(8,128)(2,1)}), bf16[8,32,512]{2,1,0:T(8,128)(2,1)S(1)}, u32[]{:S(2)}, u32[]{:S(2)}) async-start(bf16[8,32,512]{2,1,0:T(8,128)(2,1)} %get-tuple-element.126), calls=%async_computation.2 | async-start | bytes 524288 | tf_op jit(solution)/shard_map/all_to_all | solution.py:57
  92.0 9.3 %all-to-all-done.2.args_6_ = bf16[8,32,512]{2,1,0:T(8,128)(2,1)S(1)} async-done(((bf16[8,32,512]{2,1,0:T(8,128)(2,1)}), bf16[8,32,512]{2,1,0:T(8,128)(2,1)S(1)}, u32[]{:S(2)}, u32[]{:S(2)}) %all-to-all-start.2) | async-done | bytes 262176 | tf_op jit(solution)/shard_map/all_to_all | solution.py:57
  101.3 3.1 project_from.2
  104.5 3.4 all-to-all-start.3
  107.9 8.0 %broadcast_select_fusion.6 = (bf16[4096,512]{1,0:T(8,128)(2,1)}, bf16[4096,512]{1,0:T(8,128)(2,1)}) fusion(pred[]{:T(512)S(6)} %eq.50, bf16[4096,512]{1,0:T(8,128)(2,1)} %collective-permute-done.args_1_, pred[]{:T(512)S(6)} %eq.49, bf16[4096,512]{1,0:T(8,128)(2,1)} %collective-permute-done.3.args_2_.args_4_, ...), kind=kLoop, calls=%fused_computation.7 | loop fusion | flops 8388608 | bytes 25165826 | tf_op jit(solution)/shard_map/jit(_where)/select_n | solution.py:334
  121.3 11.5 %collective-permute-done.10.args_4_ = bf16[4096,512]{1,0:T(8,128)(2,1)} collective-permute-done((bf16[4096,512]{1,0:T(8,128)(2,1)}, bf16[4096,512]{1,0:T(8,128)(2,1)}, u32[]{:S(2)}, u32[]{:S(2)}) %collective-permute-start.10) | collective-permute-done | bytes 4194336 | tf_op jit(solution)/shard_map/ppermute | solution.py:307
  132.8 3.2 collective-permute-start.11
  136.0 6.8 %all-to-all-start.4 = ((bf16[8,32,512]{2,1,0:T(8,128)(2,1)}), bf16[8,32,512]{2,1,0:T(8,128)(2,1)S(1)}, u32[]{:S(2)}, u32[]{:S(2)}) async-start(bf16[8,32,512]{2,1,0:T(8,128)(2,1)} %get-tuple-element.134), calls=%async_computation.4 | async-start | bytes 524288 | tf_op jit(solution)/shard_map/all_to_all | solution.py:57
  142.9 9.3 %all-to-all-done.4.args_6_ = bf16[8,32,512]{2,1,0:T(8,128)(2,1)S(1)} async-done(((bf16[8,32,512]{2,1,0:T(8,128)(2,1)}), bf16[8,32,512]{2,1,0:T(8,128)(2,1)S(1)}, u32[]{:S(2)}, u32[]{:S(2)}) %all-to-all-start.4) | async-done | bytes 262176 | tf_op jit(solution)/shard_map/all_to_all | solution.py:57
  152.2 3.2 project_from.3
  155.4 3.4 all-to-all-start.5
  158.8 6.3 broadcast_select_fusion.4
  165.1 2.9 all-to-all-done.5.rows_ref
  171.4 12.9 %all_to_all.170.quant_ref = bf16[8,32,512]{2,1,0:T(8,128)(2,1)S(1)} all-to-all(bf16[8,32,512]{2,1,0:T(8,128)(2,1)S(1)} %get-tuple-element.154), channel_id=1, replica_groups=mesh['section'=16,'dp'=4,'tp'=8] {'tp'}, dimensions={0} | all-to-all | bytes 524288 | tf_op jit(solution)/shard_map/all_to_all | solution.py:57
  185.1 12.2 %all_to_all.171.rows_ref = bf16[8,32,512]{2,1,0:T(8,128)(2,1)S(1)} all-to-all(bf16[8,32,512]{2,1,0:T(8,128)(2,1)S(1)} %get-tuple-element.157), channel_id=1, replica_groups=mesh['section'=16,'dp'=4,'tp'=8] {'tp'}, dimensions={0} | all-to-all | bytes 524288 | tf_op jit(solution)/shard_map/all_to_all | solution.py:57
  198.5 13.5 %all_to_all.172.quant_ref = bf16[8,32,512]{2,1,0:T(8,128)(2,1)S(1)} all-to-all(bf16[8,32,512]{2,1,0:T(8,128)(2,1)S(1)} %get-tuple-element.160), channel_id=1, replica_groups=mesh['section'=16,'dp'=4,'tp'=8] {'tp'}, dimensions={0} | all-to-all | bytes 524288 | tf_op jit(solution)/shard_map/all_to_all | solution.py:57
  216.8 14.1 %all_to_all.173.rows_ref = bf16[8,32,512]{2,1,0:T(8,128)(2,1)S(1)} all-to-all(bf16[8,32,512]{2,1,0:T(8,128)(2,1)S(1)} %spread.3), channel_id=1, replica_groups=mesh['section'=16,'dp'=4,'tp'=8] {'tp'}, dimensions={0} | all-to-all | bytes 524288 | tf_op jit(solution)/shard_map/all_to_all | solution.py:57
  232.0 12.7 %all_to_all.174.quant_ref = bf16[8,32,512]{2,1,0:T(8,128)(2,1)S(1)} all-to-all(bf16[8,32,512]{2,1,0:T(8,128)(2,1)S(1)} %get-tuple-element.166), channel_id=1, replica_groups=mesh['section'=16,'dp'=4,'tp'=8] {'tp'}, dimensions={0} | all-to-all | bytes 524288 | tf_op jit(solution)/shard_map/all_to_all | solution.py:57
  245.6 12.0 %all_to_all.175.rows_ref = bf16[8,32,512]{2,1,0:T(8,128)(2,1)S(1)} all-to-all(bf16[8,32,512]{2,1,0:T(8,128)(2,1)S(1)} %get-tuple-element.168), channel_id=1, replica_groups=mesh['section'=16,'dp'=4,'tp'=8] {'tp'}, dimensions={0} | all-to-all | bytes 524288 | tf_op jit(solution)/shard_map/all_to_all | solution.py:57
  258.7 12.2 %all_to_all.176.quant_ref = bf16[8,32,512]{2,1,0:T(8,128)(2,1)S(1)} all-to-all(bf16[8,32,512]{2,1,0:T(8,128)(2,1)S(1)} %get-tuple-element.171), channel_id=1, replica_groups=mesh['section'=16,'dp'=4,'tp'=8] {'tp'}, dimensions={0} | all-to-all | bytes 524288 | tf_op jit(solution)/shard_map/all_to_all | solution.py:57
  271.7 11.8 %all_to_all.177.rows_ref = bf16[8,32,512]{2,1,0:T(8,128)(2,1)S(1)} all-to-all(bf16[8,32,512]{2,1,0:T(8,128)(2,1)S(1)} %get-tuple-element.174), channel_id=1, replica_groups=mesh['section'=16,'dp'=4,'tp'=8] {'tp'}, dimensions={0} | all-to-all | bytes 524288 | tf_op jit(solution)/shard_map/all_to_all | solution.py:57
  284.7 11.7 %all_to_all.178.quant_ref = bf16[8,32,512]{2,1,0:T(8,128)(2,1)S(1)} all-to-all(bf16[8,32,512]{2,1,0:T(8,128)(2,1)S(1)} %get-tuple-element.177), channel_id=1, replica_groups=mesh['section'=16,'dp'=4,'tp'=8] {'tp'}, dimensions={0} | all-to-all | bytes 524288 | tf_op jit(solution)/shard_map/all_to_all | solution.py:57
  297.3 11.7 %all_to_all.179.rows_ref = bf16[8,32,512]{2,1,0:T(8,128)(2,1)S(1)} all-to-all(bf16[8,32,512]{2,1,0:T(8,128)(2,1)S(1)} %get-tuple-element.179), channel_id=1, replica_groups=mesh['section'=16,'dp'=4,'tp'=8] {'tp'}, dimensions={0} | all-to-all | bytes 524288 | tf_op jit(solution)/shard_map/all_to_all | solution.py:57
  310.1 11.7 %all_to_all.180.quant_ref = bf16[8,32,512]{2,1,0:T(8,128)(2,1)S(1)} all-to-all(bf16[8,32,512]{2,1,0:T(8,128)(2,1)S(1)} %get-tuple-element.182), channel_id=1, replica_groups=mesh['section'=16,'dp'=4,'tp'=8] {'tp'}, dimensions={0} | all-to-all | bytes 524288 | tf_op jit(solution)/shard_map/all_to_all | solution.py:57
  323.4 6.0 collective-permute-start.13
  330.5 11.7 %all_to_all.181.rows_ref = bf16[8,32,512]{2,1,0:T(8,128)(2,1)S(1)} all-to-all(bf16[8,32,512]{2,1,0:T(8,128)(2,1)S(1)} %spread.4), channel_id=1, replica_groups=mesh['section'=16,'dp'=4,'tp'=8] {'tp'}, dimensions={0} | all-to-all | bytes 524288 | tf_op jit(solution)/shard_map/all_to_all | solution.py:57
  343.3 12.0 %all_to_all.182.quant_ref = bf16[8,32,512]{2,1,0:T(8,128)(2,1)S(1)} all-to-all(bf16[8,32,512]{2,1,0:T(8,128)(2,1)S(1)} %get-tuple-element.187), channel_id=1, replica_groups=mesh['section'=16,'dp'=4,'tp'=8] {'tp'}, dimensions={0} | all-to-all | bytes 524288 | tf_op jit(solution)/shard_map/all_to_all | solution.py:57
  356.2 13.6 %all_to_all.183.rows_ref = bf16[8,32,512]{2,1,0:T(8,128)(2,1)S(1)} all-to-all(bf16[8,32,512]{2,1,0:T(8,128)(2,1)S(1)} %get-tuple-element.188), channel_id=1, replica_groups=mesh['section'=16,'dp'=4,'tp'=8] {'tp'}, dimensions={0} | all-to-all | bytes 524288 | tf_op jit(solution)/shard_map/all_to_all | solution.py:57
  371.0 14.8 %all_to_all.184.quant_ref = bf16[8,32,512]{2,1,0:T(8,128)(2,1)S(1)} all-to-all(bf16[8,32,512]{2,1,0:T(8,128)(2,1)S(1)} %get-tuple-element.191), channel_id=1, replica_groups=mesh['section'=16,'dp'=4,'tp'=8] {'tp'}, dimensions={0} | all-to-all | bytes 524288 | tf_op jit(solution)/shard_map/all_to_all | solution.py:57
  386.6 13.4 %all_to_all.185.rows_ref = bf16[8,32,512]{2,1,0:T(8,128)(2,1)S(1)} all-to-all(bf16[8,32,512]{2,1,0:T(8,128)(2,1)S(1)} %get-tuple-element.193), channel_id=1, replica_groups=mesh['section'=16,'dp'=4,'tp'=8] {'tp'}, dimensions={0} | all-to-all | bytes 524288 | tf_op jit(solution)/shard_map/all_to_all | solution.py:57
  401.2 12.2 %all_to_all.186.quant_ref = bf16[8,32,512]{2,1,0:T(8,128)(2,1)S(1)} all-to-all(bf16[8,32,512]{2,1,0:T(8,128)(2,1)S(1)} %get-tuple-element.196), channel_id=1, replica_groups=mesh['section'=16,'dp'=4,'tp'=8] {'tp'}, dimensions={0} | all-to-all | bytes 524288 | tf_op jit(solution)/shard_map/all_to_all | solution.py:57
  414.2 12.2 %all_to_all.187.rows_ref = bf16[8,32,512]{2,1,0:T(8,128)(2,1)S(1)} all-to-all(bf16[8,32,512]{2,1,0:T(8,128)(2,1)S(1)} %get-tuple-element.198), channel_id=1, replica_groups=mesh['section'=16,'dp'=4,'tp'=8] {'tp'}, dimensions={0} | all-to-all | bytes 524288 | tf_op jit(solution)/shard_map/all_to_all | solution.py:57
  427.6 11.9 %all_to_all.188.quant_ref = bf16[8,32,512]{2,1,0:T(8,128)(2,1)S(1)} all-to-all(bf16[8,32,512]{2,1,0:T(8,128)(2,1)S(1)} %get-tuple-element.201), channel_id=1, replica_groups=mesh['section'=16,'dp'=4,'tp'=8] {'tp'}, dimensions={0} | all-to-all | bytes 524288 | tf_op jit(solution)/shard_map/all_to_all | solution.py:57
  441.0 4.9 collective-permute-start.14
  446.9 13.3 %all_to_all.189.rows_ref = bf16[8,32,512]{2,1,0:T(8,128)(2,1)S(1)} all-to-all(bf16[8,32,512]{2,1,0:T(8,128)(2,1)S(1)} %spread.5), channel_id=1, replica_groups=mesh['section'=16,'dp'=4,'tp'=8] {'tp'}, dimensions={0} | all-to-all | bytes 524288 | tf_op jit(solution)/shard_map/all_to_all | solution.py:57
  461.3 11.7 %all_to_all.190.quant_ref = bf16[8,32,512]{2,1,0:T(8,128)(2,1)S(1)} all-to-all(bf16[8,32,512]{2,1,0:T(8,128)(2,1)S(1)} %get-tuple-element.206), channel_id=1, replica_groups=mesh['section'=16,'dp'=4,'tp'=8] {'tp'}, dimensions={0} | all-to-all | bytes 524288 | tf_op jit(solution)/shard_map/all_to_all | solution.py:57
  473.9 11.7 %all_to_all.191.rows_ref = bf16[8,32,512]{2,1,0:T(8,128)(2,1)S(1)} all-to-all(bf16[8,32,512]{2,1,0:T(8,128)(2,1)S(1)} %get-tuple-element.207), channel_id=1, replica_groups=mesh['section'=16,'dp'=4,'tp'=8] {'tp'}, dimensions={0} | all-to-all | bytes 524288 | tf_op jit(solution)/shard_map/all_to_all | solution.py:57
  486.8 11.7 %all_to_all.192.quant_ref = bf16[8,32,512]{2,1,0:T(8,128)(2,1)S(1)} all-to-all(bf16[8,32,512]{2,1,0:T(8,128)(2,1)S(1)} %get-tuple-element.210), channel_id=1, replica_groups=mesh['section'=16,'dp'=4,'tp'=8] {'tp'}, dimensions={0} | all-to-all | bytes 524288 | tf_op jit(solution)/shard_map/all_to_all | solution.py:57
  499.4 11.7 %all_to_all.193.rows_ref = bf16[8,32,512]{2,1,0:T(8,128)(2,1)S(1)} all-to-all(bf16[8,32,512]{2,1,0:T(8,128)(2,1)S(1)} %get-tuple-element.212), channel_id=1, replica_groups=mesh['section'=16,'dp'=4,'tp'=8] {'tp'}, dimensions={0} | all-to-all | bytes 524288 | tf_op jit(solution)/shard_map/all_to_all | solution.py:57
  512.2 11.7 %all_to_all.194.quant_ref = bf16[8,32,512]{2,1,0:T(8,128)(2,1)S(1)} all-to-all(bf16[8,32,512]{2,1,0:T(8,128)(2,1)S(1)} %get-tuple-element.215), channel_id=1, replica_groups=mesh['section'=16,'dp'=4,'tp'=8] {'tp'}, dimensions={0} | all-to-all | bytes 524288 | tf_op jit(solution)/shard_map/all_to_all | solution.py:57
  525.4 11.8 %all_to_all.195.rows_ref = bf16[8,32,512]{2,1,0:T(8,128)(2,1)S(1)} all-to-all(bf16[8,32,512]{2,1,0:T(8,128)(2,1)S(1)} %get-tuple-element.217), channel_id=1, replica_groups=mesh['section'=16,'dp'=4,'tp'=8] {'tp'}, dimensions={0} | all-to-all | bytes 524288 | tf_op jit(solution)/shard_map/all_to_all | solution.py:57
  540.2 8.3 %collective-permute-start.17 = (bf16[1536,128]{1,0:T(8,128)(2,1)S(1)}, bf16[1536,128]{1,0:T(8,128)(2,1)S(1)}, u32[]{:S(2)}, u32[]{:S(2)}) collective-permute-start(bf16[1536,128]{1,0:T(8,128)(2,1)S(1)} %get-tuple-element.239), channel_id=1, source_target_pairs={{0,24},{8,0},{16,8},{24,16},{1,25},{9,1},{17,9},{25,17},{2,26},{10... | collective-permute-start | bytes 1179656 | tf_op jit(solution)/shard_map/ppermute | solution.py:379
  550.4 2.5 collective-permute-start.15
  554.3 4.1 all-to-all-start.32
  558.6 4.4 collective-permute-done.15
  564.0 30.7 %collective-permute-start.18 = (bf16[8,64,512]{2,1,0:T(8,128)(2,1)S(1)}, bf16[8,64,512]{2,1,0:T(8,128)(2,1)S(1)}, u32[]{:S(2)}, u32[]{:S(2)}) collective-permute-start(bf16[8,64,512]{2,1,0:T(8,128)(2,1)S(1)} %get-tuple-element.228), channel_id=1, source_target_pairs={{0,32},{32,0},{64,96},{96,64},{128,160},{160,128},{192,224},{224,1... | collective-permute-start | bytes 1572872 | tf_op jit(solution)/shard_map/ppermute | solution.py:65
  594.7 4.3 collective-permute-start.19
  600.2 30.3 %all_to_all.196 = bf16[8,72,512]{2,1,0:T(8,128)(2,1)S(1)} all-to-all(bf16[8,72,512]{2,1,0:T(8,128)(2,1)S(1)} %pad_maximum_fusion.1), channel_id=1, replica_groups={{0,64,128,192,256,320,384,448},{32,96,160,224,288,352,416,480},{1,65,12..., dimensions={0} | all-to-all | bytes 1179648 | tf_op jit(solution)/shard_map/all_to_all | solution.py:398
  (121 shorter events, 67.1 us)
Async XLA Ops:
  0.6 32.2 %copy-start = (bf16[4,32,512]{2,1,0:T(8,128)(2,1)S(1)}, bf16[4,32,512]{2,1,0:T(8,128)(2,1)}, u32[]{:S(2)}) copy-start(bf16[4,32,512]{2,1,0:T(8,128)(2,1)} %param.5) | copy-start | bytes 393220
  0.6 33.3 %collective-permute-start = (bf16[4096,512]{1,0:T(8,128)(2,1)}, bf16[4096,512]{1,0:T(8,128)(2,1)}, u32[]{:S(2)}, u32[]{:S(2)}) collective-permute-start(bf16[4096,512]{1,0:T(8,128)(2,1)} %bitcast.1.args_0_), channel_id=1, source_target_pairs={{0,32},{32,0},{64,96},{96,64},{128,160},{160,128},{192,224},{224,1... | collective-permute-start | bytes 12582920 | tf_op jit(solution)/shard_map/ppermute | solution.py:65
  11.3 22.7 %all-to-all-start = ((bf16[8,64,512]{2,1,0:T(8,128)(2,1)}), bf16[8,64,512]{2,1,0:T(8,128)(2,1)S(1)}, u32[]{:S(2)}, u32[]{:S(2)}) async-start(bf16[8,64,512]{2,1,0:T(8,128)(2,1)} %broadcast_in_dim.78), calls=%async_computation | async-start | bytes 1048576 | tf_op jit(solution)/shard_map/all_to_all | solution.py:287
  17.4 12.0 %collective-permute-start.1 = (f32[1,4608]{1,0:T(1,128)S(1)}, f32[1,4608]{1,0:T(1,128)S(1)}, u32[]{:S(2)}, u32[]{:S(2)}) collective-permute-start(f32[1,4608]{1,0:T(1,128)S(1)} %pad_maximum_fusion.7), channel_id=1, source_target_pairs={{0,64},{32,96},{64,0},{96,32},{128,192},{160,224},{192,128},{224,1... | collective-permute-start | bytes 55304 | tf_op jit(solution)/shard_map/ppermute | solution.py:65
  20.8 25.4 %collective-permute-start.4 = (f32[1,4608]{1,0:T(1,128)S(1)}, f32[1,4608]{1,0:T(1,128)S(1)}, u32[]{:S(2)}, u32[]{:S(2)}) collective-permute-start(f32[1,4608]{1,0:T(1,128)S(1)} %pad_maximum_fusion.7), channel_id=1, source_target_pairs={{0,32},{32,0},{64,96},{96,64},{128,160},{160,128},{192,224},{224,1... | collective-permute-start | bytes 55304 | tf_op jit(solution)/shard_map/ppermute | solution.py:65
  29.4 4.2 collective-permute-start.2
  34.0 47.9 %collective-permute-start.3 = (bf16[4096,512]{1,0:T(8,128)(2,1)}, bf16[4096,512]{1,0:T(8,128)(2,1)}, u32[]{:S(2)}, u32[]{:S(2)}) collective-permute-start(bf16[4096,512]{1,0:T(8,128)(2,1)} %bitcast.1.args_0_), channel_id=1, source_target_pairs={{0,64},{64,0},{128,192},{192,128},{256,320},{320,256},{384,448},{4... | collective-permute-start | bytes 12582920 | tf_op jit(solution)/shard_map/ppermute | solution.py:293
  38.4 7.9 %copy-start.10 = (f32[1,4096]{1,0:T(1,128)S(1)}, f32[1,4096]{1,0:T(1,128)}, u32[]{:S(2)}) copy-start(f32[1,4096]{1,0:T(1,128)} %param.8) | copy-start | bytes 49156
  38.4 30.8 %all-to-all-start.1 = ((bf16[4,8,64,512]{3,2,1,0:T(8,128)(2,1)}), bf16[4,8,64,512]{3,2,1,0:T(8,128)(2,1)}, u32[]{:S(2)}, u32[]{:S(2)}) async-start(bf16[4,8,64,512]{3,2,1,0:T(8,128)(2,1)} %broadcast_in_dim.81), calls=%async_computation.1 | async-start | bytes 4194304 | tf_op jit(solution)/shard_map/all_to_all | solution.py:57
  43.0 5.1 collective-permute-start.5
  48.1 6.3 collective-permute-start.6
  54.5 10.6 %collective-permute-start.7 = (bf16[4,32,512]{2,1,0:T(8,128)(2,1)S(1)}, bf16[4,32,512]{2,1,0:T(8,128)(2,1)S(1)}, u32[]{:S(2)}, u32[]{:S(2)}) collective-permute-start(bf16[4,32,512]{2,1,0:T(8,128)(2,1)S(1)} %pad_maximum_fusion.3), channel_id=1, source_target_pairs={{0,4},{1,5},{2,6},{3,7},{4,0},{5,1},{6,2},{7,3},{8,12},{9,13},{10,... | collective-permute-start | bytes 393224 | tf_op jit(solution)/shard_map/ppermute | solution.py:72
  69.2 7.2 %collective-permute-start.8 = (bf16[4,8,64,512]{3,2,1,0:T(8,128)(2,1)}, bf16[4,8,64,512]{3,2,1,0:T(8,128)(2,1)}, u32[]{:S(2)}, u32[]{:S(2)}) collective-permute-start(bf16[4,8,64,512]{3,2,1,0:T(8,128)(2,1)} %all-to-all-done.1), channel_id=1, source_target_pairs={{0,32},{32,0},{64,96},{96,64},{128,160},{160,128},{192,224},{224,1... | collective-permute-start | bytes 6291464 | tf_op jit(solution)/shard_map/ppermute | solution.py:65
  79.8 2.2 copy-start.2
  81.9 19.4 %collective-permute-start.9 = (bf16[4096,512]{1,0:T(8,128)(2,1)}, bf16[4096,512]{1,0:T(8,128)(2,1)}, u32[]{:S(2)}, u32[]{:S(2)}) collective-permute-start(bf16[4096,512]{1,0:T(8,128)(2,1)} %collective-permute-done.3.args_2_.args_4_), channel_id=1, source_target_pairs={{0,32},{64,96},{128,160},{192,224},{256,288},{320,352},{384,416},{... | collective-permute-start | bytes 12582920 | tf_op jit(solution)/shard_map/ppermute | solution.py:345
  83.2 49.6 %collective-permute-start.10 = (bf16[4096,512]{1,0:T(8,128)(2,1)}, bf16[4096,512]{1,0:T(8,128)(2,1)}, u32[]{:S(2)}, u32[]{:S(2)}) collective-permute-start(bf16[4096,512]{1,0:T(8,128)(2,1)} %bitcast.1.args_0_), channel_id=1, source_target_pairs={{32,96},{96,32},{160,224},{224,160},{288,352},{352,288},{416,480},... | collective-permute-start | bytes 12582920 | tf_op jit(solution)/shard_map/ppermute | solution.py:307
  85.2 16.2 %all-to-all-start.2 = ((bf16[8,32,512]{2,1,0:T(8,128)(2,1)}), bf16[8,32,512]{2,1,0:T(8,128)(2,1)S(1)}, u32[]{:S(2)}, u32[]{:S(2)}) async-start(bf16[8,32,512]{2,1,0:T(8,128)(2,1)} %get-tuple-element.126), calls=%async_computation.2 | async-start | bytes 524288 | tf_op jit(solution)/shard_map/all_to_all | solution.py:57
  104.5 12.7 %all-to-all-start.3 = ((bf16[8,32,512]{2,1,0:T(8,128)(2,1)}), bf16[8,32,512]{2,1,0:T(8,128)(2,1)S(1)}, u32[]{:S(2)}, u32[]{:S(2)}) async-start(bf16[8,32,512]{2,1,0:T(8,128)(2,1)} %get-tuple-element.130), calls=%async_computation.3 | async-start | bytes 524288 | tf_op jit(solution)/shard_map/all_to_all | solution.py:57
  117.2 2.2 copy-start.3
  132.8 19.4 %collective-permute-start.11 = (bf16[4096,512]{1,0:T(8,128)(2,1)}, bf16[4096,512]{1,0:T(8,128)(2,1)}, u32[]{:S(2)}, u32[]{:S(2)}) collective-permute-start(bf16[4096,512]{1,0:T(8,128)(2,1)} %collective-permute-done.10.args_4_), channel_id=1, source_target_pairs={{32,0},{96,64},{160,128},{224,192},{288,256},{352,320},{416,384},{... | collective-permute-start | bytes 12582920 | tf_op jit(solution)/shard_map/ppermute | solution.py:349
  136.0 16.2 %all-to-all-start.4 = ((bf16[8,32,512]{2,1,0:T(8,128)(2,1)}), bf16[8,32,512]{2,1,0:T(8,128)(2,1)S(1)}, u32[]{:S(2)}, u32[]{:S(2)}) async-start(bf16[8,32,512]{2,1,0:T(8,128)(2,1)} %get-tuple-element.134), calls=%async_computation.4 | async-start | bytes 524288 | tf_op jit(solution)/shard_map/all_to_all | solution.py:57
  155.4 12.7 %all-to-all-start.5 = ((bf16[8,32,512]{2,1,0:T(8,128)(2,1)}), bf16[8,32,512]{2,1,0:T(8,128)(2,1)S(1)}, u32[]{:S(2)}, u32[]{:S(2)}) async-start(bf16[8,32,512]{2,1,0:T(8,128)(2,1)} %get-tuple-element.137), calls=%async_computation.5 | async-start | bytes 524288 | tf_op jit(solution)/shard_map/all_to_all | solution.py:57
  168.0 2.2 copy-start.4
  170.2 14.1 %copy-start.6 = (bf16[4096,512]{1,0:T(8,128)(2,1)S(1)}, bf16[4096,512]{1,0:T(8,128)(2,1)}, u32[]{:S(2)}) copy-start(bf16[4096,512]{1,0:T(8,128)(2,1)} %get-tuple-element.155.weight_ref) | copy-start | bytes 12582916
  184.3 13.0 %copy-start.5 = (bf16[8,2,4,64,512]{4,3,2,1,0:T(8,128)(2,1)S(1)}, bf16[8,2,4,64,512]{4,3,2,1,0:T(8,128)(2,1)}, u32[]{:S(2)}) copy-start(bf16[8,2,4,64,512]{4,3,2,1,0:T(8,128)(2,1)} %copy-done.2) | copy-start | bytes 12582916
  197.3 14.7 %copy-start.9 = (bf16[4096,512]{1,0:T(8,128)(2,1)S(1)}, bf16[4096,512]{1,0:T(8,128)(2,1)}, u32[]{:S(2)}) copy-start(bf16[4096,512]{1,0:T(8,128)(2,1)} %get-tuple-element.161.weight_ref) | copy-start | bytes 12582916
  213.6 3.2 collective-permute-start.12
  230.9 13.8 %copy-start.7 = (bf16[4096,512]{1,0:T(8,128)(2,1)S(1)}, bf16[4096,512]{1,0:T(8,128)(2,1)}, u32[]{:S(2)}) copy-start(bf16[4096,512]{1,0:T(8,128)(2,1)} %get-tuple-element.167.weight_ref) | copy-start | bytes 12582916
  257.6 13.3 %copy-start.8 = (bf16[4096,512]{1,0:T(8,128)(2,1)S(1)}, bf16[4096,512]{1,0:T(8,128)(2,1)}, u32[]{:S(2)}) copy-start(bf16[4096,512]{1,0:T(8,128)(2,1)} %get-tuple-element.172.weight_ref) | copy-start | bytes 12582916
  323.4 7.1 %collective-permute-start.13 = (bf16[32,512]{1,0:T(8,128)(2,1)S(1)}, bf16[32,512]{1,0:T(8,128)(2,1)S(1)}, u32[]{:S(2)}, u32[]{:S(2)}) collective-permute-start(bf16[32,512]{1,0:T(8,128)(2,1)S(1)} %get-tuple-element.184), channel_id=1, source_target_pairs={{0,128},{32,160},{64,192},{96,224},{128,256},{160,288},{192,320},{... | collective-permute-start | bytes 98312 | tf_op jit(solution)/shard_map/ppermute | solution.py:357
  441.0 5.9 collective-permute-start.14
  540.2 18.1 %collective-permute-start.17 = (bf16[1536,128]{1,0:T(8,128)(2,1)S(1)}, bf16[1536,128]{1,0:T(8,128)(2,1)S(1)}, u32[]{:S(2)}, u32[]{:S(2)}) collective-permute-start(bf16[1536,128]{1,0:T(8,128)(2,1)S(1)} %get-tuple-element.239), channel_id=1, source_target_pairs={{0,24},{8,0},{16,8},{24,16},{1,25},{9,1},{17,9},{25,17},{2,26},{10... | collective-permute-start | bytes 1179656 | tf_op jit(solution)/shard_map/ppermute | solution.py:379
  548.5 10.1 %collective-permute-start.16 = (bf16[1536,128]{1,0:T(8,128)(2,1)S(1)}, bf16[1536,128]{1,0:T(8,128)(2,1)S(1)}, u32[]{:S(2)}, u32[]{:S(2)}) collective-permute-start(bf16[1536,128]{1,0:T(8,128)(2,1)S(1)} %get-tuple-element.238), channel_id=1, source_target_pairs={{0,16},{8,24},{16,0},{24,8},{1,17},{9,25},{17,1},{25,9},{2,18},{10... | collective-permute-start | bytes 1179656 | tf_op jit(solution)/shard_map/ppermute | solution.py:379
  550.4 12.6 %collective-permute-start.15 = (bf16[1536,128]{1,0:T(8,128)(2,1)S(1)}, bf16[1536,128]{1,0:T(8,128)(2,1)S(1)}, u32[]{:S(2)}, u32[]{:S(2)}) collective-permute-start(bf16[1536,128]{1,0:T(8,128)(2,1)S(1)} %get-tuple-element.237), channel_id=1, source_target_pairs={{0,8},{8,16},{16,24},{24,0},{1,9},{9,17},{17,25},{25,1},{2,10},{10... | collective-permute-start | bytes 1179656 | tf_op jit(solution)/shard_map/ppermute | solution.py:379
  554.3 40.4 %all-to-all-start.32 = ((f32[32,8,128]{2,1,0:T(8,128)}), f32[32,8,128]{2,1,0:T(8,128)S(1)}, u32[]{:S(2)}, u32[]{:S(2)}) async-start(f32[32,8,128]{2,1,0:T(8,128)} %broadcast_in_dim_broadcast_in_dim_broadcast_in_dim.3), calls=%async_computation.32 | async-start | bytes 262144 | tf_op jit(solution)/shard_map/all_to_all | solution.py:57
  564.0 36.0 %collective-permute-start.18 = (bf16[8,64,512]{2,1,0:T(8,128)(2,1)S(1)}, bf16[8,64,512]{2,1,0:T(8,128)(2,1)S(1)}, u32[]{:S(2)}, u32[]{:S(2)}) collective-permute-start(bf16[8,64,512]{2,1,0:T(8,128)(2,1)S(1)} %get-tuple-element.228), channel_id=1, source_target_pairs={{0,32},{32,0},{64,96},{96,64},{128,160},{160,128},{192,224},{224,1... | collective-permute-start | bytes 1572872 | tf_op jit(solution)/shard_map/ppermute | solution.py:65
  594.7 5.2 collective-permute-start.19
  599.9 32.6 %copy-start.1 = (bf16[4,32,512]{2,1,0:T(8,128)(2,1)S(1)}, bf16[4,32,512]{2,1,0:T(8,128)(2,1)}, u32[]{:S(2)}) copy-start(bf16[4,32,512]{2,1,0:T(8,128)(2,1)} %param.5) | copy-start | bytes 393220

commit v11 on v10

--- a/solution.py
+++ b/solution.py
@@ -287,39 +287,46 @@
     along_z = lax.all_to_all(
         copies_of(rotation, planes), "section", 0, 0, axis_index_groups=same_core, tiled=True
     )
-    params_by3 = crossed(params_by2, 1)
-    along_z, by1, params_by2, params_by3 = lax.optimization_barrier((along_z, by1, params_by2, params_by3))
+    along_z, by1, params_by2 = lax.optimization_barrier((along_z, by1, params_by2))
     own_now, _ = lax.optimization_barrier((own, params_by2))
     even_mine = lax.ppermute(own_now, "section", [(i, i ^ 2) for i in range(0, sections, 2)])
-    found = jnp.concatenate([params, params_by1, params_by2, params_by3], axis=0)
-    params = jnp.stack([lax.dynamic_index_in_dim(found, place ^ k, 0, False) for k in range(STAGE)])
-    gains, scales = params[:, :D], params[:, D:]
-
     along_x = gather(along_z, "dp")
     stream = lax.dynamic_index_in_dim(hidden_in, place, 0, keepdims=False)
     stream, _ = lax.optimization_barrier((stream, along_z))
     first_rows = doubled(stream)
-    along_x, gains, scales, stream, first_rows = lax.optimization_barrier(
-        (along_x, gains, scales, stream, first_rows)
-    )
+    keeps = [jnp.full((1,), 1, jnp.int32)]
+    keeps += [(stage_pos == stage).astype(jnp.int32)[None] for stage in range(1, stages)]
+    dp_pos = lax.axis_index("dp").astype(jnp.uint32)
+    partners = [lax.rem(dp_pos + jnp.uint32(step), jnp.uint32(replicas)) for step in range(replicas)]
+    which, where = core[None].astype(jnp.int32), place[None].astype(jnp.int32)
+    on_core, low_plane = [core == 0, core == 1], place // 2 == 0
+    ahead = (keeps, partners, which, where, on_core, low_plane)
+    along_x, stream, first_rows, ahead = lax.optimization_barrier((along_x, stream, first_rows, ahead))
+    keeps, partners, which, where, on_core, low_plane = ahead
+    params_by2, _ = lax.optimization_barrier((params_by2, along_x))
+    params_by3 = crossed(params_by2, 1)
+    found = jnp.concatenate([params, params_by1, params_by2, params_by3], axis=0)
+    params = jnp.stack([lax.dynamic_index_in_dim(found, place ^ k, 0, False) for k in range(STAGE)])
+    gains, scales = params[:, :D], params[:, D:]
+    row_scales = jnp.repeat(scales, tok_rows, axis=0)
     other_rows = crossed(along_x, 1)
     own_later, _ = lax.optimization_barrier((own, other_rows))
     odd_mine = lax.ppermute(own_later, "section", [(i, i ^ 2) for i in range(1, sections, 2)])
     even_rows = jnp.where(core == 0, along_x, other_rows)
     odd_rows = jnp.where(core == 0, other_rows, along_x)
     rot_cols = jnp.stack([even_rows, odd_rows]).transpose(2, 0, 1, 3, 4).reshape(D, part_cols)
-
-    where = place[None].astype(jnp.int32)
+    rot_cols, row_scales = lax.optimization_barrier((rot_cols, row_scales))
+
     all_rows = STAGE * tok_rows
     kept = (jnp.zeros((all_rows, D), jnp.bfloat16), jnp.zeros((all_rows, part_cols), jnp.float32))
     weights = []
-    keeps = [jnp.full((1,), 1, jnp.int32)]
-    keeps += [(stage_pos == stage).astype(jnp.int32)[None] for stage in range(1, stages)]
-    row_scales = jnp.repeat(scales, tok_rows, axis=0)
-    dp_pos = lax.axis_index("dp").astype(jnp.uint32)
-    partners = [lax.rem(dp_pos + jnp.uint32(step), jnp.uint32(replicas)) for step in range(replicas)]
-    which = core[None].astype(jnp.int32)
-    ahead = (keeps, row_scales, partners, which)
+
+    def ordered(odd):
+        mine, other = sources[4:] if odd else sources[2:4]
+        far = jnp.where(on_core[odd], mine, other)
+        near = jnp.where(on_core[odd], own, by1)
+        return jnp.where(low_plane, near, far), jnp.where(low_plane, far, near)
+
     for stage in range(stages):
         keep = keeps[stage]
         for layer in range(STAGE):
@@ -327,14 +334,8 @@
             gain, scale = gains[layer : layer + 1], scales[layer : layer + 1]
             rows = exchange(copies, "tp") if stage or layer else first_rows
             if stage == 0 and layer in (1, 2):
-                odd = layer - 1
-                mine, other = sources[4:] if odd else sources[2:4]
-                far = jnp.where(core == odd, mine, other)
-                near = jnp.where(core == odd, own, by1)
-                pair = jnp.where(place // 2 == 0, near, far), jnp.where(place // 2 == 0, far, near)
-                rows, pair, ahead = lax.optimization_barrier((rows, pair, ahead))
+                rows, pair = lax.optimization_barrier((rows, ordered(layer - 1)))
                 weights.append(pair)
-                keeps, row_scales, partners, which = ahead
             results = rotate(layer, last, keep, rows, gain, rot_cols, scale, kept)
             kept = results[:2]
             if last:

time: 636 us -> 645 us (1.014)
  blocking collectives: 353 us -> 387 us
  waiting for transfers between devices: 64 us -> 46.1 us
  starting transfers between devices: 141 us -> 131 us
    all_to_all x26 -> x28, blocking collectives: 322 us -> 361 us  [exchange(): return lax.all_to_all(copies, axis, 0, 0, tiled=True)]
    all_to_all x6 -> x4, waiting for transfers between devices: 26.9 us -> 7.51 us  [exchange(): return lax.all_to_all(copies, axis, 0, 0, tiled=True)]
    all_to_all x6 -> x4, starting transfers between devices: 29.2 us -> 19.1 us  [exchange(): return lax.all_to_all(copies, axis, 0, 0, tiled=True)]
  transfers between devices with their start and end apart: 27 -> 25, of which waited for: 19 -> 16; matrix products, arithmetic and copies ran while one was open for 4% -> 4% of each run, Pallas kernels for 1% -> 1%
where the time goes in v11:
time: 645 us; the launch traced here: 642 us
  blocking collectives  387 us (60%)
  starting transfers between devices  131 us (20%)
  waiting for transfers between devices  46.1 us (7%)
  Pallas kernels  41.8 us (6%)
  other arithmetic  21.4 us (3%)
  local copies, waits for them, and re-layouts  11.6 us (2%)
    all_to_all x28, blocking collectives, exchange(): return lax.all_to_all(copies, axis, 0, 0, tiled=True)  361 us
    ppermute x7, starting transfers between devices, crossed(): lax.ppermute(value, 'section', [(i, i ^ mask) for i in range(lax.axis_siz...  58.7 us
    all_to_all x1, blocking collectives, local(): lax.all_to_all(sent, 'section', 0, 0, axis_index_groups=same_core, tiled=...  25.5 us
    all_to_all x4, starting transfers between devices, exchange(): return lax.all_to_all(copies, axis, 0, 0, tiled=True)  19.1 us
    pallas_call x16, Pallas kernels, rotate(): pl.pallas_call(functools.partial(rotate_kernel, layer, last), out_shape=s...  18.1 us
    ppermute x3, starting transfers between devices, doubled(): other = lax.ppermute(value, 'tp', [(i, i ^ mask) for i in range(count)])  15.6 us
    select_n x2, other arithmetic, ordered(): return (jnp.where(low_plane, near, far), jnp.where(low_plane, far, near))  14 us
    pallas_call x13, Pallas kernels, project(): pl.pallas_call(project_kernel, out_shape=[jax.ShapeDtypeStruct(quant_rows...  13.6 us
  transfers between devices with their start and end apart: 25, of which 16 were waited for; matrix products, arithmetic and copies ran while one was open for 4% of the time, Pallas kernels for 1%

profile of v11, /device:TPU:1, one launch (start us, length us, event | category | flops | bytes accessed | tf_op | source)
XLA Modules:
  0.0 642.2 jit_solution(4374348199045989954)
XLA Ops:
  0.6 8.9 %collective-permute-start = (bf16[4096,512]{1,0:T(8,128)(2,1)}, bf16[4096,512]{1,0:T(8,128)(2,1)}, u32[]{:S(2)}, u32[]{:S(2)}) collective-permute-start(bf16[4096,512]{1,0:T(8,128)(2,1)} %bitcast.args_0_), channel_id=1, source_target_pairs={{0,32},{32,0},{64,96},{96,64},{128,160},{160,128},{192,224},{224,1... | collective-permute-start | bytes 12582920 | tf_op jit(solution)/shard_map/ppermute | solution.py:65
  11.3 4.7 all-to-all-start
  17.4 3.4 collective-permute-start.1
  20.8 8.6 %collective-permute-done.1 = f32[1,4608]{1,0:T(1,128)S(1)} collective-permute-done((f32[1,4608]{1,0:T(1,128)S(1)}, f32[1,4608]{1,0:T(1,128)S(1)}, u32[]{:S(2)}, u32[]{:S(2)}) %collective-permute-start.1) | collective-permute-done | bytes 18464 | tf_op jit(solution)/shard_map/ppermute | solution.py:65
  29.4 4.6 all-to-all-done
  35.6 4.5 all-to-all-start.1
  40.2 2.8 collective-permute-start.5
  42.9 3.2 collective-permute-start.2
  48.0 4.2 collective-permute-start.3
  52.2 2.1 collective-permute-done.3
  54.4 8.2 %collective-permute-start.4 = (bf16[4,32,512]{2,1,0:T(8,128)(2,1)S(1)}, bf16[4,32,512]{2,1,0:T(8,128)(2,1)S(1)}, u32[]{:S(2)}, u32[]{:S(2)}) collective-permute-start(bf16[4,32,512]{2,1,0:T(8,128)(2,1)S(1)} %pad_maximum_fusion.3), channel_id=1, source_target_pairs={{0,4},{1,5},{2,6},{3,7},{4,0},{5,1},{6,2},{7,3},{8,12},{9,13},{10,... | collective-permute-start | bytes 393224 | tf_op jit(solution)/shard_map/ppermute | solution.py:72
  62.6 2.4 collective-permute-done.4
  66.1 5.0 collective-permute-start.8
  73.0 2.4 collective-permute-start.7
  76.6 2.5 select_bitcast_fusion.1
  83.3 2.0 collective-permute-start.10
  85.3 15.9 %all_to_all.170.args_6_ = bf16[8,32,512]{2,1,0:T(8,128)(2,1)S(1)} all-to-all(bf16[8,32,512]{2,1,0:T(8,128)(2,1)S(1)} %get-tuple-element.126), channel_id=1, replica_groups=mesh['section'=16,'dp'=4,'tp'=8] {'tp'}, dimensions={0} | all-to-all | bytes 524288 | tf_op jit(solution)/shard_map/all_to_all | solution.py:57
  102.2 4.7 project_from.2
  106.9 6.8 %all-to-all-start.3 = ((bf16[8,32,512]{2,1,0:T(8,128)(2,1)}), bf16[8,32,512]{2,1,0:T(8,128)(2,1)S(1)}, u32[]{:S(2)}, u32[]{:S(2)}) async-start(bf16[8,32,512]{2,1,0:T(8,128)(2,1)} %get-tuple-element.130), calls=%async_computation.3 | async-start | bytes 524288 | tf_op jit(solution)/shard_map/all_to_all | solution.py:57
  113.7 8.0 %broadcast_select_fusion.6 = (bf16[4096,512]{1,0:T(8,128)(2,1)}, bf16[4096,512]{1,0:T(8,128)(2,1)}) fusion(pred[]{:T(512)S(6)} %eq.49, bf16[4096,512]{1,0:T(8,128)(2,1)} %collective-permute-done.args_1_, pred[]{:T(512)S(6)} %eq.47, bf16[4096,512]{1,0:T(8,128)(2,1)} %collective-permute-done.5.args_2_.args_4_, bf16[4096,512]{1,0:T(8,128)(2,1)} %copy-done.10, ...), kind=kLoop, calls=%fused_computation.7 | loop fusion | flops 8388608 | bytes 25165826 | tf_op jit(solution)/shard_map/jit(_where)/select_n | solution.py:328
  123.1 2.2 copy-done.3
  126.4 9.2 %collective-permute-done.10.args_4_ = bf16[4096,512]{1,0:T(8,128)(2,1)} collective-permute-done((bf16[4096,512]{1,0:T(8,128)(2,1)}, bf16[4096,512]{1,0:T(8,128)(2,1)}, u32[]{:S(2)}, u32[]{:S(2)}) %collective-permute-start.10) | collective-permute-done | bytes 4194336 | tf_op jit(solution)/shard_map/ppermute | solution.py:314
  135.7 4.2 collective-permute-start.11
  139.9 14.2 %all_to_all.171.args_6_ = bf16[8,32,512]{2,1,0:T(8,128)(2,1)S(1)} all-to-all(bf16[8,32,512]{2,1,0:T(8,128)(2,1)S(1)} %get-tuple-element.136), channel_id=1, replica_groups=mesh['section'=16,'dp'=4,'tp'=8] {'tp'}, dimensions={0} | all-to-all | bytes 524288 | tf_op jit(solution)/shard_map/all_to_all | solution.py:57
  154.1 4.7 project_from.3
  158.8 3.4 all-to-all-start.5
  162.2 6.1 broadcast_select_fusion.4
  168.3 5.1 all-to-all-done.5.rows_ref
  173.4 2.2 copy-done.4
  176.7 14.9 %all_to_all.172.quant_ref = bf16[8,32,512]{2,1,0:T(8,128)(2,1)S(1)} all-to-all(bf16[8,32,512]{2,1,0:T(8,128)(2,1)S(1)} %get-tuple-element.144), channel_id=1, replica_groups=mesh['section'=16,'dp'=4,'tp'=8] {'tp'}, dimensions={0} | all-to-all | bytes 524288 | tf_op jit(solution)/shard_map/all_to_all | solution.py:57
  192.5 14.8 %all_to_all.173.rows_ref = bf16[8,32,512]{2,1,0:T(8,128)(2,1)S(1)} all-to-all(bf16[8,32,512]{2,1,0:T(8,128)(2,1)S(1)} %get-tuple-element.147), channel_id=1, replica_groups=mesh['section'=16,'dp'=4,'tp'=8] {'tp'}, dimensions={0} | all-to-all | bytes 524288 | tf_op jit(solution)/shard_map/all_to_all | solution.py:57
  208.5 14.3 %all_to_all.174.quant_ref = bf16[8,32,512]{2,1,0:T(8,128)(2,1)S(1)} all-to-all(bf16[8,32,512]{2,1,0:T(8,128)(2,1)S(1)} %get-tuple-element.150), channel_id=1, replica_groups=mesh['section'=16,'dp'=4,'tp'=8] {'tp'}, dimensions={0} | all-to-all | bytes 524288 | tf_op jit(solution)/shard_map/all_to_all | solution.py:57
  227.4 11.8 %all_to_all.175.rows_ref = bf16[8,32,512]{2,1,0:T(8,128)(2,1)S(1)} all-to-all(bf16[8,32,512]{2,1,0:T(8,128)(2,1)S(1)} %spread.3), channel_id=1, replica_groups=mesh['section'=16,'dp'=4,'tp'=8] {'tp'}, dimensions={0} | all-to-all | bytes 524288 | tf_op jit(solution)/shard_map/all_to_all | solution.py:57
  240.3 11.9 %all_to_all.176.quant_ref = bf16[8,32,512]{2,1,0:T(8,128)(2,1)S(1)} all-to-all(bf16[8,32,512]{2,1,0:T(8,128)(2,1)S(1)} %get-tuple-element.156), channel_id=1, replica_groups=mesh['section'=16,'dp'=4,'tp'=8] {'tp'}, dimensions={0} | all-to-all | bytes 524288 | tf_op jit(solution)/shard_map/all_to_all | solution.py:57
  253.0 11.9 %all_to_all.177.rows_ref = bf16[8,32,512]{2,1,0:T(8,128)(2,1)S(1)} all-to-all(bf16[8,32,512]{2,1,0:T(8,128)(2,1)S(1)} %get-tuple-element.158), channel_id=1, replica_groups=mesh['section'=16,'dp'=4,'tp'=8] {'tp'}, dimensions={0} | all-to-all | bytes 524288 | tf_op jit(solution)/shard_map/all_to_all | solution.py:57
  266.1 11.9 %all_to_all.178.quant_ref = bf16[8,32,512]{2,1,0:T(8,128)(2,1)S(1)} all-to-all(bf16[8,32,512]{2,1,0:T(8,128)(2,1)S(1)} %get-tuple-element.161), channel_id=1, replica_groups=mesh['section'=16,'dp'=4,'tp'=8] {'tp'}, dimensions={0} | all-to-all | bytes 524288 | tf_op jit(solution)/shard_map/all_to_all | solution.py:57
  278.8 11.7 %all_to_all.179.rows_ref = bf16[8,32,512]{2,1,0:T(8,128)(2,1)S(1)} all-to-all(bf16[8,32,512]{2,1,0:T(8,128)(2,1)S(1)} %get-tuple-element.164), channel_id=1, replica_groups=mesh['section'=16,'dp'=4,'tp'=8] {'tp'}, dimensions={0} | all-to-all | bytes 524288 | tf_op jit(solution)/shard_map/all_to_all | solution.py:57
  291.6 11.6 %all_to_all.180.quant_ref = bf16[8,32,512]{2,1,0:T(8,128)(2,1)S(1)} all-to-all(bf16[8,32,512]{2,1,0:T(8,128)(2,1)S(1)} %get-tuple-element.167), channel_id=1, replica_groups=mesh['section'=16,'dp'=4,'tp'=8] {'tp'}, dimensions={0} | all-to-all | bytes 524288 | tf_op jit(solution)/shard_map/all_to_all | solution.py:57
  304.0 11.7 %all_to_all.181.rows_ref = bf16[8,32,512]{2,1,0:T(8,128)(2,1)S(1)} all-to-all(bf16[8,32,512]{2,1,0:T(8,128)(2,1)S(1)} %get-tuple-element.169), channel_id=1, replica_groups=mesh['section'=16,'dp'=4,'tp'=8] {'tp'}, dimensions={0} | all-to-all | bytes 524288 | tf_op jit(solution)/shard_map/all_to_all | solution.py:57
  316.9 12.2 %all_to_all.182.quant_ref = bf16[8,32,512]{2,1,0:T(8,128)(2,1)S(1)} all-to-all(bf16[8,32,512]{2,1,0:T(8,128)(2,1)S(1)} %get-tuple-element.172), channel_id=1, replica_groups=mesh['section'=16,'dp'=4,'tp'=8] {'tp'}, dimensions={0} | all-to-all | bytes 524288 | tf_op jit(solution)/shard_map/all_to_all | solution.py:57
  330.7 5.1 collective-permute-start.13
  336.8 11.7 %all_to_all.183.rows_ref = bf16[8,32,512]{2,1,0:T(8,128)(2,1)S(1)} all-to-all(bf16[8,32,512]{2,1,0:T(8,128)(2,1)S(1)} %spread.4), channel_id=1, replica_groups=mesh['section'=16,'dp'=4,'tp'=8] {'tp'}, dimensions={0} | all-to-all | bytes 524288 | tf_op jit(solution)/shard_map/all_to_all | solution.py:57
  349.6 14.8 %all_to_all.184.quant_ref = bf16[8,32,512]{2,1,0:T(8,128)(2,1)S(1)} all-to-all(bf16[8,32,512]{2,1,0:T(8,128)(2,1)S(1)} %get-tuple-element.177), channel_id=1, replica_groups=mesh['section'=16,'dp'=4,'tp'=8] {'tp'}, dimensions={0} | all-to-all | bytes 524288 | tf_op jit(solution)/shard_map/all_to_all | solution.py:57
  365.2 13.2 %all_to_all.185.rows_ref = bf16[8,32,512]{2,1,0:T(8,128)(2,1)S(1)} all-to-all(bf16[8,32,512]{2,1,0:T(8,128)(2,1)S(1)} %get-tuple-element.178), channel_id=1, replica_groups=mesh['section'=16,'dp'=4,'tp'=8] {'tp'}, dimensions={0} | all-to-all | bytes 524288 | tf_op jit(solution)/shard_map/all_to_all | solution.py:57
  379.6 12.1 %all_to_all.186.quant_ref = bf16[8,32,512]{2,1,0:T(8,128)(2,1)S(1)} all-to-all(bf16[8,32,512]{2,1,0:T(8,128)(2,1)S(1)} %get-tuple-element.181), channel_id=1, replica_groups=mesh['section'=16,'dp'=4,'tp'=8] {'tp'}, dimensions={0} | all-to-all | bytes 524288 | tf_op jit(solution)/shard_map/all_to_all | solution.py:57
  392.5 12.2 %all_to_all.187.rows_ref = bf16[8,32,512]{2,1,0:T(8,128)(2,1)S(1)} all-to-all(bf16[8,32,512]{2,1,0:T(8,128)(2,1)S(1)} %get-tuple-element.183), channel_id=1, replica_groups=mesh['section'=16,'dp'=4,'tp'=8] {'tp'}, dimensions={0} | all-to-all | bytes 524288 | tf_op jit(solution)/shard_map/all_to_all | solution.py:57
  405.8 11.9 %all_to_all.188.quant_ref = bf16[8,32,512]{2,1,0:T(8,128)(2,1)S(1)} all-to-all(bf16[8,32,512]{2,1,0:T(8,128)(2,1)S(1)} %get-tuple-element.186), channel_id=1, replica_groups=mesh['section'=16,'dp'=4,'tp'=8] {'tp'}, dimensions={0} | all-to-all | bytes 524288 | tf_op jit(solution)/shard_map/all_to_all | solution.py:57
  418.6 11.7 %all_to_all.189.rows_ref = bf16[8,32,512]{2,1,0:T(8,128)(2,1)S(1)} all-to-all(bf16[8,32,512]{2,1,0:T(8,128)(2,1)S(1)} %get-tuple-element.188), channel_id=1, replica_groups=mesh['section'=16,'dp'=4,'tp'=8] {'tp'}, dimensions={0} | all-to-all | bytes 524288 | tf_op jit(solution)/shard_map/all_to_all | solution.py:57
  431.4 11.7 %all_to_all.190.quant_ref = bf16[8,32,512]{2,1,0:T(8,128)(2,1)S(1)} all-to-all(bf16[8,32,512]{2,1,0:T(8,128)(2,1)S(1)} %get-tuple-element.191), channel_id=1, replica_groups=mesh['section'=16,'dp'=4,'tp'=8] {'tp'}, dimensions={0} | all-to-all | bytes 524288 | tf_op jit(solution)/shard_map/all_to_all | solution.py:57
  444.7 4.8 collective-permute-start.14
  450.6 13.1 %all_to_all.191.rows_ref = bf16[8,32,512]{2,1,0:T(8,128)(2,1)S(1)} all-to-all(bf16[8,32,512]{2,1,0:T(8,128)(2,1)S(1)} %spread.5), channel_id=1, replica_groups=mesh['section'=16,'dp'=4,'tp'=8] {'tp'}, dimensions={0} | all-to-all | bytes 524288 | tf_op jit(solution)/shard_map/all_to_all | solution.py:57
  464.8 11.7 %all_to_all.192.quant_ref = bf16[8,32,512]{2,1,0:T(8,128)(2,1)S(1)} all-to-all(bf16[8,32,512]{2,1,0:T(8,128)(2,1)S(1)} %get-tuple-element.196), channel_id=1, replica_groups=mesh['section'=16,'dp'=4,'tp'=8] {'tp'}, dimensions={0} | all-to-all | bytes 524288 | tf_op jit(solution)/shard_map/all_to_all | solution.py:57
  477.4 11.7 %all_to_all.193.rows_ref = bf16[8,32,512]{2,1,0:T(8,128)(2,1)S(1)} all-to-all(bf16[8,32,512]{2,1,0:T(8,128)(2,1)S(1)} %get-tuple-element.197), channel_id=1, replica_groups=mesh['section'=16,'dp'=4,'tp'=8] {'tp'}, dimensions={0} | all-to-all | bytes 524288 | tf_op jit(solution)/shard_map/all_to_all | solution.py:57
  490.2 12.8 %all_to_all.194.quant_ref = bf16[8,32,512]{2,1,0:T(8,128)(2,1)S(1)} all-to-all(bf16[8,32,512]{2,1,0:T(8,128)(2,1)S(1)} %get-tuple-element.200), channel_id=1, replica_groups=mesh['section'=16,'dp'=4,'tp'=8] {'tp'}, dimensions={0} | all-to-all | bytes 524288 | tf_op jit(solution)/shard_map/all_to_all | solution.py:57
  503.9 14.1 %all_to_all.195.rows_ref = bf16[8,32,512]{2,1,0:T(8,128)(2,1)S(1)} all-to-all(bf16[8,32,512]{2,1,0:T(8,128)(2,1)S(1)} %get-tuple-element.202), channel_id=1, replica_groups=mesh['section'=16,'dp'=4,'tp'=8] {'tp'}, dimensions={0} | all-to-all | bytes 524288 | tf_op jit(solution)/shard_map/all_to_all | solution.py:57
  519.3 14.8 %all_to_all.196.quant_ref = bf16[8,32,512]{2,1,0:T(8,128)(2,1)S(1)} all-to-all(bf16[8,32,512]{2,1,0:T(8,128)(2,1)S(1)} %get-tuple-element.205), channel_id=1, replica_groups=mesh['section'=16,'dp'=4,'tp'=8] {'tp'}, dimensions={0} | all-to-all | bytes 524288 | tf_op jit(solution)/shard_map/all_to_all | solution.py:57
  535.5 14.8 %all_to_all.197.rows_ref = bf16[8,32,512]{2,1,0:T(8,128)(2,1)S(1)} all-to-all(bf16[8,32,512]{2,1,0:T(8,128)(2,1)S(1)} %get-tuple-element.207), channel_id=1, replica_groups=mesh['section'=16,'dp'=4,'tp'=8] {'tp'}, dimensions={0} | all-to-all | bytes 524288 | tf_op jit(solution)/shard_map/all_to_all | solution.py:57
  553.3 6.6 %collective-permute-start.17 = (bf16[1536,128]{1,0:T(8,128)(2,1)S(1)}, bf16[1536,128]{1,0:T(8,128)(2,1)S(1)}, u32[]{:S(2)}, u32[]{:S(2)}) collective-permute-start(bf16[1536,128]{1,0:T(8,128)(2,1)S(1)} %get-tuple-element.229), channel_id=1, source_target_pairs={{0,24},{8,0},{16,8},{24,16},{1,25},{9,1},{17,9},{25,17},{2,26},{10... | collective-permute-start | bytes 1179656 | tf_op jit(solution)/shard_map/ppermute | solution.py:380
  559.9 2.6 collective-permute-start.16
  565.8 4.3 all-to-all-start.32
  570.2 4.3 collective-permute-done.15
  575.4 32.1 %collective-permute-start.18 = (bf16[8,64,512]{2,1,0:T(8,128)(2,1)S(1)}, bf16[8,64,512]{2,1,0:T(8,128)(2,1)S(1)}, u32[]{:S(2)}, u32[]{:S(2)}) collective-permute-start(bf16[8,64,512]{2,1,0:T(8,128)(2,1)S(1)} %get-tuple-element.218), channel_id=1, source_target_pairs={{0,32},{32,0},{64,96},{96,64},{128,160},{160,128},{192,224},{224,1... | collective-permute-start | bytes 1572872 | tf_op jit(solution)/shard_map/ppermute | solution.py:65
  607.5 5.0 collective-permute-start.19
  613.6 25.5 %all_to_all.198 = bf16[8,72,512]{2,1,0:T(8,128)(2,1)S(1)} all-to-all(bf16[8,72,512]{2,1,0:T(8,128)(2,1)S(1)} %pad_maximum_fusion.1), channel_id=1, replica_groups={{0,64,128,192,256,320,384,448},{32,96,160,224,288,352,416,480},{1,65,12..., dimensions={0} | all-to-all | bytes 1179648 | tf_op jit(solution)/shard_map/all_to_all | solution.py:399
  (123 shorter events, 61.5 us)
Async XLA Ops:
  0.6 42.3 %copy-start = (bf16[4,32,512]{2,1,0:T(8,128)(2,1)S(1)}, bf16[4,32,512]{2,1,0:T(8,128)(2,1)}, u32[]{:S(2)}) copy-start(bf16[4,32,512]{2,1,0:T(8,128)(2,1)} %param.5) | copy-start | bytes 393220
  0.6 33.4 %collective-permute-start = (bf16[4096,512]{1,0:T(8,128)(2,1)}, bf16[4096,512]{1,0:T(8,128)(2,1)}, u32[]{:S(2)}, u32[]{:S(2)}) collective-permute-start(bf16[4096,512]{1,0:T(8,128)(2,1)} %bitcast.args_0_), channel_id=1, source_target_pairs={{0,32},{32,0},{64,96},{96,64},{128,160},{160,128},{192,224},{224,1... | collective-permute-start | bytes 12582920 | tf_op jit(solution)/shard_map/ppermute | solution.py:65
  11.3 22.7 %all-to-all-start = ((bf16[8,64,512]{2,1,0:T(8,128)(2,1)}), bf16[8,64,512]{2,1,0:T(8,128)(2,1)S(1)}, u32[]{:S(2)}, u32[]{:S(2)}) async-start(bf16[8,64,512]{2,1,0:T(8,128)(2,1)} %broadcast_in_dim.77), calls=%async_computation | async-start | bytes 1048576 | tf_op jit(solution)/shard_map/all_to_all | solution.py:287
  17.4 12.0 %collective-permute-start.1 = (f32[1,4608]{1,0:T(1,128)S(1)}, f32[1,4608]{1,0:T(1,128)S(1)}, u32[]{:S(2)}, u32[]{:S(2)}) collective-permute-start(f32[1,4608]{1,0:T(1,128)S(1)} %pad_maximum_fusion.6), channel_id=1, source_target_pairs={{0,64},{32,96},{64,0},{96,32},{128,192},{160,224},{192,128},{224,1... | collective-permute-start | bytes 55304 | tf_op jit(solution)/shard_map/ppermute | solution.py:65
  35.6 30.5 %all-to-all-start.1 = ((bf16[4,8,64,512]{3,2,1,0:T(8,128)(2,1)}), bf16[4,8,64,512]{3,2,1,0:T(8,128)(2,1)}, u32[]{:S(2)}, u32[]{:S(2)}) async-start(bf16[4,8,64,512]{3,2,1,0:T(8,128)(2,1)} %broadcast_in_dim.80), calls=%async_computation.1 | async-start | bytes 4194304 | tf_op jit(solution)/shard_map/all_to_all | solution.py:57
  40.1 36.1 %copy-start.13 = (f32[1,4096]{1,0:T(1,128)S(1)}, f32[1,4096]{1,0:T(1,128)}, u32[]{:S(2)}) copy-start(f32[1,4096]{1,0:T(1,128)} %param.8) | copy-start | bytes 49156
  40.2 41.9 %collective-permute-start.5 = (bf16[4096,512]{1,0:T(8,128)(2,1)}, bf16[4096,512]{1,0:T(8,128)(2,1)}, u32[]{:S(2)}, u32[]{:S(2)}) collective-permute-start(bf16[4096,512]{1,0:T(8,128)(2,1)} %bitcast.args_0_), channel_id=1, source_target_pairs={{0,64},{64,0},{128,192},{192,128},{256,320},{320,256},{384,448},{4... | collective-permute-start | bytes 12582920 | tf_op jit(solution)/shard_map/ppermute | solution.py:292
  42.9 5.0 collective-permute-start.2
  48.0 6.3 collective-permute-start.3
  54.4 10.6 %collective-permute-start.4 = (bf16[4,32,512]{2,1,0:T(8,128)(2,1)S(1)}, bf16[4,32,512]{2,1,0:T(8,128)(2,1)S(1)}, u32[]{:S(2)}, u32[]{:S(2)}) collective-permute-start(bf16[4,32,512]{2,1,0:T(8,128)(2,1)S(1)} %pad_maximum_fusion.3), channel_id=1, source_target_pairs={{0,4},{1,5},{2,6},{3,7},{4,0},{5,1},{6,2},{7,3},{8,12},{9,13},{10,... | collective-permute-start | bytes 393224 | tf_op jit(solution)/shard_map/ppermute | solution.py:72
  66.1 10.5 %collective-permute-start.8 = (bf16[4,8,64,512]{3,2,1,0:T(8,128)(2,1)}, bf16[4,8,64,512]{3,2,1,0:T(8,128)(2,1)}, u32[]{:S(2)}, u32[]{:S(2)}) collective-permute-start(bf16[4,8,64,512]{3,2,1,0:T(8,128)(2,1)} %all-to-all-done.1), channel_id=1, source_target_pairs={{0,32},{32,0},{64,96},{96,64},{128,160},{160,128},{192,224},{224,1... | collective-permute-start | bytes 6291464 | tf_op jit(solution)/shard_map/ppermute | solution.py:65
  71.1 4.4 collective-permute-start.6
  73.0 3.2 collective-permute-start.7
  80.0 2.0 copy-start.2
  82.0 20.2 %collective-permute-start.9 = (bf16[4096,512]{1,0:T(8,128)(2,1)}, bf16[4096,512]{1,0:T(8,128)(2,1)S(1)}, u32[]{:S(2)}, u32[]{:S(2)}) collective-permute-start(bf16[4096,512]{1,0:T(8,128)(2,1)} %collective-permute-done.5.args_2_.args_4_), channel_id=1, source_target_pairs={{0,32},{64,96},{128,160},{192,224},{256,288},{320,352},{384,416},{... | collective-permute-start | bytes 12582920 | tf_op jit(solution)/shard_map/ppermute | solution.py:346
  83.3 52.3 %collective-permute-start.10 = (bf16[4096,512]{1,0:T(8,128)(2,1)}, bf16[4096,512]{1,0:T(8,128)(2,1)}, u32[]{:S(2)}, u32[]{:S(2)}) collective-permute-start(bf16[4096,512]{1,0:T(8,128)(2,1)} %bitcast.args_0_), channel_id=1, source_target_pairs={{32,96},{96,32},{160,224},{224,160},{288,352},{352,288},{416,480},... | collective-permute-start | bytes 12582920 | tf_op jit(solution)/shard_map/ppermute | solution.py:314
  102.2 4.7 copy-start.10
  106.9 16.2 %all-to-all-start.3 = ((bf16[8,32,512]{2,1,0:T(8,128)(2,1)}), bf16[8,32,512]{2,1,0:T(8,128)(2,1)S(1)}, u32[]{:S(2)}, u32[]{:S(2)}) async-start(bf16[8,32,512]{2,1,0:T(8,128)(2,1)} %get-tuple-element.130), calls=%async_computation.3 | async-start | bytes 524288 | tf_op jit(solution)/shard_map/all_to_all | solution.py:57
  123.1 2.2 copy-start.3
  125.3 28.8 %copy-start.11 = (bf16[4096,512]{1,0:T(8,128)(2,1)S(1)}, bf16[4096,512]{1,0:T(8,128)(2,1)}, u32[]{:S(2)}) copy-start(bf16[4096,512]{1,0:T(8,128)(2,1)} %copy-done.10) | copy-start | bytes 12582916
  135.7 18.4 %collective-permute-start.11 = (bf16[4096,512]{1,0:T(8,128)(2,1)}, bf16[4096,512]{1,0:T(8,128)(2,1)S(1)}, u32[]{:S(2)}, u32[]{:S(2)}) collective-permute-start(bf16[4096,512]{1,0:T(8,128)(2,1)} %collective-permute-done.10.args_4_), channel_id=1, source_target_pairs={{32,0},{96,64},{160,128},{224,192},{288,256},{352,320},{416,384},{... | collective-permute-start | bytes 12582920 | tf_op jit(solution)/shard_map/ppermute | solution.py:350
  154.1 4.7 copy-start.12
  158.8 14.6 %all-to-all-start.5 = ((bf16[8,32,512]{2,1,0:T(8,128)(2,1)}), bf16[8,32,512]{2,1,0:T(8,128)(2,1)S(1)}, u32[]{:S(2)}, u32[]{:S(2)}) async-start(bf16[8,32,512]{2,1,0:T(8,128)(2,1)} %get-tuple-element.139), calls=%async_computation.5 | async-start | bytes 524288 | tf_op jit(solution)/shard_map/all_to_all | solution.py:57
  173.4 2.2 copy-start.4
  175.6 16.1 %copy-start.6 = (bf16[4096,512]{1,0:T(8,128)(2,1)S(1)}, bf16[4096,512]{1,0:T(8,128)(2,1)}, u32[]{:S(2)}) copy-start(bf16[4096,512]{1,0:T(8,128)(2,1)} %get-tuple-element.145.weight_ref) | copy-start | bytes 12582916
  191.7 15.7 %copy-start.5 = (bf16[8,2,4,64,512]{4,3,2,1,0:T(8,128)(2,1)S(1)}, bf16[8,2,4,64,512]{4,3,2,1,0:T(8,128)(2,1)}, u32[]{:S(2)}) copy-start(bf16[8,2,4,64,512]{4,3,2,1,0:T(8,128)(2,1)} %copy-done.2) | copy-start | bytes 12582916
  207.4 15.5 %copy-start.9 = (bf16[4096,512]{1,0:T(8,128)(2,1)S(1)}, bf16[4096,512]{1,0:T(8,128)(2,1)}, u32[]{:S(2)}) copy-start(bf16[4096,512]{1,0:T(8,128)(2,1)} %get-tuple-element.151.weight_ref) | copy-start | bytes 12582916
  224.4 2.9 collective-permute-start.12
  239.2 13.0 %copy-start.7 = (bf16[4096,512]{1,0:T(8,128)(2,1)S(1)}, bf16[4096,512]{1,0:T(8,128)(2,1)}, u32[]{:S(2)}) copy-start(bf16[4096,512]{1,0:T(8,128)(2,1)} %get-tuple-element.157.weight_ref) | copy-start | bytes 12582916
  265.0 13.0 %copy-start.8 = (bf16[4096,512]{1,0:T(8,128)(2,1)S(1)}, bf16[4096,512]{1,0:T(8,128)(2,1)}, u32[]{:S(2)}) copy-start(bf16[4096,512]{1,0:T(8,128)(2,1)} %get-tuple-element.162.weight_ref) | copy-start | bytes 12582916
  330.7 6.1 collective-permute-start.13
  444.7 5.8 collective-permute-start.14
  553.3 16.8 %collective-permute-start.17 = (bf16[1536,128]{1,0:T(8,128)(2,1)S(1)}, bf16[1536,128]{1,0:T(8,128)(2,1)S(1)}, u32[]{:S(2)}, u32[]{:S(2)}) collective-permute-start(bf16[1536,128]{1,0:T(8,128)(2,1)S(1)} %get-tuple-element.229), channel_id=1, source_target_pairs={{0,24},{8,0},{16,8},{24,16},{1,25},{9,1},{17,9},{25,17},{2,26},{10... | collective-permute-start | bytes 1179656 | tf_op jit(solution)/shard_map/ppermute | solution.py:380
  559.9 10.3 %collective-permute-start.16 = (bf16[1536,128]{1,0:T(8,128)(2,1)S(1)}, bf16[1536,128]{1,0:T(8,128)(2,1)S(1)}, u32[]{:S(2)}, u32[]{:S(2)}) collective-permute-start(bf16[1536,128]{1,0:T(8,128)(2,1)S(1)} %get-tuple-element.228), channel_id=1, source_target_pairs={{0,16},{8,24},{16,0},{24,8},{1,17},{9,25},{17,1},{25,9},{2,18},{10... | collective-permute-start | bytes 1179656 | tf_op jit(solution)/shard_map/ppermute | solution.py:380
  562.6 11.9 %collective-permute-start.15 = (bf16[1536,128]{1,0:T(8,128)(2,1)S(1)}, bf16[1536,128]{1,0:T(8,128)(2,1)S(1)}, u32[]{:S(2)}, u32[]{:S(2)}) collective-permute-start(bf16[1536,128]{1,0:T(8,128)(2,1)S(1)} %get-tuple-element.227), channel_id=1, source_target_pairs={{0,8},{8,16},{16,24},{24,0},{1,9},{9,17},{17,25},{25,1},{2,10},{10... | collective-permute-start | bytes 1179656 | tf_op jit(solution)/shard_map/ppermute | solution.py:380
  565.8 41.6 %all-to-all-start.32 = ((f32[32,8,128]{2,1,0:T(8,128)}), f32[32,8,128]{2,1,0:T(8,128)S(1)}, u32[]{:S(2)}, u32[]{:S(2)}) async-start(f32[32,8,128]{2,1,0:T(8,128)} %broadcast_in_dim_broadcast_in_dim_broadcast_in_dim.3), calls=%async_computation.32 | async-start | bytes 262144 | tf_op jit(solution)/shard_map/all_to_all | solution.py:57
  575.4 38.0 %collective-permute-start.18 = (bf16[8,64,512]{2,1,0:T(8,128)(2,1)S(1)}, bf16[8,64,512]{2,1,0:T(8,128)(2,1)S(1)}, u32[]{:S(2)}, u32[]{:S(2)}) collective-permute-start(bf16[8,64,512]{2,1,0:T(8,128)(2,1)S(1)} %get-tuple-element.218), channel_id=1, source_target_pairs={{0,32},{32,0},{64,96},{96,64},{128,160},{160,128},{192,224},{224,1... | collective-permute-start | bytes 1572872 | tf_op jit(solution)/shard_map/ppermute | solution.py:65
  607.5 5.8 collective-permute-start.19
  613.3 27.8 %copy-start.1 = (bf16[4,32,512]{2,1,0:T(8,128)(2,1)S(1)}, bf16[4,32,512]{2,1,0:T(8,128)(2,1)}, u32[]{:S(2)}) copy-start(bf16[4,32,512]{2,1,0:T(8,128)(2,1)} %param.5) | copy-start | bytes 393220

commit v12 on v10

--- a/solution.py
+++ b/solution.py
@@ -289,7 +289,7 @@
     )
     params_by3 = crossed(params_by2, 1)
     along_z, by1, params_by2, params_by3 = lax.optimization_barrier((along_z, by1, params_by2, params_by3))
-    own_now, _ = lax.optimization_barrier((own, params_by2))
+    own_now, _ = lax.optimization_barrier((own, params_by1))
     even_mine = lax.ppermute(own_now, "section", [(i, i ^ 2) for i in range(0, sections, 2)])
     found = jnp.concatenate([params, params_by1, params_by2, params_by3], axis=0)
     params = jnp.stack([lax.dynamic_index_in_dim(found, place ^ k, 0, False) for k in range(STAGE)])

time: 636 us -> 635 us (level)
  transfers between devices with their start and end apart: 27 -> 27, of which waited for: 19 -> 16; matrix products, arithmetic and copies ran while one was open for 4% -> 4% of each run, Pallas kernels for 1% -> 1%
where the time goes in v12:
time: 635 us; the launch traced here: 632 us
  blocking collectives  352 us (55%)
  starting transfers between devices  141 us (22%)
  waiting for transfers between devices  63.9 us (10%)
  Pallas kernels  40.1 us (6%)
  other arithmetic  21.4 us (3%)
  local copies, waits for them, and re-layouts  10.8 us (2%)
    all_to_all x26, blocking collectives, exchange(): return lax.all_to_all(copies, axis, 0, 0, tiled=True)  322 us
    ppermute x7, starting transfers between devices, crossed(): lax.ppermute(value, 'section', [(i, i ^ mask) for i in range(lax.axis_siz...  57.7 us
    all_to_all x1, blocking collectives, local(): lax.all_to_all(sent, 'section', 0, 0, axis_index_groups=same_core, tiled=...  30.1 us
    all_to_all x6, starting transfers between devices, exchange(): return lax.all_to_all(copies, axis, 0, 0, tiled=True)  26 us
    all_to_all x6, waiting for transfers between devices, exchange(): return lax.all_to_all(copies, axis, 0, 0, tiled=True)  25.5 us
    pallas_call x16, Pallas kernels, rotate(): pl.pallas_call(functools.partial(rotate_kernel, layer, last), out_shape=s...  19.5 us
    ppermute x3, starting transfers between devices, doubled(): other = lax.ppermute(value, 'tp', [(i, i ^ mask) for i in range(count)])  16.5 us
    ppermute x3, starting transfers between devices, local(): lax.ppermute(stream, 'section', [(i, i + STAGE) for i in range(sections -...  14 us
  transfers between devices with their start and end apart: 27, of which 16 were waited for; matrix products, arithmetic and copies ran while one was open for 4% of the time, Pallas kernels for 1%

profile of v12, /device:TPU:1, one launch (start us, length us, event | category | flops | bytes accessed | tf_op | source)
XLA Modules:
  0.0 632.5 jit_solution(16792717824079173664)
XLA Ops:
  0.6 8.9 %collective-permute-start = (bf16[4096,512]{1,0:T(8,128)(2,1)}, bf16[4096,512]{1,0:T(8,128)(2,1)}, u32[]{:S(2)}, u32[]{:S(2)}) collective-permute-start(bf16[4096,512]{1,0:T(8,128)(2,1)} %bitcast.1.args_0_), channel_id=1, source_target_pairs={{0,32},{32,0},{64,96},{96,64},{128,160},{160,128},{192,224},{224,1... | collective-permute-start | bytes 12582920 | tf_op jit(solution)/shard_map/ppermute | solution.py:65
  11.3 4.7 all-to-all-start
  17.4 3.4 collective-permute-start.1
  20.8 2.8 collective-permute-start.3
  23.6 5.8 collective-permute-done.1
  29.4 3.4 collective-permute-start.2
  32.8 2.7 collective-permute-start.4
  37.2 4.6 all-to-all-start.1
  41.8 3.2 collective-permute-start.5
  47.0 4.2 collective-permute-start.6
  53.7 9.0 %collective-permute-start.7 = (bf16[4,32,512]{2,1,0:T(8,128)(2,1)S(1)}, bf16[4,32,512]{2,1,0:T(8,128)(2,1)S(1)}, u32[]{:S(2)}, u32[]{:S(2)}) collective-permute-start(bf16[4,32,512]{2,1,0:T(8,128)(2,1)S(1)} %pad_maximum_fusion.3), channel_id=1, source_target_pairs={{0,4},{1,5},{2,6},{3,7},{4,0},{5,1},{6,2},{7,3},{8,12},{9,13},{10,... | collective-permute-start | bytes 393224 | tf_op jit(solution)/shard_map/ppermute | solution.py:72
  62.8 3.2 collective-permute-done.7
  68.4 3.6 collective-permute-start.8
  72.1 4.0 collective-permute-done.8
  76.1 2.5 select_bitcast_fusion.1
  84.9 5.4 all-to-all-start.2
  90.3 9.3 %all-to-all-done.2.args_6_ = bf16[8,32,512]{2,1,0:T(8,128)(2,1)S(1)} async-done(((bf16[8,32,512]{2,1,0:T(8,128)(2,1)}), bf16[8,32,512]{2,1,0:T(8,128)(2,1)S(1)}, u32[]{:S(2)}, u32[]{:S(2)}) %all-to-all-start.2) | async-done | bytes 262176 | tf_op jit(solution)/shard_map/all_to_all | solution.py:57
  99.6 3.1 project_from.2
  102.8 3.4 all-to-all-start.3
  106.2 8.0 %broadcast_select_fusion.6 = (bf16[4096,512]{1,0:T(8,128)(2,1)}, bf16[4096,512]{1,0:T(8,128)(2,1)}) fusion(pred[]{:T(512)S(6)} %eq.50, bf16[4096,512]{1,0:T(8,128)(2,1)} %collective-permute-done.args_1_, pred[]{:T(512)S(6)} %eq.49, bf16[4096,512]{1,0:T(8,128)(2,1)} %collective-permute-done.4.args_2_.args_4_, ...), kind=kLoop, calls=%fused_computation.7 | loop fusion | flops 8388608 | bytes 25165826 | tf_op jit(solution)/shard_map/jit(_where)/select_n | solution.py:334
  119.6 13.0 %collective-permute-done.10.args_4_ = bf16[4096,512]{1,0:T(8,128)(2,1)} collective-permute-done((bf16[4096,512]{1,0:T(8,128)(2,1)}, bf16[4096,512]{1,0:T(8,128)(2,1)}, u32[]{:S(2)}, u32[]{:S(2)}) %collective-permute-start.10) | collective-permute-done | bytes 4194336 | tf_op jit(solution)/shard_map/ppermute | solution.py:307
  132.6 3.2 collective-permute-start.11
  135.8 5.4 all-to-all-start.4
  141.1 9.3 %all-to-all-done.4.args_6_ = bf16[8,32,512]{2,1,0:T(8,128)(2,1)S(1)} async-done(((bf16[8,32,512]{2,1,0:T(8,128)(2,1)}), bf16[8,32,512]{2,1,0:T(8,128)(2,1)S(1)}, u32[]{:S(2)}, u32[]{:S(2)}) %all-to-all-start.4) | async-done | bytes 262176 | tf_op jit(solution)/shard_map/all_to_all | solution.py:57
  150.5 3.2 project_from.3
  153.6 3.4 all-to-all-start.5
  157.1 6.0 broadcast_select_fusion.4
  163.1 3.3 all-to-all-done.5.rows_ref
  169.7 12.6 %all_to_all.170.quant_ref = bf16[8,32,512]{2,1,0:T(8,128)(2,1)S(1)} all-to-all(bf16[8,32,512]{2,1,0:T(8,128)(2,1)S(1)} %get-tuple-element.154), channel_id=1, replica_groups=mesh['section'=16,'dp'=4,'tp'=8] {'tp'}, dimensions={0} | all-to-all | bytes 524288 | tf_op jit(solution)/shard_map/all_to_all | solution.py:57
  183.1 12.2 %all_to_all.171.rows_ref = bf16[8,32,512]{2,1,0:T(8,128)(2,1)S(1)} all-to-all(bf16[8,32,512]{2,1,0:T(8,128)(2,1)S(1)} %get-tuple-element.157), channel_id=1, replica_groups=mesh['section'=16,'dp'=4,'tp'=8] {'tp'}, dimensions={0} | all-to-all | bytes 524288 | tf_op jit(solution)/shard_map/all_to_all | solution.py:57
  196.5 13.5 %all_to_all.172.quant_ref = bf16[8,32,512]{2,1,0:T(8,128)(2,1)S(1)} all-to-all(bf16[8,32,512]{2,1,0:T(8,128)(2,1)S(1)} %get-tuple-element.160), channel_id=1, replica_groups=mesh['section'=16,'dp'=4,'tp'=8] {'tp'}, dimensions={0} | all-to-all | bytes 524288 | tf_op jit(solution)/shard_map/all_to_all | solution.py:57
  211.6 2.8 collective-permute-start.12
  215.5 14.1 %all_to_all.173.rows_ref = bf16[8,32,512]{2,1,0:T(8,128)(2,1)S(1)} all-to-all(bf16[8,32,512]{2,1,0:T(8,128)(2,1)S(1)} %spread.3), channel_id=1, replica_groups=mesh['section'=16,'dp'=4,'tp'=8] {'tp'}, dimensions={0} | all-to-all | bytes 524288 | tf_op jit(solution)/shard_map/all_to_all | solution.py:57
  230.7 12.7 %all_to_all.174.quant_ref = bf16[8,32,512]{2,1,0:T(8,128)(2,1)S(1)} all-to-all(bf16[8,32,512]{2,1,0:T(8,128)(2,1)S(1)} %get-tuple-element.166), channel_id=1, replica_groups=mesh['section'=16,'dp'=4,'tp'=8] {'tp'}, dimensions={0} | all-to-all | bytes 524288 | tf_op jit(solution)/shard_map/all_to_all | solution.py:57
  244.3 12.1 %all_to_all.175.rows_ref = bf16[8,32,512]{2,1,0:T(8,128)(2,1)S(1)} all-to-all(bf16[8,32,512]{2,1,0:T(8,128)(2,1)S(1)} %get-tuple-element.168), channel_id=1, replica_groups=mesh['section'=16,'dp'=4,'tp'=8] {'tp'}, dimensions={0} | all-to-all | bytes 524288 | tf_op jit(solution)/shard_map/all_to_all | solution.py:57
  257.4 12.1 %all_to_all.176.quant_ref = bf16[8,32,512]{2,1,0:T(8,128)(2,1)S(1)} all-to-all(bf16[8,32,512]{2,1,0:T(8,128)(2,1)S(1)} %get-tuple-element.171), channel_id=1, replica_groups=mesh['section'=16,'dp'=4,'tp'=8] {'tp'}, dimensions={0} | all-to-all | bytes 524288 | tf_op jit(solution)/shard_map/all_to_all | solution.py:57
  270.4 11.8 %all_to_all.177.rows_ref = bf16[8,32,512]{2,1,0:T(8,128)(2,1)S(1)} all-to-all(bf16[8,32,512]{2,1,0:T(8,128)(2,1)S(1)} %get-tuple-element.174), channel_id=1, replica_groups=mesh['section'=16,'dp'=4,'tp'=8] {'tp'}, dimensions={0} | all-to-all | bytes 524288 | tf_op jit(solution)/shard_map/all_to_all | solution.py:57
  283.4 11.7 %all_to_all.178.quant_ref = bf16[8,32,512]{2,1,0:T(8,128)(2,1)S(1)} all-to-all(bf16[8,32,512]{2,1,0:T(8,128)(2,1)S(1)} %get-tuple-element.177), channel_id=1, replica_groups=mesh['section'=16,'dp'=4,'tp'=8] {'tp'}, dimensions={0} | all-to-all | bytes 524288 | tf_op jit(solution)/shard_map/all_to_all | solution.py:57
  296.0 11.7 %all_to_all.179.rows_ref = bf16[8,32,512]{2,1,0:T(8,128)(2,1)S(1)} all-to-all(bf16[8,32,512]{2,1,0:T(8,128)(2,1)S(1)} %get-tuple-element.179), channel_id=1, replica_groups=mesh['section'=16,'dp'=4,'tp'=8] {'tp'}, dimensions={0} | all-to-all | bytes 524288 | tf_op jit(solution)/shard_map/all_to_all | solution.py:57
  308.8 11.7 %all_to_all.180.quant_ref = bf16[8,32,512]{2,1,0:T(8,128)(2,1)S(1)} all-to-all(bf16[8,32,512]{2,1,0:T(8,128)(2,1)S(1)} %get-tuple-element.182), channel_id=1, replica_groups=mesh['section'=16,'dp'=4,'tp'=8] {'tp'}, dimensions={0} | all-to-all | bytes 524288 | tf_op jit(solution)/shard_map/all_to_all | solution.py:57
  322.1 6.3 collective-permute-start.13
  329.4 11.7 %all_to_all.181.rows_ref = bf16[8,32,512]{2,1,0:T(8,128)(2,1)S(1)} all-to-all(bf16[8,32,512]{2,1,0:T(8,128)(2,1)S(1)} %spread.4), channel_id=1, replica_groups=mesh['section'=16,'dp'=4,'tp'=8] {'tp'}, dimensions={0} | all-to-all | bytes 524288 | tf_op jit(solution)/shard_map/all_to_all | solution.py:57
  342.3 12.0 %all_to_all.182.quant_ref = bf16[8,32,512]{2,1,0:T(8,128)(2,1)S(1)} all-to-all(bf16[8,32,512]{2,1,0:T(8,128)(2,1)S(1)} %get-tuple-element.187), channel_id=1, replica_groups=mesh['section'=16,'dp'=4,'tp'=8] {'tp'}, dimensions={0} | all-to-all | bytes 524288 | tf_op jit(solution)/shard_map/all_to_all | solution.py:57
  355.1 13.5 %all_to_all.183.rows_ref = bf16[8,32,512]{2,1,0:T(8,128)(2,1)S(1)} all-to-all(bf16[8,32,512]{2,1,0:T(8,128)(2,1)S(1)} %get-tuple-element.188), channel_id=1, replica_groups=mesh['section'=16,'dp'=4,'tp'=8] {'tp'}, dimensions={0} | all-to-all | bytes 524288 | tf_op jit(solution)/shard_map/all_to_all | solution.py:57
  369.8 14.8 %all_to_all.184.quant_ref = bf16[8,32,512]{2,1,0:T(8,128)(2,1)S(1)} all-to-all(bf16[8,32,512]{2,1,0:T(8,128)(2,1)S(1)} %get-tuple-element.191), channel_id=1, replica_groups=mesh['section'=16,'dp'=4,'tp'=8] {'tp'}, dimensions={0} | all-to-all | bytes 524288 | tf_op jit(solution)/shard_map/all_to_all | solution.py:57
  385.5 13.4 %all_to_all.185.rows_ref = bf16[8,32,512]{2,1,0:T(8,128)(2,1)S(1)} all-to-all(bf16[8,32,512]{2,1,0:T(8,128)(2,1)S(1)} %get-tuple-element.193), channel_id=1, replica_groups=mesh['section'=16,'dp'=4,'tp'=8] {'tp'}, dimensions={0} | all-to-all | bytes 524288 | tf_op jit(solution)/shard_map/all_to_all | solution.py:57
  400.0 12.2 %all_to_all.186.quant_ref = bf16[8,32,512]{2,1,0:T(8,128)(2,1)S(1)} all-to-all(bf16[8,32,512]{2,1,0:T(8,128)(2,1)S(1)} %get-tuple-element.196), channel_id=1, replica_groups=mesh['section'=16,'dp'=4,'tp'=8] {'tp'}, dimensions={0} | all-to-all | bytes 524288 | tf_op jit(solution)/shard_map/all_to_all | solution.py:57
  413.0 12.3 %all_to_all.187.rows_ref = bf16[8,32,512]{2,1,0:T(8,128)(2,1)S(1)} all-to-all(bf16[8,32,512]{2,1,0:T(8,128)(2,1)S(1)} %get-tuple-element.198), channel_id=1, replica_groups=mesh['section'=16,'dp'=4,'tp'=8] {'tp'}, dimensions={0} | all-to-all | bytes 524288 | tf_op jit(solution)/shard_map/all_to_all | solution.py:57
  426.4 11.9 %all_to_all.188.quant_ref = bf16[8,32,512]{2,1,0:T(8,128)(2,1)S(1)} all-to-all(bf16[8,32,512]{2,1,0:T(8,128)(2,1)S(1)} %get-tuple-element.201), channel_id=1, replica_groups=mesh['section'=16,'dp'=4,'tp'=8] {'tp'}, dimensions={0} | all-to-all | bytes 524288 | tf_op jit(solution)/shard_map/all_to_all | solution.py:57
  439.8 4.8 collective-permute-start.14
  445.7 13.3 %all_to_all.189.rows_ref = bf16[8,32,512]{2,1,0:T(8,128)(2,1)S(1)} all-to-all(bf16[8,32,512]{2,1,0:T(8,128)(2,1)S(1)} %spread.5), channel_id=1, replica_groups=mesh['section'=16,'dp'=4,'tp'=8] {'tp'}, dimensions={0} | all-to-all | bytes 524288 | tf_op jit(solution)/shard_map/all_to_all | solution.py:57
  460.2 11.7 %all_to_all.190.quant_ref = bf16[8,32,512]{2,1,0:T(8,128)(2,1)S(1)} all-to-all(bf16[8,32,512]{2,1,0:T(8,128)(2,1)S(1)} %get-tuple-element.206), channel_id=1, replica_groups=mesh['section'=16,'dp'=4,'tp'=8] {'tp'}, dimensions={0} | all-to-all | bytes 524288 | tf_op jit(solution)/shard_map/all_to_all | solution.py:57
  472.7 11.7 %all_to_all.191.rows_ref = bf16[8,32,512]{2,1,0:T(8,128)(2,1)S(1)} all-to-all(bf16[8,32,512]{2,1,0:T(8,128)(2,1)S(1)} %get-tuple-element.207), channel_id=1, replica_groups=mesh['section'=16,'dp'=4,'tp'=8] {'tp'}, dimensions={0} | all-to-all | bytes 524288 | tf_op jit(solution)/shard_map/all_to_all | solution.py:57
  485.6 11.7 %all_to_all.192.quant_ref = bf16[8,32,512]{2,1,0:T(8,128)(2,1)S(1)} all-to-all(bf16[8,32,512]{2,1,0:T(8,128)(2,1)S(1)} %get-tuple-element.210), channel_id=1, replica_groups=mesh['section'=16,'dp'=4,'tp'=8] {'tp'}, dimensions={0} | all-to-all | bytes 524288 | tf_op jit(solution)/shard_map/all_to_all | solution.py:57
  498.2 11.7 %all_to_all.193.rows_ref = bf16[8,32,512]{2,1,0:T(8,128)(2,1)S(1)} all-to-all(bf16[8,32,512]{2,1,0:T(8,128)(2,1)S(1)} %get-tuple-element.212), channel_id=1, replica_groups=mesh['section'=16,'dp'=4,'tp'=8] {'tp'}, dimensions={0} | all-to-all | bytes 524288 | tf_op jit(solution)/shard_map/all_to_all | solution.py:57
  511.0 11.7 %all_to_all.194.quant_ref = bf16[8,32,512]{2,1,0:T(8,128)(2,1)S(1)} all-to-all(bf16[8,32,512]{2,1,0:T(8,128)(2,1)S(1)} %get-tuple-element.215), channel_id=1, replica_groups=mesh['section'=16,'dp'=4,'tp'=8] {'tp'}, dimensions={0} | all-to-all | bytes 524288 | tf_op jit(solution)/shard_map/all_to_all | solution.py:57
  524.2 11.8 %all_to_all.195.rows_ref = bf16[8,32,512]{2,1,0:T(8,128)(2,1)S(1)} all-to-all(bf16[8,32,512]{2,1,0:T(8,128)(2,1)S(1)} %get-tuple-element.217), channel_id=1, replica_groups=mesh['section'=16,'dp'=4,'tp'=8] {'tp'}, dimensions={0} | all-to-all | bytes 524288 | tf_op jit(solution)/shard_map/all_to_all | solution.py:57
  539.1 8.0 %collective-permute-start.17 = (bf16[1536,128]{1,0:T(8,128)(2,1)S(1)}, bf16[1536,128]{1,0:T(8,128)(2,1)S(1)}, u32[]{:S(2)}, u32[]{:S(2)}) collective-permute-start(bf16[1536,128]{1,0:T(8,128)(2,1)S(1)} %get-tuple-element.239), channel_id=1, source_target_pairs={{0,24},{8,0},{16,8},{24,16},{1,25},{9,1},{17,9},{25,17},{2,26},{10... | collective-permute-start | bytes 1179656 | tf_op jit(solution)/shard_map/ppermute | solution.py:379
  547.1 2.5 collective-permute-start.16
  553.3 3.9 all-to-all-start.32
  557.2 4.4 collective-permute-done.15
  562.5 30.7 %collective-permute-start.18 = (bf16[8,64,512]{2,1,0:T(8,128)(2,1)S(1)}, bf16[8,64,512]{2,1,0:T(8,128)(2,1)S(1)}, u32[]{:S(2)}, u32[]{:S(2)}) collective-permute-start(bf16[8,64,512]{2,1,0:T(8,128)(2,1)S(1)} %get-tuple-element.228), channel_id=1, source_target_pairs={{0,32},{32,0},{64,96},{96,64},{128,160},{160,128},{192,224},{224,1... | collective-permute-start | bytes 1572872 | tf_op jit(solution)/shard_map/ppermute | solution.py:65
  593.3 4.9 collective-permute-start.19
  599.3 30.1 %all_to_all.196 = bf16[8,72,512]{2,1,0:T(8,128)(2,1)S(1)} all-to-all(bf16[8,72,512]{2,1,0:T(8,128)(2,1)S(1)} %pad_maximum_fusion.1), channel_id=1, replica_groups={{0,64,128,192,256,320,384,448},{32,96,160,224,288,352,416,480},{1,65,12..., dimensions={0} | all-to-all | bytes 1179648 | tf_op jit(solution)/shard_map/all_to_all | solution.py:398
  (121 shorter events, 66.8 us)
Async XLA Ops:
  0.6 32.1 %copy-start = (bf16[4,32,512]{2,1,0:T(8,128)(2,1)S(1)}, bf16[4,32,512]{2,1,0:T(8,128)(2,1)}, u32[]{:S(2)}) copy-start(bf16[4,32,512]{2,1,0:T(8,128)(2,1)} %param.5) | copy-start | bytes 393220
  0.6 34.9 %collective-permute-start = (bf16[4096,512]{1,0:T(8,128)(2,1)}, bf16[4096,512]{1,0:T(8,128)(2,1)}, u32[]{:S(2)}, u32[]{:S(2)}) collective-permute-start(bf16[4096,512]{1,0:T(8,128)(2,1)} %bitcast.1.args_0_), channel_id=1, source_target_pairs={{0,32},{32,0},{64,96},{96,64},{128,160},{160,128},{192,224},{224,1... | collective-permute-start | bytes 12582920 | tf_op jit(solution)/shard_map/ppermute | solution.py:65
  11.3 24.3 %all-to-all-start = ((bf16[8,64,512]{2,1,0:T(8,128)(2,1)}), bf16[8,64,512]{2,1,0:T(8,128)(2,1)S(1)}, u32[]{:S(2)}, u32[]{:S(2)}) async-start(bf16[8,64,512]{2,1,0:T(8,128)(2,1)} %broadcast_in_dim.78), calls=%async_computation | async-start | bytes 1048576 | tf_op jit(solution)/shard_map/all_to_all | solution.py:287
  17.4 12.0 %collective-permute-start.1 = (f32[1,4608]{1,0:T(1,128)S(1)}, f32[1,4608]{1,0:T(1,128)S(1)}, u32[]{:S(2)}, u32[]{:S(2)}) collective-permute-start(f32[1,4608]{1,0:T(1,128)S(1)} %pad_maximum_fusion.7), channel_id=1, source_target_pairs={{0,64},{32,96},{64,0},{96,32},{128,192},{160,224},{192,128},{224,1... | collective-permute-start | bytes 55304 | tf_op jit(solution)/shard_map/ppermute | solution.py:65
  20.8 12.0 %collective-permute-start.3 = (f32[1,4608]{1,0:T(1,128)S(1)}, f32[1,4608]{1,0:T(1,128)S(1)}, u32[]{:S(2)}, u32[]{:S(2)}) collective-permute-start(f32[1,4608]{1,0:T(1,128)S(1)} %pad_maximum_fusion.7), channel_id=1, source_target_pairs={{0,32},{32,0},{64,96},{96,64},{128,160},{160,128},{192,224},{224,1... | collective-permute-start | bytes 55304 | tf_op jit(solution)/shard_map/ppermute | solution.py:65
  29.4 6.2 collective-permute-start.2
  32.8 48.9 %collective-permute-start.4 = (bf16[4096,512]{1,0:T(8,128)(2,1)}, bf16[4096,512]{1,0:T(8,128)(2,1)}, u32[]{:S(2)}, u32[]{:S(2)}) collective-permute-start(bf16[4096,512]{1,0:T(8,128)(2,1)} %bitcast.1.args_0_), channel_id=1, source_target_pairs={{0,64},{64,0},{128,192},{192,128},{256,320},{320,256},{384,448},{4... | collective-permute-start | bytes 12582920 | tf_op jit(solution)/shard_map/ppermute | solution.py:293
  37.2 7.8 %copy-start.10 = (f32[1,4096]{1,0:T(1,128)S(1)}, f32[1,4096]{1,0:T(1,128)}, u32[]{:S(2)}) copy-start(f32[1,4096]{1,0:T(1,128)} %param.8) | copy-start | bytes 49156
  37.2 31.2 %all-to-all-start.1 = ((bf16[4,8,64,512]{3,2,1,0:T(8,128)(2,1)}), bf16[4,8,64,512]{3,2,1,0:T(8,128)(2,1)}, u32[]{:S(2)}, u32[]{:S(2)}) async-start(bf16[4,8,64,512]{3,2,1,0:T(8,128)(2,1)} %broadcast_in_dim.81), calls=%async_computation.1 | async-start | bytes 4194304 | tf_op jit(solution)/shard_map/all_to_all | solution.py:57
  41.8 5.1 collective-permute-start.5
  47.0 6.6 %collective-permute-start.6 = (bf16[2,32,512]{2,1,0:T(8,128)(2,1)S(1)}, bf16[2,32,512]{2,1,0:T(8,128)(2,1)S(1)}, u32[]{:S(2)}, u32[]{:S(2)}) collective-permute-start(bf16[2,32,512]{2,1,0:T(8,128)(2,1)S(1)} %pad_maximum_fusion.6), channel_id=1, source_target_pairs={{0,2},{1,3},{2,0},{3,1},{4,6},{5,7},{6,4},{7,5},{8,10},{9,11},{10,... | collective-permute-start | bytes 196616 | tf_op jit(solution)/shard_map/ppermute | solution.py:72
  53.7 12.3 %collective-permute-start.7 = (bf16[4,32,512]{2,1,0:T(8,128)(2,1)S(1)}, bf16[4,32,512]{2,1,0:T(8,128)(2,1)S(1)}, u32[]{:S(2)}, u32[]{:S(2)}) collective-permute-start(bf16[4,32,512]{2,1,0:T(8,128)(2,1)S(1)} %pad_maximum_fusion.3), channel_id=1, source_target_pairs={{0,4},{1,5},{2,6},{3,7},{4,0},{5,1},{6,2},{7,3},{8,12},{9,13},{10,... | collective-permute-start | bytes 393224 | tf_op jit(solution)/shard_map/ppermute | solution.py:72
  68.4 7.7 %collective-permute-start.8 = (bf16[4,8,64,512]{3,2,1,0:T(8,128)(2,1)}, bf16[4,8,64,512]{3,2,1,0:T(8,128)(2,1)}, u32[]{:S(2)}, u32[]{:S(2)}) collective-permute-start(bf16[4,8,64,512]{3,2,1,0:T(8,128)(2,1)} %all-to-all-done.1), channel_id=1, source_target_pairs={{0,32},{32,0},{64,96},{96,64},{128,160},{160,128},{192,224},{224,1... | collective-permute-start | bytes 6291464 | tf_op jit(solution)/shard_map/ppermute | solution.py:65
  79.5 2.2 copy-start.2
  81.7 17.9 %collective-permute-start.9 = (bf16[4096,512]{1,0:T(8,128)(2,1)}, bf16[4096,512]{1,0:T(8,128)(2,1)}, u32[]{:S(2)}, u32[]{:S(2)}) collective-permute-start(bf16[4096,512]{1,0:T(8,128)(2,1)} %collective-permute-done.4.args_2_.args_4_), channel_id=1, source_target_pairs={{0,32},{64,96},{128,160},{192,224},{256,288},{320,352},{384,416},{... | collective-permute-start | bytes 12582920 | tf_op jit(solution)/shard_map/ppermute | solution.py:345
  83.0 49.6 %collective-permute-start.10 = (bf16[4096,512]{1,0:T(8,128)(2,1)}, bf16[4096,512]{1,0:T(8,128)(2,1)}, u32[]{:S(2)}, u32[]{:S(2)}) collective-permute-start(bf16[4096,512]{1,0:T(8,128)(2,1)} %bitcast.1.args_0_), channel_id=1, source_target_pairs={{32,96},{96,32},{160,224},{224,160},{288,352},{352,288},{416,480},... | collective-permute-start | bytes 12582920 | tf_op jit(solution)/shard_map/ppermute | solution.py:307
  84.9 14.7 %all-to-all-start.2 = ((bf16[8,32,512]{2,1,0:T(8,128)(2,1)}), bf16[8,32,512]{2,1,0:T(8,128)(2,1)S(1)}, u32[]{:S(2)}, u32[]{:S(2)}) async-start(bf16[8,32,512]{2,1,0:T(8,128)(2,1)} %get-tuple-element.126), calls=%async_computation.2 | async-start | bytes 524288 | tf_op jit(solution)/shard_map/all_to_all | solution.py:57
  102.8 12.7 %all-to-all-start.3 = ((bf16[8,32,512]{2,1,0:T(8,128)(2,1)}), bf16[8,32,512]{2,1,0:T(8,128)(2,1)S(1)}, u32[]{:S(2)}, u32[]{:S(2)}) async-start(bf16[8,32,512]{2,1,0:T(8,128)(2,1)} %get-tuple-element.130), calls=%async_computation.3 | async-start | bytes 524288 | tf_op jit(solution)/shard_map/all_to_all | solution.py:57
  115.5 2.2 copy-start.3
  132.6 17.9 %collective-permute-start.11 = (bf16[4096,512]{1,0:T(8,128)(2,1)}, bf16[4096,512]{1,0:T(8,128)(2,1)}, u32[]{:S(2)}, u32[]{:S(2)}) collective-permute-start(bf16[4096,512]{1,0:T(8,128)(2,1)} %collective-permute-done.10.args_4_), channel_id=1, source_target_pairs={{32,0},{96,64},{160,128},{224,192},{288,256},{352,320},{416,384},{... | collective-permute-start | bytes 12582920 | tf_op jit(solution)/shard_map/ppermute | solution.py:349
  135.8 14.7 %all-to-all-start.4 = ((bf16[8,32,512]{2,1,0:T(8,128)(2,1)}), bf16[8,32,512]{2,1,0:T(8,128)(2,1)S(1)}, u32[]{:S(2)}, u32[]{:S(2)}) async-start(bf16[8,32,512]{2,1,0:T(8,128)(2,1)} %get-tuple-element.134), calls=%async_computation.4 | async-start | bytes 524288 | tf_op jit(solution)/shard_map/all_to_all | solution.py:57
  153.6 12.7 %all-to-all-start.5 = ((bf16[8,32,512]{2,1,0:T(8,128)(2,1)}), bf16[8,32,512]{2,1,0:T(8,128)(2,1)S(1)}, u32[]{:S(2)}, u32[]{:S(2)}) async-start(bf16[8,32,512]{2,1,0:T(8,128)(2,1)} %get-tuple-element.137), calls=%async_computation.5 | async-start | bytes 524288 | tf_op jit(solution)/shard_map/all_to_all | solution.py:57
  166.3 2.2 copy-start.4
  168.5 13.8 %copy-start.6 = (bf16[4096,512]{1,0:T(8,128)(2,1)S(1)}, bf16[4096,512]{1,0:T(8,128)(2,1)}, u32[]{:S(2)}) copy-start(bf16[4096,512]{1,0:T(8,128)(2,1)} %get-tuple-element.155.weight_ref) | copy-start | bytes 12582916
  182.3 13.1 %copy-start.5 = (bf16[8,2,4,64,512]{4,3,2,1,0:T(8,128)(2,1)S(1)}, bf16[8,2,4,64,512]{4,3,2,1,0:T(8,128)(2,1)}, u32[]{:S(2)}) copy-start(bf16[8,2,4,64,512]{4,3,2,1,0:T(8,128)(2,1)} %copy-done.2) | copy-start | bytes 12582916
  195.3 14.7 %copy-start.9 = (bf16[4096,512]{1,0:T(8,128)(2,1)S(1)}, bf16[4096,512]{1,0:T(8,128)(2,1)}, u32[]{:S(2)}) copy-start(bf16[4096,512]{1,0:T(8,128)(2,1)} %get-tuple-element.161.weight_ref) | copy-start | bytes 12582916
  211.6 3.9 collective-permute-start.12
  229.6 13.8 %copy-start.7 = (bf16[4096,512]{1,0:T(8,128)(2,1)S(1)}, bf16[4096,512]{1,0:T(8,128)(2,1)}, u32[]{:S(2)}) copy-start(bf16[4096,512]{1,0:T(8,128)(2,1)} %get-tuple-element.167.weight_ref) | copy-start | bytes 12582916
  256.3 13.3 %copy-start.8 = (bf16[4096,512]{1,0:T(8,128)(2,1)S(1)}, bf16[4096,512]{1,0:T(8,128)(2,1)}, u32[]{:S(2)}) copy-start(bf16[4096,512]{1,0:T(8,128)(2,1)} %get-tuple-element.172.weight_ref) | copy-start | bytes 12582916
  322.1 7.3 %collective-permute-start.13 = (bf16[32,512]{1,0:T(8,128)(2,1)S(1)}, bf16[32,512]{1,0:T(8,128)(2,1)S(1)}, u32[]{:S(2)}, u32[]{:S(2)}) collective-permute-start(bf16[32,512]{1,0:T(8,128)(2,1)S(1)} %get-tuple-element.184), channel_id=1, source_target_pairs={{0,128},{32,160},{64,192},{96,224},{128,256},{160,288},{192,320},{... | collective-permute-start | bytes 98312 | tf_op jit(solution)/shard_map/ppermute | solution.py:357
  439.8 5.8 collective-permute-start.14
  539.1 18.1 %collective-permute-start.17 = (bf16[1536,128]{1,0:T(8,128)(2,1)S(1)}, bf16[1536,128]{1,0:T(8,128)(2,1)S(1)}, u32[]{:S(2)}, u32[]{:S(2)}) collective-permute-start(bf16[1536,128]{1,0:T(8,128)(2,1)S(1)} %get-tuple-element.239), channel_id=1, source_target_pairs={{0,24},{8,0},{16,8},{24,16},{1,25},{9,1},{17,9},{25,17},{2,26},{10... | collective-permute-start | bytes 1179656 | tf_op jit(solution)/shard_map/ppermute | solution.py:379
  547.1 10.1 %collective-permute-start.16 = (bf16[1536,128]{1,0:T(8,128)(2,1)S(1)}, bf16[1536,128]{1,0:T(8,128)(2,1)S(1)}, u32[]{:S(2)}, u32[]{:S(2)}) collective-permute-start(bf16[1536,128]{1,0:T(8,128)(2,1)S(1)} %get-tuple-element.238), channel_id=1, source_target_pairs={{0,16},{8,24},{16,0},{24,8},{1,17},{9,25},{17,1},{25,9},{2,18},{10... | collective-permute-start | bytes 1179656 | tf_op jit(solution)/shard_map/ppermute | solution.py:379
  549.6 12.0 %collective-permute-start.15 = (bf16[1536,128]{1,0:T(8,128)(2,1)S(1)}, bf16[1536,128]{1,0:T(8,128)(2,1)S(1)}, u32[]{:S(2)}, u32[]{:S(2)}) collective-permute-start(bf16[1536,128]{1,0:T(8,128)(2,1)S(1)} %get-tuple-element.237), channel_id=1, source_target_pairs={{0,8},{8,16},{16,24},{24,0},{1,9},{9,17},{17,25},{25,1},{2,10},{10... | collective-permute-start | bytes 1179656 | tf_op jit(solution)/shard_map/ppermute | solution.py:379
  553.3 39.9 %all-to-all-start.32 = ((f32[32,8,128]{2,1,0:T(8,128)}), f32[32,8,128]{2,1,0:T(8,128)S(1)}, u32[]{:S(2)}, u32[]{:S(2)}) async-start(f32[32,8,128]{2,1,0:T(8,128)} %broadcast_in_dim_broadcast_in_dim_broadcast_in_dim.3), calls=%async_computation.32 | async-start | bytes 262144 | tf_op jit(solution)/shard_map/all_to_all | solution.py:57
  562.5 36.5 %collective-permute-start.18 = (bf16[8,64,512]{2,1,0:T(8,128)(2,1)S(1)}, bf16[8,64,512]{2,1,0:T(8,128)(2,1)S(1)}, u32[]{:S(2)}, u32[]{:S(2)}) collective-permute-start(bf16[8,64,512]{2,1,0:T(8,128)(2,1)S(1)} %get-tuple-element.228), channel_id=1, source_target_pairs={{0,32},{32,0},{64,96},{96,64},{128,160},{160,128},{192,224},{224,1... | collective-permute-start | bytes 1572872 | tf_op jit(solution)/shard_map/ppermute | solution.py:65
  593.3 5.7 collective-permute-start.19
  599.0 32.3 %copy-start.1 = (bf16[4,32,512]{2,1,0:T(8,128)(2,1)S(1)}, bf16[4,32,512]{2,1,0:T(8,128)(2,1)}, u32[]{:S(2)}) copy-start(bf16[4,32,512]{2,1,0:T(8,128)(2,1)} %param.5) | copy-start | bytes 393220

commit v13 on v12

--- a/solution.py
+++ b/solution.py
@@ -65,13 +65,15 @@
     return lax.ppermute(value, "section", [(i, i ^ mask) for i in range(lax.axis_size("section"))])
 
 
-def doubled(value):
+def doubled(value, after):
     count, position = lax.axis_size("tp"), lax.axis_index("tp")
     value, mask = value[None], 1
     while mask < count:
         other = lax.ppermute(value, "tp", [(i, i ^ mask) for i in range(count)])
         upper = position & mask != 0
         value = jnp.concatenate([jnp.where(upper, other, value), jnp.where(upper, value, other)], axis=0)
+        if mask == 1:
+            value, _ = lax.optimization_barrier((value, after))
         mask *= 2
     return value
 
@@ -297,8 +299,8 @@
 
     along_x = gather(along_z, "dp")
     stream = lax.dynamic_index_in_dim(hidden_in, place, 0, keepdims=False)
-    stream, _ = lax.optimization_barrier((stream, along_z))
-    first_rows = doubled(stream)
+    stream, _ = lax.optimization_barrier((stream, params_by1))
+    first_rows = doubled(stream, along_z)
     along_x, gains, scales, stream, first_rows = lax.optimization_barrier(
         (along_x, gains, scales, stream, first_rows)
     )

time: 635 us -> 633 us (level)
  transfers between devices with their start and end apart: 27 -> 27, of which waited for: 16 -> 17; matrix products, arithmetic and copies ran while one was open for 4% -> 4% of each run, Pallas kernels for 1% -> 1%
where the time goes in v13:
time: 633 us; the launch traced here: 631 us
  blocking collectives  357 us (56%)
  starting transfers between devices  139 us (22%)
  waiting for transfers between devices  59.7 us (9%)
  Pallas kernels  40.1 us (6%)
  other arithmetic  21.4 us (3%)
  local copies, waits for them, and re-layouts  10.8 us (2%)
    all_to_all x26, blocking collectives, exchange(): return lax.all_to_all(copies, axis, 0, 0, tiled=True)  322 us
    ppermute x7, starting transfers between devices, crossed(): lax.ppermute(value, 'section', [(i, i ^ mask) for i in range(lax.axis_siz...  57.6 us
    all_to_all x1, blocking collectives, local(): lax.all_to_all(sent, 'section', 0, 0, axis_index_groups=same_core, tiled=...  34.5 us
    all_to_all x6, waiting for transfers between devices, exchange(): return lax.all_to_all(copies, axis, 0, 0, tiled=True)  30.6 us
    all_to_all x6, starting transfers between devices, exchange(): return lax.all_to_all(copies, axis, 0, 0, tiled=True)  29.2 us
    pallas_call x16, Pallas kernels, rotate(): pl.pallas_call(functools.partial(rotate_kernel, layer, last), out_shape=s...  19.5 us
    ppermute x3, starting transfers between devices, doubled(): other = lax.ppermute(value, 'tp', [(i, i ^ mask) for i in range(count)])  16.7 us
    select_n x2, other arithmetic, local(): jnp.where(place // 2 == 0, far, near)  14 us
  transfers between devices with their start and end apart: 27, of which 17 were waited for; matrix products, arithmetic and copies ran while one was open for 4% of the time, Pallas kernels for 1%

profile of v13, /device:TPU:1, one launch (start us, length us, event | category | flops | bytes accessed | tf_op | source)
XLA Modules:
  0.0 630.8 jit_solution(12382914988546845786)
XLA Ops:
  0.6 8.9 %collective-permute-start = (bf16[4096,512]{1,0:T(8,128)(2,1)}, bf16[4096,512]{1,0:T(8,128)(2,1)}, u32[]{:S(2)}, u32[]{:S(2)}) collective-permute-start(bf16[4096,512]{1,0:T(8,128)(2,1)} %bitcast.1.args_0_), channel_id=1, source_target_pairs={{0,32},{32,0},{64,96},{96,64},{128,160},{160,128},{192,224},{224,1... | collective-permute-start | bytes 12582920 | tf_op jit(solution)/shard_map/ppermute | solution.py:65
  11.3 4.7 all-to-all-start
  20.5 3.2 collective-permute-start.5
  23.7 3.6 collective-permute-start.1
  27.3 2.7 collective-permute-start.4
  30.0 2.7 collective-permute-start.2
  35.6 4.6 all-to-all-start.1
  40.2 4.2 collective-permute-start.6
  46.6 9.3 %collective-permute-start.7 = (bf16[4,32,512]{2,1,0:T(8,128)(2,1)S(1)}, bf16[4,32,512]{2,1,0:T(8,128)(2,1)S(1)}, u32[]{:S(2)}, u32[]{:S(2)}) collective-permute-start(bf16[4,32,512]{2,1,0:T(8,128)(2,1)S(1)} %pad_maximum_fusion.3), channel_id=1, source_target_pairs={{0,4},{1,5},{2,6},{3,7},{4,0},{5,1},{6,2},{7,3},{8,12},{9,13},{10,... | collective-permute-start | bytes 393224 | tf_op jit(solution)/shard_map/ppermute | solution.py:72
  56.0 2.8 collective-permute-done.7
  58.8 7.4 %all-to-all-done.1 = bf16[4,8,64,512]{3,2,1,0:T(8,128)(2,1)} async-done(((bf16[4,8,64,512]{3,2,1,0:T(8,128)(2,1)}), bf16[4,8,64,512]{3,2,1,0:T(8,128)(2,1)}, u32[]{:S(2)}, u32[]{:S(2)}) %all-to-all-start.1) | async-done | bytes 2097184 | tf_op jit(solution)/shard_map/all_to_all | solution.py:57
  66.2 3.3 collective-permute-start.8
  69.6 4.0 collective-permute-done.8
  73.6 2.5 select_bitcast_fusion.1
  80.5 2.6 collective-permute-start.10
  83.1 6.2 all-to-all-start.2
  89.3 9.3 %all-to-all-done.2.args_6_ = bf16[8,32,512]{2,1,0:T(8,128)(2,1)S(1)} async-done(((bf16[8,32,512]{2,1,0:T(8,128)(2,1)}), bf16[8,32,512]{2,1,0:T(8,128)(2,1)S(1)}, u32[]{:S(2)}, u32[]{:S(2)}) %all-to-all-start.2) | async-done | bytes 262176 | tf_op jit(solution)/shard_map/all_to_all | solution.py:57
  98.6 3.1 project_from.2
  101.7 3.4 all-to-all-start.3
  105.2 8.0 %broadcast_select_fusion.6 = (bf16[4096,512]{1,0:T(8,128)(2,1)}, bf16[4096,512]{1,0:T(8,128)(2,1)}) fusion(pred[]{:T(512)S(6)} %eq.50, bf16[4096,512]{1,0:T(8,128)(2,1)} %collective-permute-done.args_1_, pred[]{:T(512)S(6)} %eq.49, bf16[4096,512]{1,0:T(8,128)(2,1)} %collective-permute-done.4.args_2_.args_4_, ...), kind=kLoop, calls=%fused_computation.7 | loop fusion | flops 8388608 | bytes 25165826 | tf_op jit(solution)/shard_map/jit(_where)/select_n | solution.py:336
  118.5 11.5 %collective-permute-done.10.args_4_ = bf16[4096,512]{1,0:T(8,128)(2,1)} collective-permute-done((bf16[4096,512]{1,0:T(8,128)(2,1)}, bf16[4096,512]{1,0:T(8,128)(2,1)}, u32[]{:S(2)}, u32[]{:S(2)}) %collective-permute-start.10) | collective-permute-done | bytes 4194336 | tf_op jit(solution)/shard_map/ppermute | solution.py:309
  130.1 3.2 collective-permute-start.11
  133.3 6.8 %all-to-all-start.4 = ((bf16[8,32,512]{2,1,0:T(8,128)(2,1)}), bf16[8,32,512]{2,1,0:T(8,128)(2,1)S(1)}, u32[]{:S(2)}, u32[]{:S(2)}) async-start(bf16[8,32,512]{2,1,0:T(8,128)(2,1)} %get-tuple-element.136), calls=%async_computation.4 | async-start | bytes 524288 | tf_op jit(solution)/shard_map/all_to_all | solution.py:57
  140.1 9.3 %all-to-all-done.4.args_6_ = bf16[8,32,512]{2,1,0:T(8,128)(2,1)S(1)} async-done(((bf16[8,32,512]{2,1,0:T(8,128)(2,1)}), bf16[8,32,512]{2,1,0:T(8,128)(2,1)S(1)}, u32[]{:S(2)}, u32[]{:S(2)}) %all-to-all-start.4) | async-done | bytes 262176 | tf_op jit(solution)/shard_map/all_to_all | solution.py:57
  149.5 3.2 project_from.3
  152.6 3.4 all-to-all-start.5
  156.0 6.0 broadcast_select_fusion.4
  162.0 3.3 all-to-all-done.5.rows_ref
  168.7 12.6 %all_to_all.170.quant_ref = bf16[8,32,512]{2,1,0:T(8,128)(2,1)S(1)} all-to-all(bf16[8,32,512]{2,1,0:T(8,128)(2,1)S(1)} %get-tuple-element.156), channel_id=1, replica_groups=mesh['section'=16,'dp'=4,'tp'=8] {'tp'}, dimensions={0} | all-to-all | bytes 524288 | tf_op jit(solution)/shard_map/all_to_all | solution.py:57
  182.1 12.2 %all_to_all.171.rows_ref = bf16[8,32,512]{2,1,0:T(8,128)(2,1)S(1)} all-to-all(bf16[8,32,512]{2,1,0:T(8,128)(2,1)S(1)} %get-tuple-element.159), channel_id=1, replica_groups=mesh['section'=16,'dp'=4,'tp'=8] {'tp'}, dimensions={0} | all-to-all | bytes 524288 | tf_op jit(solution)/shard_map/all_to_all | solution.py:57
  195.5 13.5 %all_to_all.172.quant_ref = bf16[8,32,512]{2,1,0:T(8,128)(2,1)S(1)} all-to-all(bf16[8,32,512]{2,1,0:T(8,128)(2,1)S(1)} %get-tuple-element.162), channel_id=1, replica_groups=mesh['section'=16,'dp'=4,'tp'=8] {'tp'}, dimensions={0} | all-to-all | bytes 524288 | tf_op jit(solution)/shard_map/all_to_all | solution.py:57
  210.6 2.7 collective-permute-start.12
  214.3 14.1 %all_to_all.173.rows_ref = bf16[8,32,512]{2,1,0:T(8,128)(2,1)S(1)} all-to-all(bf16[8,32,512]{2,1,0:T(8,128)(2,1)S(1)} %spread.3), channel_id=1, replica_groups=mesh['section'=16,'dp'=4,'tp'=8] {'tp'}, dimensions={0} | all-to-all | bytes 524288 | tf_op jit(solution)/shard_map/all_to_all | solution.py:57
  229.5 12.7 %all_to_all.174.quant_ref = bf16[8,32,512]{2,1,0:T(8,128)(2,1)S(1)} all-to-all(bf16[8,32,512]{2,1,0:T(8,128)(2,1)S(1)} %get-tuple-element.168), channel_id=1, replica_groups=mesh['section'=16,'dp'=4,'tp'=8] {'tp'}, dimensions={0} | all-to-all | bytes 524288 | tf_op jit(solution)/shard_map/all_to_all | solution.py:57
  243.0 12.1 %all_to_all.175.rows_ref = bf16[8,32,512]{2,1,0:T(8,128)(2,1)S(1)} all-to-all(bf16[8,32,512]{2,1,0:T(8,128)(2,1)S(1)} %get-tuple-element.170), channel_id=1, replica_groups=mesh['section'=16,'dp'=4,'tp'=8] {'tp'}, dimensions={0} | all-to-all | bytes 524288 | tf_op jit(solution)/shard_map/all_to_all | solution.py:57
  256.2 12.1 %all_to_all.176.quant_ref = bf16[8,32,512]{2,1,0:T(8,128)(2,1)S(1)} all-to-all(bf16[8,32,512]{2,1,0:T(8,128)(2,1)S(1)} %get-tuple-element.173), channel_id=1, replica_groups=mesh['section'=16,'dp'=4,'tp'=8] {'tp'}, dimensions={0} | all-to-all | bytes 524288 | tf_op jit(solution)/shard_map/all_to_all | solution.py:57
  269.2 11.8 %all_to_all.177.rows_ref = bf16[8,32,512]{2,1,0:T(8,128)(2,1)S(1)} all-to-all(bf16[8,32,512]{2,1,0:T(8,128)(2,1)S(1)} %get-tuple-element.176), channel_id=1, replica_groups=mesh['section'=16,'dp'=4,'tp'=8] {'tp'}, dimensions={0} | all-to-all | bytes 524288 | tf_op jit(solution)/shard_map/all_to_all | solution.py:57
  282.2 11.7 %all_to_all.178.quant_ref = bf16[8,32,512]{2,1,0:T(8,128)(2,1)S(1)} all-to-all(bf16[8,32,512]{2,1,0:T(8,128)(2,1)S(1)} %get-tuple-element.179), channel_id=1, replica_groups=mesh['section'=16,'dp'=4,'tp'=8] {'tp'}, dimensions={0} | all-to-all | bytes 524288 | tf_op jit(solution)/shard_map/all_to_all | solution.py:57
  294.7 11.7 %all_to_all.179.rows_ref = bf16[8,32,512]{2,1,0:T(8,128)(2,1)S(1)} all-to-all(bf16[8,32,512]{2,1,0:T(8,128)(2,1)S(1)} %get-tuple-element.181), channel_id=1, replica_groups=mesh['section'=16,'dp'=4,'tp'=8] {'tp'}, dimensions={0} | all-to-all | bytes 524288 | tf_op jit(solution)/shard_map/all_to_all | solution.py:57
  307.6 11.7 %all_to_all.180.quant_ref = bf16[8,32,512]{2,1,0:T(8,128)(2,1)S(1)} all-to-all(bf16[8,32,512]{2,1,0:T(8,128)(2,1)S(1)} %get-tuple-element.184), channel_id=1, replica_groups=mesh['section'=16,'dp'=4,'tp'=8] {'tp'}, dimensions={0} | all-to-all | bytes 524288 | tf_op jit(solution)/shard_map/all_to_all | solution.py:57
  320.9 5.6 collective-permute-start.13
  327.5 11.7 %all_to_all.181.rows_ref = bf16[8,32,512]{2,1,0:T(8,128)(2,1)S(1)} all-to-all(bf16[8,32,512]{2,1,0:T(8,128)(2,1)S(1)} %spread.4), channel_id=1, replica_groups=mesh['section'=16,'dp'=4,'tp'=8] {'tp'}, dimensions={0} | all-to-all | bytes 524288 | tf_op jit(solution)/shard_map/all_to_all | solution.py:57
  340.3 12.0 %all_to_all.182.quant_ref = bf16[8,32,512]{2,1,0:T(8,128)(2,1)S(1)} all-to-all(bf16[8,32,512]{2,1,0:T(8,128)(2,1)S(1)} %get-tuple-element.189), channel_id=1, replica_groups=mesh['section'=16,'dp'=4,'tp'=8] {'tp'}, dimensions={0} | all-to-all | bytes 524288 | tf_op jit(solution)/shard_map/all_to_all | solution.py:57
  353.2 13.5 %all_to_all.183.rows_ref = bf16[8,32,512]{2,1,0:T(8,128)(2,1)S(1)} all-to-all(bf16[8,32,512]{2,1,0:T(8,128)(2,1)S(1)} %get-tuple-element.190), channel_id=1, replica_groups=mesh['section'=16,'dp'=4,'tp'=8] {'tp'}, dimensions={0} | all-to-all | bytes 524288 | tf_op jit(solution)/shard_map/all_to_all | solution.py:57
  367.8 14.8 %all_to_all.184.quant_ref = bf16[8,32,512]{2,1,0:T(8,128)(2,1)S(1)} all-to-all(bf16[8,32,512]{2,1,0:T(8,128)(2,1)S(1)} %get-tuple-element.193), channel_id=1, replica_groups=mesh['section'=16,'dp'=4,'tp'=8] {'tp'}, dimensions={0} | all-to-all | bytes 524288 | tf_op jit(solution)/shard_map/all_to_all | solution.py:57
  383.5 13.4 %all_to_all.185.rows_ref = bf16[8,32,512]{2,1,0:T(8,128)(2,1)S(1)} all-to-all(bf16[8,32,512]{2,1,0:T(8,128)(2,1)S(1)} %get-tuple-element.195), channel_id=1, replica_groups=mesh['section'=16,'dp'=4,'tp'=8] {'tp'}, dimensions={0} | all-to-all | bytes 524288 | tf_op jit(solution)/shard_map/all_to_all | solution.py:57
  398.0 12.2 %all_to_all.186.quant_ref = bf16[8,32,512]{2,1,0:T(8,128)(2,1)S(1)} all-to-all(bf16[8,32,512]{2,1,0:T(8,128)(2,1)S(1)} %get-tuple-element.198), channel_id=1, replica_groups=mesh['section'=16,'dp'=4,'tp'=8] {'tp'}, dimensions={0} | all-to-all | bytes 524288 | tf_op jit(solution)/shard_map/all_to_all | solution.py:57
  411.1 12.2 %all_to_all.187.rows_ref = bf16[8,32,512]{2,1,0:T(8,128)(2,1)S(1)} all-to-all(bf16[8,32,512]{2,1,0:T(8,128)(2,1)S(1)} %get-tuple-element.200), channel_id=1, replica_groups=mesh['section'=16,'dp'=4,'tp'=8] {'tp'}, dimensions={0} | all-to-all | bytes 524288 | tf_op jit(solution)/shard_map/all_to_all | solution.py:57
  424.4 11.9 %all_to_all.188.quant_ref = bf16[8,32,512]{2,1,0:T(8,128)(2,1)S(1)} all-to-all(bf16[8,32,512]{2,1,0:T(8,128)(2,1)S(1)} %get-tuple-element.203), channel_id=1, replica_groups=mesh['section'=16,'dp'=4,'tp'=8] {'tp'}, dimensions={0} | all-to-all | bytes 524288 | tf_op jit(solution)/shard_map/all_to_all | solution.py:57
  437.9 4.8 collective-permute-start.14
  443.8 13.3 %all_to_all.189.rows_ref = bf16[8,32,512]{2,1,0:T(8,128)(2,1)S(1)} all-to-all(bf16[8,32,512]{2,1,0:T(8,128)(2,1)S(1)} %spread.5), channel_id=1, replica_groups=mesh['section'=16,'dp'=4,'tp'=8] {'tp'}, dimensions={0} | all-to-all | bytes 524288 | tf_op jit(solution)/shard_map/all_to_all | solution.py:57
  458.2 11.7 %all_to_all.190.quant_ref = bf16[8,32,512]{2,1,0:T(8,128)(2,1)S(1)} all-to-all(bf16[8,32,512]{2,1,0:T(8,128)(2,1)S(1)} %get-tuple-element.208), channel_id=1, replica_groups=mesh['section'=16,'dp'=4,'tp'=8] {'tp'}, dimensions={0} | all-to-all | bytes 524288 | tf_op jit(solution)/shard_map/all_to_all | solution.py:57
  470.8 11.7 %all_to_all.191.rows_ref = bf16[8,32,512]{2,1,0:T(8,128)(2,1)S(1)} all-to-all(bf16[8,32,512]{2,1,0:T(8,128)(2,1)S(1)} %get-tuple-element.209), channel_id=1, replica_groups=mesh['section'=16,'dp'=4,'tp'=8] {'tp'}, dimensions={0} | all-to-all | bytes 524288 | tf_op jit(solution)/shard_map/all_to_all | solution.py:57
  483.6 11.7 %all_to_all.192.quant_ref = bf16[8,32,512]{2,1,0:T(8,128)(2,1)S(1)} all-to-all(bf16[8,32,512]{2,1,0:T(8,128)(2,1)S(1)} %get-tuple-element.212), channel_id=1, replica_groups=mesh['section'=16,'dp'=4,'tp'=8] {'tp'}, dimensions={0} | all-to-all | bytes 524288 | tf_op jit(solution)/shard_map/all_to_all | solution.py:57
  496.2 11.7 %all_to_all.193.rows_ref = bf16[8,32,512]{2,1,0:T(8,128)(2,1)S(1)} all-to-all(bf16[8,32,512]{2,1,0:T(8,128)(2,1)S(1)} %get-tuple-element.214), channel_id=1, replica_groups=mesh['section'=16,'dp'=4,'tp'=8] {'tp'}, dimensions={0} | all-to-all | bytes 524288 | tf_op jit(solution)/shard_map/all_to_all | solution.py:57
  509.1 11.7 %all_to_all.194.quant_ref = bf16[8,32,512]{2,1,0:T(8,128)(2,1)S(1)} all-to-all(bf16[8,32,512]{2,1,0:T(8,128)(2,1)S(1)} %get-tuple-element.217), channel_id=1, replica_groups=mesh['section'=16,'dp'=4,'tp'=8] {'tp'}, dimensions={0} | all-to-all | bytes 524288 | tf_op jit(solution)/shard_map/all_to_all | solution.py:57
  522.3 11.8 %all_to_all.195.rows_ref = bf16[8,32,512]{2,1,0:T(8,128)(2,1)S(1)} all-to-all(bf16[8,32,512]{2,1,0:T(8,128)(2,1)S(1)} %get-tuple-element.219), channel_id=1, replica_groups=mesh['section'=16,'dp'=4,'tp'=8] {'tp'}, dimensions={0} | all-to-all | bytes 524288 | tf_op jit(solution)/shard_map/all_to_all | solution.py:57
  537.1 2.8 collective-permute-start.17
  539.9 3.1 collective-permute-start.16
  546.2 4.8 all-to-all-start.32
  551.0 3.1 collective-permute-done.15
  555.1 30.1 %collective-permute-start.18 = (bf16[8,64,512]{2,1,0:T(8,128)(2,1)S(1)}, bf16[8,64,512]{2,1,0:T(8,128)(2,1)S(1)}, u32[]{:S(2)}, u32[]{:S(2)}) collective-permute-start(bf16[8,64,512]{2,1,0:T(8,128)(2,1)S(1)} %get-tuple-element.230), channel_id=1, source_target_pairs={{0,32},{32,0},{64,96},{96,64},{128,160},{160,128},{192,224},{224,1... | collective-permute-start | bytes 1572872 | tf_op jit(solution)/shard_map/ppermute | solution.py:65
  585.3 6.7 %collective-permute-start.19 = (f32[8,128]{1,0:T(8,128)S(1)}, f32[8,128]{1,0:T(8,128)S(1)}, u32[]{:S(2)}, u32[]{:S(2)}) collective-permute-start(f32[8,128]{1,0:T(8,128)S(1)} %reduce_sum.37), channel_id=1, source_target_pairs={{0,32},{32,0},{64,96},{96,64},{128,160},{160,128},{192,224},{224,1... | collective-permute-start | bytes 12296 | tf_op jit(solution)/shard_map/ppermute | solution.py:65
  593.1 34.5 %all_to_all.196 = bf16[8,72,512]{2,1,0:T(8,128)(2,1)S(1)} all-to-all(bf16[8,72,512]{2,1,0:T(8,128)(2,1)S(1)} %pad_maximum_fusion.1), channel_id=1, replica_groups={{0,64,128,192,256,320,384,448},{32,96,160,224,288,352,416,480},{1,65,12..., dimensions={0} | all-to-all | bytes 1179648 | tf_op jit(solution)/shard_map/all_to_all | solution.py:400
  (121 shorter events, 64.0 us)
Async XLA Ops:
  0.6 19.0 %copy-start = (bf16[4,32,512]{2,1,0:T(8,128)(2,1)S(1)}, bf16[4,32,512]{2,1,0:T(8,128)(2,1)}, u32[]{:S(2)}) copy-start(bf16[4,32,512]{2,1,0:T(8,128)(2,1)} %param.5) | copy-start | bytes 393220
  0.6 33.3 %collective-permute-start = (bf16[4096,512]{1,0:T(8,128)(2,1)}, bf16[4096,512]{1,0:T(8,128)(2,1)}, u32[]{:S(2)}, u32[]{:S(2)}) collective-permute-start(bf16[4096,512]{1,0:T(8,128)(2,1)} %bitcast.1.args_0_), channel_id=1, source_target_pairs={{0,32},{32,0},{64,96},{96,64},{128,160},{160,128},{192,224},{224,1... | collective-permute-start | bytes 12582920 | tf_op jit(solution)/shard_map/ppermute | solution.py:65
  11.3 22.7 %all-to-all-start = ((bf16[8,64,512]{2,1,0:T(8,128)(2,1)}), bf16[8,64,512]{2,1,0:T(8,128)(2,1)S(1)}, u32[]{:S(2)}, u32[]{:S(2)}) async-start(bf16[8,64,512]{2,1,0:T(8,128)(2,1)} %broadcast_in_dim.78), calls=%async_computation | async-start | bytes 1048576 | tf_op jit(solution)/shard_map/all_to_all | solution.py:289
  17.4 3.1 collective-permute-start.3
  20.5 12.3 %collective-permute-start.5 = (bf16[1,32,512]{2,1,0:T(8,128)(2,1)S(1)}, bf16[1,32,512]{2,1,0:T(8,128)(2,1)S(1)}, u32[]{:S(2)}, u32[]{:S(2)}) collective-permute-start(bf16[1,32,512]{2,1,0:T(8,128)(2,1)S(1)} %bitcast.61), channel_id=1, source_target_pairs={{0,1},{1,0},{2,3},{3,2},{4,5},{5,4},{6,7},{7,6},{8,9},{9,8},{10,11... | collective-permute-start | bytes 98312 | tf_op jit(solution)/shard_map/ppermute | solution.py:72
  23.7 6.3 %collective-permute-start.1 = (f32[1,4608]{1,0:T(1,128)S(1)}, f32[1,4608]{1,0:T(1,128)S(1)}, u32[]{:S(2)}, u32[]{:S(2)}) collective-permute-start(f32[1,4608]{1,0:T(1,128)S(1)} %pad_maximum_fusion.7), channel_id=1, source_target_pairs={{0,64},{32,96},{64,0},{96,32},{128,192},{160,224},{192,128},{224,1... | collective-permute-start | bytes 55304 | tf_op jit(solution)/shard_map/ppermute | solution.py:65
  27.3 51.9 %collective-permute-start.4 = (bf16[4096,512]{1,0:T(8,128)(2,1)}, bf16[4096,512]{1,0:T(8,128)(2,1)}, u32[]{:S(2)}, u32[]{:S(2)}) collective-permute-start(bf16[4096,512]{1,0:T(8,128)(2,1)} %bitcast.1.args_0_), channel_id=1, source_target_pairs={{0,64},{64,0},{128,192},{192,128},{256,320},{320,256},{384,448},{4... | collective-permute-start | bytes 12582920 | tf_op jit(solution)/shard_map/ppermute | solution.py:295
  30.0 3.6 collective-permute-start.2
  35.6 8.8 %copy-start.10 = (f32[1,4096]{1,0:T(1,128)S(1)}, f32[1,4096]{1,0:T(1,128)}, u32[]{:S(2)}) copy-start(f32[1,4096]{1,0:T(1,128)} %param.8) | copy-start | bytes 49156
  35.6 30.6 %all-to-all-start.1 = ((bf16[4,8,64,512]{3,2,1,0:T(8,128)(2,1)}), bf16[4,8,64,512]{3,2,1,0:T(8,128)(2,1)}, u32[]{:S(2)}, u32[]{:S(2)}) async-start(bf16[4,8,64,512]{3,2,1,0:T(8,128)(2,1)} %broadcast_in_dim.81), calls=%async_computation.1 | async-start | bytes 4194304 | tf_op jit(solution)/shard_map/all_to_all | solution.py:57
  40.2 6.3 %collective-permute-start.6 = (bf16[2,32,512]{2,1,0:T(8,128)(2,1)S(1)}, bf16[2,32,512]{2,1,0:T(8,128)(2,1)S(1)}, u32[]{:S(2)}, u32[]{:S(2)}) collective-permute-start(bf16[2,32,512]{2,1,0:T(8,128)(2,1)S(1)} %pad_maximum_fusion.6), channel_id=1, source_target_pairs={{0,2},{1,3},{2,0},{3,1},{4,6},{5,7},{6,4},{7,5},{8,10},{9,11},{10,... | collective-permute-start | bytes 196616 | tf_op jit(solution)/shard_map/ppermute | solution.py:72
  46.6 12.2 %collective-permute-start.7 = (bf16[4,32,512]{2,1,0:T(8,128)(2,1)S(1)}, bf16[4,32,512]{2,1,0:T(8,128)(2,1)S(1)}, u32[]{:S(2)}, u32[]{:S(2)}) collective-permute-start(bf16[4,32,512]{2,1,0:T(8,128)(2,1)S(1)} %pad_maximum_fusion.3), channel_id=1, source_target_pairs={{0,4},{1,5},{2,6},{3,7},{4,0},{5,1},{6,2},{7,3},{8,12},{9,13},{10,... | collective-permute-start | bytes 393224 | tf_op jit(solution)/shard_map/ppermute | solution.py:72
  66.2 7.4 %collective-permute-start.8 = (bf16[4,8,64,512]{3,2,1,0:T(8,128)(2,1)}, bf16[4,8,64,512]{3,2,1,0:T(8,128)(2,1)}, u32[]{:S(2)}, u32[]{:S(2)}) collective-permute-start(bf16[4,8,64,512]{3,2,1,0:T(8,128)(2,1)} %all-to-all-done.1), channel_id=1, source_target_pairs={{0,32},{32,0},{64,96},{96,64},{128,160},{160,128},{192,224},{224,1... | collective-permute-start | bytes 6291464 | tf_op jit(solution)/shard_map/ppermute | solution.py:65
  77.0 2.2 copy-start.2
  79.2 19.4 %collective-permute-start.9 = (bf16[4096,512]{1,0:T(8,128)(2,1)}, bf16[4096,512]{1,0:T(8,128)(2,1)}, u32[]{:S(2)}, u32[]{:S(2)}) collective-permute-start(bf16[4096,512]{1,0:T(8,128)(2,1)} %collective-permute-done.4.args_2_.args_4_), channel_id=1, source_target_pairs={{0,32},{64,96},{128,160},{192,224},{256,288},{320,352},{384,416},{... | collective-permute-start | bytes 12582920 | tf_op jit(solution)/shard_map/ppermute | solution.py:347
  80.5 49.6 %collective-permute-start.10 = (bf16[4096,512]{1,0:T(8,128)(2,1)}, bf16[4096,512]{1,0:T(8,128)(2,1)}, u32[]{:S(2)}, u32[]{:S(2)}) collective-permute-start(bf16[4096,512]{1,0:T(8,128)(2,1)} %bitcast.1.args_0_), channel_id=1, source_target_pairs={{32,96},{96,32},{160,224},{224,160},{288,352},{352,288},{416,480},... | collective-permute-start | bytes 12582920 | tf_op jit(solution)/shard_map/ppermute | solution.py:309
  83.1 15.5 %all-to-all-start.2 = ((bf16[8,32,512]{2,1,0:T(8,128)(2,1)}), bf16[8,32,512]{2,1,0:T(8,128)(2,1)S(1)}, u32[]{:S(2)}, u32[]{:S(2)}) async-start(bf16[8,32,512]{2,1,0:T(8,128)(2,1)} %get-tuple-element.128), calls=%async_computation.2 | async-start | bytes 524288 | tf_op jit(solution)/shard_map/all_to_all | solution.py:57
  101.7 12.7 %all-to-all-start.3 = ((bf16[8,32,512]{2,1,0:T(8,128)(2,1)}), bf16[8,32,512]{2,1,0:T(8,128)(2,1)S(1)}, u32[]{:S(2)}, u32[]{:S(2)}) async-start(bf16[8,32,512]{2,1,0:T(8,128)(2,1)} %get-tuple-element.132), calls=%async_computation.3 | async-start | bytes 524288 | tf_op jit(solution)/shard_map/all_to_all | solution.py:57
  114.4 2.2 copy-start.3
  130.1 19.4 %collective-permute-start.11 = (bf16[4096,512]{1,0:T(8,128)(2,1)}, bf16[4096,512]{1,0:T(8,128)(2,1)}, u32[]{:S(2)}, u32[]{:S(2)}) collective-permute-start(bf16[4096,512]{1,0:T(8,128)(2,1)} %collective-permute-done.10.args_4_), channel_id=1, source_target_pairs={{32,0},{96,64},{160,128},{224,192},{288,256},{352,320},{416,384},{... | collective-permute-start | bytes 12582920 | tf_op jit(solution)/shard_map/ppermute | solution.py:351
  133.3 16.2 %all-to-all-start.4 = ((bf16[8,32,512]{2,1,0:T(8,128)(2,1)}), bf16[8,32,512]{2,1,0:T(8,128)(2,1)S(1)}, u32[]{:S(2)}, u32[]{:S(2)}) async-start(bf16[8,32,512]{2,1,0:T(8,128)(2,1)} %get-tuple-element.136), calls=%async_computation.4 | async-start | bytes 524288 | tf_op jit(solution)/shard_map/all_to_all | solution.py:57
  152.6 12.7 %all-to-all-start.5 = ((bf16[8,32,512]{2,1,0:T(8,128)(2,1)}), bf16[8,32,512]{2,1,0:T(8,128)(2,1)S(1)}, u32[]{:S(2)}, u32[]{:S(2)}) async-start(bf16[8,32,512]{2,1,0:T(8,128)(2,1)} %get-tuple-element.139), calls=%async_computation.5 | async-start | bytes 524288 | tf_op jit(solution)/shard_map/all_to_all | solution.py:57
  165.3 2.2 copy-start.4
  167.5 13.8 %copy-start.6 = (bf16[4096,512]{1,0:T(8,128)(2,1)S(1)}, bf16[4096,512]{1,0:T(8,128)(2,1)}, u32[]{:S(2)}) copy-start(bf16[4096,512]{1,0:T(8,128)(2,1)} %get-tuple-element.157.weight_ref) | copy-start | bytes 12582916
  181.2 13.1 %copy-start.5 = (bf16[8,2,4,64,512]{4,3,2,1,0:T(8,128)(2,1)S(1)}, bf16[8,2,4,64,512]{4,3,2,1,0:T(8,128)(2,1)}, u32[]{:S(2)}) copy-start(bf16[8,2,4,64,512]{4,3,2,1,0:T(8,128)(2,1)} %copy-done.2) | copy-start | bytes 12582916
  194.3 14.7 %copy-start.9 = (bf16[4096,512]{1,0:T(8,128)(2,1)S(1)}, bf16[4096,512]{1,0:T(8,128)(2,1)}, u32[]{:S(2)}) copy-start(bf16[4096,512]{1,0:T(8,128)(2,1)} %get-tuple-element.163.weight_ref) | copy-start | bytes 12582916
  210.6 3.7 collective-permute-start.12
  228.4 13.8 %copy-start.7 = (bf16[4096,512]{1,0:T(8,128)(2,1)S(1)}, bf16[4096,512]{1,0:T(8,128)(2,1)}, u32[]{:S(2)}) copy-start(bf16[4096,512]{1,0:T(8,128)(2,1)} %get-tuple-element.169.weight_ref) | copy-start | bytes 12582916
  255.1 13.3 %copy-start.8 = (bf16[4096,512]{1,0:T(8,128)(2,1)S(1)}, bf16[4096,512]{1,0:T(8,128)(2,1)}, u32[]{:S(2)}) copy-start(bf16[4096,512]{1,0:T(8,128)(2,1)} %get-tuple-element.174.weight_ref) | copy-start | bytes 12582916
  320.9 6.6 %collective-permute-start.13 = (bf16[32,512]{1,0:T(8,128)(2,1)S(1)}, bf16[32,512]{1,0:T(8,128)(2,1)S(1)}, u32[]{:S(2)}, u32[]{:S(2)}) collective-permute-start(bf16[32,512]{1,0:T(8,128)(2,1)S(1)} %get-tuple-element.186), channel_id=1, source_target_pairs={{0,128},{32,160},{64,192},{96,224},{128,256},{160,288},{192,320},{... | collective-permute-start | bytes 98312 | tf_op jit(solution)/shard_map/ppermute | solution.py:359
  437.9 5.9 collective-permute-start.14
  537.1 13.9 %collective-permute-start.17 = (bf16[1536,128]{1,0:T(8,128)(2,1)S(1)}, bf16[1536,128]{1,0:T(8,128)(2,1)S(1)}, u32[]{:S(2)}, u32[]{:S(2)}) collective-permute-start(bf16[1536,128]{1,0:T(8,128)(2,1)S(1)} %get-tuple-element.241), channel_id=1, source_target_pairs={{0,24},{8,0},{16,8},{24,16},{1,25},{9,1},{17,9},{25,17},{2,26},{10... | collective-permute-start | bytes 1179656 | tf_op jit(solution)/shard_map/ppermute | solution.py:381
  539.9 11.1 %collective-permute-start.16 = (bf16[1536,128]{1,0:T(8,128)(2,1)S(1)}, bf16[1536,128]{1,0:T(8,128)(2,1)S(1)}, u32[]{:S(2)}, u32[]{:S(2)}) collective-permute-start(bf16[1536,128]{1,0:T(8,128)(2,1)S(1)} %get-tuple-element.240), channel_id=1, source_target_pairs={{0,16},{8,24},{16,0},{24,8},{1,17},{9,25},{17,1},{25,9},{2,18},{10... | collective-permute-start | bytes 1179656 | tf_op jit(solution)/shard_map/ppermute | solution.py:381
  543.0 11.2 %collective-permute-start.15 = (bf16[1536,128]{1,0:T(8,128)(2,1)S(1)}, bf16[1536,128]{1,0:T(8,128)(2,1)S(1)}, u32[]{:S(2)}, u32[]{:S(2)}) collective-permute-start(bf16[1536,128]{1,0:T(8,128)(2,1)S(1)} %get-tuple-element.239), channel_id=1, source_target_pairs={{0,8},{8,16},{16,24},{24,0},{1,9},{9,17},{17,25},{25,1},{2,10},{10... | collective-permute-start | bytes 1179656 | tf_op jit(solution)/shard_map/ppermute | solution.py:381
  546.2 39.0 %all-to-all-start.32 = ((f32[32,8,128]{2,1,0:T(8,128)}), f32[32,8,128]{2,1,0:T(8,128)S(1)}, u32[]{:S(2)}, u32[]{:S(2)}) async-start(f32[32,8,128]{2,1,0:T(8,128)} %broadcast_in_dim_broadcast_in_dim_broadcast_in_dim.3), calls=%async_computation.32 | async-start | bytes 262144 | tf_op jit(solution)/shard_map/all_to_all | solution.py:57
  555.1 37.8 %collective-permute-start.18 = (bf16[8,64,512]{2,1,0:T(8,128)(2,1)S(1)}, bf16[8,64,512]{2,1,0:T(8,128)(2,1)S(1)}, u32[]{:S(2)}, u32[]{:S(2)}) collective-permute-start(bf16[8,64,512]{2,1,0:T(8,128)(2,1)S(1)} %get-tuple-element.230), channel_id=1, source_target_pairs={{0,32},{32,0},{64,96},{96,64},{128,160},{160,128},{192,224},{224,1... | collective-permute-start | bytes 1572872 | tf_op jit(solution)/shard_map/ppermute | solution.py:65
  585.3 7.6 %collective-permute-start.19 = (f32[8,128]{1,0:T(8,128)S(1)}, f32[8,128]{1,0:T(8,128)S(1)}, u32[]{:S(2)}, u32[]{:S(2)}) collective-permute-start(f32[8,128]{1,0:T(8,128)S(1)} %reduce_sum.37), channel_id=1, source_target_pairs={{0,32},{32,0},{64,96},{96,64},{128,160},{160,128},{192,224},{224,1... | collective-permute-start | bytes 12296 | tf_op jit(solution)/shard_map/ppermute | solution.py:65
  592.8 36.8 %copy-start.1 = (bf16[4,32,512]{2,1,0:T(8,128)(2,1)S(1)}, bf16[4,32,512]{2,1,0:T(8,128)(2,1)}, u32[]{:S(2)}) copy-start(bf16[4,32,512]{2,1,0:T(8,128)(2,1)} %param.5) | copy-start | bytes 393220
